TPU v7x, 256 devices: a whole 4x4x8 slice. The times are simulated.
256 devices in a mesh: section: 2 (over core), row: 16 (over z, x_lo), col: 8 (over y, x_hi).
Axes of the slice: x: 4 (x_hi: 2, x_lo: 2; x = x_hi * 2 + x_lo), y: 4, z: 8, core: 2. Of those that a mesh axis runs over, the one named last changes fastest.
Arguments:
- inputs: bfloat16 [2, 128, 6144], P(None, None, 'row'), may hold values from -6 to 6
- cotangent: bfloat16 [2, 128, 6144], P(None, None, 'row'), may hold values from -1.5 to 1.5
- w_up: bfloat16 [2, 6144, 24576], P('section', 'row', 'col'), may hold values from -0.078125 to 0.078125
- w_down: bfloat16 [2, 24576, 6144], P('section', 'col', 'row'), may hold values from -0.0390625 to 0.0390625
Outputs:
- states: bfloat16 [2, 2, 128, 6144], P('section', None, 'col', 'row')
- input_grads: bfloat16 [2, 2, 128, 6144], P('section', None, 'col', 'row')
- w_up_grad: float32 [2, 6144, 24576], P('section', 'row', 'col')
- w_down_grad: float32 [2, 24576, 6144], P('section', 'col', 'row')
All inputs are finite; a program needn't handle non-finite values.
Results may differ from a plain program's by a relative error of at most 0.009.
Values may be sent and summed in bfloat16 or wider, within the bound.
No kernel may reach another device: no remote copies, remote signals or barrier semaphores. Data moves between devices by JAX's collectives and lax.ppermute only.
A program may use at most 64 MiB of HBM per device.

v0:
```python
import jax
import jax.numpy as jnp
from jax import lax
from jax.sharding import PartitionSpec as P

root_two_over_pi = 0.7978845608028654
cubic = 0.044715


def from_behind(block, axis, distance):
    devices = range(lax.axis_size(axis))
    route = [(i - distance, i) for i in devices if i - distance in devices]
    return lax.ppermute(block, axis, route)


def gelu_value(pre):
    inner = root_two_over_pi * (pre + cubic * pre * pre * pre)
    return 0.5 * pre * (1.0 + jnp.tanh(inner))


def gelu_slope(pre):
    inner = root_two_over_pi * (pre + cubic * pre * pre * pre)
    tangent = jnp.tanh(inner)
    return 0.5 * (1.0 + tangent) + 0.5 * pre * (1.0 - tangent * tangent) * root_two_over_pi * (
        1.0 + 3.0 * cubic * pre * pre
    )


def contract_rows(left, right):
    return lax.dot_general(
        left, right, (((0,), (0,)), ((), ())), preferred_element_type=jnp.float32
    )


def contract_cols(left, right):
    return lax.dot_general(
        left, right, (((1,), (1,)), ((), ())), preferred_element_type=jnp.float32
    )


def local(inputs, cotangent, w_up, w_down):
    col_count = lax.axis_size("col")
    layers = lax.axis_size("section")
    batches = inputs.shape[0]
    mb_tokens = inputs.shape[1]
    up_shard = w_up[0]
    down_shard = w_down[0]
    layer = lax.axis_index("section")
    col_pos = lax.axis_index("col")
    ticks = batches + layers - 1
    out_len = mb_tokens // col_count
    out_start = col_pos * out_len
    width_rows = inputs.shape[2]
    unit_cols = up_shard.shape[1]

    def finish(base, partial_value):
        total = lax.psum(partial_value, "col")
        return (base.astype(jnp.float32) + total).astype(jnp.bfloat16)

    carried = jnp.zeros_like(inputs[0])
    saved_in = []
    saved_pre = []
    states_out = jnp.zeros((batches, out_len, width_rows), jnp.bfloat16)
    for tick in range(ticks):
        index = tick - layer
        valid = (index >= 0) & (index < batches)
        clipped = jnp.clip(index, 0, batches - 1)
        fresh = lax.dynamic_index_in_dim(inputs, clipped, 0, keepdims=False)
        current = jnp.where(layer == 0, fresh, carried)
        pre = lax.psum_scatter(
            jnp.dot(current, up_shard, preferred_element_type=jnp.float32),
            "row",
            scatter_dimension=0,
            tiled=True,
        )
        hidden = gelu_value(pre).astype(jnp.bfloat16)
        partial_value = jnp.dot(
            lax.all_gather(hidden, "row", axis=0, tiled=True),
            down_shard,
            preferred_element_type=jnp.float32,
        )
        result = finish(current, partial_value)
        saved_in.append(current)
        saved_pre.append(pre)
        piece = lax.dynamic_slice_in_dim(result, out_start, out_len, 0)
        states_out = jnp.where(
            valid, lax.dynamic_update_index_in_dim(states_out, piece, clipped, 0), states_out
        )
        if tick + 1 < ticks:
            carried = from_behind(result, "section", 1)
    stacked_in = jnp.stack(saved_in)
    stacked_pre = jnp.stack(saved_pre)
    carried = jnp.zeros_like(cotangent[0])
    grad_up = jnp.zeros((width_rows, unit_cols), jnp.float32)
    grad_down = jnp.zeros((unit_cols, width_rows), jnp.float32)
    grads_out = jnp.zeros((batches, out_len, width_rows), jnp.bfloat16)
    for tick in range(ticks):
        index = tick - (layers - 1 - layer)
        valid = (index >= 0) & (index < batches)
        clipped = jnp.clip(index, 0, batches - 1)
        fresh = lax.dynamic_index_in_dim(cotangent, clipped, 0, keepdims=False)
        grad_in = jnp.where(layer == layers - 1, fresh, carried)
        forward_tick = clipped + layer
        current = lax.dynamic_index_in_dim(stacked_in, forward_tick, 0, keepdims=False)
        pre = lax.dynamic_index_in_dim(stacked_pre, forward_tick, 0, keepdims=False)
        masked_grad = jnp.where(valid, grad_in, jnp.zeros_like(grad_in))
        masked_in = jnp.where(valid, current, jnp.zeros_like(current))
        d_hidden = lax.psum_scatter(
            contract_cols(grad_in, down_shard), "row", scatter_dimension=0, tiled=True
        )
        d_pre = (d_hidden * gelu_slope(pre)).astype(jnp.bfloat16)
        hidden = gelu_value(pre).astype(jnp.bfloat16)
        grad_down = grad_down + contract_rows(
            lax.all_gather(hidden, "row", axis=0, tiled=True), masked_grad
        )
        empty = jnp.zeros((mb_tokens, width_rows), jnp.float32)
        add_piece = lax.all_gather(d_pre, "row", axis=0, tiled=True)
        part = contract_cols(add_piece, up_shard)
        summed = (empty, grad_up)[1] + contract_rows(masked_in, add_piece)
        grad_up = summed
        result = finish(grad_in, part)
        piece = lax.dynamic_slice_in_dim(result, out_start, out_len, 0)
        grads_out = jnp.where(
            valid, lax.dynamic_update_index_in_dim(grads_out, piece, clipped, 0), grads_out
        )
        if tick + 1 < ticks:
            carried = from_behind(result, "section", -1)
    return (states_out[None], grads_out[None], grad_up[None], grad_down[None])


def solution(mesh):
    in_specs = (
        P(None, None, "row"),
        P(None, None, "row"),
        P("section", "row", "col"),
        P("section", "col", "row"),
    )
    out_specs = (
        P("section", None, "col", "row"),
        P("section", None, "col", "row"),
        P("section", "row", "col"),
        P("section", "col", "row"),
    )
    return jax.shard_map(local, mesh=mesh, in_specs=in_specs, out_specs=out_specs, check_vma=False)
```

profile of v0, /device:TPU:1, one launch (start us, length us, event | category | flops | bytes accessed | tf_op | source)
XLA Modules:
  0.0 1189.8 jit_solution(17641397138557369180)
XLA Ops:
  7.2 1.1 dynamic-slice_select_fusion.1
  8.9 3.4 fusion.22
  12.4 65.6 %reduce-scatter.7.cloned.1.call-done = f32[8,3072]{1,0:T(8,128)} async-done(((f32[128,3072]{1,0:T(8,128)}), f32[8,3072]{1,0:T(8,128)}) %reduce-scatter.7.cloned.1.call-update) | async-done | bytes 98320 | tf_op jit(solution)/shard_map/reduce_scatter | solution.py:70
  78.9 30.0 %all_gather.27 = bf16[128,3072]{1,0:T(8,128)(2,1)S(1)} all-gather(bf16[8,3072]{1,0:T(8,128)(2,1)S(1)} %fusion.28), channel_id=1, replica_groups=mesh['section'=2,'row'=16,'col'=8] {'row'}, dimensions={0}, use_global_device_ids=true | all-gather | bytes 835584 | tf_op jit(solution)/shard_map/all_gather | solution.py:78
  108.9 1.3 fusion.10
  110.3 100.5 %all-reduce.7.cloned.1.call-done = f32[128,384]{1,0:T(8,128)} async-done(((f32[128,384]{1,0:T(8,128)}), f32[128,384]{1,0:T(8,128)}) %all-reduce.7.cloned.1.call-update) | async-done | bytes 196624 | tf_op jit(solution)/shard_map/psum | solution.py:57
  211.7 1.3 collective-permute-start
  213.0 6.7 collective-permute-done
  219.7 3.4 fusion.20
  223.2 59.1 %reduce-scatter.9.cloned.1.call-done = f32[8,3072]{1,0:T(8,128)} async-done(((f32[128,3072]{1,0:T(8,128)}), f32[8,3072]{1,0:T(8,128)}) %reduce-scatter.9.cloned.1.call-update) | async-done | bytes 98320 | tf_op jit(solution)/shard_map/reduce_scatter | solution.py:70
  283.3 29.8 %all_gather.28 = bf16[128,3072]{1,0:T(8,128)(2,1)S(1)} all-gather(bf16[8,3072]{1,0:T(8,128)(2,1)S(1)} %fusion.33), channel_id=1, replica_groups=mesh['section'=2,'row'=16,'col'=8] {'row'}, dimensions={0}, use_global_device_ids=true | all-gather | bytes 835584 | tf_op jit(solution)/shard_map/all_gather | solution.py:78
  313.1 1.3 fusion.8
  314.5 100.7 %all-reduce.9.cloned.1.call-done = f32[128,384]{1,0:T(8,128)} async-done(((f32[128,384]{1,0:T(8,128)}), f32[128,384]{1,0:T(8,128)}) %all-reduce.9.cloned.1.call-update) | async-done | bytes 196624 | tf_op jit(solution)/shard_map/psum | solution.py:57
  416.1 1.3 collective-permute-start.1
  417.4 6.7 collective-permute-done.1
  424.7 3.4 fusion.18
  428.3 2.0 fusion.4
  430.4 56.9 %reduce-scatter.11.cloned.1.call-done = f32[8,3072]{1,0:T(8,128)} async-done(((f32[128,3072]{1,0:T(8,128)}), f32[8,3072]{1,0:T(8,128)}) %reduce-scatter.11.cloned.1.call-update) | async-done | bytes 98320 | tf_op jit(solution)/shard_map/reduce_scatter | solution.py:70
  488.2 74.5 %reduce-scatter.13.cloned.1.call-done = f32[8,3072]{1,0:T(8,128)} async-done(((f32[128,3072]{1,0:T(8,128)}), f32[8,3072]{1,0:T(8,128)}) %reduce-scatter.13.cloned.1.call-update) | async-done | bytes 98320 | tf_op jit(solution)/shard_map/reduce_scatter | solution.py:108
  562.6 1.7 multiply_convert_fusion
  564.3 29.5 %all_gather.30 = bf16[128,3072]{1,0:T(8,128)(2,1)S(1)} all-gather(bf16[8,3072]{1,0:T(8,128)(2,1)S(1)} %get-tuple-element.7), channel_id=1, replica_groups=mesh['section'=2,'row'=16,'col'=8] {'row'}, dimensions={0}, use_global_device_ids=true | all-gather | bytes 835584 | tf_op jit(solution)/shard_map/all_gather | solution.py:117
  593.8 3.2 fusion.16
  597.0 100.6 %all-reduce.11.cloned.1.call-done = f32[128,384]{1,0:T(8,128)} async-done(((f32[128,384]{1,0:T(8,128)}), f32[128,384]{1,0:T(8,128)}) %all-reduce.11.cloned.1.call-update) | async-done | bytes 196624 | tf_op jit(solution)/shard_map/psum | solution.py:57
  697.7 1.0 add_convert_fusion.1
  698.7 7.8 collective-permute-start.2
  708.4 2.0 fusion.2
  713.1 1.8 pad_maximum_fusion.1
  714.9 1.5 fusion.38
  716.4 53.6 %reduce-scatter.15.cloned.1.call-done = f32[8,3072]{1,0:T(8,128)} async-done(((f32[128,3072]{1,0:T(8,128)}), f32[8,3072]{1,0:T(8,128)}) %reduce-scatter.15.cloned.1.call-update) | async-done | bytes 98320 | tf_op jit(solution)/shard_map/reduce_scatter | solution.py:108
  771.0 29.4 %all_gather.31 = bf16[128,3072]{1,0:T(8,128)(2,1)S(1)} all-gather(bf16[8,3072]{1,0:T(8,128)(2,1)S(1)} %fusion.52), channel_id=1, replica_groups=mesh['section'=2,'row'=16,'col'=8] {'row'}, dimensions={0}, use_global_device_ids=true | all-gather | bytes 835584 | tf_op jit(solution)/shard_map/all_gather | solution.py:117
  801.3 3.2 fusion.14
  804.6 30.4 %all_gather.29 = bf16[128,3072]{1,0:T(8,128)(2,1)} all-gather(bf16[8,3072]{1,0:T(8,128)(2,1)} %fusion.38), channel_id=1, replica_groups=mesh['section'=2,'row'=16,'col'=8] {'row'}, dimensions={0}, use_global_device_ids=true | all-gather | bytes 835584 | tf_op jit(solution)/shard_map/all_gather | solution.py:78
  835.0 71.6 %all-reduce.13.cloned.1.call-done = f32[128,384]{1,0:T(8,128)} async-done(((f32[128,384]{1,0:T(8,128)}), f32[128,384]{1,0:T(8,128)}) %all-reduce.13.cloned.1.call-update) | async-done | bytes 196624 | tf_op jit(solution)/shard_map/psum | solution.py:57
  907.6 8.0 collective-permute-start.3
  915.5 3.9 fusion.65
  920.1 2.1 fusion
  922.3 1.3 fusion.6
  923.6 42.3 %all_gather.33 = bf16[128,3072]{1,0:T(8,128)(2,1)S(1)} all-gather(bf16[8,3072]{1,0:T(8,128)(2,1)S(1)} %copy-done.20), channel_id=1, replica_groups=mesh['section'=2,'row'=16,'col'=8] {'row'}, dimensions={0}, use_global_device_ids=true | all-gather | bytes 835584 | tf_op jit(solution)/shard_map/all_gather | solution.py:114
  966.7 38.8 %all_gather.34 = bf16[128,3072]{1,0:T(8,128)(2,1)S(1)} all-gather(bf16[8,3072]{1,0:T(8,128)(2,1)S(1)} %copy-done.19), channel_id=1, replica_groups=mesh['section'=2,'row'=16,'col'=8] {'row'}, dimensions={0}, use_global_device_ids=true | all-gather | bytes 835584 | tf_op jit(solution)/shard_map/all_gather | solution.py:114
  1005.5 28.6 %all_gather.35 = bf16[128,3072]{1,0:T(8,128)(2,1)S(1)} all-gather(bf16[8,3072]{1,0:T(8,128)(2,1)S(1)} %copy-done.18), channel_id=1, replica_groups=mesh['section'=2,'row'=16,'col'=8] {'row'}, dimensions={0}, use_global_device_ids=true | all-gather | bytes 835584 | tf_op jit(solution)/shard_map/all_gather | solution.py:114
  1036.0 2.9 fusion.63
  1040.3 3.0 add_bitcast_fusion
  1043.3 1.0 fusion.59
  1044.3 28.5 %all_gather.32 = bf16[128,3072]{1,0:T(8,128)(2,1)S(1)} all-gather(bf16[8,3072]{1,0:T(8,128)(2,1)S(1)} %fusion.59), channel_id=1, replica_groups=mesh['section'=2,'row'=16,'col'=8] {'row'}, dimensions={0}, use_global_device_ids=true | all-gather | bytes 835584 | tf_op jit(solution)/shard_map/all_gather | solution.py:117
  1072.8 3.2 fusion.12
  1076.0 6.8 add_bitcast_fusion.1
  1082.8 99.0 %all-reduce.15.cloned.1.call-done = (f32[128,384]{1,0:T(8,128)}, f32[128,384]{1,0:T(8,128)}) async-done(((f32[128,384]{1,0:T(8,128)}, f32[128,384]{1,0:T(8,128)}), (f32[128,384]{1,0:T(8,128)}, f32[128,384]{1,0:T(8,128)})) %all-reduce.15.cloned.1.call-update) | async-done | bytes 393232 | tf_op jit(solution)/shard_map/psum | solution.py:57
  1181.8 1.4 fusion.97
  (96 shorter events, 18.6 us)
Async XLA Ops:
  7.2 101.8 %copy-start = (bf16[1,3072,384]{2,1,0:T(8,128)(2,1)S(1)}, bf16[1,3072,384]{2,1,0:T(8,128)(2,1)}, u32[]{:S(2)}) copy-start(bf16[1,3072,384]{2,1,0:T(8,128)(2,1)} %param.7) | copy-start | bytes 7077892
  7.2 70.8 %reduce-scatter.7.cloned.1.call-start = ((), (), s32[]{:S(2)}) async-start(), calls=%async_computation.6 | async-start | bytes 1671168 | tf_op jit(solution)/shard_map/reduce_scatter | solution.py:70
  8.3 0.6 copy-start.12
  12.3 198.4 %copy-start.13 = (bf16[2,128,384]{2,1,0:T(8,128)(2,1)S(1)}, bf16[2,128,384]{2,1,0:T(8,128)(2,1)}, u32[]{:S(2)}) copy-start(bf16[2,128,384]{2,1,0:T(8,128)(2,1)} %param.4) | copy-start | bytes 589828
  12.4 198.4 %all-reduce.7.cloned.1.call-start = ((), (), s32[]{:S(2)}) async-start(), calls=%async_computation.7 | async-start | bytes 393216 | tf_op jit(solution)/shard_map/psum | solution.py:57
  110.2 172.2 %reduce-scatter.9.cloned.1.call-start = ((), (), s32[]{:S(2)}) async-start(), calls=%async_computation.8 | async-start | bytes 1671168 | tf_op jit(solution)/shard_map/reduce_scatter | solution.py:70
  211.7 1.3 copy-start.21
  211.7 8.0 collective-permute-start
  219.7 195.4 %copy-start.4 = (bf16[128,384]{1,0:T(8,128)(2,1)}, bf16[128,384]{1,0:T(8,128)(2,1)S(1)}, u32[]{:S(2)}) copy-start(bf16[128,384]{1,0:T(8,128)(2,1)S(1)} %bitcast_select_fusion.3) | copy-start | bytes 294916
  223.2 192.0 %all-reduce.9.cloned.1.call-start = ((), (), s32[]{:S(2)}) async-start(), calls=%async_computation.9 | async-start | bytes 393216 | tf_op jit(solution)/shard_map/psum | solution.py:57
  314.4 172.9 %reduce-scatter.11.cloned.1.call-start = ((), (), s32[]{:S(2)}) async-start(), calls=%async_computation.10 | async-start | bytes 1671168 | tf_op jit(solution)/shard_map/reduce_scatter | solution.py:70
  416.1 12.1 %copy-start.22 = (bf16[128,384]{1,0:T(8,128)(2,1)}, bf16[128,384]{1,0:T(8,128)(2,1)S(1)}, u32[]{:S(2)}) copy-start(bf16[128,384]{1,0:T(8,128)(2,1)S(1)} %add_convert_fusion.2) | copy-start | bytes 294916
  416.1 8.0 collective-permute-start.1
  424.1 0.6 copy-start.11
  424.7 3.5 copy-start.5
  428.2 134.4 %reduce-scatter.13.cloned.1.call-start = ((), (), s32[]{:S(2)}) async-start(), calls=%async_computation.11 | async-start | bytes 1671168 | tf_op jit(solution)/shard_map/reduce_scatter | solution.py:108
  428.3 59.0 %copy-start.14 = (f32[8,3072]{1,0:T(8,128)S(1)}, f32[8,3072]{1,0:T(8,128)}, u32[]{:S(2)}) copy-start(f32[8,3072]{1,0:T(8,128)} %reduce-scatter.7.cloned.1.call-done) | copy-start | bytes 294916
  428.3 59.0 %copy-start.15 = (f32[8,3072]{1,0:T(8,128)S(1)}, f32[8,3072]{1,0:T(8,128)}, u32[]{:S(2)}) copy-start(f32[8,3072]{1,0:T(8,128)} %reduce-scatter.9.cloned.1.call-done) | copy-start | bytes 294916
  430.3 267.3 %all-reduce.11.cloned.1.call-start = ((), (), s32[]{:S(2)}) async-start(), calls=%async_computation.12 | async-start | bytes 393216 | tf_op jit(solution)/shard_map/psum | solution.py:57
  597.0 173.1 %reduce-scatter.15.cloned.1.call-start = ((), (), s32[]{:S(2)}) async-start(), calls=%async_computation.13 | async-start | bytes 1671168 | tf_op jit(solution)/shard_map/reduce_scatter | solution.py:108
  698.7 7.8 copy-start.23
  698.7 8.8 collective-permute-start.2
  710.4 196.2 %all-reduce.13.cloned.1.call-start = ((), (), s32[]{:S(2)}) async-start(), calls=%async_computation.14 | async-start | bytes 393216 | tf_op jit(solution)/shard_map/psum | solution.py:57
  711.9 0.6 copy-start.17
  800.5 0.9 copy-start.1
  804.5 238.8 %reduce-scatter.17.cloned.1.call-start = ((), (), s32[]{:S(2)}) async-start(), calls=%async_computation.15 | async-start | bytes 1671168 | tf_op jit(solution)/shard_map/reduce_scatter | solution.py:108
  907.6 11.9 copy-start.24
  907.6 11.9 copy-start.6
  907.6 11.8 collective-permute-start.3
  919.5 0.6 copy-start.9
  920.1 2.2 copy-start.3
  922.2 259.6 %all-reduce.15.cloned.1.call-start = ((), (), s32[]{:S(2)}) async-start(), calls=%async_computation.16 | async-start | bytes 786432 | tf_op jit(solution)/shard_map/psum | solution.py:57
  922.3 1.3 copy-start.20
  922.3 43.6 %copy-start.7 = (bf16[2,128,384]{2,1,0:T(8,128)(2,1)S(1)}, bf16[2,128,384]{2,1,0:T(8,128)(2,1)}, u32[]{:S(2)}) copy-start(bf16[2,128,384]{2,1,0:T(8,128)(2,1)} %param.5) | copy-start | bytes 589828
  965.9 0.8 copy-start.19
  965.9 39.6 %copy-start.18 = (bf16[8,3072]{1,0:T(8,128)(2,1)S(1)}, bf16[8,3072]{1,0:T(8,128)(2,1)}, u32[]{:S(2)}) copy-start(bf16[8,3072]{1,0:T(8,128)(2,1)} %get-tuple-element.6) | copy-start | bytes 147460
  1034.8 1.1 copy-start.2
  1034.8 1.2 copy-start.8
  1036.0 4.3 copy-start.10
  1039.7 3.6 copy-start.16
Sparse Core Ops, SparseCore 0:
  12.5 65.4 reduce-scatter.6
  110.3 100.3 all-reduce.6
  223.3 59.0 reduce-scatter.8
  314.5 100.5 all-reduce.8
  428.3 58.9 reduce-scatter.10
  490.4 72.2 reduce-scatter.12
  597.1 100.4 all-reduce.10
  710.5 59.5 reduce-scatter.14
  804.7 101.8 all-reduce.12
  922.3 68.6 reduce-scatter.16
  1076.2 105.6 all-reduce.14
where the time goes:
time: 1200 us; the launch traced here: 1190 us
  waiting for transfers between devices  797 us (66%)
  blocking collectives  287 us (24%)
  matrix products  47.8 us (4%)
  other arithmetic  19.9 us (2%)
  starting transfers between devices  18.8 us (2%)
  between operations  14.2 us (1%)
    psum x5, waiting for transfers between devices, finish(): total = lax.psum(partial_value, 'col')  472 us
    all_gather x6, blocking collectives, local(): lax.all_gather(hidden, 'row', axis=0, tiled=True)  200 us
    reduce_scatter x3, waiting for transfers between devices, local(): lax.psum_scatter(jnp.dot(current, up_shard, preferred_element_type=jnp.fl...  182 us
    reduce_scatter x3, waiting for transfers between devices, local(): lax.psum_scatter(contract_cols(grad_in, down_shard), 'row', scatter_dimen...  128 us
    all_gather x3, blocking collectives, local(): add_piece = lax.all_gather(d_pre, 'row', axis=0, tiled=True)  87.5 us
  transfers between devices with their start and end apart: 15, of which 13 were waited for; matrix products, arithmetic and copies ran while one was open for 3% of the time, Pallas kernels for 0%

commit v1 on v0

v1 whole, which is shorter than its diff:
```python
import functools

import jax
import jax.numpy as jnp
from jax import lax
from jax.experimental import pallas as pl
from jax.experimental.pallas import tpu as pltpu
from jax.sharding import Mesh, PartitionSpec as P

root_two_over_pi = 0.7978845608028654
cubic = 0.044715
f32 = jnp.float32
bf16 = jnp.bfloat16
CHUNK = 512
VMEM = pl.BlockSpec(memory_space=pltpu.VMEM)
HBM = pl.BlockSpec(memory_space=pltpu.HBM)
ANY = pl.BlockSpec(memory_space=pl.ANY)
LIMIT = pltpu.CompilerParams(vmem_limit_bytes=14 * 1024 * 1024)


def gelu_both(pre):
    inner = root_two_over_pi * (pre + cubic * pre * pre * pre)
    tangent = jnp.tanh(inner)
    value = 0.5 * pre * (1.0 + tangent)
    slope = 0.5 * (1.0 + tangent) + 0.5 * pre * (1.0 - tangent * tangent) * root_two_over_pi * (
        1.0 + 3.0 * cubic * pre * pre
    )
    return value, slope


def dot(left, right, dims):
    return lax.dot_general(left, right, (dims, ((), ())), preferred_element_type=f32)


def shape_of(shape, dtype=bf16):
    return jax.ShapeDtypeStruct(shape, dtype)


def load_weights(layer, by_rows, refs, held, sems):
    mine = lax.axis_index("section") == layer

    def copy(source, part, i):
        where = pl.ds(i * CHUNK, CHUNK)
        block = source.at[where, :] if by_rows else source.at[:, where]
        return pltpu.make_async_copy(block, held.at[part, i], sems.at[part, i])

    def start(which):
        for i in range(held.shape[1]):
            for part, pair in enumerate(refs):
                copy(pair[which], part, i).start()

    pl.when(mine)(lambda: start(0))
    pl.when(jnp.logical_not(mine))(lambda: start(1))
    return lambda part, i: copy(refs[part][0], part, i).wait()


def widen(xs, by_rows, wait, held, put):
    for i in range(held.shape[1]):
        total = None
        for part, x in enumerate(xs):
            wait(part, i)
            got = dot(x, held[part, i], ((1,), (1 if by_rows else 0,)))
            total = got if total is None else total + got
        put(i, total)


def widen_first_kernel(layer, by_rows, x_ref, own, other, out_ref, held, sems, stage, out_sems):
    wait = load_weights(layer, by_rows, ((own, other),), held, sems)
    per_half = stage.shape[4] // CHUNK

    def out_copy(half):
        return pltpu.make_async_copy(stage.at[:, half], out_ref.at[:, half], out_sems.at[half])

    def put(i, total):
        half, at = i // per_half, (i % per_half) * CHUNK
        total = total.astype(stage.dtype).reshape(stage.shape[2], stage.shape[0], stage.shape[3], CHUNK)
        for mate in range(stage.shape[2]):
            stage[:, half, mate, :, pl.ds(at, CHUNK)] = total[mate]
        if i % per_half == per_half - 1:
            out_copy(half).start()

    widen((x_ref[...],), by_rows, wait, held, put)
    out_copy(0).wait()
    out_copy(1).wait()


def widen_next_kernel(
    layer, by_rows, arrived, base, own, other, own_mate, other_mate, out_ref, x_out, held, sems, stage, out_sems
):
    wait = load_weights(layer, by_rows, ((own, other), (own_mate, other_mate)), held, sems)
    width, per_half = base.shape[1] // 2, stage.shape[3] // CHUNK
    total = arrived[0].astype(f32)
    for i in range(1, arrived.shape[0]):
        total = total + arrived[i].astype(f32)
    x = (base[...].astype(f32) + total).astype(bf16)
    x_out[...] = x

    def out_copy(half):
        return pltpu.make_async_copy(stage.at[:, half], out_ref.at[:, half], out_sems.at[half])

    def put(i, total):
        half, at = i // per_half, (i % per_half) * CHUNK
        stage[:, half, :, pl.ds(at, CHUNK)] = total.astype(bf16).reshape(stage.shape[0], stage.shape[2], CHUNK)
        if i % per_half == per_half - 1:
            out_copy(half).start()

    widen((x[:, :width], x[:, width:]), by_rows, wait, held, put)
    out_copy(0).wait()
    out_copy(1).wait()


def narrow(by_rows, which, arrived, wait, held):
    per_half = arrived.shape[4] // CHUNK
    totals = [None, None]
    for i in range(held.shape[1]):
        left = arrived[:, i // per_half, which, :, pl.ds((i % per_half) * CHUNK, CHUNK)]
        left = left.reshape(left.shape[0] * left.shape[1], CHUNK)
        for part in range(2):
            wait(part, i)
            got = dot(left, held[part, i], ((1,), (0 if by_rows else 1,)))
            totals[part] = got if i == 0 else totals[part] + got
    return [total.astype(bf16) for total in totals]


def narrow_kernel(
    layer, by_rows, which, arrived, own, other, own_mate, other_mate, out_ref, held, sems, stage, out_sems
):
    wait = load_weights(layer, by_rows, ((own, other), (own_mate, other_mate)), held, sems)
    near, far = narrow(by_rows, which, arrived, wait, held)
    width = near.shape[1]
    stage[:, :width] = near
    stage[:, width:] = far
    copies = [
        pltpu.make_async_copy(stage, out_ref.at[i], out_sems.at[i]) for i in range(out_ref.shape[0])
    ]
    for copy in copies:
        copy.start()
    for copy in copies:
        copy.wait()


def narrow_last_kernel(
    layer, by_rows, arrived, own, other, own_mate, other_mate, beside, out_ref, held, sems, stage, out_sems
):
    wait = load_weights(layer, by_rows, ((own, other), (own_mate, other_mate)), held, sems)
    near, far = narrow(by_rows, 0, arrived, wait, held)
    width = near.shape[1]
    groups, _, tokens, _ = stage.shape
    stage[:, 0] = beside[...].reshape(groups, tokens, 2 * width)
    stage[:, 1, :, :width] = near.reshape(groups, tokens, width)
    stage[:, 1, :, width:] = far.reshape(groups, tokens, width)
    copies = [pltpu.make_async_copy(stage, out_ref.at[i], out_sems.at[i]) for i in range(2)]
    for copy in copies:
        copy.start()
    for copy in copies:
        copy.wait()


def held_scratch(weight, by_rows, parts):
    units = max(weight.shape)
    chunk = (CHUNK, weight.shape[1]) if by_rows else (weight.shape[0], CHUNK)
    return [
        pltpu.VMEM((parts, units // CHUNK) + chunk, bf16),
        pltpu.SemaphoreType.DMA((parts, units // CHUNK)),
    ]


def kernel_call(body, outs, out_specs, in_specs, scratch, operands, flops=0, moved=0):
    return pl.pallas_call(
        body,
        out_shape=outs,
        in_specs=in_specs,
        out_specs=out_specs,
        scratch_shapes=scratch,
        compiler_params=LIMIT,
        cost_estimate=pl.CostEstimate(flops=flops, bytes_accessed=moved, transcendentals=0),
    )(*operands)


def widen_first(layer, by_rows, x, weights, shape, dtype):
    return kernel_call(
        functools.partial(widen_first_kernel, layer, by_rows),
        shape_of(shape, dtype),
        HBM,
        [VMEM, HBM, HBM],
        held_scratch(weights[0], by_rows, 1) + [pltpu.VMEM(shape, dtype), pltpu.SemaphoreType.DMA((2,))],
        (x,) + weights[:2],
        flops=2 * x.shape[0] * weights[0].size,
        moved=2 * weights[0].size,
    )


def widen_next(layer, by_rows, arrived, base, weights, shape):
    return kernel_call(
        functools.partial(widen_next_kernel, layer, by_rows),
        (shape_of(shape), shape_of(base.shape)),
        (HBM, VMEM),
        [VMEM, VMEM] + [HBM] * 4,
        held_scratch(weights[0], by_rows, 2) + [pltpu.VMEM(shape, bf16), pltpu.SemaphoreType.DMA((2,))],
        (arrived, base) + weights,
        flops=4 * base.shape[0] * weights[0].size,
        moved=4 * weights[0].size,
    )


def narrow_next(layer, by_rows, which, arrived, weights, copies):
    tokens, width = arrived.shape[0] * arrived.shape[3], 2 * min(weights[0].shape)
    return kernel_call(
        functools.partial(narrow_kernel, layer, by_rows, which),
        shape_of((copies, tokens, width)),
        HBM,
        [VMEM] + [HBM] * 4,
        held_scratch(weights[0], by_rows, 2)
        + [pltpu.VMEM((tokens, width), bf16), pltpu.SemaphoreType.DMA((copies,))],
        (arrived,) + weights,
        flops=4 * tokens * weights[0].size,
        moved=4 * weights[0].size,
    )


def narrow_last(layer, by_rows, arrived, weights, beside):
    groups, tokens, width = arrived.shape[0], arrived.shape[3], 2 * min(weights[0].shape)
    return kernel_call(
        functools.partial(narrow_last_kernel, layer, by_rows),
        shape_of((2, groups, 2, tokens, width)),
        HBM,
        [VMEM] + [HBM] * 4 + [VMEM],
        held_scratch(weights[0], by_rows, 2)
        + [pltpu.VMEM((groups, 2, tokens, width), bf16), pltpu.SemaphoreType.DMA((2,))],
        (arrived,) + weights + (beside,),
        flops=4 * groups * tokens * weights[0].size,
        moved=4 * weights[0].size,
    )


def summed(ref, place):
    total = ref[0, :, place].astype(f32)
    for i in range(1, ref.shape[0]):
        total = total + ref[i, :, place].astype(f32)
    return total


def spread(stage, out_ref, sems):
    copies = [pltpu.make_async_copy(stage, out_ref.at[i], sems.at[i]) for i in range(out_ref.shape[0])]
    for copy in copies:
        copy.start()
    for copy in copies:
        copy.wait()


def act_first_kernel(arrived, out_ref, slope_ref, stage, sems):
    for at in range(0, arrived.shape[2], CHUNK):
        place = pl.ds(at, CHUNK)
        value, slope = gelu_both(summed(arrived, place))
        stage[0, :, place] = value.astype(bf16)
        slope_ref[:, place] = slope
    spread(stage, out_ref, sems)


def act_last_kernel(arrived, d_hid, out_ref, stage, sems):
    for at in range(0, arrived.shape[2], CHUNK):
        place = pl.ds(at, CHUNK)
        value, slope = gelu_both(summed(arrived, place))
        stage[0, :, place] = (d_hid[:, place] * slope).astype(bf16)
        stage[1, :, place] = value.astype(bf16)
    spread(stage, out_ref, sems)


def act_back_kernel(arrived, slope_ref, out_ref, stage, sems):
    for at in range(0, arrived.shape[2], CHUNK):
        place = pl.ds(at, CHUNK)
        stage[0, :, place] = (summed(arrived, place) * slope_ref[:, place]).astype(bf16)
    spread(stage, out_ref, sems)


def activation(body, kinds, peers, piece, operands, in_specs, slope=False):
    outs, out_specs = [shape_of((peers, kinds) + piece)], [HBM]
    if slope:
        outs, out_specs = outs + [shape_of(piece, f32)], out_specs + [VMEM]
    return kernel_call(
        body,
        outs,
        out_specs,
        in_specs,
        [pltpu.VMEM((kinds,) + piece, bf16), pltpu.SemaphoreType.DMA((peers,))],
        operands,
        flops=2000000,
        moved=2000000,
    )


def grad_down_kernel(*refs):
    lefts, right, out_ref = refs[:4], refs[4], refs[-1]
    left = jnp.concatenate([ref[...].reshape(-1, CHUNK) for ref in lefts])
    out_ref[...] = dot(left, right[...], ((0,), (0,)))


def grad_down(hids, grads):
    groups, halves, tokens, wide = hids[0].shape
    per_half, units, width = wide // CHUNK, halves * wide, grads.shape[1]
    block = pl.BlockSpec((groups, 1, tokens, CHUNK), lambda i: (0, i // per_half, 0, i % per_half))
    return pl.pallas_call(
        grad_down_kernel,
        out_shape=shape_of((units, width), f32),
        grid=(units // CHUNK,),
        in_specs=[block] * 4 + [pl.BlockSpec(grads.shape, lambda i: (0, 0))],
        out_specs=pl.BlockSpec((CHUNK, width), lambda i: (i, 0)),
        compiler_params=LIMIT,
        cost_estimate=pl.CostEstimate(
            flops=2 * grads.size * units, bytes_accessed=4 * width * units, transcendentals=0
        ),
    )(*hids, grads)


def grad_up_kernel(x_ref, *refs):
    choices, (out_ref, held, turned, sems) = (refs[:4], refs[4:8]), refs[8:]
    step = pl.program_id(0)
    section = lax.axis_index("section")

    def copy(choice, i):
        return pltpu.make_async_copy(choices[choice][i], held.at[i], sems.at[i])

    @pl.when(step == 0)
    def _():
        for choice in range(2):

            @pl.when(section == choice)
            def _():
                for i in range(4):
                    copy(choice, i).start()

        turned[...] = x_ref[...].T
        for i in range(4):
            copy(0, i).wait()

    per_half = held.shape[4] // CHUNK
    place = pl.ds(pl.multiple_of((step % per_half) * CHUNK, CHUNK), CHUNK)
    right = held[:, :, step // per_half, :, place]
    out_ref[...] = dot(turned[...], right.reshape(-1, CHUNK), ((1,), (0,)))


def grad_up(xs, layer0, layer1):
    groups, halves, tokens, wide = layer0[0].shape
    units, (all_tokens, width) = halves * wide, xs.shape
    return pl.pallas_call(
        grad_up_kernel,
        out_shape=shape_of((width, units), f32),
        grid=(units // CHUNK,),
        in_specs=[pl.BlockSpec(xs.shape, lambda i: (0, 0))] + [ANY] * 8,
        out_specs=pl.BlockSpec((width, CHUNK), lambda i: (0, i)),
        scratch_shapes=[
            pltpu.VMEM((4,) + layer0[0].shape, bf16),
            pltpu.VMEM((width, all_tokens), bf16),
            pltpu.SemaphoreType.DMA((4,)),
        ],
        compiler_params=LIMIT,
        cost_estimate=pl.CostEstimate(
            flops=2 * xs.size * units, bytes_accessed=4 * width * units, transcendentals=0
        ),
    )(xs, *layer0, *layer1)


def exchange(blocks, axes):
    return lax.all_to_all(blocks, axes, 0, 0)


CORES = ("section", "x_lo")


def to_other_core(block):
    return lax.ppermute(block, "section", [(0, 1), (1, 0)])


def to_mate(block):
    return lax.ppermute(block, "x_lo", [(0, 1), (1, 0)])


def to_other_core_of_mate(block):
    return lax.ppermute(block, CORES, [(0, 3), (3, 0), (1, 2), (2, 1)])


def only_to_mate(block, section):
    at = 2 * section
    return lax.ppermute(block, CORES, [(at, at + 1), (at + 1, at)])


def only_to_core(block, section):
    return lax.ppermute(block, "section", [(1 - section, section)])


def only_to_core_of_mate(block, section):
    at, source = 2 * section, 2 * (1 - section)
    return lax.ppermute(block, CORES, [(source, at + 1), (source + 1, at)])


def late(block, after):
    return lax.optimization_barrier((block, after))[0]


def local(inputs, cotangent, w_up, w_down):
    col = ("y", "x_hi")
    section, mate_pos, col_pos = (lax.axis_index(name) for name in ("section", "x_lo", col))
    first = section == 0
    own_up, own_down = w_up[0], w_down[0]
    tokens, width = inputs.shape[1:]
    half_len = tokens // 2
    rings = lax.axis_size("z")
    piece = (tokens // rings, own_up.shape[1] // 2)
    blocks = (half_len // piece[0], 2) + piece
    wide_blocks = (blocks[0], 2, 2) + piece

    def half_of(array, which):
        return lax.dynamic_slice_in_dim(array, which * half_len, half_len, 0)

    def batch(array, which):
        return lax.dynamic_index_in_dim(array, which, 0, keepdims=False)

    def both_widths(array):
        return jnp.concatenate([half_of(array, mate_pos), to_mate(half_of(array, 1 - mate_pos))], axis=1)

    x0, g2 = batch(inputs, section), batch(cotangent, section)
    other_up = to_other_core(own_up)
    other_down = to_other_core(own_down)

    x0_both, g2_both = both_widths(x0), both_widths(g2)
    mate_down0 = only_to_mate(late(own_down, (x0_both, g2_both)), 0)
    mate_up1 = only_to_mate(late(own_up, (x0_both, g2_both)), 1)

    arrived = widen_first(0, False, x0, (own_up, other_up), wide_blocks, bf16)
    g2 = late(g2, arrived)
    arrived = exchange(arrived.reshape((2 * rings,) + piece), ("z", "x_lo"))
    d_hid1 = widen_first(1, True, g2, (own_down, other_down), wide_blocks, f32)
    d_hid1 = lax.psum_scatter(
        d_hid1.reshape(2 * tokens, piece[1]), ("z", "x_lo"), scatter_dimension=0, tiled=True
    )
    value0, slope0 = activation(act_first_kernel, 1, rings, piece, (arrived,), [VMEM], slope=True)
    mate_down0 = late(mate_down0, value0)
    down0 = own_down, other_down, mate_down0, only_to_core(mate_down0, 1)
    hid0 = exchange(value0, "z").reshape(blocks[:2] + (1,) + piece)
    part = narrow_next(0, True, 0, hid0, down0, lax.axis_size(col))
    mate_up1 = late(mate_up1, part)
    up1 = own_up, other_up, mate_up1, only_to_core(mate_up1, 0)
    mate_down1 = only_to_mate(late(own_down, down0[3]), 1)
    mate_up0 = only_to_mate(late(own_up, up1[3]), 0)
    arrived = exchange(part, col)

    pre1, x1 = widen_next(1, False, arrived, x0_both, up1, blocks)
    arrived = exchange(pre1.reshape((rings,) + piece), "z")
    (acts1,) = activation(act_last_kernel, 2, rings, piece, (arrived, d_hid1), [VMEM, VMEM])
    acts1 = exchange(acts1, "z").reshape(blocks[:2] + (2,) + piece)
    part = narrow_next(1, False, 0, acts1, up1, lax.axis_size(col))
    mate_down1 = late(mate_down1, part)
    down1 = own_down, other_down, mate_down1, only_to_core(mate_down1, 0)
    arrived = exchange(part, col)

    d_hid0, g1 = widen_next(0, True, arrived, g2_both, down0, blocks)
    hid0, acts1, mate_up0, x1, g1 = late((hid0, acts1, mate_up0, x1, g1), d_hid0)
    up0 = own_up, other_up, mate_up0, only_to_core(mate_up0, 1)
    arrived = exchange(d_hid0.reshape((rings,) + piece), "z")
    x2_part = narrow_next(1, True, 1, acts1, down1, 1)
    (d_pre0,) = activation(act_back_kernel, 1, rings, piece, late((arrived, slope0), x2_part), [VMEM, VMEM])
    after_act = d_pre0
    d_pre0 = exchange(d_pre0, "z").reshape(blocks[:2] + (1,) + piece)

    hid0, d_pre1, hid1 = hid0[:, :, 0], acts1[:, :, 0], acts1[:, :, 1]
    kept, given = jnp.where(first, hid0, hid1), jnp.where(first, hid1, hid0)
    hids = kept, to_other_core(given), to_mate(kept), to_other_core_of_mate(given)
    near, far = slice(None, width), slice(width, None)
    traded = (
        jnp.where(first, g1[:, near], x1[:, near]),
        to_other_core(jnp.where(first, x1[:, near], g1[:, near])),
        to_mate(jnp.where(first, g1[:, far], x1[:, far])),
        to_other_core_of_mate(jnp.where(first, x1[:, far], g1[:, far])),
    )

    def all_tokens(array):
        return [
            half_of(batch(array, which), half)
            for half in (mate_pos, 1 - mate_pos)
            for which in (section, 1 - section)
        ]

    traded = jnp.concatenate(traded)
    xs = jnp.where(first, jnp.concatenate(all_tokens(inputs)), traded)
    gs = jnp.where(first, traded, jnp.concatenate(all_tokens(cotangent)))
    down_grad = grad_down(late(hids, after_act), gs)

    out = narrow_last(0, False, late(d_pre0, down_grad), up0, x2_part[0])
    arrived = exchange(out.reshape((lax.axis_size(col),) + out.shape[2:]), col)

    d_pre0 = d_pre0[:, :, 0]

    def gathered(array, section):
        return (
            array,
            only_to_core(array, section),
            only_to_mate(array, section),
            only_to_core_of_mate(array, section),
        )

    up_grad = grad_up(xs, gathered(d_pre0, 0), gathered(d_pre1, 1))

    out_len = out.shape[3]
    here = col_pos // blocks[0] == mate_pos
    x1, g1 = (lax.dynamic_slice_in_dim(a, (col_pos % blocks[0]) * out_len, out_len, 0) for a in (x1, g1))
    ended = jnp.sum(arrived.astype(f32), axis=0)
    x2 = (x1.astype(f32) + ended[0]).astype(bf16)
    g0 = (g1.astype(f32) + ended[1]).astype(bf16)
    layer0, layer1 = jnp.stack([x1, g0]), jnp.stack([x2, g1])
    kept, given = jnp.where(first, layer0, layer1), jnp.where(first, layer1, layer0)
    kept, given = (
        jnp.where(here, kept[..., near], to_mate(kept[..., far])),
        jnp.where(here, to_other_core(given[..., near]), to_other_core_of_mate(given[..., far])),
    )
    states, grads = (
        jnp.where(first, jnp.stack([kept[i], given[i]]), jnp.stack([given[i], kept[i]]))[None] for i in (0, 1)
    )
    return states, grads, up_grad[None], down_grad[None]


def solution(mesh):
    sections, rows, cols = mesh.devices.shape
    finer = Mesh(
        mesh.devices.reshape(sections, rows // 2, 2, cols // 2, 2),
        ("section", "z", "x_lo", "y", "x_hi"),
    )
    row, col = ("z", "x_lo"), ("y", "x_hi")
    in_specs = (
        P(None, None, row),
        P(None, None, row),
        P("section", row, col),
        P("section", col, row),
    )
    out_specs = (
        P("section", None, col, row),
        P("section", None, col, row),
        P("section", row, col),
        P("section", col, row),
    )
    return jax.shard_map(local, mesh=finer, in_specs=in_specs, out_specs=out_specs, check_vma=False)
```

time: 1200 us -> 323 us (0.27)
  waiting for transfers between devices: 797 us -> 130 us
  blocking collectives: 287 us -> 0 us
  starting transfers between devices: 18.8 us -> 109 us
  matrix products: 47.8 us -> 0 us
  Pallas kernels: 0 us -> 42 us
  local copies, waits for them, and re-layouts: 5.05 us -> 21.6 us
  other arithmetic: 19.9 us -> 4.08 us
    psum x5 -> x0, waiting for transfers between devices: 472 us -> none  [finish(): total = lax.psum(partial_value, 'col')]
    reduce_scatter x6 -> x1, waiting for transfers between devices: 310 us -> 9.6 us  [local(): lax.psum_scatter(d_hid1.reshape(2 * tokens, piece[1]), ('z', 'x_lo'), sca...]
    all_gather x9 -> x0, blocking collectives: 287 us -> none  [the longest x6 200 us: local(): lax.all_gather(hidden, 'row', axis=0, tiled=True)]
    all_to_all x0 -> x9, waiting for transfers between devices: none -> 85.7 us  [exchange(): return lax.all_to_all(blocks, axes, 0, 0)]
    dot_general x18 -> x0, matrix products: 47.8 us -> none  [the longest x6 18.2 us: contract_rows(): lax.dot_general(left, right, (((0,), (0,)), ((), ())), preferred_element_...]
    ppermute x4 -> x27, starting transfers between devices: 18.4 us -> 64.2 us  [the longest x6 26.6 us: only_to_core(): return lax.ppermute(block, 'section', [(1 - section, section)])]
    all_to_all x0 -> x9, starting transfers between devices: none -> 44.4 us  [exchange(): return lax.all_to_all(blocks, axes, 0, 0)]
    pallas_call x0 -> x13, Pallas kernels: none -> 42 us  [the longest x11 33.3 us: kernel_call(): pl.pallas_call(body, out_shape=outs, in_specs=in_specs, out_specs=out_spe...]
  transfers between devices with their start and end apart: 15 -> 37, of which waited for: 13 -> 17; matrix products, arithmetic and copies ran while one was open for 3% -> 3% of each run, Pallas kernels for 0% -> 10%
where the time goes in v1:
time: 323 us; the launch traced here: 321 us
  waiting for transfers between devices  130 us (40%)
  starting transfers between devices  109 us (34%)
  Pallas kernels  42 us (13%)
  local copies, waits for them, and re-layouts  21.6 us (7%)
  between operations  14.8 us (5%)
  other arithmetic  4.08 us (1%)
    all_to_all x9, waiting for transfers between devices, exchange(): return lax.all_to_all(blocks, axes, 0, 0)  85.7 us
    all_to_all x9, starting transfers between devices, exchange(): return lax.all_to_all(blocks, axes, 0, 0)  44.4 us
    pallas_call x11, Pallas kernels, kernel_call(): pl.pallas_call(body, out_shape=outs, in_specs=in_specs, out_specs=out_spe...  33.3 us
    ppermute x6, starting transfers between devices, only_to_core(): return lax.ppermute(block, 'section', [(1 - section, section)])  26.6 us
    ppermute x5, waiting for transfers between devices, to_mate(): return lax.ppermute(block, 'x_lo', [(0, 1), (1, 0)])  18.6 us
    unnamed x64, local copies, waits for them, and re-layouts  14.6 us
    ppermute x5, starting transfers between devices, to_other_core(): return lax.ppermute(block, 'section', [(0, 1), (1, 0)])  12.1 us
    ppermute x6, starting transfers between devices, only_to_mate(): return lax.ppermute(block, CORES, [(at, at + 1), (at + 1, at)])  11.1 us
  transfers between devices with their start and end apart: 37, of which 17 were waited for; matrix products, arithmetic and copies ran while one was open for 3% of the time, Pallas kernels for 10%

profile of v1, /device:TPU:1, one launch (start us, length us, event | category | flops | bytes accessed | tf_op | source)
XLA Modules:
  0.0 320.6 jit_solution(9465360924272024734)
XLA Ops:
  7.2 3.3 %collective-permute-start = (bf16[384,3072]{1,0:T(8,128)(2,1)}, bf16[384,3072]{1,0:T(8,128)(2,1)}, u32[]{:S(2)}, u32[]{:S(2)}) collective-permute-start(bf16[384,3072]{1,0:T(8,128)(2,1)} %bitcast.82), channel_id=1, source_target_pairs={{0,128},{128,0},{1,129},{129,1},{2,130},{130,2},{3,131},{131,3},{4... | collective-permute-start | bytes 7077896 | tf_op jit(solution)/shard_map/ppermute | solution.py:371
  17.7 2.1 collective-permute-start.4
  20.8 1.8 copy-done.1
  22.6 2.6 shard_map.75
  26.0 7.5 %all-to-all-start = ((bf16[16,16,1536]{2,1,0:T(8,128)(2,1)}), bf16[16,16,1536]{2,1,0:T(8,128)(2,1)S(1)}, u32[]{:S(2)}, u32[]{:S(2)}) async-start(bf16[16,16,1536]{2,1,0:T(8,128)(2,1)} %bitcast.98), calls=%async_computation | async-start | bytes 1572864 | tf_op jit(solution)/shard_map/all_to_all | solution.py:364
  33.6 2.3 collective-permute-start.1
  35.8 16.8 %all-to-all-done.arrived = bf16[16,16,1536]{2,1,0:T(8,128)(2,1)S(1)} async-done(((bf16[16,16,1536]{2,1,0:T(8,128)(2,1)}), bf16[16,16,1536]{2,1,0:T(8,128)(2,1)S(1)}, u32[]{:S(2)}, u32[]{:S(2)}) %all-to-all-start) | async-done | bytes 786464 | tf_op jit(solution)/shard_map/all_to_all | solution.py:364
  55.5 2.1 collective-permute-start.6
  57.7 6.0 %all-to-all-start.1 = ((bf16[8,1,16,1536]{3,2,1,0:T(8,128)(2,1)}), bf16[8,1,16,1536]{3,2,1,0:T(8,128)(2,1)S(1)}, u32[]{:S(2)}, u32[]{:S(2)}) async-start(bf16[8,1,16,1536]{3,2,1,0:T(8,128)(2,1)} %get-tuple-element.30), calls=%async_computation.1 | async-start | bytes 786432 | tf_op jit(solution)/shard_map/all_to_all | solution.py:364
  63.8 2.9 shard_map.79
  67.9 6.6 %all-to-all-done.1 = bf16[8,1,16,1536]{3,2,1,0:T(8,128)(2,1)S(1)} async-done(((bf16[8,1,16,1536]{3,2,1,0:T(8,128)(2,1)}), bf16[8,1,16,1536]{3,2,1,0:T(8,128)(2,1)S(1)}, u32[]{:S(2)}, u32[]{:S(2)}) %all-to-all-start.1) | async-done | bytes 393248 | tf_op jit(solution)/shard_map/all_to_all | solution.py:364
  74.4 4.3 %shard_map.77 = bf16[8,64,768]{2,1,0:T(8,128)(2,1)S(1)} custom-call(bf16[4,2,1,16,1536]{4,3,2,1,0:T(8,128)(2,1)S(1)} %bitcast.96, bf16[3072,384]{1,0:T(8,128)(2,1)S(1)} %bitcast.78, bf16[3072,384]{1,0:T(8,128)(2,1)} %collective-permute-done.1.other, bf16[3072,384]{1,0:T(8,128)(2,1)} %collective-permute-done.4.own_mate, ...), custom_call_target="tpu_custom_call" | custom-call | flops 301989888 | bytes 4718592 | tf_op jit(solution)/shard_map/pallas_call | solution.py:169
  79.7 5.8 %collective-permute-done.6.own_mate = bf16[384,3072]{1,0:T(8,128)(2,1)} collective-permute-done((bf16[384,3072]{1,0:T(8,128)(2,1)}, bf16[384,3072]{1,0:T(8,128)(2,1)}, u32[]{:S(2)}, u32[]{:S(2)}) %collective-permute-start.6) | collective-permute-done | bytes 2359328 | tf_op jit(solution)/shard_map/ppermute | solution.py:384
  85.4 8.3 %collective-permute-start.7 = (bf16[384,3072]{1,0:T(8,128)(2,1)}, bf16[384,3072]{1,0:T(8,128)(2,1)}, u32[]{:S(2)}, u32[]{:S(2)}) collective-permute-start(bf16[384,3072]{1,0:T(8,128)(2,1)} %collective-permute-done.6.own_mate), channel_id=1, source_target_pairs={{128,0},{129,1},{130,2},{131,3},{132,4},{133,5},{134,6},{135,7},{1... | collective-permute-start | bytes 7077896 | tf_op jit(solution)/shard_map/ppermute | solution.py:388
  93.7 5.8 %all-to-all-start.2 = ((bf16[8,64,768]{2,1,0:T(8,128)(2,1)}), bf16[8,64,768]{2,1,0:T(8,128)(2,1)S(1)}, u32[]{:S(2)}, u32[]{:S(2)}) async-start(bf16[8,64,768]{2,1,0:T(8,128)(2,1)} %copy-done.8), calls=%async_computation.2 | async-start | bytes 1572864 | tf_op jit(solution)/shard_map/all_to_all | solution.py:364
  99.6 1.9 collective-permute-start.9
  101.5 21.6 %all-to-all-done.2.arrived = bf16[8,64,768]{2,1,0:T(8,128)(2,1)S(1)} async-done(((bf16[8,64,768]{2,1,0:T(8,128)(2,1)}), bf16[8,64,768]{2,1,0:T(8,128)(2,1)S(1)}, u32[]{:S(2)}, u32[]{:S(2)}) %all-to-all-start.2) | async-done | bytes 786464 | tf_op jit(solution)/shard_map/all_to_all | solution.py:364
  123.1 1.7 copy-done.2
  125.7 3.0 shard_map.78
  130.1 3.5 %all-to-all-start.3 = ((bf16[8,16,1536]{2,1,0:T(8,128)(2,1)}), bf16[8,16,1536]{2,1,0:T(8,128)(2,1)S(1)}, u32[]{:S(2)}, u32[]{:S(2)}) async-start(bf16[8,16,1536]{2,1,0:T(8,128)(2,1)} %bitcast.100), calls=%async_computation.3 | async-start | bytes 786432 | tf_op jit(solution)/shard_map/all_to_all | solution.py:364
  133.6 9.6 %reduce-scatter.2.cloned.1.call-done.d_hid = f32[16,1536]{1,0:T(8,128)} async-done(((f32[256,1536]{1,0:T(8,128)}), f32[16,1536]{1,0:T(8,128)}) %reduce-scatter.2.cloned.1.call-update) | async-done | bytes 98320 | tf_op jit(solution)/shard_map/reduce_scatter | solution.py:433
  143.2 4.4 %all-to-all-done.3.arrived = bf16[8,16,1536]{2,1,0:T(8,128)(2,1)S(1)} async-done(((bf16[8,16,1536]{2,1,0:T(8,128)(2,1)}), bf16[8,16,1536]{2,1,0:T(8,128)(2,1)S(1)}, u32[]{:S(2)}, u32[]{:S(2)}) %all-to-all-start.3) | async-done | bytes 393248 | tf_op jit(solution)/shard_map/all_to_all | solution.py:364
  150.6 3.5 %all-to-all-start.4 = ((bf16[8,2,16,1536]{3,2,1,0:T(8,128)(2,1)}), bf16[8,2,16,1536]{3,2,1,0:T(8,128)(2,1)S(1)}, u32[]{:S(2)}, u32[]{:S(2)}) async-start(bf16[8,2,16,1536]{3,2,1,0:T(8,128)(2,1)} %copy-done.6), calls=%async_computation.5 | async-start | bytes 1572864 | tf_op jit(solution)/shard_map/all_to_all | solution.py:364
  154.1 2.1 collective-permute-start.8
  156.2 12.7 %all-to-all-done.4 = bf16[8,2,16,1536]{3,2,1,0:T(8,128)(2,1)S(1)} async-done(((bf16[8,2,16,1536]{3,2,1,0:T(8,128)(2,1)}), bf16[8,2,16,1536]{3,2,1,0:T(8,128)(2,1)S(1)}, u32[]{:S(2)}, u32[]{:S(2)}) %all-to-all-start.4) | async-done | bytes 786464 | tf_op jit(solution)/shard_map/all_to_all | solution.py:364
  168.9 1.7 copy-done.3
  170.6 4.4 %shard_map.81 = bf16[8,64,768]{2,1,0:T(8,128)(2,1)S(1)} custom-call(bf16[4,2,2,16,1536]{4,3,2,1,0:T(8,128)(2,1)S(1)} %bitcast.89, bf16[384,3072]{1,0:T(8,128)(2,1)S(1)} %bitcast.87, bf16[384,3072]{1,0:T(8,128)(2,1)} %collective-permute-done.other, bf16[384,3072]{1,0:T(8,128)(2,1)} %collective-permute-done.6.own_mate, ...), custom_call_target="tpu_custom_call" | custom-call | flops 301989888 | bytes 4718592 | tf_op jit(solution)/shard_map/pallas_call | solution.py:169
  175.9 12.9 %collective-permute-start.10 = (bf16[3072,384]{1,0:T(8,128)(2,1)}, bf16[3072,384]{1,0:T(8,128)(2,1)}, u32[]{:S(2)}, u32[]{:S(2)}) collective-permute-start(bf16[3072,384]{1,0:T(8,128)(2,1)} %collective-permute-done.9.own_mate), channel_id=1, source_target_pairs={{128,0},{129,1},{130,2},{131,3},{132,4},{133,5},{134,6},{135,7},{1... | collective-permute-start | bytes 7077896 | tf_op jit(solution)/shard_map/ppermute | solution.py:388
  188.8 7.5 %all-to-all-start.5 = ((bf16[8,64,768]{2,1,0:T(8,128)(2,1)}), bf16[8,64,768]{2,1,0:T(8,128)(2,1)}, u32[]{:S(2)}, u32[]{:S(2)}) async-start(bf16[8,64,768]{2,1,0:T(8,128)(2,1)} %copy-done.9), calls=%async_computation.6 | async-start | bytes 1572864 | tf_op jit(solution)/shard_map/all_to_all | solution.py:364
  197.3 12.6 %all-to-all-done.5.arrived = bf16[8,64,768]{2,1,0:T(8,128)(2,1)} async-done(((bf16[8,64,768]{2,1,0:T(8,128)(2,1)}), bf16[8,64,768]{2,1,0:T(8,128)(2,1)}, u32[]{:S(2)}, u32[]{:S(2)}) %all-to-all-start.5) | async-done | bytes 786464 | tf_op jit(solution)/shard_map/all_to_all | solution.py:364
  210.8 5.4 %shard_map.82 = (bf16[4,2,16,1536]{3,2,1,0:T(8,128)(2,1)}, bf16[64,768]{1,0:T(8,128)(2,1)S(1)}) custom-call(bf16[8,64,768]{2,1,0:T(8,128)(2,1)} %all-to-all-done.5.arrived, bf16[64,768]{1,0:T(8,128)(2,1)S(1)} %copy-done.10, bf16[3072,384]{1,0:T(8,128)(2,1)S(1)} %bitcast.80, bf16[3072,384]{1,0:T(8,128)(2,1)} %collective-permute-done.1.other, ...), custom_call_target="tpu_custom_call" | custom-call | flops 301989888 | bytes 4718592 | tf_op jit(solution)/shard_map/pallas_call | solution.py:169
  217.5 3.6 %all-to-all-start.6 = ((bf16[8,16,1536]{2,1,0:T(8,128)(2,1)}), bf16[8,16,1536]{2,1,0:T(8,128)(2,1)S(1)}, u32[]{:S(2)}, u32[]{:S(2)}) async-start(bf16[8,16,1536]{2,1,0:T(8,128)(2,1)} %bitcast.16), calls=%async_computation.7 | async-start | bytes 786432 | tf_op jit(solution)/shard_map/all_to_all | solution.py:364
  222.4 3.4 %shard_map.83 = bf16[1,64,768]{2,1,0:T(8,128)(2,1)S(1)} custom-call(bf16[4,2,2,16,1536]{4,3,2,1,0:T(8,128)(2,1)S(1)} %copy.11.arrived, bf16[3072,384]{1,0:T(8,128)(2,1)S(1)} %bitcast.81, bf16[3072,384]{1,0:T(8,128)(2,1)} %collective-permute-done.1.other, bf16[3072,384]{1,0:T(8,128)(2,1)} %collective-permute-done.9.own_mate, ...), custom_call_target="tpu_custom_call" | custom-call | flops 301989888 | bytes 4718592 | tf_op jit(solution)/shard_map/pallas_call | solution.py:169
  225.8 6.7 %all-to-all-done.6.arrived = bf16[8,16,1536]{2,1,0:T(8,128)(2,1)S(1)} async-done(((bf16[8,16,1536]{2,1,0:T(8,128)(2,1)}), bf16[8,16,1536]{2,1,0:T(8,128)(2,1)S(1)}, u32[]{:S(2)}, u32[]{:S(2)}) %all-to-all-start.6) | async-done | bytes 393248 | tf_op jit(solution)/shard_map/all_to_all | solution.py:364
  233.5 3.5 %all-to-all-start.7 = ((bf16[8,1,16,1536]{3,2,1,0:T(8,128)(2,1)}), bf16[8,1,16,1536]{3,2,1,0:T(8,128)(2,1)S(1)}, u32[]{:S(2)}, u32[]{:S(2)}) async-start(bf16[8,1,16,1536]{3,2,1,0:T(8,128)(2,1)} %shard_map.84), calls=%async_computation.8 | async-start | bytes 786432 | tf_op jit(solution)/shard_map/all_to_all | solution.py:364
  238.1 3.5 %collective-permute-start.11 = (bf16[4,2,16,1536]{3,2,1,0:T(8,128)(2,1)S(1)}, bf16[4,2,16,1536]{3,2,1,0:T(8,128)(2,1)S(1)}, u32[]{:S(2)}, u32[]{:S(2)}) collective-permute-start(bf16[4,2,16,1536]{3,2,1,0:T(8,128)(2,1)S(1)} %get-tuple-element.56), channel_id=1, source_target_pairs={{0,128},{128,0},{1,129},{129,1},{2,130},{130,2},{3,131},{131,3},{4... | collective-permute-start | bytes 1179656 | tf_op jit(solution)/shard_map/ppermute | solution.py:371
  244.8 16.9 %collective-permute-done.15 = bf16[64,384]{1,0:T(8,128)(2,1)S(1)} collective-permute-done((bf16[64,384]{1,0:T(8,128)(2,1)S(1)}, bf16[64,384]{1,0:T(8,128)(2,1)S(1)}, u32[]{:S(2)}, u32[]{:S(2)}) %collective-permute-start.15) | collective-permute-done | bytes 49184 | tf_op jit(solution)/shard_map/ppermute | solution.py:375
  262.6 3.2 %collective-permute-done.16 = bf16[64,384]{1,0:T(8,128)(2,1)S(1)} collective-permute-done((bf16[64,384]{1,0:T(8,128)(2,1)S(1)}, bf16[64,384]{1,0:T(8,128)(2,1)S(1)}, u32[]{:S(2)}, u32[]{:S(2)}) %collective-permute-start.16) | collective-permute-done | bytes 49184 | tf_op jit(solution)/shard_map/ppermute | solution.py:379
  266.0 4.1 %shard_map.85 = f32[3072,384]{1,0:T(8,128)} custom-call(bf16[4,2,16,1536]{3,2,1,0:T(8,128)(2,1)S(1)} %get-tuple-element.50.refs_0_, bf16[4,2,16,1536]{3,2,1,0:T(8,128)(2,1)S(1)} %collective-permute-done.11.refs_1_, bf16[4,2,16,1536]{3,2,1,0:T(8,128)(2,1)S(1)} %collective-permute-done.12.refs_2_, ...), custom_call_target="tpu_custom_call" | custom-call | flops 603979776 | bytes 4718592 | tf_op jit(solution)/shard_map/pallas_call | solution.py:302
  270.1 4.3 %shard_map.86 = bf16[2,4,2,16,768]{4,3,2,1,0:T(8,128)(2,1)} custom-call(bf16[4,2,1,16,1536]{4,3,2,1,0:T(8,128)(2,1)S(1)} %bitcast.91, bf16[384,3072]{1,0:T(8,128)(2,1)S(1)} %bitcast.88, bf16[384,3072]{1,0:T(8,128)(2,1)} %collective-permute-done.other, bf16[384,3072]{1,0:T(8,128)(2,1)} %collective-permute-done.8.own_mate, ...), custom_call_target="tpu_custom_call" | custom-call | flops 301989888 | bytes 4718592 | tf_op jit(solution)/shard_map/pallas_call | solution.py:169
  274.4 3.5 %all-to-all-start.8 = ((bf16[8,2,16,768]{3,2,1,0:T(8,128)(2,1)}), bf16[8,2,16,768]{3,2,1,0:T(8,128)(2,1)S(1)}, u32[]{:S(2)}, u32[]{:S(2)}) async-start(bf16[8,2,16,768]{3,2,1,0:T(8,128)(2,1)} %bitcast.23), calls=%async_computation.9 | async-start | bytes 786432 | tf_op jit(solution)/shard_map/all_to_all | solution.py:364
  279.2 2.2 collective-permute-start.25
  283.5 4.2 %all-to-all-done.8 = bf16[8,2,16,768]{3,2,1,0:T(8,128)(2,1)S(1)} async-done(((bf16[8,2,16,768]{3,2,1,0:T(8,128)(2,1)}), bf16[8,2,16,768]{3,2,1,0:T(8,128)(2,1)S(1)}, u32[]{:S(2)}, u32[]{:S(2)}) %all-to-all-start.8) | async-done | bytes 393248 | tf_op jit(solution)/shard_map/all_to_all | solution.py:364
  288.9 2.2 collective-permute-start.19
  291.6 2.9 collective-permute-start.20
  296.7 6.1 %collective-permute-start.23 = (bf16[4,2,16,1536]{3,2,1,0:T(8,128)(2,1)S(1)}, bf16[4,2,16,1536]{3,2,1,0:T(8,128)(2,1)S(1)}, u32[]{:S(2)}, u32[]{:S(2)}) collective-permute-start(bf16[4,2,16,1536]{3,2,1,0:T(8,128)(2,1)S(1)} %bitcast.94), channel_id=1, source_target_pairs={{128,8},{136,0},{129,9},{137,1},{130,10},{138,2},{131,11},{139,3},... | collective-permute-start | bytes 1179656 | tf_op jit(solution)/shard_map/ppermute | solution.py:393
  303.5 5.7 %collective-permute-done.23.refs_3_ = bf16[4,2,16,1536]{3,2,1,0:T(8,128)(2,1)S(1)} collective-permute-done((bf16[4,2,16,1536]{3,2,1,0:T(8,128)(2,1)S(1)}, bf16[4,2,16,1536]{3,2,1,0:T(8,128)(2,1)S(1)}, u32[]{:S(2)}, u32[]{:S(2)}) %collective-permute-start.23) | collective-permute-done | bytes 393248 | tf_op jit(solution)/shard_map/ppermute | solution.py:393
  309.1 4.6 %shard_map.87 = f32[384,3072]{1,0:T(8,128)} custom-call(bf16[256,384]{1,0:T(8,128)(2,1)S(1)} %get-tuple-element.59.x_ref, bf16[4,2,16,1536]{3,2,1,0:T(8,128)(2,1)S(1)} %bitcast.95, bf16[4,2,16,1536]{3,2,1,0:T(8,128)(2,1)S(1)} %collective-permute-done.21.refs_1_, bf16[4,2,16,1536]{3,2,1,0:T(8,128)(2,1)S(1)} %collective-permute-done.22.refs_2_, ...), custom_call_target="tpu_custom_call" | custom-call | flops 603979776 | bytes 4718592 | tf_op jit(solution)/shard_map/pallas_call | solution.py:345
  (127 shorter events, 38.5 us)
Async XLA Ops:
  7.2 13.6 %collective-permute-start = (bf16[384,3072]{1,0:T(8,128)(2,1)}, bf16[384,3072]{1,0:T(8,128)(2,1)}, u32[]{:S(2)}, u32[]{:S(2)}) collective-permute-start(bf16[384,3072]{1,0:T(8,128)(2,1)} %bitcast.82), channel_id=1, source_target_pairs={{0,128},{128,0},{1,129},{129,1},{2,130},{130,2},{3,131},{131,3},{4... | collective-permute-start | bytes 7077896 | tf_op jit(solution)/shard_map/ppermute | solution.py:371
  12.1 3.3 %collective-permute-start.2 = (bf16[64,384]{1,0:T(8,128)(2,1)S(1)}, bf16[64,384]{1,0:T(8,128)(2,1)S(1)}, u32[]{:S(2)}, u32[]{:S(2)}) collective-permute-start(bf16[64,384]{1,0:T(8,128)(2,1)S(1)} %get-tuple-element.62), channel_id=1, source_target_pairs={{0,8},{8,0},{1,9},{9,1},{2,10},{10,2},{3,11},{11,3},{4,12},{12,4},... | collective-permute-start | bytes 147464 | tf_op jit(solution)/shard_map/ppermute | solution.py:375
  13.7 3.3 %collective-permute-start.3 = (bf16[64,384]{1,0:T(8,128)(2,1)S(1)}, bf16[64,384]{1,0:T(8,128)(2,1)S(1)}, u32[]{:S(2)}, u32[]{:S(2)}) collective-permute-start(bf16[64,384]{1,0:T(8,128)(2,1)S(1)} %get-tuple-element.70), channel_id=1, source_target_pairs={{0,8},{8,0},{1,9},{9,1},{2,10},{10,2},{3,11},{11,3},{4,12},{12,4},... | collective-permute-start | bytes 147464 | tf_op jit(solution)/shard_map/ppermute | solution.py:375
  17.7 36.6 %collective-permute-start.4 = (bf16[3072,384]{1,0:T(8,128)(2,1)}, bf16[3072,384]{1,0:T(8,128)(2,1)}, u32[]{:S(2)}, u32[]{:S(2)}) collective-permute-start(bf16[3072,384]{1,0:T(8,128)(2,1)} %bitcast.75), channel_id=1, source_target_pairs={{0,8},{8,0},{1,9},{9,1},{2,10},{10,2},{3,11},{11,3},{4,12},{12,4},... | collective-permute-start | bytes 7077896 | tf_op jit(solution)/shard_map/ppermute | solution.py:384
  26.0 37.7 %copy-start.23 = (bf16[2,128,384]{2,1,0:T(8,128)(2,1)S(1)}, bf16[2,128,384]{2,1,0:T(8,128)(2,1)}, u32[]{:S(2)}) copy-start(bf16[2,128,384]{2,1,0:T(8,128)(2,1)} %param.5) | copy-start | bytes 589828
  26.0 26.6 %all-to-all-start = ((bf16[16,16,1536]{2,1,0:T(8,128)(2,1)}), bf16[16,16,1536]{2,1,0:T(8,128)(2,1)S(1)}, u32[]{:S(2)}, u32[]{:S(2)}) async-start(bf16[16,16,1536]{2,1,0:T(8,128)(2,1)} %bitcast.98), calls=%async_computation | async-start | bytes 1572864 | tf_op jit(solution)/shard_map/all_to_all | solution.py:364
  33.6 30.2 %collective-permute-start.1 = (bf16[3072,384]{1,0:T(8,128)(2,1)S(1)}, bf16[3072,384]{1,0:T(8,128)(2,1)}, u32[]{:S(2)}, u32[]{:S(2)}) collective-permute-start(bf16[3072,384]{1,0:T(8,128)(2,1)S(1)} %bitcast.76), channel_id=1, source_target_pairs={{0,128},{128,0},{1,129},{129,1},{2,130},{130,2},{3,131},{131,3},{4... | collective-permute-start | bytes 7077896 | tf_op jit(solution)/shard_map/ppermute | solution.py:371
  54.2 20.2 %collective-permute-start.5 = (bf16[3072,384]{1,0:T(8,128)(2,1)}, bf16[3072,384]{1,0:T(8,128)(2,1)}, u32[]{:S(2)}, u32[]{:S(2)}) collective-permute-start(bf16[3072,384]{1,0:T(8,128)(2,1)} %collective-permute-done.4.own_mate), channel_id=1, source_target_pairs={{0,128},{1,129},{2,130},{3,131},{4,132},{5,133},{6,134},{7,135},{8... | collective-permute-start | bytes 7077896 | tf_op jit(solution)/shard_map/ppermute | solution.py:388
  55.5 29.9 %collective-permute-start.6 = (bf16[384,3072]{1,0:T(8,128)(2,1)}, bf16[384,3072]{1,0:T(8,128)(2,1)}, u32[]{:S(2)}, u32[]{:S(2)}) collective-permute-start(bf16[384,3072]{1,0:T(8,128)(2,1)} %bitcast.83), channel_id=1, source_target_pairs={{128,136},{136,128},{129,137},{137,129},{130,138},{138,130},{131,1... | collective-permute-start | bytes 7077896 | tf_op jit(solution)/shard_map/ppermute | solution.py:384
  57.7 16.8 %all-to-all-start.1 = ((bf16[8,1,16,1536]{3,2,1,0:T(8,128)(2,1)}), bf16[8,1,16,1536]{3,2,1,0:T(8,128)(2,1)S(1)}, u32[]{:S(2)}, u32[]{:S(2)}) async-start(bf16[8,1,16,1536]{3,2,1,0:T(8,128)(2,1)} %get-tuple-element.30), calls=%async_computation.1 | async-start | bytes 786432 | tf_op jit(solution)/shard_map/all_to_all | solution.py:364
  63.7 79.5 %reduce-scatter.2.cloned.1.call-start = ((), (), s32[]{:S(2)}) async-start(), calls=%async_computation.10 | async-start | bytes 1671168 | tf_op jit(solution)/shard_map/reduce_scatter | solution.py:433
  85.4 37.7 %collective-permute-start.7 = (bf16[384,3072]{1,0:T(8,128)(2,1)}, bf16[384,3072]{1,0:T(8,128)(2,1)}, u32[]{:S(2)}, u32[]{:S(2)}) collective-permute-start(bf16[384,3072]{1,0:T(8,128)(2,1)} %collective-permute-done.6.own_mate), channel_id=1, source_target_pairs={{128,0},{129,1},{130,2},{131,3},{132,4},{133,5},{134,6},{135,7},{1... | collective-permute-start | bytes 7077896 | tf_op jit(solution)/shard_map/ppermute | solution.py:388
  93.7 29.4 %all-to-all-start.2 = ((bf16[8,64,768]{2,1,0:T(8,128)(2,1)}), bf16[8,64,768]{2,1,0:T(8,128)(2,1)S(1)}, u32[]{:S(2)}, u32[]{:S(2)}) async-start(bf16[8,64,768]{2,1,0:T(8,128)(2,1)} %copy-done.8), calls=%async_computation.2 | async-start | bytes 1572864 | tf_op jit(solution)/shard_map/all_to_all | solution.py:364
  99.6 76.3 %collective-permute-start.9 = (bf16[3072,384]{1,0:T(8,128)(2,1)S(1)}, bf16[3072,384]{1,0:T(8,128)(2,1)}, u32[]{:S(2)}, u32[]{:S(2)}) collective-permute-start(bf16[3072,384]{1,0:T(8,128)(2,1)S(1)} %bitcast.79), channel_id=1, source_target_pairs={{128,136},{136,128},{129,137},{137,129},{130,138},{138,130},{131,1... | collective-permute-start | bytes 7077896 | tf_op jit(solution)/shard_map/ppermute | solution.py:384
  130.1 17.5 %all-to-all-start.3 = ((bf16[8,16,1536]{2,1,0:T(8,128)(2,1)}), bf16[8,16,1536]{2,1,0:T(8,128)(2,1)S(1)}, u32[]{:S(2)}, u32[]{:S(2)}) async-start(bf16[8,16,1536]{2,1,0:T(8,128)(2,1)} %bitcast.100), calls=%async_computation.3 | async-start | bytes 786432 | tf_op jit(solution)/shard_map/all_to_all | solution.py:364
  150.6 18.4 %all-to-all-start.4 = ((bf16[8,2,16,1536]{3,2,1,0:T(8,128)(2,1)}), bf16[8,2,16,1536]{3,2,1,0:T(8,128)(2,1)S(1)}, u32[]{:S(2)}, u32[]{:S(2)}) async-start(bf16[8,2,16,1536]{3,2,1,0:T(8,128)(2,1)} %copy-done.6), calls=%async_computation.5 | async-start | bytes 1572864 | tf_op jit(solution)/shard_map/all_to_all | solution.py:364
  154.1 62.1 %collective-permute-start.8 = (bf16[384,3072]{1,0:T(8,128)(2,1)}, bf16[384,3072]{1,0:T(8,128)(2,1)}, u32[]{:S(2)}, u32[]{:S(2)}) collective-permute-start(bf16[384,3072]{1,0:T(8,128)(2,1)} %bitcast.84), channel_id=1, source_target_pairs={{0,8},{8,0},{1,9},{9,1},{2,10},{10,2},{3,11},{11,3},{4,12},{12,4},... | collective-permute-start | bytes 7077896 | tf_op jit(solution)/shard_map/ppermute | solution.py:384
  175.9 46.5 %collective-permute-start.10 = (bf16[3072,384]{1,0:T(8,128)(2,1)}, bf16[3072,384]{1,0:T(8,128)(2,1)}, u32[]{:S(2)}, u32[]{:S(2)}) collective-permute-start(bf16[3072,384]{1,0:T(8,128)(2,1)} %collective-permute-done.9.own_mate), channel_id=1, source_target_pairs={{128,0},{129,1},{130,2},{131,3},{132,4},{133,5},{134,6},{135,7},{1... | collective-permute-start | bytes 7077896 | tf_op jit(solution)/shard_map/ppermute | solution.py:388
  188.8 21.0 %all-to-all-start.5 = ((bf16[8,64,768]{2,1,0:T(8,128)(2,1)}), bf16[8,64,768]{2,1,0:T(8,128)(2,1)}, u32[]{:S(2)}, u32[]{:S(2)}) async-start(bf16[8,64,768]{2,1,0:T(8,128)(2,1)} %copy-done.9), calls=%async_computation.6 | async-start | bytes 1572864 | tf_op jit(solution)/shard_map/all_to_all | solution.py:364
  216.2 26.9 %copy-start.15 = (bf16[64,768]{1,0:T(8,128)(2,1)}, bf16[64,768]{1,0:T(8,128)(2,1)S(1)}, u32[]{:S(2)}) copy-start(bf16[64,768]{1,0:T(8,128)(2,1)S(1)} %get-tuple-element.42) | copy-start | bytes 294916
  216.2 53.9 %collective-permute-start.17 = (bf16[384,3072]{1,0:T(8,128)(2,1)}, bf16[384,3072]{1,0:T(8,128)(2,1)}, u32[]{:S(2)}, u32[]{:S(2)}) collective-permute-start(bf16[384,3072]{1,0:T(8,128)(2,1)} %collective-permute-done.8.own_mate), channel_id=1, source_target_pairs={{0,128},{1,129},{2,130},{3,131},{4,132},{5,133},{6,134},{7,135},{8... | collective-permute-start | bytes 7077896 | tf_op jit(solution)/shard_map/ppermute | solution.py:388
  217.5 15.1 %all-to-all-start.6 = ((bf16[8,16,1536]{2,1,0:T(8,128)(2,1)}), bf16[8,16,1536]{2,1,0:T(8,128)(2,1)S(1)}, u32[]{:S(2)}, u32[]{:S(2)}) async-start(bf16[8,16,1536]{2,1,0:T(8,128)(2,1)} %bitcast.16), calls=%async_computation.7 | async-start | bytes 786432 | tf_op jit(solution)/shard_map/all_to_all | solution.py:364
  225.7 17.4 %copy-start.14 = (bf16[64,768]{1,0:T(8,128)(2,1)S(1)}, bf16[64,768]{1,0:T(8,128)(2,1)}, u32[]{:S(2)}) copy-start(bf16[64,768]{1,0:T(8,128)(2,1)} %copy-done.13) | copy-start | bytes 294916
  225.7 40.0 %copy-start.20 = (bf16[64,384]{1,0:T(8,128)(2,1)S(1)}, bf16[64,384]{1,0:T(8,128)(2,1)}, u32[]{:S(2)}) copy-start(bf16[64,384]{1,0:T(8,128)(2,1)} %copy-done.19) | copy-start | bytes 147460
  225.8 40.0 %copy-start.22 = (bf16[64,384]{1,0:T(8,128)(2,1)S(1)}, bf16[64,384]{1,0:T(8,128)(2,1)}, u32[]{:S(2)}) copy-start(bf16[64,384]{1,0:T(8,128)(2,1)} %copy-done.21) | copy-start | bytes 147460
  225.8 40.0 %copy-start.24 = (bf16[64,384]{1,0:T(8,128)(2,1)S(1)}, bf16[64,384]{1,0:T(8,128)(2,1)}, u32[]{:S(2)}) copy-start(bf16[64,384]{1,0:T(8,128)(2,1)} %get-tuple-element.61) | copy-start | bytes 147460
  225.8 40.0 %copy-start.26 = (bf16[64,384]{1,0:T(8,128)(2,1)S(1)}, bf16[64,384]{1,0:T(8,128)(2,1)}, u32[]{:S(2)}) copy-start(bf16[64,384]{1,0:T(8,128)(2,1)} %copy-done.25) | copy-start | bytes 147460
  225.8 40.0 %copy-start.27 = (bf16[64,384]{1,0:T(8,128)(2,1)S(1)}, bf16[64,384]{1,0:T(8,128)(2,1)}, u32[]{:S(2)}) copy-start(bf16[64,384]{1,0:T(8,128)(2,1)} %get-tuple-element.64) | copy-start | bytes 147460
  225.8 40.0 %copy-start.28 = (bf16[64,384]{1,0:T(8,128)(2,1)S(1)}, bf16[64,384]{1,0:T(8,128)(2,1)}, u32[]{:S(2)}) copy-start(bf16[64,384]{1,0:T(8,128)(2,1)} %get-tuple-element.69) | copy-start | bytes 147460
  225.8 40.0 %copy-start.30 = (bf16[64,384]{1,0:T(8,128)(2,1)S(1)}, bf16[64,384]{1,0:T(8,128)(2,1)}, u32[]{:S(2)}) copy-start(bf16[64,384]{1,0:T(8,128)(2,1)} %copy-done.29) | copy-start | bytes 147460
  225.8 40.0 %copy-start.31 = (bf16[64,384]{1,0:T(8,128)(2,1)S(1)}, bf16[64,384]{1,0:T(8,128)(2,1)}, u32[]{:S(2)}) copy-start(bf16[64,384]{1,0:T(8,128)(2,1)} %get-tuple-element.72) | copy-start | bytes 147460
  233.5 36.7 %all-to-all-start.7 = ((bf16[8,1,16,1536]{3,2,1,0:T(8,128)(2,1)}), bf16[8,1,16,1536]{3,2,1,0:T(8,128)(2,1)S(1)}, u32[]{:S(2)}, u32[]{:S(2)}) async-start(bf16[8,1,16,1536]{3,2,1,0:T(8,128)(2,1)} %shard_map.84), calls=%async_computation.8 | async-start | bytes 786432 | tf_op jit(solution)/shard_map/all_to_all | solution.py:364
  238.1 27.8 %collective-permute-start.11 = (bf16[4,2,16,1536]{3,2,1,0:T(8,128)(2,1)S(1)}, bf16[4,2,16,1536]{3,2,1,0:T(8,128)(2,1)S(1)}, u32[]{:S(2)}, u32[]{:S(2)}) collective-permute-start(bf16[4,2,16,1536]{3,2,1,0:T(8,128)(2,1)S(1)} %get-tuple-element.56), channel_id=1, source_target_pairs={{0,128},{128,0},{1,129},{129,1},{2,130},{130,2},{3,131},{131,3},{4... | collective-permute-start | bytes 1179656 | tf_op jit(solution)/shard_map/ppermute | solution.py:371
  241.7 24.3 %collective-permute-start.13 = (bf16[4,2,16,1536]{3,2,1,0:T(8,128)(2,1)S(1)}, bf16[4,2,16,1536]{3,2,1,0:T(8,128)(2,1)S(1)}, u32[]{:S(2)}, u32[]{:S(2)}) collective-permute-start(bf16[4,2,16,1536]{3,2,1,0:T(8,128)(2,1)S(1)} %get-tuple-element.56), channel_id=1, source_target_pairs={{0,136},{136,0},{8,128},{128,8},{1,137},{137,1},{9,129},{129,9},{2... | collective-permute-start | bytes 1179656 | tf_op jit(solution)/shard_map/ppermute | solution.py:379
  241.7 24.3 %collective-permute-start.12 = (bf16[4,2,16,1536]{3,2,1,0:T(8,128)(2,1)S(1)}, bf16[4,2,16,1536]{3,2,1,0:T(8,128)(2,1)S(1)}, u32[]{:S(2)}, u32[]{:S(2)}) collective-permute-start(bf16[4,2,16,1536]{3,2,1,0:T(8,128)(2,1)S(1)} %get-tuple-element.50.refs_0_), channel_id=1, source_target_pairs={{0,8},{8,0},{1,9},{9,1},{2,10},{10,2},{3,11},{11,3},{4,12},{12,4},... | collective-permute-start | bytes 1179656 | tf_op jit(solution)/shard_map/ppermute | solution.py:375
  243.2 1.7 collective-permute-start.14
  244.8 16.9 %collective-permute-start.15 = (bf16[64,384]{1,0:T(8,128)(2,1)S(1)}, bf16[64,384]{1,0:T(8,128)(2,1)S(1)}, u32[]{:S(2)}, u32[]{:S(2)}) collective-permute-start(bf16[64,384]{1,0:T(8,128)(2,1)S(1)} %get-tuple-element.67), channel_id=1, source_target_pairs={{0,8},{8,0},{1,9},{9,1},{2,10},{10,2},{3,11},{11,3},{4,12},{12,4},... | collective-permute-start | bytes 147464 | tf_op jit(solution)/shard_map/ppermute | solution.py:375
  261.7 4.1 %collective-permute-start.16 = (bf16[64,384]{1,0:T(8,128)(2,1)S(1)}, bf16[64,384]{1,0:T(8,128)(2,1)S(1)}, u32[]{:S(2)}, u32[]{:S(2)}) collective-permute-start(bf16[64,384]{1,0:T(8,128)(2,1)S(1)} %get-tuple-element.68), channel_id=1, source_target_pairs={{0,136},{136,0},{8,128},{128,8},{1,137},{137,1},{9,129},{129,9},{2... | collective-permute-start | bytes 147464 | tf_op jit(solution)/shard_map/ppermute | solution.py:379
  274.4 13.2 %all-to-all-start.8 = ((bf16[8,2,16,768]{3,2,1,0:T(8,128)(2,1)}), bf16[8,2,16,768]{3,2,1,0:T(8,128)(2,1)S(1)}, u32[]{:S(2)}, u32[]{:S(2)}) async-start(bf16[8,2,16,768]{3,2,1,0:T(8,128)(2,1)} %bitcast.23), calls=%async_computation.9 | async-start | bytes 786432 | tf_op jit(solution)/shard_map/all_to_all | solution.py:364
  277.9 18.8 %collective-permute-start.24 = (bf16[4,2,16,1536]{3,2,1,0:T(8,128)(2,1)S(1)}, bf16[4,2,16,1536]{3,2,1,0:T(8,128)(2,1)S(1)}, u32[]{:S(2)}, u32[]{:S(2)}) collective-permute-start(bf16[4,2,16,1536]{3,2,1,0:T(8,128)(2,1)S(1)} %get-tuple-element.58.refs_4_), channel_id=1, source_target_pairs={{0,128},{1,129},{2,130},{3,131},{4,132},{5,133},{6,134},{7,135},{8... | collective-permute-start | bytes 1179656 | tf_op jit(solution)/shard_map/ppermute | solution.py:388
  279.2 24.2 %collective-permute-start.25 = (bf16[4,2,16,1536]{3,2,1,0:T(8,128)(2,1)S(1)}, bf16[4,2,16,1536]{3,2,1,0:T(8,128)(2,1)S(1)}, u32[]{:S(2)}, u32[]{:S(2)}) collective-permute-start(bf16[4,2,16,1536]{3,2,1,0:T(8,128)(2,1)S(1)} %get-tuple-element.58.refs_4_), channel_id=1, source_target_pairs={{128,136},{136,128},{129,137},{137,129},{130,138},{138,130},{131,1... | collective-permute-start | bytes 1179656 | tf_op jit(solution)/shard_map/ppermute | solution.py:384
  281.4 22.0 %collective-permute-start.26 = (bf16[4,2,16,1536]{3,2,1,0:T(8,128)(2,1)S(1)}, bf16[4,2,16,1536]{3,2,1,0:T(8,128)(2,1)S(1)}, u32[]{:S(2)}, u32[]{:S(2)}) collective-permute-start(bf16[4,2,16,1536]{3,2,1,0:T(8,128)(2,1)S(1)} %get-tuple-element.58.refs_4_), channel_id=1, source_target_pairs={{0,136},{8,128},{1,137},{9,129},{2,138},{10,130},{3,139},{11,131},... | collective-permute-start | bytes 1179656 | tf_op jit(solution)/shard_map/ppermute | solution.py:393
  288.5 3.1 collective-permute-start.18
  288.9 5.6 %collective-permute-start.19 = (bf16[2,16,384]{2,1,0:T(8,128)(2,1)S(1)}, bf16[2,16,384]{2,1,0:T(8,128)(2,1)S(1)}, u32[]{:S(2)}, u32[]{:S(2)}) collective-permute-start(bf16[2,16,384]{2,1,0:T(8,128)(2,1)S(1)} %get-tuple-element.78), channel_id=1, source_target_pairs={{0,128},{128,0},{1,129},{129,1},{2,130},{130,2},{3,131},{131,3},{4... | collective-permute-start | bytes 73736 | tf_op jit(solution)/shard_map/ppermute | solution.py:371
  291.6 4.4 %collective-permute-start.20 = (bf16[2,16,384]{2,1,0:T(8,128)(2,1)S(1)}, bf16[2,16,384]{2,1,0:T(8,128)(2,1)S(1)}, u32[]{:S(2)}, u32[]{:S(2)}) collective-permute-start(bf16[2,16,384]{2,1,0:T(8,128)(2,1)S(1)} %get-tuple-element.77), channel_id=1, source_target_pairs={{0,136},{136,0},{8,128},{128,8},{1,137},{137,1},{9,129},{129,9},{2... | collective-permute-start | bytes 73736 | tf_op jit(solution)/shard_map/ppermute | solution.py:379
  294.5 8.9 %collective-permute-start.21 = (bf16[4,2,16,1536]{3,2,1,0:T(8,128)(2,1)S(1)}, bf16[4,2,16,1536]{3,2,1,0:T(8,128)(2,1)S(1)}, u32[]{:S(2)}, u32[]{:S(2)}) collective-permute-start(bf16[4,2,16,1536]{3,2,1,0:T(8,128)(2,1)S(1)} %bitcast.92), channel_id=1, source_target_pairs={{128,0},{129,1},{130,2},{131,3},{132,4},{133,5},{134,6},{135,7},{1... | collective-permute-start | bytes 1179656 | tf_op jit(solution)/shard_map/ppermute | solution.py:388
  296.0 7.4 %collective-permute-start.22 = (bf16[4,2,16,1536]{3,2,1,0:T(8,128)(2,1)S(1)}, bf16[4,2,16,1536]{3,2,1,0:T(8,128)(2,1)S(1)}, u32[]{:S(2)}, u32[]{:S(2)}) collective-permute-start(bf16[4,2,16,1536]{3,2,1,0:T(8,128)(2,1)S(1)} %bitcast.93), channel_id=1, source_target_pairs={{0,8},{8,0},{1,9},{9,1},{2,10},{10,2},{3,11},{11,3},{4,12},{12,4},... | collective-permute-start | bytes 1179656 | tf_op jit(solution)/shard_map/ppermute | solution.py:384
  296.7 12.4 %collective-permute-start.23 = (bf16[4,2,16,1536]{3,2,1,0:T(8,128)(2,1)S(1)}, bf16[4,2,16,1536]{3,2,1,0:T(8,128)(2,1)S(1)}, u32[]{:S(2)}, u32[]{:S(2)}) collective-permute-start(bf16[4,2,16,1536]{3,2,1,0:T(8,128)(2,1)S(1)} %bitcast.94), channel_id=1, source_target_pairs={{128,8},{136,0},{129,9},{137,1},{130,10},{138,2},{131,11},{139,3},... | collective-permute-start | bytes 1179656 | tf_op jit(solution)/shard_map/ppermute | solution.py:393
  (21 other events, 73.1 us)
Sparse Core Ops, SparseCore 0:
  68.0 75.1 reduce-scatter.1

commit v2 on v1

v2 whole, which is shorter than its diff:
```python
import functools

import jax
import jax.numpy as jnp
from jax import lax
from jax.experimental import pallas as pl
from jax.experimental.pallas import tpu as pltpu
from jax.sharding import Mesh, PartitionSpec as P

root_two_over_pi = 0.7978845608028654
cubic = 0.044715
f32 = jnp.float32
bf16 = jnp.bfloat16
CHUNK = 512
VMEM = pl.BlockSpec(memory_space=pltpu.VMEM)
HBM = pl.BlockSpec(memory_space=pltpu.HBM)
ANY = pl.BlockSpec(memory_space=pl.ANY)
LIMIT = pltpu.CompilerParams(vmem_limit_bytes=64 * 1024 * 1024)


def gelu_both(pre):
    inner = root_two_over_pi * (pre + cubic * pre * pre * pre)
    tangent = jnp.tanh(inner)
    value = 0.5 * pre * (1.0 + tangent)
    slope = 0.5 * (1.0 + tangent) + 0.5 * pre * (1.0 - tangent * tangent) * root_two_over_pi * (
        1.0 + 3.0 * cubic * pre * pre
    )
    return value, slope


def dot(left, right, dims):
    return lax.dot_general(left, right, (dims, ((), ())), preferred_element_type=f32)


def shape_of(shape, dtype=bf16):
    return jax.ShapeDtypeStruct(shape, dtype)


def load_weights(layer, by_rows, refs, held, sems):
    mine = lax.axis_index("section") == layer

    def copy(source, part, i):
        where = pl.ds(i * CHUNK, CHUNK)
        block = source.at[where, :] if by_rows else source.at[:, where]
        return pltpu.make_async_copy(block, held.at[part, i], sems.at[part, i])

    def start(which):
        for i in range(held.shape[1]):
            for part, pair in enumerate(refs):
                copy(pair[which], part, i).start()

    pl.when(mine)(lambda: start(0))
    pl.when(jnp.logical_not(mine))(lambda: start(1))
    return lambda part, i: copy(refs[part][0], part, i).wait()


def widen(xs, by_rows, wait, held, put):
    for i in range(held.shape[1]):
        total = None
        for part, x in enumerate(xs):
            wait(part, i)
            got = dot(x, held[part, i], ((1,), (1 if by_rows else 0,)))
            total = got if total is None else total + got
        put(i, total)


def widen_first_kernel(layer, by_rows, mate_at, x_ref, own, other, out_ref, held, sems, stage, out_sems):
    wait = load_weights(layer, by_rows, ((own, other),), held, sems)
    groups, tokens, wide = stage.shape[1 if mate_at == 0 else 0], stage.shape[3], stage.shape[4]
    per_half = wide // CHUNK

    def out_copy(half):
        where = (slice(None),) * (2 if mate_at == 0 else 1) + (half,)
        return pltpu.make_async_copy(stage.at[where], out_ref.at[where], out_sems.at[half])

    def put(i, total):
        half, place = i // per_half, pl.ds((i % per_half) * CHUNK, CHUNK)
        total = total.astype(bf16).reshape(2, groups, tokens, CHUNK)
        for mate in range(2):
            if mate_at == 0:
                stage[mate, :, half, :, place] = total[mate]
            else:
                stage[:, half, mate, :, place] = total[mate]
        if i % per_half == per_half - 1:
            out_copy(half).start()

    widen((x_ref[...],), by_rows, wait, held, put)
    out_copy(0).wait()
    out_copy(1).wait()


def widen_next_kernel(layer, by_rows, riders, arrived, base, own, other, own_mate, other_mate, *rest):
    out_ref, x_out, held, sems, stage, out_sems = rest[riders:]
    wait = load_weights(layer, by_rows, ((own, other), (own_mate, other_mate)), held, sems)
    copies = [
        pltpu.make_async_copy(rest[i], out_ref.at[:, :, 1 + i], out_sems.at[2 + i]) for i in range(riders)
    ]
    for copy in copies:
        copy.start()
    width, per_half = base.shape[1] // 2, stage.shape[3] // CHUNK
    total = arrived[0].astype(f32)
    for i in range(1, arrived.shape[0]):
        total = total + arrived[i].astype(f32)
    x = (base[...].astype(f32) + total).astype(bf16)
    x_out[...] = x

    def out_copy(half):
        return pltpu.make_async_copy(stage.at[:, half], out_ref.at[:, half, 0], out_sems.at[half])

    def put(i, total):
        half, at = i // per_half, (i % per_half) * CHUNK
        stage[:, half, :, pl.ds(at, CHUNK)] = total.astype(bf16).reshape(stage.shape[0], stage.shape[2], CHUNK)
        if i % per_half == per_half - 1:
            out_copy(half).start()

    widen((x[:, :width], x[:, width:]), by_rows, wait, held, put)
    for copy in [out_copy(0), out_copy(1)] + copies:
        copy.wait()


def narrow(by_rows, which, arrived, wait, held):
    per_half = arrived.shape[4] // CHUNK
    totals = [None, None]
    for i in range(held.shape[1]):
        left = arrived[:, i // per_half, which, :, pl.ds((i % per_half) * CHUNK, CHUNK)]
        left = left.reshape(left.shape[0] * left.shape[1], CHUNK)
        for part in range(2):
            wait(part, i)
            got = dot(left, held[part, i], ((1,), (0 if by_rows else 1,)))
            totals[part] = got if i == 0 else totals[part] + got
    return [total.astype(bf16) for total in totals]


def narrow_kernel(
    layer, by_rows, which, arrived, own, other, own_mate, other_mate, out_ref, held, sems, stage, out_sems
):
    wait = load_weights(layer, by_rows, ((own, other), (own_mate, other_mate)), held, sems)
    near, far = narrow(by_rows, which, arrived, wait, held)
    width = near.shape[1]
    stage[:, :width] = near
    stage[:, width:] = far
    copies = [
        pltpu.make_async_copy(stage, out_ref.at[i], out_sems.at[i]) for i in range(out_ref.shape[0])
    ]
    for copy in copies:
        copy.start()
    for copy in copies:
        copy.wait()


def held_scratch(weight, by_rows, parts):
    units = max(weight.shape)
    chunk = (CHUNK, weight.shape[1]) if by_rows else (weight.shape[0], CHUNK)
    return [
        pltpu.VMEM((parts, units // CHUNK) + chunk, bf16),
        pltpu.SemaphoreType.DMA((parts, units // CHUNK)),
    ]


def kernel_call(body, outs, out_specs, in_specs, scratch, operands, flops=0, moved=0):
    return pl.pallas_call(
        body,
        out_shape=outs,
        in_specs=in_specs,
        out_specs=out_specs,
        scratch_shapes=scratch,
        compiler_params=LIMIT,
        cost_estimate=pl.CostEstimate(flops=flops, bytes_accessed=moved, transcendentals=0),
    )(*operands)


def widen_first(layer, by_rows, mate_at, x, weights, blocks):
    shape = blocks[:mate_at] + (2,) + blocks[mate_at:]
    return kernel_call(
        functools.partial(widen_first_kernel, layer, by_rows, mate_at),
        shape_of(shape),
        HBM,
        [VMEM, HBM, HBM],
        held_scratch(weights[0], by_rows, 1) + [pltpu.VMEM(shape, bf16), pltpu.SemaphoreType.DMA((2,))],
        (x,) + weights[:2],
        flops=2 * x.shape[0] * weights[0].size,
        moved=2 * weights[0].size,
    )


def widen_next(layer, by_rows, arrived, base, weights, blocks, riders=()):
    return kernel_call(
        functools.partial(widen_next_kernel, layer, by_rows, len(riders)),
        (shape_of(blocks[:2] + (1 + len(riders),) + blocks[2:]), shape_of(base.shape)),
        (HBM, VMEM),
        [VMEM, VMEM] + [HBM] * (4 + len(riders)),
        held_scratch(weights[0], by_rows, 2)
        + [pltpu.VMEM(blocks, bf16), pltpu.SemaphoreType.DMA((2 + len(riders),))],
        (arrived, base) + weights + riders,
        flops=4 * base.shape[0] * weights[0].size,
        moved=4 * weights[0].size,
    )


def narrow_next(layer, by_rows, which, arrived, weights, copies):
    tokens, width = arrived.shape[0] * arrived.shape[3], 2 * min(weights[0].shape)
    return kernel_call(
        functools.partial(narrow_kernel, layer, by_rows, which),
        shape_of((copies, tokens, width)),
        HBM,
        [VMEM] + [HBM] * 4,
        held_scratch(weights[0], by_rows, 2)
        + [pltpu.VMEM((tokens, width), bf16), pltpu.SemaphoreType.DMA((copies,))],
        (arrived,) + weights,
        flops=4 * tokens * weights[0].size,
        moved=4 * weights[0].size,
    )


def summed(ref, kind, place):
    total = ref[0, kind, :, place].astype(f32)
    for i in range(1, ref.shape[0]):
        total = total + ref[i, kind, :, place].astype(f32)
    return total


def spread(stage, out_ref, sems):
    copies = [pltpu.make_async_copy(stage, out_ref.at[i], sems.at[i]) for i in range(out_ref.shape[0])]
    for copy in copies:
        copy.start()
    for copy in copies:
        copy.wait()


def act_first_kernel(arrived, out_ref, slope_ref, stage, sems):
    for at in range(0, arrived.shape[3], CHUNK):
        place = pl.ds(at, CHUNK)
        value, slope = gelu_both(summed(arrived, 0, place))
        stage[0, :, place] = value.astype(bf16)
        slope_ref[:, place] = slope
    spread(stage, out_ref, sems)


def act_last_kernel(arrived, out_ref, stage, sems):
    for at in range(0, arrived.shape[3], CHUNK):
        place = pl.ds(at, CHUNK)
        value, slope = gelu_both(summed(arrived, 0, place))
        stage[0, :, place] = (summed(arrived, 1, place) * slope).astype(bf16)
        stage[1, :, place] = value.astype(bf16)
    spread(stage, out_ref, sems)


def act_back_kernel(arrived, slope_ref, out_ref, stage, sems):
    for at in range(0, arrived.shape[3], CHUNK):
        place = pl.ds(at, CHUNK)
        stage[0, :, place] = (summed(arrived, 0, place) * slope_ref[:, place]).astype(bf16)
    spread(stage, out_ref, sems)


def activation(body, kinds, peers, piece, operands, in_specs, slope=False):
    outs, out_specs = [shape_of((peers, kinds) + piece)], [HBM]
    if slope:
        outs, out_specs = outs + [shape_of(piece, f32)], out_specs + [VMEM]
    return kernel_call(
        body,
        outs,
        out_specs,
        in_specs,
        [pltpu.VMEM((kinds,) + piece, bf16), pltpu.SemaphoreType.DMA((peers,))],
        operands,
        flops=2000000,
        moved=2000000,
    )


def pick_copies(layer0, layer1, kind, held, sems, start):
    section = lax.axis_index("section")

    def copy(layer, i):
        source = (layer0, layer1)[layer][i].at[:, :, 0 if layer == 0 else kind]
        return pltpu.make_async_copy(source, held.at[i], sems.at[i])

    if start:
        for layer in range(2):

            @pl.when(section == layer)
            def _():
                for i in range(4):
                    copy(layer, i).start()
    else:
        for i in range(4):
            copy(0, i).wait()


def step_chunk(held, step):
    per_half = held.shape[4] // CHUNK
    place = pl.ds(pl.multiple_of((step % per_half) * CHUNK, CHUNK), CHUNK)
    return held[:, :, step // per_half, :, place].reshape(-1, CHUNK)


def grad_down_kernel(g_ref, *refs):
    layer0, layer1, (out_ref, held, sems) = refs[:4], refs[4:8], refs[8:]
    step = pl.program_id(0)

    @pl.when(step == 0)
    def _():
        pick_copies(layer0, layer1, 1, held, sems, True)
        pick_copies(layer0, layer1, 1, held, sems, False)

    out_ref[...] = dot(step_chunk(held, step), g_ref[...], ((0,), (0,)))


def grad_up_kernel(x_ref, *refs):
    layer0, layer1, (out_ref, held, turned, sems) = refs[:4], refs[4:8], refs[8:]
    step = pl.program_id(0)

    @pl.when(step == 0)
    def _():
        pick_copies(layer0, layer1, 0, held, sems, True)
        turned[...] = x_ref[...].T
        pick_copies(layer0, layer1, 0, held, sems, False)

    out_ref[...] = dot(turned[...], step_chunk(held, step), ((1,), (0,)))


def weight_grad(down, narrow, layer0, layer1):
    groups, halves, _, tokens, wide = layer0[0].shape
    units, (all_tokens, width) = halves * wide, narrow.shape
    shape, block = ((units, width), (CHUNK, width)) if down else ((width, units), (width, CHUNK))
    turned = [] if down else [pltpu.VMEM((width, all_tokens), bf16)]
    return pl.pallas_call(
        grad_down_kernel if down else grad_up_kernel,
        out_shape=shape_of(shape, f32),
        grid=(units // CHUNK,),
        in_specs=[pl.BlockSpec(narrow.shape, lambda i: (0, 0))] + [HBM] * 8,
        out_specs=pl.BlockSpec(block, lambda i: (i, 0) if down else (0, i)),
        scratch_shapes=[pltpu.VMEM((4, groups, halves, tokens, wide), bf16)]
        + turned
        + [pltpu.SemaphoreType.DMA((4,))],
        compiler_params=LIMIT,
        cost_estimate=pl.CostEstimate(
            flops=2 * narrow.size * units, bytes_accessed=4 * width * units, transcendentals=0
        ),
    )(narrow, *layer0, *layer1)


def last_kernel(up, down, *refs):
    layer0, layer1, rest = refs[:4], refs[4:8], refs[8:]
    out_ref, held, up_held, down_held, stage, sems, up_sems, down_sems, out_sem = rest
    section, mate_pos = lax.axis_index("section"), lax.axis_index("x_lo")
    groups, halves, tokens, wide = held.shape[1:]
    per_half, count = wide // CHUNK, up_held.shape[0]
    pick_copies(layer0, layer1, 1, held, sems, True)

    def run(weight, by_rows, weight_held, weight_sems):
        copies = []
        for i in range(count):
            where = pl.ds(i * CHUNK, CHUNK)
            source = weight.at[where, :] if by_rows else weight.at[:, where]
            copies.append(pltpu.make_async_copy(source, weight_held.at[i], weight_sems.at[i]))
        for copy in copies:
            copy.start()
        pick_copies(layer0, layer1, 1, held, sems, False)
        total = None
        for i in range(count):
            left = held[:, :, i // per_half, :, pl.ds((i % per_half) * CHUNK, CHUNK)].reshape(-1, CHUNK)
            copies[i].wait()
            got = dot(left, weight_held[i], ((1,), (0 if by_rows else 1,)))
            total = got if total is None else total + got
        total = total.astype(bf16).reshape(4, groups, tokens, -1)
        for i in range(4):
            half = mate_pos if i < 2 else 1 - mate_pos
            which = section if i % 2 == 0 else 1 - section
            stage[pl.ds(half * groups, groups), which] = total[i]

    pl.when(section == 0)(lambda: run(up, False, up_held, up_sems))
    pl.when(section == 1)(lambda: run(down, True, down_held, down_sems))
    copy = pltpu.make_async_copy(stage, out_ref, out_sem)
    copy.start()
    copy.wait()


def last_product(up, down, layer0, layer1):
    groups, halves, _, tokens, wide = layer0[0].shape
    width, units = up.shape
    out = (2 * groups, 2, tokens, width)
    return kernel_call(
        last_kernel,
        shape_of(out),
        HBM,
        [HBM] * 10,
        [
            pltpu.VMEM((4, groups, halves, tokens, wide), bf16),
            pltpu.VMEM((units // CHUNK, width, CHUNK), bf16),
            pltpu.VMEM((units // CHUNK, CHUNK, width), bf16),
            pltpu.VMEM(out, bf16),
            pltpu.SemaphoreType.DMA((4,)),
            pltpu.SemaphoreType.DMA((units // CHUNK,)),
            pltpu.SemaphoreType.DMA((units // CHUNK,)),
            pltpu.SemaphoreType.DMA,
        ],
        (up, down) + layer0 + layer1,
        flops=8 * groups * tokens * up.size,
        moved=6 * up.size,
    )


def exchange(blocks, axes):
    return lax.all_to_all(blocks, axes, 0, 0)


CORES = ("section", "x_lo")


def to_other_core(block):
    return lax.ppermute(block, "section", [(0, 1), (1, 0)])


def to_mate(block):
    return lax.ppermute(block, "x_lo", [(0, 1), (1, 0)])


def to_other_core_of_mate(block):
    return lax.ppermute(block, CORES, [(0, 3), (3, 0), (1, 2), (2, 1)])


def only_to_mate(block, section):
    at = 2 * section
    return lax.ppermute(block, CORES, [(at, at + 1), (at + 1, at)])


def only_to_core(block, section):
    return lax.ppermute(block, "section", [(1 - section, section)])


def to_owner(block, section):
    at, source = 2 * section, 2 * (1 - section)
    across = lax.ppermute(block, CORES, [(source, at + 1), (source + 1, at)])
    return block, only_to_core(block, section), only_to_mate(block, section), across


def late(block, after):
    return lax.optimization_barrier((block, after))[0]


def local(inputs, cotangent, w_up, w_down):
    col = ("y", "x_hi")
    section, mate_pos, col_pos = (lax.axis_index(name) for name in ("section", "x_lo", col))
    first = section == 0
    own_up, own_down = w_up[0], w_down[0]
    tokens, width = inputs.shape[1:]
    half_len = tokens // 2
    rings = lax.axis_size("z")
    piece = (tokens // rings, own_up.shape[1] // 2)
    blocks = (half_len // piece[0], 2) + piece

    def half_of(array, which):
        return lax.dynamic_slice_in_dim(array, which * half_len, half_len, 0)

    def batch(array, which):
        return lax.dynamic_index_in_dim(array, which, 0, keepdims=False)

    def both_widths(array):
        return jnp.concatenate([half_of(array, mate_pos), to_mate(half_of(array, 1 - mate_pos))], axis=1)

    x0, g2 = batch(inputs, section), batch(cotangent, section)
    other_up = to_other_core(own_up)
    first_part = widen_first(0, False, 2, x0, (own_up, other_up), blocks)
    mate_down0 = only_to_mate(late(own_down, other_up), 0)
    arrived = exchange(first_part.reshape((2 * rings, 1) + piece), ("z", "x_lo"))

    other_down = to_other_core(late(own_down, other_up))
    d_hid1 = widen_first(1, True, 0, late(g2, first_part), (own_down, other_down), blocks)
    arrived, mate_down0 = late((arrived, mate_down0), d_hid1)
    d_hid1, given = batch(d_hid1, mate_pos), to_mate(batch(d_hid1, 1 - mate_pos))
    down0 = own_down, other_down, mate_down0, only_to_core(mate_down0, 1)

    value0, slope0 = activation(act_first_kernel, 1, rings, piece, (arrived,), [VMEM], slope=True)
    mate_up1 = only_to_mate(late(own_up, value0), 1)
    hid0 = exchange(value0, "z").reshape(blocks[:2] + (1,) + piece)
    x0_both, g2_both = (both_widths(late(array, value0)) for array in (x0, g2))
    d_hid1 = (d_hid1.astype(f32) + late(given, value0).astype(f32)).astype(bf16)
    hid0 = late(hid0, d_hid1)
    part = narrow_next(0, True, 0, hid0, down0, lax.axis_size(col))
    mate_up1, x0_both, g2_both = late((mate_up1, x0_both, g2_both), part)
    up1 = own_up, other_up, mate_up1, only_to_core(mate_up1, 0)
    arrived = exchange(part, col)

    pre1, x1 = widen_next(1, False, arrived, x0_both, up1, blocks, (d_hid1,))
    hid0s = to_owner(late(hid0, pre1), 0)
    arrived = exchange(pre1.reshape((rings, 2) + piece), "z")
    (acts1,) = activation(act_last_kernel, 2, rings, piece, (arrived,), [VMEM])
    acts1 = late(exchange(acts1, "z").reshape(blocks[:2] + (2,) + piece), hid0s)
    part = narrow_next(1, False, 0, acts1, up1, lax.axis_size(col))
    arrived = exchange(part, col)

    d_hid0, g1 = widen_next(0, True, arrived, g2_both, down0, blocks)
    acts1, both1 = late((acts1, jnp.stack([x1, g1])), d_hid0)
    acts1s = to_owner(acts1, 1)
    arrived = exchange(d_hid0.reshape((rings, 1) + piece), "z")
    near, far = both1[..., :width], both1[..., width:]
    both1 = jnp.stack([near, to_other_core(near), to_mate(far), to_other_core_of_mate(far)])
    both1 = both1.reshape((2, 2) + near.shape)

    def all_tokens(array):
        return jnp.concatenate(
            [
                half_of(batch(array, which), half)
                for half in (mate_pos, 1 - mate_pos)
                for which in (section, 1 - section)
            ]
        )

    x1s, g1s = both1[:, :, 0].reshape(2 * tokens, width), both1[:, :, 1].reshape(2 * tokens, width)
    xs = jnp.where(first, all_tokens(inputs), x1s)
    gs = jnp.where(first, g1s, all_tokens(cotangent))

    (d_pre0,) = activation(act_back_kernel, 1, rings, piece, (arrived, slope0), [VMEM, VMEM])
    d_pre0 = late(exchange(d_pre0, "z").reshape(blocks[:2] + (1,) + piece), acts1s)
    down_grad = weight_grad(True, late(gs, d_pre0), hid0s, acts1s)
    d_pre0s = late(to_owner(d_pre0, 0), down_grad)

    last = last_product(own_up, own_down, d_pre0s, acts1s)
    xs, d_pre0s = late((xs, d_pre0s), last)
    arrived = exchange(last, col)
    up_grad = weight_grad(False, xs, d_pre0s, acts1s)

    out_len = tokens // lax.axis_size(col)
    per_half = half_len // out_len
    away = jnp.where(col_pos // per_half == mate_pos, 0, 1)
    pieces = lax.dynamic_index_in_dim(both1, away, 0, keepdims=False)
    pieces = lax.dynamic_slice_in_dim(pieces, (col_pos % per_half) * out_len, out_len, 2)
    pieces = jnp.where(first, pieces, pieces[::-1])
    x1, g1 = pieces[:, 0], pieces[:, 1]
    ended = jnp.sum(arrived.astype(f32), axis=0)
    ended = (jnp.where(first, g1, x1).astype(f32) + ended).astype(bf16)
    states, grads = jnp.where(first, x1, ended), jnp.where(first, ended, g1)
    return states[None], grads[None], up_grad[None], down_grad[None]


def solution(mesh):
    sections, rows, cols = mesh.devices.shape
    finer = Mesh(
        mesh.devices.reshape(sections, rows // 2, 2, cols // 2, 2),
        ("section", "z", "x_lo", "y", "x_hi"),
    )
    row, col = ("z", "x_lo"), ("y", "x_hi")
    in_specs = (
        P(None, None, row),
        P(None, None, row),
        P("section", row, col),
        P("section", col, row),
    )
    out_specs = (
        P("section", None, col, row),
        P("section", None, col, row),
        P("section", row, col),
        P("section", col, row),
    )
    return jax.shard_map(local, mesh=finer, in_specs=in_specs, out_specs=out_specs, check_vma=False)
```

time: 323 us -> 280 us (0.87)
  waiting for transfers between devices: 130 us -> 73.2 us
  blocking collectives: 0 us -> 51.8 us
  starting transfers between devices: 109 us -> 69.6 us
  Pallas kernels: 42 us -> 63.4 us
  between operations: 14.8 us -> 0.97 us
  local copies, waits for them, and re-layouts: 21.6 us -> 8.28 us
  other arithmetic: 4.08 us -> 10.9 us
    all_to_all x9 -> x6, waiting for transfers between devices: 85.7 us -> 31.2 us  [exchange(): return lax.all_to_all(blocks, axes, 0, 0)]
    all_to_all x0 -> x3, blocking collectives: none -> 51.8 us  [exchange(): return lax.all_to_all(blocks, axes, 0, 0)]
    pallas_call x11 -> x10, Pallas kernels: 33.3 us -> 51 us  [kernel_call(): pl.pallas_call(body, out_shape=outs, in_specs=in_specs, out_specs=out_spe...]
    ppermute x6 -> x5, starting transfers between devices: 26.6 us -> 10.5 us  [only_to_core(): return lax.ppermute(block, 'section', [(1 - section, section)])]
    unnamed x64 -> x10, local copies, waits for them, and re-layouts: 14.6 us -> 0.02 us
    all_to_all x9 -> x6, starting transfers between devices: 44.4 us -> 32 us  [exchange(): return lax.all_to_all(blocks, axes, 0, 0)]
    reduce_scatter x1 -> x0, waiting for transfers between devices: 9.6 us -> none  [local(): lax.psum_scatter(d_hid1.reshape(2 * tokens, piece[1]), ('z', 'x_lo'), sca...]
    ppermute x5 -> x3, starting transfers between devices: 12.1 us -> 3.7 us  [to_other_core(): return lax.ppermute(block, 'section', [(0, 1), (1, 0)])]
  transfers between devices with their start and end apart: 37 -> 27, of which waited for: 17 -> 10; matrix products, arithmetic and copies ran while one was open for 3% -> 6% of each run, Pallas kernels for 10% -> 11%
where the time goes in v2:
time: 280 us; the launch traced here: 278 us
  waiting for transfers between devices  73.2 us (26%)
  starting transfers between devices  69.6 us (25%)
  Pallas kernels  63.4 us (23%)
  blocking collectives  51.8 us (18%)
  other arithmetic  10.9 us (4%)
  local copies, waits for them, and re-layouts  8.28 us (3%)
    all_to_all x3, blocking collectives, exchange(): return lax.all_to_all(blocks, axes, 0, 0)  51.8 us
    pallas_call x10, Pallas kernels, kernel_call(): pl.pallas_call(body, out_shape=outs, in_specs=in_specs, out_specs=out_spe...  51 us
    all_to_all x6, starting transfers between devices, exchange(): return lax.all_to_all(blocks, axes, 0, 0)  32 us
    all_to_all x6, waiting for transfers between devices, exchange(): return lax.all_to_all(blocks, axes, 0, 0)  31.2 us
    ppermute x4, waiting for transfers between devices, to_mate(): return lax.ppermute(block, 'x_lo', [(0, 1), (1, 0)])  26.8 us
    pallas_call x2, Pallas kernels, weight_grad(): pl.pallas_call(grad_down_kernel if down else grad_up_kernel, out_shape=sh...  12.4 us
    ppermute x5, starting transfers between devices, only_to_core(): return lax.ppermute(block, 'section', [(1 - section, section)])  10.5 us
    ppermute x5, starting transfers between devices, only_to_mate(): return lax.ppermute(block, CORES, [(at, at + 1), (at + 1, at)])  9.1 us
  transfers between devices with their start and end apart: 27, of which 10 were waited for; matrix products, arithmetic and copies ran while one was open for 6% of the time, Pallas kernels for 11%

profile of v2, /device:TPU:1, one launch (start us, length us, event | category | flops | bytes accessed | tf_op | source)
XLA Modules:
  0.0 278.0 jit_solution(2183046436308855267)
XLA Ops:
  0.6 3.3 %collective-permute-start = (bf16[384,3072]{1,0:T(8,128)(2,1)}, bf16[384,3072]{1,0:T(8,128)(2,1)}, u32[]{:S(2)}, u32[]{:S(2)}) collective-permute-start(bf16[384,3072]{1,0:T(8,128)(2,1)} %bitcast.78), channel_id=1, source_target_pairs={{0,128},{128,0},{1,129},{129,1},{2,130},{130,2},{3,131},{131,3},{4... | collective-permute-start | bytes 7077896 | tf_op jit(solution)/shard_map/ppermute | solution.py:411
  4.0 4.5 %collective-permute-done.other = bf16[384,3072]{1,0:T(8,128)(2,1)} collective-permute-done((bf16[384,3072]{1,0:T(8,128)(2,1)}, bf16[384,3072]{1,0:T(8,128)(2,1)}, u32[]{:S(2)}, u32[]{:S(2)}) %collective-permute-start) | collective-permute-done | bytes 2359328 | tf_op jit(solution)/shard_map/ppermute | solution.py:411
  8.8 2.1 collective-permute-start.1
  10.9 1.6 dynamic-slice_bitcast_fusion.1
  12.6 4.1 %shard_map.75 = bf16[4,2,2,16,1536]{4,3,2,1,0:T(8,128)(2,1)} custom-call(bf16[128,384]{1,0:T(8,128)(2,1)} %get-tuple-element.45.x_ref, bf16[384,3072]{1,0:T(8,128)(2,1)} %bitcast.79, bf16[384,3072]{1,0:T(8,128)(2,1)} %collective-permute-done.other), custom_call_target="tpu_custom_call" | custom-call | flops 301989888 | bytes 2359296 | tf_op jit(solution)/shard_map/pallas_call | solution.py:161
  16.7 7.5 %all-to-all-start = ((bf16[16,1,16,1536]{3,2,1,0:T(8,128)(2,1)}), bf16[16,1,16,1536]{3,2,1,0:T(8,128)(2,1)}, u32[]{:S(2)}, u32[]{:S(2)}) async-start(bf16[16,1,16,1536]{3,2,1,0:T(8,128)(2,1)} %bitcast.86), calls=%async_computation | async-start | bytes 1572864 | tf_op jit(solution)/shard_map/all_to_all | solution.py:404
  24.2 4.3 %shard_map.76 = bf16[2,4,2,16,1536]{4,3,2,1,0:T(8,128)(2,1)} custom-call(bf16[128,384]{1,0:T(8,128)(2,1)} %get-tuple-element.46.x_ref, bf16[3072,384]{1,0:T(8,128)(2,1)} %bitcast.74, bf16[3072,384]{1,0:T(8,128)(2,1)} %collective-permute-done.2.other), custom_call_target="tpu_custom_call" | custom-call | flops 301989888 | bytes 2359296 | tf_op jit(solution)/shard_map/pallas_call | solution.py:161
  28.5 16.5 %all-to-all-done.arrived = bf16[16,1,16,1536]{3,2,1,0:T(8,128)(2,1)} async-done(((bf16[16,1,16,1536]{3,2,1,0:T(8,128)(2,1)}), bf16[16,1,16,1536]{3,2,1,0:T(8,128)(2,1)}, u32[]{:S(2)}, u32[]{:S(2)}) %all-to-all-start) | async-done | bytes 786464 | tf_op jit(solution)/shard_map/all_to_all | solution.py:404
  46.4 2.7 shard_map.77
  49.1 2.1 collective-permute-start.5
  51.2 5.4 %all-to-all-start.1 = ((bf16[8,1,16,1536]{3,2,1,0:T(8,128)(2,1)}), bf16[8,1,16,1536]{3,2,1,0:T(8,128)(2,1)}, u32[]{:S(2)}, u32[]{:S(2)}) async-start(bf16[8,1,16,1536]{3,2,1,0:T(8,128)(2,1)} %get-tuple-element.40), calls=%async_computation.1 | async-start | bytes 786432 | tf_op jit(solution)/shard_map/all_to_all | solution.py:404
  62.2 26.8 %collective-permute-done.6 = bf16[64,384]{1,0:T(8,128)(2,1)S(1)} collective-permute-done((bf16[64,384]{1,0:T(8,128)(2,1)S(1)}, bf16[64,384]{1,0:T(8,128)(2,1)S(1)}, u32[]{:S(2)}, u32[]{:S(2)}) %collective-permute-start.6) | collective-permute-done | bytes 49184 | tf_op jit(solution)/shard_map/ppermute | solution.py:415
  91.2 5.2 %shard_map.78 = bf16[8,64,768]{2,1,0:T(8,128)(2,1)} custom-call(bf16[4,2,1,16,1536]{4,3,2,1,0:T(8,128)(2,1)} %bitcast.5.arrived.refs_0_, bf16[3072,384]{1,0:T(8,128)(2,1)} %bitcast.75, bf16[3072,384]{1,0:T(8,128)(2,1)} %collective-permute-done.2.other, bf16[3072,384]{1,0:T(8,128)(2,1)} %collective-permute-done.1.own_mate, ...), custom_call_target="tpu_custom_call" | custom-call | flops 301989888 | bytes 4718592 | tf_op jit(solution)/shard_map/pallas_call | solution.py:161
  96.4 2.7 collective-permute-start.8
  99.1 16.8 %all_to_all.45.arrived = bf16[8,64,768]{2,1,0:T(8,128)(2,1)} all-to-all(bf16[8,64,768]{2,1,0:T(8,128)(2,1)} %shard_map.78), channel_id=1, replica_groups=mesh['section'=2,'z'=8,'x_lo'=2,'y'=4,'x_hi'=2] {'y','x_hi'}, dimensions={0} | all-to-all | bytes 1572864 | tf_op jit(solution)/shard_map/all_to_all | solution.py:404
  115.9 14.9 %shard_map.79 = (bf16[4,2,2,16,1536]{4,3,2,1,0:T(8,128)(2,1)}, bf16[64,768]{1,0:T(8,128)(2,1)}) custom-call(bf16[8,64,768]{2,1,0:T(8,128)(2,1)} %all_to_all.45.arrived, bf16[64,768]{1,0:T(8,128)(2,1)} %pad_maximum_fusion.2.base, bf16[384,3072]{1,0:T(8,128)(2,1)} %bitcast.81, bf16[384,3072]{1,0:T(8,128)(2,1)} %collective-permute-done.other, ...), custom_call_target="tpu_custom_call" | custom-call | flops 301989888 | bytes 4718592 | tf_op jit(solution)/shard_map/pallas_call | solution.py:161
  130.9 20.3 %all_to_all.46.arrived = bf16[8,2,16,1536]{3,2,1,0:T(8,128)(2,1)} all-to-all(bf16[8,2,16,1536]{3,2,1,0:T(8,128)(2,1)} %bitcast.89), channel_id=1, replica_groups=mesh['section'=2,'z'=8,'x_lo'=2,'y'=4,'x_hi'=2] {'z'}, dimensions={0} | all-to-all | bytes 1572864 | tf_op jit(solution)/shard_map/all_to_all | solution.py:404
  151.2 2.2 shard_map.80
  153.4 4.2 %all-to-all-start.4 = ((bf16[8,2,16,1536]{3,2,1,0:T(8,128)(2,1)}), bf16[8,2,16,1536]{3,2,1,0:T(8,128)(2,1)}, u32[]{:S(2)}, u32[]{:S(2)}) async-start(bf16[8,2,16,1536]{3,2,1,0:T(8,128)(2,1)} %shard_map.80), calls=%async_computation.4 | async-start | bytes 1572864 | tf_op jit(solution)/shard_map/all_to_all | solution.py:404
  157.7 2.1 collective-permute-start.9
  159.7 1.4 collective-permute-start.10
  161.2 2.0 collective-permute-start.11
  163.2 4.3 %collective-permute-done.11.refs_3_ = bf16[4,2,1,16,1536]{4,3,2,1,0:T(8,128)(2,1)} collective-permute-done((bf16[4,2,1,16,1536]{4,3,2,1,0:T(8,128)(2,1)}, bf16[4,2,1,16,1536]{4,3,2,1,0:T(8,128)(2,1)}, u32[]{:S(2)}, u32[]{:S(2)}) %collective-permute-start.11) | collective-permute-done | bytes 393248 | tf_op jit(solution)/shard_map/ppermute | solution.py:433
  167.5 6.2 %all-to-all-done.4 = bf16[8,2,16,1536]{3,2,1,0:T(8,128)(2,1)} async-done(((bf16[8,2,16,1536]{3,2,1,0:T(8,128)(2,1)}), bf16[8,2,16,1536]{3,2,1,0:T(8,128)(2,1)}, u32[]{:S(2)}, u32[]{:S(2)}) %all-to-all-start.4) | async-done | bytes 786464 | tf_op jit(solution)/shard_map/all_to_all | solution.py:404
  173.7 5.6 %shard_map.81 = bf16[8,64,768]{2,1,0:T(8,128)(2,1)} custom-call(bf16[4,2,2,16,1536]{4,3,2,1,0:T(8,128)(2,1)} %bitcast.9.arrived.refs_4_, bf16[384,3072]{1,0:T(8,128)(2,1)} %bitcast.82, bf16[384,3072]{1,0:T(8,128)(2,1)} %collective-permute-done.other, bf16[384,3072]{1,0:T(8,128)(2,1)} %collective-permute-done.5.own_mate, ...), custom_call_target="tpu_custom_call" | custom-call | flops 301989888 | bytes 4718592 | tf_op jit(solution)/shard_map/pallas_call | solution.py:161
  179.2 14.7 %all_to_all.47.arrived = bf16[8,64,768]{2,1,0:T(8,128)(2,1)} all-to-all(bf16[8,64,768]{2,1,0:T(8,128)(2,1)} %shard_map.81), channel_id=1, replica_groups=mesh['section'=2,'z'=8,'x_lo'=2,'y'=4,'x_hi'=2] {'y','x_hi'}, dimensions={0} | all-to-all | bytes 1572864 | tf_op jit(solution)/shard_map/all_to_all | solution.py:404
  193.9 6.0 %shard_map.82 = (bf16[4,2,1,16,1536]{4,3,2,1,0:T(8,128)(2,1)}, bf16[64,768]{1,0:T(8,128)(2,1)}) custom-call(bf16[8,64,768]{2,1,0:T(8,128)(2,1)} %all_to_all.47.arrived, bf16[64,768]{1,0:T(8,128)(2,1)} %pad_maximum_fusion.3.base, bf16[3072,384]{1,0:T(8,128)(2,1)} %bitcast.76, bf16[3072,384]{1,0:T(8,128)(2,1)} %collective-permute-done.2.other, ...), custom_call_target="tpu_custom_call" | custom-call | flops 301989888 | bytes 4718592 | tf_op jit(solution)/shard_map/pallas_call | solution.py:161
  200.0 5.7 %all-to-all-start.6 = ((bf16[8,1,16,1536]{3,2,1,0:T(8,128)(2,1)}), bf16[8,1,16,1536]{3,2,1,0:T(8,128)(2,1)}, u32[]{:S(2)}, u32[]{:S(2)}) async-start(bf16[8,1,16,1536]{3,2,1,0:T(8,128)(2,1)} %bitcast.90), calls=%async_computation.6 | async-start | bytes 786432 | tf_op jit(solution)/shard_map/all_to_all | solution.py:404
  206.6 1.3 collective-permute-start.15
  207.9 2.1 collective-permute-start.16
  212.0 3.3 %collective-permute-start.14 = (bf16[2,64,384]{2,1,0:T(8,128)(2,1)}, bf16[2,64,384]{2,1,0:T(8,128)(2,1)}, u32[]{:S(2)}, u32[]{:S(2)}) collective-permute-start(bf16[2,64,384]{2,1,0:T(8,128)(2,1)} %get-tuple-element.83), channel_id=1, source_target_pairs={{0,136},{136,0},{8,128},{128,8},{1,137},{137,1},{9,129},{129,9},{2... | collective-permute-start | bytes 294920 | tf_op jit(solution)/shard_map/ppermute | solution.py:419
  215.3 1.6 dynamic-slice_bitcast_fusion.10
  216.9 1.3 collective-permute-start.13
  218.3 1.7 all-to-all-done.6.arrived
  220.0 1.9 shard_map.83
  221.9 5.1 %all-to-all-start.7 = ((bf16[8,1,16,1536]{3,2,1,0:T(8,128)(2,1)}), bf16[8,1,16,1536]{3,2,1,0:T(8,128)(2,1)}, u32[]{:S(2)}, u32[]{:S(2)}) async-start(bf16[8,1,16,1536]{3,2,1,0:T(8,128)(2,1)} %shard_map.83), calls=%async_computation.7 | async-start | bytes 786432 | tf_op jit(solution)/shard_map/all_to_all | solution.py:404
  227.0 5.7 %collective-permute-done.14 = bf16[2,64,384]{2,1,0:T(8,128)(2,1)} collective-permute-done((bf16[2,64,384]{2,1,0:T(8,128)(2,1)}, bf16[2,64,384]{2,1,0:T(8,128)(2,1)}, u32[]{:S(2)}, u32[]{:S(2)}) %collective-permute-start.14) | collective-permute-done | bytes 98336 | tf_op jit(solution)/shard_map/ppermute | solution.py:419
  236.1 6.1 %all-to-all-done.7 = bf16[8,1,16,1536]{3,2,1,0:T(8,128)(2,1)} async-done(((bf16[8,1,16,1536]{3,2,1,0:T(8,128)(2,1)}), bf16[8,1,16,1536]{3,2,1,0:T(8,128)(2,1)}, u32[]{:S(2)}, u32[]{:S(2)}) %all-to-all-start.7) | async-done | bytes 393248 | tf_op jit(solution)/shard_map/all_to_all | solution.py:404
  242.2 3.1 %collective-permute-start.18 = (bf16[4,2,1,16,1536]{4,3,2,1,0:T(8,128)(2,1)}, bf16[4,2,1,16,1536]{4,3,2,1,0:T(8,128)(2,1)}, u32[]{:S(2)}, u32[]{:S(2)}) collective-permute-start(bf16[4,2,1,16,1536]{4,3,2,1,0:T(8,128)(2,1)} %bitcast.21.refs_0_), channel_id=1, source_target_pairs={{128,0},{129,1},{130,2},{131,3},{132,4},{133,5},{134,6},{135,7},{1... | collective-permute-start | bytes 1179656 | tf_op jit(solution)/shard_map/ppermute | solution.py:428
  245.4 1.4 collective-permute-start.19
  246.8 3.4 %collective-permute-start.20 = (bf16[4,2,1,16,1536]{4,3,2,1,0:T(8,128)(2,1)}, bf16[4,2,1,16,1536]{4,3,2,1,0:T(8,128)(2,1)}, u32[]{:S(2)}, u32[]{:S(2)}) collective-permute-start(bf16[4,2,1,16,1536]{4,3,2,1,0:T(8,128)(2,1)} %bitcast.21.refs_0_), channel_id=1, source_target_pairs={{128,8},{136,0},{129,9},{137,1},{130,10},{138,2},{131,11},{139,3},... | collective-permute-start | bytes 1179656 | tf_op jit(solution)/shard_map/ppermute | solution.py:433
  251.6 6.3 %shard_map.84 = f32[3072,384]{1,0:T(8,128)} custom-call(bf16[256,384]{1,0:T(8,128)(2,1)} %maximum_select_fusion.g_ref, bf16[4,2,1,16,1536]{4,3,2,1,0:T(8,128)(2,1)} %bitcast.5.arrived.refs_0_, bf16[4,2,1,16,1536]{4,3,2,1,0:T(8,128)(2,1)} %collective-permute-done.9.refs_1_, bf16[4,2,1,16,1536]{4,3,2,1,0:T(8,128)(2,1)} %collective-permute-done.10.refs_2_, ...), custom_call_target="tpu_custom_call" | custom-call | flops 603979776 | bytes 4718592 | tf_op jit(solution)/shard_map/pallas_call | solution.py:326
  258.0 4.0 %shard_map.85 = bf16[8,2,16,384]{3,2,1,0:T(8,128)(2,1)} custom-call(bf16[384,3072]{1,0:T(8,128)(2,1)} %bitcast.83, bf16[3072,384]{1,0:T(8,128)(2,1)} %bitcast.77, bf16[4,2,1,16,1536]{4,3,2,1,0:T(8,128)(2,1)} %bitcast.21.refs_0_, bf16[4,2,1,16,1536]{4,3,2,1,0:T(8,128)(2,1)} %collective-permute-done.18.refs_1_, ...), custom_call_target="tpu_custom_call" | custom-call | flops 603979776 | bytes 7077888 | tf_op jit(solution)/shard_map/pallas_call | solution.py:161
  262.0 4.0 %all-to-all-start.8 = ((bf16[8,2,16,384]{3,2,1,0:T(8,128)(2,1)}), bf16[8,2,16,384]{3,2,1,0:T(8,128)(2,1)}, u32[]{:S(2)}, u32[]{:S(2)}) async-start(bf16[8,2,16,384]{3,2,1,0:T(8,128)(2,1)} %shard_map.85), calls=%async_computation.8 | async-start | bytes 393216 | tf_op jit(solution)/shard_map/all_to_all | solution.py:404
  266.1 1.5 reverse_select_fusion
  267.6 6.0 %shard_map.86 = f32[384,3072]{1,0:T(8,128)} custom-call(bf16[256,384]{1,0:T(8,128)(2,1)} %maximum_select_fusion.1.x_ref, bf16[4,2,1,16,1536]{4,3,2,1,0:T(8,128)(2,1)} %bitcast.21.refs_0_, bf16[4,2,1,16,1536]{4,3,2,1,0:T(8,128)(2,1)} %collective-permute-done.18.refs_1_, bf16[4,2,1,16,1536]{4,3,2,1,0:T(8,128)(2,1)} %collective-permute-done.19.refs_2_, ...), custom_call_target="tpu_custom_call" | custom-call | flops 603979776 | bytes 4718592 | tf_op jit(solution)/shard_map/pallas_call | solution.py:326
  275.2 1.4 broadcast_select_fusion
  276.6 1.4 broadcast_select_fusion.1
  (51 shorter events, 18.8 us)
Async XLA Ops:
  0.6 7.8 %collective-permute-start = (bf16[384,3072]{1,0:T(8,128)(2,1)}, bf16[384,3072]{1,0:T(8,128)(2,1)}, u32[]{:S(2)}, u32[]{:S(2)}) collective-permute-start(bf16[384,3072]{1,0:T(8,128)(2,1)} %bitcast.78), channel_id=1, source_target_pairs={{0,128},{128,0},{1,129},{129,1},{2,130},{130,2},{3,131},{131,3},{4... | collective-permute-start | bytes 7077896 | tf_op jit(solution)/shard_map/ppermute | solution.py:411
  8.5 15.8 %collective-permute-start.2 = (bf16[3072,384]{1,0:T(8,128)(2,1)}, bf16[3072,384]{1,0:T(8,128)(2,1)}, u32[]{:S(2)}, u32[]{:S(2)}) collective-permute-start(bf16[3072,384]{1,0:T(8,128)(2,1)} %bitcast.72), channel_id=1, source_target_pairs={{0,128},{128,0},{1,129},{129,1},{2,130},{130,2},{3,131},{131,3},{4... | collective-permute-start | bytes 7077896 | tf_op jit(solution)/shard_map/ppermute | solution.py:411
  8.8 36.3 %collective-permute-start.1 = (bf16[3072,384]{1,0:T(8,128)(2,1)}, bf16[3072,384]{1,0:T(8,128)(2,1)}, u32[]{:S(2)}, u32[]{:S(2)}) collective-permute-start(bf16[3072,384]{1,0:T(8,128)(2,1)} %bitcast.73), channel_id=1, source_target_pairs={{0,8},{8,0},{1,9},{9,1},{2,10},{10,2},{3,11},{11,3},{4,12},{12,4},... | collective-permute-start | bytes 7077896 | tf_op jit(solution)/shard_map/ppermute | solution.py:424
  16.7 28.4 %all-to-all-start = ((bf16[16,1,16,1536]{3,2,1,0:T(8,128)(2,1)}), bf16[16,1,16,1536]{3,2,1,0:T(8,128)(2,1)}, u32[]{:S(2)}, u32[]{:S(2)}) async-start(bf16[16,1,16,1536]{3,2,1,0:T(8,128)(2,1)} %bitcast.86), calls=%async_computation | async-start | bytes 1572864 | tf_op jit(solution)/shard_map/all_to_all | solution.py:404
  45.1 46.1 %collective-permute-start.4 = (bf16[3072,384]{1,0:T(8,128)(2,1)}, bf16[3072,384]{1,0:T(8,128)(2,1)}, u32[]{:S(2)}, u32[]{:S(2)}) collective-permute-start(bf16[3072,384]{1,0:T(8,128)(2,1)} %collective-permute-done.1.own_mate), channel_id=1, source_target_pairs={{0,128},{1,129},{2,130},{3,131},{4,132},{5,133},{6,134},{7,135},{8... | collective-permute-start | bytes 7077896 | tf_op jit(solution)/shard_map/ppermute | solution.py:428
  49.1 41.2 %copy-start = (bf16[2,4,2,16,1536]{4,3,2,1,0:T(8,128)(2,1)S(1)}, bf16[2,4,2,16,1536]{4,3,2,1,0:T(8,128)(2,1)}, u32[]{:S(2)}) copy-start(bf16[2,4,2,16,1536]{4,3,2,1,0:T(8,128)(2,1)} %shard_map.76) | copy-start | bytes 2359300
  49.1 47.3 %collective-permute-start.5 = (bf16[384,3072]{1,0:T(8,128)(2,1)}, bf16[384,3072]{1,0:T(8,128)(2,1)}, u32[]{:S(2)}, u32[]{:S(2)}) collective-permute-start(bf16[384,3072]{1,0:T(8,128)(2,1)} %bitcast.80), channel_id=1, source_target_pairs={{128,136},{136,128},{129,137},{137,129},{130,138},{138,130},{131,1... | collective-permute-start | bytes 7077896 | tf_op jit(solution)/shard_map/ppermute | solution.py:424
  51.2 40.0 %all-to-all-start.1 = ((bf16[8,1,16,1536]{3,2,1,0:T(8,128)(2,1)}), bf16[8,1,16,1536]{3,2,1,0:T(8,128)(2,1)}, u32[]{:S(2)}, u32[]{:S(2)}) async-start(bf16[8,1,16,1536]{3,2,1,0:T(8,128)(2,1)} %get-tuple-element.40), calls=%async_computation.1 | async-start | bytes 786432 | tf_op jit(solution)/shard_map/all_to_all | solution.py:404
  57.6 32.7 %collective-permute-start.3 = (bf16[4,2,16,1536]{3,2,1,0:T(8,128)(2,1)S(1)}, bf16[4,2,16,1536]{3,2,1,0:T(8,128)(2,1)S(1)}, u32[]{:S(2)}, u32[]{:S(2)}) collective-permute-start(bf16[4,2,16,1536]{3,2,1,0:T(8,128)(2,1)S(1)} %dynamic-slice_bitcast_fusion), channel_id=1, source_target_pairs={{0,8},{8,0},{1,9},{9,1},{2,10},{10,2},{3,11},{11,3},{4,12},{12,4},... | collective-permute-start | bytes 1179656 | tf_op jit(solution)/shard_map/ppermute | solution.py:415
  59.7 29.3 %collective-permute-start.6 = (bf16[64,384]{1,0:T(8,128)(2,1)S(1)}, bf16[64,384]{1,0:T(8,128)(2,1)S(1)}, u32[]{:S(2)}, u32[]{:S(2)}) collective-permute-start(bf16[64,384]{1,0:T(8,128)(2,1)S(1)} %get-tuple-element.88), channel_id=1, source_target_pairs={{0,8},{8,0},{1,9},{9,1},{2,10},{10,2},{3,11},{11,3},{4,12},{12,4},... | collective-permute-start | bytes 147464 | tf_op jit(solution)/shard_map/ppermute | solution.py:415
  61.0 28.8 %collective-permute-start.7 = (bf16[64,384]{1,0:T(8,128)(2,1)S(1)}, bf16[64,384]{1,0:T(8,128)(2,1)S(1)}, u32[]{:S(2)}, u32[]{:S(2)}) collective-permute-start(bf16[64,384]{1,0:T(8,128)(2,1)S(1)} %get-tuple-element.86), channel_id=1, source_target_pairs={{0,8},{8,0},{1,9},{9,1},{2,10},{10,2},{3,11},{11,3},{4,12},{12,4},... | collective-permute-start | bytes 147464 | tf_op jit(solution)/shard_map/ppermute | solution.py:415
  96.4 19.5 %collective-permute-start.8 = (bf16[384,3072]{1,0:T(8,128)(2,1)}, bf16[384,3072]{1,0:T(8,128)(2,1)}, u32[]{:S(2)}, u32[]{:S(2)}) collective-permute-start(bf16[384,3072]{1,0:T(8,128)(2,1)} %collective-permute-done.5.own_mate), channel_id=1, source_target_pairs={{128,0},{129,1},{130,2},{131,3},{132,4},{133,5},{134,6},{135,7},{1... | collective-permute-start | bytes 7077896 | tf_op jit(solution)/shard_map/ppermute | solution.py:428
  153.4 20.2 %all-to-all-start.4 = ((bf16[8,2,16,1536]{3,2,1,0:T(8,128)(2,1)}), bf16[8,2,16,1536]{3,2,1,0:T(8,128)(2,1)}, u32[]{:S(2)}, u32[]{:S(2)}) async-start(bf16[8,2,16,1536]{3,2,1,0:T(8,128)(2,1)} %shard_map.80), calls=%async_computation.4 | async-start | bytes 1572864 | tf_op jit(solution)/shard_map/all_to_all | solution.py:404
  157.7 5.5 %collective-permute-start.9 = (bf16[4,2,1,16,1536]{4,3,2,1,0:T(8,128)(2,1)}, bf16[4,2,1,16,1536]{4,3,2,1,0:T(8,128)(2,1)}, u32[]{:S(2)}, u32[]{:S(2)}) collective-permute-start(bf16[4,2,1,16,1536]{4,3,2,1,0:T(8,128)(2,1)} %bitcast.5.arrived.refs_0_), channel_id=1, source_target_pairs={{128,0},{129,1},{130,2},{131,3},{132,4},{133,5},{134,6},{135,7},{1... | collective-permute-start | bytes 1179656 | tf_op jit(solution)/shard_map/ppermute | solution.py:428
  159.7 3.5 %collective-permute-start.10 = (bf16[4,2,1,16,1536]{4,3,2,1,0:T(8,128)(2,1)}, bf16[4,2,1,16,1536]{4,3,2,1,0:T(8,128)(2,1)}, u32[]{:S(2)}, u32[]{:S(2)}) collective-permute-start(bf16[4,2,1,16,1536]{4,3,2,1,0:T(8,128)(2,1)} %bitcast.5.arrived.refs_0_), channel_id=1, source_target_pairs={{0,8},{8,0},{1,9},{9,1},{2,10},{10,2},{3,11},{11,3},{4,12},{12,4},... | collective-permute-start | bytes 1179656 | tf_op jit(solution)/shard_map/ppermute | solution.py:424
  161.2 6.3 %collective-permute-start.11 = (bf16[4,2,1,16,1536]{4,3,2,1,0:T(8,128)(2,1)}, bf16[4,2,1,16,1536]{4,3,2,1,0:T(8,128)(2,1)}, u32[]{:S(2)}, u32[]{:S(2)}) collective-permute-start(bf16[4,2,1,16,1536]{4,3,2,1,0:T(8,128)(2,1)} %bitcast.5.arrived.refs_0_), channel_id=1, source_target_pairs={{128,8},{136,0},{129,9},{137,1},{130,10},{138,2},{131,11},{139,3},... | collective-permute-start | bytes 1179656 | tf_op jit(solution)/shard_map/ppermute | solution.py:433
  200.0 20.0 %all-to-all-start.6 = ((bf16[8,1,16,1536]{3,2,1,0:T(8,128)(2,1)}), bf16[8,1,16,1536]{3,2,1,0:T(8,128)(2,1)}, u32[]{:S(2)}, u32[]{:S(2)}) async-start(bf16[8,1,16,1536]{3,2,1,0:T(8,128)(2,1)} %bitcast.90), calls=%async_computation.6 | async-start | bytes 786432 | tf_op jit(solution)/shard_map/all_to_all | solution.py:404
  206.6 29.5 %collective-permute-start.15 = (bf16[4,2,2,16,1536]{4,3,2,1,0:T(8,128)(2,1)}, bf16[4,2,2,16,1536]{4,3,2,1,0:T(8,128)(2,1)}, u32[]{:S(2)}, u32[]{:S(2)}) collective-permute-start(bf16[4,2,2,16,1536]{4,3,2,1,0:T(8,128)(2,1)} %bitcast.9.arrived.refs_4_), channel_id=1, source_target_pairs={{0,128},{1,129},{2,130},{3,131},{4,132},{5,133},{6,134},{7,135},{8... | collective-permute-start | bytes 2359304 | tf_op jit(solution)/shard_map/ppermute | solution.py:428
  207.9 28.2 %collective-permute-start.16 = (bf16[4,2,2,16,1536]{4,3,2,1,0:T(8,128)(2,1)}, bf16[4,2,2,16,1536]{4,3,2,1,0:T(8,128)(2,1)}, u32[]{:S(2)}, u32[]{:S(2)}) collective-permute-start(bf16[4,2,2,16,1536]{4,3,2,1,0:T(8,128)(2,1)} %bitcast.9.arrived.refs_4_), channel_id=1, source_target_pairs={{128,136},{136,128},{129,137},{137,129},{130,138},{138,130},{131,1... | collective-permute-start | bytes 2359304 | tf_op jit(solution)/shard_map/ppermute | solution.py:424
  210.0 26.1 %collective-permute-start.17 = (bf16[4,2,2,16,1536]{4,3,2,1,0:T(8,128)(2,1)}, bf16[4,2,2,16,1536]{4,3,2,1,0:T(8,128)(2,1)}, u32[]{:S(2)}, u32[]{:S(2)}) collective-permute-start(bf16[4,2,2,16,1536]{4,3,2,1,0:T(8,128)(2,1)} %bitcast.9.arrived.refs_4_), channel_id=1, source_target_pairs={{0,136},{8,128},{1,137},{9,129},{2,138},{10,130},{3,139},{11,131},... | collective-permute-start | bytes 2359304 | tf_op jit(solution)/shard_map/ppermute | solution.py:433
  212.0 20.7 %collective-permute-start.14 = (bf16[2,64,384]{2,1,0:T(8,128)(2,1)}, bf16[2,64,384]{2,1,0:T(8,128)(2,1)}, u32[]{:S(2)}, u32[]{:S(2)}) collective-permute-start(bf16[2,64,384]{2,1,0:T(8,128)(2,1)} %get-tuple-element.83), channel_id=1, source_target_pairs={{0,136},{136,0},{8,128},{128,8},{1,137},{137,1},{9,129},{129,9},{2... | collective-permute-start | bytes 294920 | tf_op jit(solution)/shard_map/ppermute | solution.py:419
  216.9 16.7 %collective-permute-start.13 = (bf16[2,64,384]{2,1,0:T(8,128)(2,1)}, bf16[2,64,384]{2,1,0:T(8,128)(2,1)}, u32[]{:S(2)}, u32[]{:S(2)}) collective-permute-start(bf16[2,64,384]{2,1,0:T(8,128)(2,1)} %get-tuple-element.83), channel_id=1, source_target_pairs={{0,8},{8,0},{1,9},{9,1},{2,10},{10,2},{3,11},{11,3},{4,12},{12,4},... | collective-permute-start | bytes 294920 | tf_op jit(solution)/shard_map/ppermute | solution.py:415
  221.8 13.5 %copy-start.1 = (bf16[64,384]{1,0:T(8,128)(2,1)S(1)}, bf16[64,384]{1,0:T(8,128)(2,1)}, u32[]{:S(2)}) copy-start(bf16[64,384]{1,0:T(8,128)(2,1)} %get-tuple-element.78) | copy-start | bytes 147460
  221.8 13.5 %copy-start.2 = (bf16[64,384]{1,0:T(8,128)(2,1)S(1)}, bf16[64,384]{1,0:T(8,128)(2,1)}, u32[]{:S(2)}) copy-start(bf16[64,384]{1,0:T(8,128)(2,1)} %get-tuple-element.79) | copy-start | bytes 147460
  221.8 13.5 %copy-start.3 = (bf16[64,384]{1,0:T(8,128)(2,1)S(1)}, bf16[64,384]{1,0:T(8,128)(2,1)}, u32[]{:S(2)}) copy-start(bf16[64,384]{1,0:T(8,128)(2,1)} %get-tuple-element.80) | copy-start | bytes 147460
  221.9 13.5 %copy-start.4 = (bf16[64,384]{1,0:T(8,128)(2,1)S(1)}, bf16[64,384]{1,0:T(8,128)(2,1)}, u32[]{:S(2)}) copy-start(bf16[64,384]{1,0:T(8,128)(2,1)} %get-tuple-element.81) | copy-start | bytes 147460
  221.9 20.4 %all-to-all-start.7 = ((bf16[8,1,16,1536]{3,2,1,0:T(8,128)(2,1)}), bf16[8,1,16,1536]{3,2,1,0:T(8,128)(2,1)}, u32[]{:S(2)}, u32[]{:S(2)}) async-start(bf16[8,1,16,1536]{3,2,1,0:T(8,128)(2,1)} %shard_map.83), calls=%async_computation.7 | async-start | bytes 786432 | tf_op jit(solution)/shard_map/all_to_all | solution.py:404
  232.7 1.5 collective-permute-start.12
  242.2 15.7 %collective-permute-start.18 = (bf16[4,2,1,16,1536]{4,3,2,1,0:T(8,128)(2,1)}, bf16[4,2,1,16,1536]{4,3,2,1,0:T(8,128)(2,1)}, u32[]{:S(2)}, u32[]{:S(2)}) collective-permute-start(bf16[4,2,1,16,1536]{4,3,2,1,0:T(8,128)(2,1)} %bitcast.21.refs_0_), channel_id=1, source_target_pairs={{128,0},{129,1},{130,2},{131,3},{132,4},{133,5},{134,6},{135,7},{1... | collective-permute-start | bytes 1179656 | tf_op jit(solution)/shard_map/ppermute | solution.py:428
  245.4 12.6 %collective-permute-start.19 = (bf16[4,2,1,16,1536]{4,3,2,1,0:T(8,128)(2,1)}, bf16[4,2,1,16,1536]{4,3,2,1,0:T(8,128)(2,1)}, u32[]{:S(2)}, u32[]{:S(2)}) collective-permute-start(bf16[4,2,1,16,1536]{4,3,2,1,0:T(8,128)(2,1)} %bitcast.21.refs_0_), channel_id=1, source_target_pairs={{0,8},{8,0},{1,9},{9,1},{2,10},{10,2},{3,11},{11,3},{4,12},{12,4},... | collective-permute-start | bytes 1179656 | tf_op jit(solution)/shard_map/ppermute | solution.py:424
  246.8 11.2 %collective-permute-start.20 = (bf16[4,2,1,16,1536]{4,3,2,1,0:T(8,128)(2,1)}, bf16[4,2,1,16,1536]{4,3,2,1,0:T(8,128)(2,1)}, u32[]{:S(2)}, u32[]{:S(2)}) collective-permute-start(bf16[4,2,1,16,1536]{4,3,2,1,0:T(8,128)(2,1)} %bitcast.21.refs_0_), channel_id=1, source_target_pairs={{128,8},{136,0},{129,9},{137,1},{130,10},{138,2},{131,11},{139,3},... | collective-permute-start | bytes 1179656 | tf_op jit(solution)/shard_map/ppermute | solution.py:433
  262.0 12.3 %all-to-all-start.8 = ((bf16[8,2,16,384]{3,2,1,0:T(8,128)(2,1)}), bf16[8,2,16,384]{3,2,1,0:T(8,128)(2,1)}, u32[]{:S(2)}, u32[]{:S(2)}) async-start(bf16[8,2,16,384]{3,2,1,0:T(8,128)(2,1)} %shard_map.85), calls=%async_computation.8 | async-start | bytes 393216 | tf_op jit(solution)/shard_map/all_to_all | solution.py:404

commit v3 on v2

v3 whole, which is shorter than its diff:
```python
import functools

import jax
import jax.numpy as jnp
from jax import lax
from jax.experimental import pallas as pl
from jax.experimental.pallas import tpu as pltpu
from jax.sharding import Mesh, PartitionSpec as P

root_two_over_pi = 0.7978845608028654
cubic = 0.044715
f32 = jnp.float32
bf16 = jnp.bfloat16
CHUNK = 512
VMEM = pl.BlockSpec(memory_space=pltpu.VMEM)
HBM = pl.BlockSpec(memory_space=pltpu.HBM)
ANY = pl.BlockSpec(memory_space=pl.ANY)
LIMIT = pltpu.CompilerParams(vmem_limit_bytes=64 * 1024 * 1024)


def gelu_both(pre):
    inner = root_two_over_pi * (pre + cubic * pre * pre * pre)
    tangent = jnp.tanh(inner)
    value = 0.5 * pre * (1.0 + tangent)
    slope = 0.5 * (1.0 + tangent) + 0.5 * pre * (1.0 - tangent * tangent) * root_two_over_pi * (
        1.0 + 3.0 * cubic * pre * pre
    )
    return value, slope


def dot(left, right, dims):
    return lax.dot_general(left, right, (dims, ((), ())), preferred_element_type=f32)


def shape_of(shape, dtype=bf16):
    return jax.ShapeDtypeStruct(shape, dtype)


def load_weights(layer, by_rows, refs, held, sems):
    mine = lax.axis_index("section") == layer

    def copy(source, part, i):
        units = pl.ds(i * CHUNK, CHUNK)
        if by_rows:
            width = source.shape[1]
            block, place = source.at[units, :], held.at[i, :, pl.ds(part * width, width)]
        else:
            width = source.shape[0]
            block, place = source.at[:, units], held.at[i, pl.ds(part * width, width), :]
        return pltpu.make_async_copy(block, place, sems.at[part, i])

    def start(which):
        for i in range(held.shape[0]):
            for part, pair in enumerate(refs):
                copy(pair[which], part, i).start()

    pl.when(mine)(lambda: start(0))
    pl.when(jnp.logical_not(mine))(lambda: start(1))

    def wait(i):
        for part, pair in enumerate(refs):
            copy(pair[0], part, i).wait()

    return wait


def wait_all(copies):
    for copy in copies:
        copy.wait()


def start_kernel(x_ref, g_ref, up, down, *rest):
    outs, (up_held, down_held, stage, up_sems, down_sems, out_sems) = rest[:4], rest[4:]
    section, mate_pos = lax.axis_index("section"), lax.axis_index("x_lo")
    groups, tokens, wide = stage.shape[1], stage.shape[3], stage.shape[4]
    per_half, count = wide // CHUNK, up_held.shape[0]

    def out_copies(half):
        return [
            pltpu.make_async_copy(stage.at[i, :, half], outs[i].at[:, half], out_sems.at[half, i])
            for i in range(4)
        ]

    def run(left_ref, weight, by_rows, held, sems):
        copies = []
        for i in range(count):
            units = pl.ds(i * CHUNK, CHUNK)
            source = weight.at[units, :] if by_rows else weight.at[:, units]
            copies.append(pltpu.make_async_copy(source, held.at[i], sems.at[i]))
            copies[-1].start()
        left = left_ref[...].reshape(-1, left_ref.shape[2])
        for i in range(count):
            half, place = i // per_half, pl.ds((i % per_half) * CHUNK, CHUNK)
            copies[i].wait()
            total = dot(left, held[i], ((1,), (1 if by_rows else 0,))).astype(bf16)
            total = total.reshape(2, 2, groups, tokens, CHUNK)
            for which in range(2):
                for token_half in range(2):
                    away = jnp.where(token_half == mate_pos, 0, 2) + jnp.where(which == section, 0, 1)
                    stage[away, :, half, :, place] = total[which, token_half]
            if i % per_half == per_half - 1:
                for copy in out_copies(half):
                    copy.start()
        wait_all(out_copies(0) + out_copies(1))

    pl.when(section == 0)(lambda: run(x_ref, up, False, up_held, up_sems))
    pl.when(section == 1)(lambda: run(g_ref, down, True, down_held, down_sems))


def start_products(x, g, up, down, blocks):
    width, units = up.shape
    count = units // CHUNK
    return kernel_call(
        start_kernel,
        [shape_of(blocks)] * 4,
        [HBM] * 4,
        [VMEM, VMEM, HBM, HBM],
        [
            pltpu.VMEM((count, width, CHUNK), bf16),
            pltpu.VMEM((count, CHUNK, width), bf16),
            pltpu.VMEM((4,) + blocks, bf16),
            pltpu.SemaphoreType.DMA((count,)),
            pltpu.SemaphoreType.DMA((count,)),
            pltpu.SemaphoreType.DMA((2, 4)),
        ],
        (x, g, up, down),
        flops=2 * x.shape[0] * x.shape[1] * up.size,
        moved=4 * up.size,
    )


def add_kernel(layer, kept, mates, other, across, out_ref, held, sems):
    mine = lax.axis_index("section") == layer

    def copies(refs):
        return [pltpu.make_async_copy(ref, held.at[i], sems.at[i]) for i, ref in enumerate(refs)]

    @pl.when(mine)
    def _():
        for copy in copies((kept, mates)):
            copy.start()

    @pl.when(jnp.logical_not(mine))
    def _():
        for copy in copies((other, across)):
            copy.start()

    wait_all(copies((kept, mates)))
    held[0] = (held[0].astype(f32) + held[1].astype(f32)).astype(bf16)
    copy = pltpu.make_async_copy(held.at[0], out_ref, sems.at[2])
    copy.start()
    copy.wait()


def add_terms(layer, terms):
    shape = terms[0].shape
    return kernel_call(
        functools.partial(add_kernel, layer),
        shape_of(shape),
        HBM,
        [HBM] * 4,
        [pltpu.VMEM((2,) + shape, bf16), pltpu.SemaphoreType.DMA((3,))],
        terms,
        flops=terms[0].size,
        moved=6 * terms[0].size,
    )


def widen_kernel(layer, by_rows, riders, arrived_ref, base, own, other, own_mate, other_mate, *rest):
    out_ref, x_out, held, sems, stage, out_sems, arrived, in_sems = rest[riders:]
    arrival = pltpu.make_async_copy(arrived_ref, arrived, in_sems.at[0])
    arrival.start()
    wait = load_weights(layer, by_rows, ((own, other), (own_mate, other_mate)), held, sems)
    rides = [
        pltpu.make_async_copy(rest[i], stage.at[:, :, 1 + i], in_sems.at[1 + i]) for i in range(riders)
    ]
    for copy in rides:
        copy.start()
    per_half = stage.shape[4] // CHUNK
    arrival.wait()
    total = arrived[0].astype(f32)
    for i in range(1, arrived.shape[0]):
        total = total + arrived[i].astype(f32)
    x = (base[...].astype(f32) + total).astype(bf16)
    x_out[...] = x
    wait_all(rides)

    def out_copy(half):
        return pltpu.make_async_copy(stage.at[:, half], out_ref.at[:, half], out_sems.at[half])

    for i in range(held.shape[0]):
        half, place = i // per_half, pl.ds((i % per_half) * CHUNK, CHUNK)
        wait(i)
        got = dot(x, held[i], ((1,), (1 if by_rows else 0,))).astype(bf16)
        stage[:, half, 0, :, place] = got.reshape(stage.shape[0], stage.shape[3], CHUNK)
        if i % per_half == per_half - 1:
            out_copy(half).start()
    wait_all([out_copy(0), out_copy(1)])


def narrow_kernel(
    layer, by_rows, arrived_ref, own, other, own_mate, other_mate, out_ref, held, sems, stage, out_sems, arrived, in_sem
):
    arrival = pltpu.make_async_copy(arrived_ref.at[:, :, 0], arrived, in_sem)
    arrival.start()
    wait = load_weights(layer, by_rows, ((own, other), (own_mate, other_mate)), held, sems)
    per_half = arrived.shape[3] // CHUNK
    total = None
    arrival.wait()
    for i in range(held.shape[0]):
        left = arrived[:, i // per_half, :, pl.ds((i % per_half) * CHUNK, CHUNK)].reshape(-1, CHUNK)
        wait(i)
        got = dot(left, held[i], ((1,), (0 if by_rows else 1,)))
        total = got if total is None else total + got
    stage[...] = total.astype(bf16)
    copies = [
        pltpu.make_async_copy(stage, out_ref.at[i], out_sems.at[i]) for i in range(out_ref.shape[0])
    ]
    for copy in copies:
        copy.start()
    wait_all(copies)


def held_scratch(weight, by_rows):
    count, width = max(weight.shape) // CHUNK, 2 * min(weight.shape)
    chunk = (CHUNK, width) if by_rows else (width, CHUNK)
    return [pltpu.VMEM((count,) + chunk, bf16), pltpu.SemaphoreType.DMA((2, count))]


def kernel_call(body, outs, out_specs, in_specs, scratch, operands, flops=0, moved=0):
    return pl.pallas_call(
        body,
        out_shape=outs,
        in_specs=in_specs,
        out_specs=out_specs,
        scratch_shapes=scratch,
        compiler_params=LIMIT,
        cost_estimate=pl.CostEstimate(flops=flops, bytes_accessed=moved, transcendentals=0),
    )(*operands)


def widen(layer, by_rows, arrived, base, weights, blocks, riders=()):
    shape = blocks[:2] + (1 + len(riders),) + blocks[2:]
    return kernel_call(
        functools.partial(widen_kernel, layer, by_rows, len(riders)),
        (shape_of(shape), shape_of(base.shape)),
        (HBM, VMEM),
        [HBM, VMEM] + [HBM] * (4 + len(riders)),
        held_scratch(weights[0], by_rows)
        + [
            pltpu.VMEM(shape, bf16),
            pltpu.SemaphoreType.DMA((2,)),
            pltpu.VMEM(arrived.shape, bf16),
            pltpu.SemaphoreType.DMA((1 + len(riders),)),
        ],
        (arrived, base) + weights + riders,
        flops=4 * base.shape[0] * weights[0].size,
        moved=4 * weights[0].size,
    )


def narrow(layer, by_rows, arrived, weights, copies):
    groups, halves, _, tokens, wide = arrived.shape
    out = groups * tokens, 2 * min(weights[0].shape)
    return kernel_call(
        functools.partial(narrow_kernel, layer, by_rows),
        shape_of((copies,) + out),
        HBM,
        [HBM] * 5,
        held_scratch(weights[0], by_rows)
        + [
            pltpu.VMEM(out, bf16),
            pltpu.SemaphoreType.DMA((copies,)),
            pltpu.VMEM((groups, halves, tokens, wide), bf16),
            pltpu.SemaphoreType.DMA,
        ],
        (arrived,) + weights,
        flops=4 * out[0] * weights[0].size,
        moved=4 * weights[0].size,
    )


def act_kernel(body, slopes, arrived_ref, *refs):
    slope_in, rest = (refs[0], refs[1:]) if slopes == "in" else (None, refs)
    out_ref, rest = rest[0], rest[1:]
    slope_out, rest = (rest[0], rest[1:]) if slopes == "out" else (None, rest)
    arrived, stage, in_sems, out_sems = rest
    steps = arrived.shape[3] // CHUNK
    places = [pl.ds(i * CHUNK, CHUNK) for i in range(steps)]
    arrivals = [
        pltpu.make_async_copy(arrived_ref.at[:, :, :, place], arrived.at[:, :, :, place], in_sems.at[i])
        for i, place in enumerate(places)
    ]
    for copy in arrivals:
        copy.start()
    copies = []
    for i, place in enumerate(places):
        arrivals[i].wait()
        sums = []
        for kind in range(arrived.shape[1]):
            total = arrived[0, kind, :, place].astype(f32)
            for source in range(1, arrived.shape[0]):
                total = total + arrived[source, kind, :, place].astype(f32)
            sums.append(total)
        values, slope = body(sums, None if slope_in is None else slope_in[:, place])
        for kind, value in enumerate(values):
            stage[kind, :, place] = value.astype(bf16)
        if slope_out is not None:
            slope_out[:, place] = slope
        for to in range(out_ref.shape[0]):
            copies.append(
                pltpu.make_async_copy(stage.at[:, :, place], out_ref.at[to, :, :, place], out_sems.at[i, to])
            )
            copies[-1].start()
    wait_all(copies)


def act_first(sums, _):
    value, slope = gelu_both(sums[0])
    return [value], slope


def act_last(sums, _):
    value, slope = gelu_both(sums[0])
    return [sums[1] * slope, value], None


def act_back(sums, slope):
    return [sums[0] * slope], None


def activation(body, arrived, kinds, slope_out=False, slope=None):
    peers, piece = arrived.shape[0], arrived.shape[2:]
    outs, out_specs, slopes = [shape_of((peers, kinds) + piece)], [HBM], "in" if slope is not None else ""
    if slope_out:
        outs, out_specs, slopes = outs + [shape_of(piece, f32)], out_specs + [VMEM], "out"
    steps = piece[1] // CHUNK
    return kernel_call(
        functools.partial(act_kernel, body, slopes),
        outs,
        out_specs,
        [HBM] + ([VMEM] if slope is not None else []),
        [
            pltpu.VMEM(arrived.shape, bf16),
            pltpu.VMEM((kinds,) + piece, bf16),
            pltpu.SemaphoreType.DMA((steps,)),
            pltpu.SemaphoreType.DMA((steps, peers)),
        ],
        (arrived,) + (() if slope is None else (slope,)),
        flops=2000000,
        moved=2000000,
    )


def finish_kernel(arrived, x1, g1, states, grads):
    total = arrived[0].astype(f32)
    for i in range(1, arrived.shape[0]):
        total = total + arrived[i].astype(f32)

    def ended(base):
        return (base[...].astype(f32) + total).astype(bf16)

    @pl.when(lax.axis_index("section") == 0)
    def _():
        states[...] = x1[...]
        grads[...] = ended(g1)

    @pl.when(lax.axis_index("section") == 1)
    def _():
        states[...] = ended(x1)
        grads[...] = g1[...]


def pick_copies(layer0, layer1, kind, held, sems, start):
    section = lax.axis_index("section")

    def copy(layer, i):
        source = (layer0, layer1)[layer][i].at[:, :, 0 if layer == 0 else kind]
        return pltpu.make_async_copy(source, held.at[i], sems.at[i])

    if start:
        for layer in range(2):

            @pl.when(section == layer)
            def _():
                for i in range(4):
                    copy(layer, i).start()
    else:
        for i in range(4):
            copy(0, i).wait()


def step_chunk(held, step):
    per_half = held.shape[4] // CHUNK
    place = pl.ds(pl.multiple_of((step % per_half) * CHUNK, CHUNK), CHUNK)
    return held[:, :, step // per_half, :, place].reshape(-1, CHUNK)


def grad_down_kernel(g_ref, *refs):
    layer0, layer1, (out_ref, held, sems) = refs[:4], refs[4:8], refs[8:]
    step = pl.program_id(0)

    @pl.when(step == 0)
    def _():
        pick_copies(layer0, layer1, 1, held, sems, True)
        pick_copies(layer0, layer1, 1, held, sems, False)

    out_ref[...] = dot(step_chunk(held, step), g_ref[...], ((0,), (0,)))


def grad_up_kernel(x_ref, *refs):
    layer0, layer1, (out_ref, held, turned, sems) = refs[:4], refs[4:8], refs[8:]
    step = pl.program_id(0)

    @pl.when(step == 0)
    def _():
        pick_copies(layer0, layer1, 0, held, sems, True)
        turned[...] = x_ref[...].T
        pick_copies(layer0, layer1, 0, held, sems, False)

    out_ref[...] = dot(turned[...], step_chunk(held, step), ((1,), (0,)))


def weight_grad(down, narrow, layer0, layer1):
    groups, halves, _, tokens, wide = layer0[0].shape
    units, (all_tokens, width) = halves * wide, narrow.shape
    shape, block = ((units, width), (CHUNK, width)) if down else ((width, units), (width, CHUNK))
    turned = [] if down else [pltpu.VMEM((width, all_tokens), bf16)]
    return pl.pallas_call(
        grad_down_kernel if down else grad_up_kernel,
        out_shape=shape_of(shape, f32),
        grid=(units // CHUNK,),
        in_specs=[pl.BlockSpec(narrow.shape, lambda i: (0, 0))] + [HBM] * 8,
        out_specs=pl.BlockSpec(block, lambda i: (i, 0) if down else (0, i)),
        scratch_shapes=[pltpu.VMEM((4, groups, halves, tokens, wide), bf16)]
        + turned
        + [pltpu.SemaphoreType.DMA((4,))],
        compiler_params=LIMIT,
        cost_estimate=pl.CostEstimate(
            flops=2 * narrow.size * units, bytes_accessed=4 * width * units, transcendentals=0
        ),
    )(narrow, *layer0, *layer1)


def last_kernel(up, down, *refs):
    layer0, layer1, rest = refs[:4], refs[4:8], refs[8:]
    out_ref, held, up_held, down_held, stage, sems, up_sems, down_sems, out_sem = rest
    section, mate_pos = lax.axis_index("section"), lax.axis_index("x_lo")
    groups, halves, tokens, wide = held.shape[1:]
    per_half, count = wide // CHUNK, up_held.shape[0]
    pick_copies(layer0, layer1, 1, held, sems, True)

    def run(weight, by_rows, weight_held, weight_sems):
        copies = []
        for i in range(count):
            where = pl.ds(i * CHUNK, CHUNK)
            source = weight.at[where, :] if by_rows else weight.at[:, where]
            copies.append(pltpu.make_async_copy(source, weight_held.at[i], weight_sems.at[i]))
        for copy in copies:
            copy.start()
        pick_copies(layer0, layer1, 1, held, sems, False)
        total = None
        for i in range(count):
            left = held[:, :, i // per_half, :, pl.ds((i % per_half) * CHUNK, CHUNK)].reshape(-1, CHUNK)
            copies[i].wait()
            got = dot(left, weight_held[i], ((1,), (0 if by_rows else 1,)))
            total = got if total is None else total + got
        total = total.astype(bf16).reshape(4, groups, tokens, -1)
        for i in range(4):
            half = mate_pos if i < 2 else 1 - mate_pos
            which = section if i % 2 == 0 else 1 - section
            stage[pl.ds(half * groups, groups), which] = total[i]

    pl.when(section == 0)(lambda: run(up, False, up_held, up_sems))
    pl.when(section == 1)(lambda: run(down, True, down_held, down_sems))
    copy = pltpu.make_async_copy(stage, out_ref, out_sem)
    copy.start()
    copy.wait()


def last_product(up, down, layer0, layer1):
    groups, halves, _, tokens, wide = layer0[0].shape
    width, units = up.shape
    out = (2 * groups, 2, tokens, width)
    return kernel_call(
        last_kernel,
        shape_of(out),
        HBM,
        [HBM] * 10,
        [
            pltpu.VMEM((4, groups, halves, tokens, wide), bf16),
            pltpu.VMEM((units // CHUNK, width, CHUNK), bf16),
            pltpu.VMEM((units // CHUNK, CHUNK, width), bf16),
            pltpu.VMEM(out, bf16),
            pltpu.SemaphoreType.DMA((4,)),
            pltpu.SemaphoreType.DMA((units // CHUNK,)),
            pltpu.SemaphoreType.DMA((units // CHUNK,)),
            pltpu.SemaphoreType.DMA,
        ],
        (up, down) + layer0 + layer1,
        flops=8 * groups * tokens * up.size,
        moved=6 * up.size,
    )


def exchange(blocks, axes):
    return lax.all_to_all(blocks, axes, 0, 0)


CORES = ("section", "x_lo")


def to_other_core(block):
    return lax.ppermute(block, "section", [(0, 1), (1, 0)])


def to_mate(block):
    return lax.ppermute(block, "x_lo", [(0, 1), (1, 0)])


def to_other_core_of_mate(block):
    return lax.ppermute(block, CORES, [(0, 3), (3, 0), (1, 2), (2, 1)])


def only_to_mate(block, section):
    at = 2 * section
    return lax.ppermute(block, CORES, [(at, at + 1), (at + 1, at)])


def only_to_core(block, section):
    return lax.ppermute(block, "section", [(1 - section, section)])


def only_across(block, section):
    at, source = 2 * section, 2 * (1 - section)
    return lax.ppermute(block, CORES, [(source, at + 1), (source + 1, at)])


def to_owner(block, section):
    return block, only_to_core(block, section), only_to_mate(block, section), only_across(block, section)


def late(block, after):
    return lax.optimization_barrier((block, after))[0]


def local(inputs, cotangent, w_up, w_down):
    col = ("y", "x_hi")
    section, mate_pos, col_pos = (lax.axis_index(name) for name in ("section", "x_lo", col))
    first = section == 0
    own_up, own_down = w_up[0], w_down[0]
    tokens, width = inputs.shape[1:]
    half_len = tokens // 2
    rings = lax.axis_size("z")
    piece = (tokens // rings, own_up.shape[1] // 2)
    blocks = (half_len // piece[0], 2) + piece

    def half_of(array, which):
        return lax.dynamic_slice_in_dim(array, which * half_len, half_len, 0)

    def batch(array, which):
        return lax.dynamic_index_in_dim(array, which, 0, keepdims=False)

    def halves_of(pair, which):
        return lax.dynamic_slice_in_dim(pair, which * half_len, half_len, 1)

    keep_own, keep_other, send_own, send_other = start_products(inputs, cotangent, own_up, own_down, blocks)
    terms = (
        keep_own,
        only_to_mate(send_own, 0),
        only_to_core(keep_other, 1),
        only_across(send_other, 1),
    )
    x0, g2 = late((inputs, cotangent), keep_own)
    ends = jnp.stack([batch(x0, section), batch(g2, section)])
    ends_mate = to_mate(halves_of(ends, 1 - mate_pos))
    pre0 = add_terms(0, terms)
    arrived = exchange(pre0.reshape((rings, 1) + piece), "z")
    own_down_late, own_up_late = late((own_down, own_up), (pre0, ends_mate))
    mate_down0 = only_to_mate(own_down_late, 0)
    other_down = only_to_core(own_down_late, 1)
    other_up = only_to_core(own_up_late, 0)

    value0, slope0 = activation(act_first, arrived, 1, slope_out=True)
    hid0 = exchange(value0, "z").reshape(blocks[:2] + (1,) + piece)
    ends, ends_mate = late((halves_of(ends, mate_pos), ends_mate), value0)
    g2_both = jnp.concatenate([ends[1], ends_mate[1]], axis=1)
    mate_down0 = late(mate_down0, g2_both)
    down0 = own_down, other_down, mate_down0, only_to_core(mate_down0, 1)
    mate_up1 = only_to_mate(late(own_up, mate_down0), 1)
    part = narrow(0, True, hid0, down0, lax.axis_size(col))
    arrived = exchange(part, col)

    ends, ends_mate = late((ends, ends_mate), part)
    x0_both = jnp.concatenate([ends[0], ends_mate[0]], axis=1)
    mate_up1 = late(mate_up1, x0_both)
    up1 = own_up, other_up, mate_up1, only_to_core(mate_up1, 0)
    keep_own, keep_other, send_own, send_other = late((keep_own, keep_other, send_own, send_other), mate_up1)
    d_hid1 = add_terms(
        1,
        (keep_own, only_to_mate(send_own, 1), only_to_core(keep_other, 0), only_across(send_other, 0)),
    )
    pre1, x1 = widen(1, False, arrived, x0_both, up1, blocks, (d_hid1,))
    hid0s = to_owner(late(hid0, pre1), 0)
    arrived = late(exchange(pre1.reshape((rings, 2) + piece), "z"), hid0s)
    (acts1,) = activation(act_last, arrived, 2)
    acts1 = exchange(acts1, "z").reshape(blocks[:2] + (2,) + piece)
    part = narrow(1, False, acts1, up1, lax.axis_size(col))
    arrived = exchange(part, col)

    d_hid0, g1 = widen(0, True, arrived, g2_both, down0, blocks)
    acts1, both1 = late((acts1, jnp.stack([x1, g1])), d_hid0)
    acts1s = to_owner(acts1, 1)
    arrived = exchange(d_hid0.reshape((rings, 1) + piece), "z")
    near, far = both1[..., :width], both1[..., width:]
    both1 = jnp.stack([near, to_other_core(near), to_mate(far), to_other_core_of_mate(far)])
    both1 = both1.reshape((2, 2) + near.shape)

    def all_tokens(array):
        return jnp.concatenate(
            [
                half_of(batch(array, which), half)
                for half in (mate_pos, 1 - mate_pos)
                for which in (section, 1 - section)
            ]
        )

    x1s, g1s = both1[:, :, 0].reshape(2 * tokens, width), both1[:, :, 1].reshape(2 * tokens, width)
    xs = jnp.where(first, all_tokens(inputs), x1s)
    gs = jnp.where(first, g1s, all_tokens(cotangent))

    (d_pre0,) = activation(act_back, arrived, 1, slope=slope0)
    d_pre0 = late(exchange(d_pre0, "z").reshape(blocks[:2] + (1,) + piece), acts1s)
    down_grad = weight_grad(True, late(gs, d_pre0), hid0s, acts1s)
    d_pre0s = late(to_owner(d_pre0, 0), down_grad)

    last = last_product(own_up, own_down, d_pre0s, acts1s)
    xs, d_pre0s = late((xs, d_pre0s), last)
    arrived = exchange(last, col)
    up_grad = weight_grad(False, xs, d_pre0s, acts1s)

    out_len = tokens // lax.axis_size(col)
    per_half = half_len // out_len
    away = jnp.where(col_pos // per_half == mate_pos, 0, 1)
    pieces = lax.dynamic_index_in_dim(both1, away, 0, keepdims=False)
    pieces = lax.dynamic_slice_in_dim(pieces, (col_pos % per_half) * out_len, out_len, 2)
    pieces = jnp.where(first, pieces, pieces[::-1])
    states, grads = kernel_call(
        finish_kernel,
        [shape_of(pieces[:, 0].shape)] * 2,
        [VMEM] * 2,
        [VMEM] * 3,
        [],
        (arrived, pieces[:, 0], pieces[:, 1]),
        flops=100000,
        moved=200000,
    )
    return states[None], grads[None], up_grad[None], down_grad[None]


def solution(mesh):
    sections, rows, cols = mesh.devices.shape
    finer = Mesh(
        mesh.devices.reshape(sections, rows // 2, 2, cols // 2, 2),
        ("section", "z", "x_lo", "y", "x_hi"),
    )
    row, col = ("z", "x_lo"), ("y", "x_hi")
    in_specs = (
        P(None, None, row),
        P(None, None, row),
        P("section", row, col),
        P("section", col, row),
    )
    out_specs = (
        P("section", None, col, row),
        P("section", None, col, row),
        P("section", row, col),
        P("section", col, row),
    )
    return jax.shard_map(local, mesh=finer, in_specs=in_specs, out_specs=out_specs, check_vma=False)
```

time: 280 us -> 292 us (1.043)
  starting transfers between devices: 69.6 us -> 106 us
  waiting for transfers between devices: 73.2 us -> 59.6 us
  Pallas kernels: 63.4 us -> 58.6 us
  other arithmetic: 10.9 us -> 6.19 us
    ppermute x5 -> x9, starting transfers between devices: 10.5 us -> 37.5 us  [only_to_core(): return lax.ppermute(block, 'section', [(1 - section, section)])]
    ppermute x4 -> x2, waiting for transfers between devices: 26.8 us -> 0.01 us  [to_mate(): return lax.ppermute(block, 'x_lo', [(0, 1), (1, 0)])]
    ppermute x3 -> x5, waiting for transfers between devices: 4.26 us -> 23.1 us  [only_across(): return lax.ppermute(block, CORES, [(source, at + 1), (source + 1, at)])]
    ppermute x5 -> x7, waiting for transfers between devices: 0.01 us -> 12.5 us  [only_to_mate(): return lax.ppermute(block, CORES, [(at, at + 1), (at + 1, at)])]
    all_to_all x6 -> x7, waiting for transfers between devices: 31.2 us -> 23.9 us  [exchange(): return lax.all_to_all(blocks, axes, 0, 0)]
    ppermute x5 -> x7, starting transfers between devices: 9.1 us -> 15.2 us  [only_to_mate(): return lax.ppermute(block, CORES, [(at, at + 1), (at + 1, at)])]
    ppermute x1, waiting for transfers between devices: 5.74 us -> 0.01 us  [to_other_core_of_mate(): return lax.ppermute(block, CORES, [(0, 3), (3, 0), (1, 2), (2, 1)])]
    ppermute x3 -> x1, waiting for transfers between devices: 5.07 us -> 0.01 us  [to_other_core(): return lax.ppermute(block, 'section', [(0, 1), (1, 0)])]
  transfers between devices with their start and end apart: 27 -> 32, of which waited for: 10 -> 13; matrix products, arithmetic and copies ran while one was open for 6% -> 5% of each run, Pallas kernels for 11% -> 9%
where the time goes in v3:
time: 292 us; the launch traced here: 290 us
  starting transfers between devices  106 us (36%)
  waiting for transfers between devices  59.6 us (20%)
  Pallas kernels  58.6 us (20%)
  blocking collectives  49.9 us (17%)
  local copies, waits for them, and re-layouts  8.17 us (3%)
  other arithmetic  6.19 us (2%)
    all_to_all x2, blocking collectives, exchange(): return lax.all_to_all(blocks, axes, 0, 0)  49.9 us
    pallas_call x12, Pallas kernels, kernel_call(): pl.pallas_call(body, out_shape=outs, in_specs=in_specs, out_specs=out_spe...  46.2 us
    ppermute x9, starting transfers between devices, only_to_core(): return lax.ppermute(block, 'section', [(1 - section, section)])  37.5 us
    all_to_all x7, starting transfers between devices, exchange(): return lax.all_to_all(blocks, axes, 0, 0)  36.4 us
    all_to_all x7, waiting for transfers between devices, exchange(): return lax.all_to_all(blocks, axes, 0, 0)  23.9 us
    ppermute x5, waiting for transfers between devices, only_across(): return lax.ppermute(block, CORES, [(source, at + 1), (source + 1, at)])  23.1 us
    ppermute x7, starting transfers between devices, only_to_mate(): return lax.ppermute(block, CORES, [(at, at + 1), (at + 1, at)])  15.2 us
    ppermute x7, waiting for transfers between devices, only_to_mate(): return lax.ppermute(block, CORES, [(at, at + 1), (at + 1, at)])  12.5 us
  transfers between devices with their start and end apart: 32, of which 13 were waited for; matrix products, arithmetic and copies ran while one was open for 5% of the time, Pallas kernels for 9%

profile of v3, /device:TPU:1, one launch (start us, length us, event | category | flops | bytes accessed | tf_op | source)
XLA Modules:
  0.0 290.0 jit_solution(9386968261750110980)
XLA Ops:
  0.6 5.1 %shard_map.75 = (bf16[4,2,16,1536]{3,2,1,0:T(8,128)(2,1)}, bf16[4,2,16,1536]{3,2,1,0:T(8,128)(2,1)}, bf16[4,2,16,1536]{3,2,1,0:T(8,128)(2,1)}, bf16[4,2,16,1536]{3,2,1,0:T(8,128)(2,1)}) custom-call(bf16[2,128,384]{2,1,0:T(8,128)(2,1)} %x_ref.1, bf16[2,128,384]{2,1,0:T(8,128)(2,1)} %g_ref.1, bf16[384,3072]{1,0:T(8,128)(2,1)} %bitcast.64, ...), custom_call_target="tpu_custom_call" | custom-call | flops 603979776 | bytes 4718592 | tf_op jit(solution)/shard_map/pallas_call | solution.py:231
  11.4 2.0 collective-permute-start.3
  13.5 9.8 %collective-permute-done.2.across = bf16[4,2,16,1536]{3,2,1,0:T(8,128)(2,1)} collective-permute-done((bf16[4,2,16,1536]{3,2,1,0:T(8,128)(2,1)}, bf16[4,2,16,1536]{3,2,1,0:T(8,128)(2,1)}, u32[]{:S(2)}, u32[]{:S(2)}) %collective-permute-start.2) | collective-permute-done | bytes 393248 | tf_op jit(solution)/shard_map/ppermute | solution.py:536
  23.3 2.0 shard_map.76
  25.3 2.1 collective-permute-start.5
  27.4 6.5 %all-to-all-start = ((bf16[8,1,16,1536]{3,2,1,0:T(8,128)(2,1)}), bf16[8,1,16,1536]{3,2,1,0:T(8,128)(2,1)}, u32[]{:S(2)}, u32[]{:S(2)}) async-start(bf16[8,1,16,1536]{3,2,1,0:T(8,128)(2,1)} %bitcast.81), calls=%async_computation | async-start | bytes 786432 | tf_op jit(solution)/shard_map/all_to_all | solution.py:507
  35.1 12.1 %all-to-all-done.arrived_ref = bf16[8,1,16,1536]{3,2,1,0:T(8,128)(2,1)} async-done(((bf16[8,1,16,1536]{3,2,1,0:T(8,128)(2,1)}), bf16[8,1,16,1536]{3,2,1,0:T(8,128)(2,1)}, u32[]{:S(2)}, u32[]{:S(2)}) %all-to-all-start) | async-done | bytes 393248 | tf_op jit(solution)/shard_map/all_to_all | solution.py:507
  47.2 2.6 shard_map.77
  53.3 5.0 %collective-permute-start.8 = (bf16[384,3072]{1,0:T(8,128)(2,1)}, bf16[384,3072]{1,0:T(8,128)(2,1)}, u32[]{:S(2)}, u32[]{:S(2)}) collective-permute-start(bf16[384,3072]{1,0:T(8,128)(2,1)} %bitcast.65), channel_id=1, source_target_pairs={{128,136},{136,128},{129,137},{137,129},{130,138},{138,130},{131,1... | collective-permute-start | bytes 7077896 | tf_op jit(solution)/shard_map/ppermute | solution.py:527
  58.4 4.1 %all-to-all-start.1 = ((bf16[8,1,16,1536]{3,2,1,0:T(8,128)(2,1)}), bf16[8,1,16,1536]{3,2,1,0:T(8,128)(2,1)}, u32[]{:S(2)}, u32[]{:S(2)}) async-start(bf16[8,1,16,1536]{3,2,1,0:T(8,128)(2,1)} %get-tuple-element.50), calls=%async_computation.1 | async-start | bytes 786432 | tf_op jit(solution)/shard_map/all_to_all | solution.py:507
  62.5 11.2 %collective-permute-start.7 = (bf16[384,3072]{1,0:T(8,128)(2,1)}, bf16[384,3072]{1,0:T(8,128)(2,1)}, u32[]{:S(2)}, u32[]{:S(2)}) collective-permute-start(bf16[384,3072]{1,0:T(8,128)(2,1)} %bitcast.66), channel_id=1, source_target_pairs={{128,0},{129,1},{130,2},{131,3},{132,4},{133,5},{134,6},{135,7},{1... | collective-permute-start | bytes 7077896 | tf_op jit(solution)/shard_map/ppermute | solution.py:531
  73.7 4.6 %shard_map.78 = bf16[8,64,768]{2,1,0:T(8,128)(2,1)} custom-call(bf16[4,2,1,16,1536]{4,3,2,1,0:T(8,128)(2,1)} %bitcast.3.arrived_ref.refs_0_, bf16[3072,384]{1,0:T(8,128)(2,1)} %bitcast.61, bf16[3072,384]{1,0:T(8,128)(2,1)} %collective-permute-done.4.other, bf16[3072,384]{1,0:T(8,128)(2,1)} %collective-permute-done.5.own_mate, ...), custom_call_target="tpu_custom_call" | custom-call | flops 301989888 | bytes 4718592 | tf_op jit(solution)/shard_map/pallas_call | solution.py:231
  80.6 4.3 %collective-permute-done.8.own_mate = bf16[384,3072]{1,0:T(8,128)(2,1)} collective-permute-done((bf16[384,3072]{1,0:T(8,128)(2,1)}, bf16[384,3072]{1,0:T(8,128)(2,1)}, u32[]{:S(2)}, u32[]{:S(2)}) %collective-permute-start.8) | collective-permute-done | bytes 2359328 | tf_op jit(solution)/shard_map/ppermute | solution.py:527
  84.9 7.8 %collective-permute-start.9 = (bf16[384,3072]{1,0:T(8,128)(2,1)}, bf16[384,3072]{1,0:T(8,128)(2,1)}, u32[]{:S(2)}, u32[]{:S(2)}) collective-permute-start(bf16[384,3072]{1,0:T(8,128)(2,1)} %collective-permute-done.8.own_mate), channel_id=1, source_target_pairs={{128,0},{129,1},{130,2},{131,3},{132,4},{133,5},{134,6},{135,7},{1... | collective-permute-start | bytes 7077896 | tf_op jit(solution)/shard_map/ppermute | solution.py:531
  92.7 7.0 %all-to-all-start.2 = ((bf16[8,64,768]{2,1,0:T(8,128)(2,1)}), bf16[8,64,768]{2,1,0:T(8,128)(2,1)}, u32[]{:S(2)}, u32[]{:S(2)}) async-start(bf16[8,64,768]{2,1,0:T(8,128)(2,1)} %shard_map.78), calls=%async_computation.2 | async-start | bytes 1572864 | tf_op jit(solution)/shard_map/all_to_all | solution.py:507
  99.7 1.9 collective-permute-start.10
  101.7 2.1 collective-permute-start.11
  103.7 2.0 collective-permute-start.12
  105.7 6.4 %collective-permute-done.10.mates = bf16[4,2,16,1536]{3,2,1,0:T(8,128)(2,1)} collective-permute-done((bf16[4,2,16,1536]{3,2,1,0:T(8,128)(2,1)}, bf16[4,2,16,1536]{3,2,1,0:T(8,128)(2,1)}, u32[]{:S(2)}, u32[]{:S(2)}) %collective-permute-start.10) | collective-permute-done | bytes 393248 | tf_op jit(solution)/shard_map/ppermute | solution.py:527
  112.2 3.7 %collective-permute-done.12.across = bf16[4,2,16,1536]{3,2,1,0:T(8,128)(2,1)} collective-permute-done((bf16[4,2,16,1536]{3,2,1,0:T(8,128)(2,1)}, bf16[4,2,16,1536]{3,2,1,0:T(8,128)(2,1)}, u32[]{:S(2)}, u32[]{:S(2)}) %collective-permute-start.12) | collective-permute-done | bytes 393248 | tf_op jit(solution)/shard_map/ppermute | solution.py:536
  115.9 2.0 shard_map.79.rest_0_
  117.9 6.7 %shard_map.80 = (bf16[4,2,2,16,1536]{4,3,2,1,0:T(8,128)(2,1)}, bf16[64,768]{1,0:T(8,128)(2,1)}) custom-call(bf16[8,64,768]{2,1,0:T(8,128)(2,1)} %all-to-all-done.2.arrived_ref, bf16[64,768]{1,0:T(8,128)(2,1)} %pad_maximum_fusion.3.base, bf16[384,3072]{1,0:T(8,128)(2,1)} %bitcast.67, bf16[384,3072]{1,0:T(8,128)(2,1)} %collective-permute-done.7.other, ...), custom_call_target="tpu_custom_call" | custom-call | flops 301989888 | bytes 4718592 | tf_op jit(solution)/shard_map/pallas_call | solution.py:231
  124.6 4.2 %all-to-all-start.3 = ((bf16[8,2,16,1536]{3,2,1,0:T(8,128)(2,1)}), bf16[8,2,16,1536]{3,2,1,0:T(8,128)(2,1)}, u32[]{:S(2)}, u32[]{:S(2)}) async-start(bf16[8,2,16,1536]{3,2,1,0:T(8,128)(2,1)} %bitcast.82), calls=%async_computation.3 | async-start | bytes 1572864 | tf_op jit(solution)/shard_map/all_to_all | solution.py:507
  128.8 3.6 %collective-permute-start.13 = (bf16[4,2,1,16,1536]{4,3,2,1,0:T(8,128)(2,1)}, bf16[4,2,1,16,1536]{4,3,2,1,0:T(8,128)(2,1)}, u32[]{:S(2)}, u32[]{:S(2)}) collective-permute-start(bf16[4,2,1,16,1536]{4,3,2,1,0:T(8,128)(2,1)} %bitcast.3.arrived_ref.refs_0_), channel_id=1, source_target_pairs={{128,0},{129,1},{130,2},{131,3},{132,4},{133,5},{134,6},{135,7},{1... | collective-permute-start | bytes 1179656 | tf_op jit(solution)/shard_map/ppermute | solution.py:531
  133.8 3.5 %collective-permute-start.15 = (bf16[4,2,1,16,1536]{4,3,2,1,0:T(8,128)(2,1)}, bf16[4,2,1,16,1536]{4,3,2,1,0:T(8,128)(2,1)}, u32[]{:S(2)}, u32[]{:S(2)}) collective-permute-start(bf16[4,2,1,16,1536]{4,3,2,1,0:T(8,128)(2,1)} %bitcast.3.arrived_ref.refs_0_), channel_id=1, source_target_pairs={{128,8},{136,0},{129,9},{137,1},{130,10},{138,2},{131,11},{139,3},... | collective-permute-start | bytes 1179656 | tf_op jit(solution)/shard_map/ppermute | solution.py:536
  137.2 7.0 %collective-permute-done.15.refs_3_ = bf16[4,2,1,16,1536]{4,3,2,1,0:T(8,128)(2,1)} collective-permute-done((bf16[4,2,1,16,1536]{4,3,2,1,0:T(8,128)(2,1)}, bf16[4,2,1,16,1536]{4,3,2,1,0:T(8,128)(2,1)}, u32[]{:S(2)}, u32[]{:S(2)}) %collective-permute-start.15) | collective-permute-done | bytes 393248 | tf_op jit(solution)/shard_map/ppermute | solution.py:536
  144.3 6.3 %all-to-all-done.3.arrived_ref = bf16[8,2,16,1536]{3,2,1,0:T(8,128)(2,1)} async-done(((bf16[8,2,16,1536]{3,2,1,0:T(8,128)(2,1)}), bf16[8,2,16,1536]{3,2,1,0:T(8,128)(2,1)}, u32[]{:S(2)}, u32[]{:S(2)}) %all-to-all-start.3) | async-done | bytes 786464 | tf_op jit(solution)/shard_map/all_to_all | solution.py:507
  150.6 2.1 shard_map.81
  152.7 24.3 %all_to_all.45 = bf16[8,2,16,1536]{3,2,1,0:T(8,128)(2,1)} all-to-all(bf16[8,2,16,1536]{3,2,1,0:T(8,128)(2,1)} %shard_map.81), channel_id=1, replica_groups=mesh['section'=2,'z'=8,'x_lo'=2,'y'=4,'x_hi'=2] {'z'}, dimensions={0} | all-to-all | bytes 1572864 | tf_op jit(solution)/shard_map/all_to_all | solution.py:507
  177.0 5.6 %shard_map.82 = bf16[8,64,768]{2,1,0:T(8,128)(2,1)} custom-call(bf16[4,2,2,16,1536]{4,3,2,1,0:T(8,128)(2,1)} %bitcast.70, bf16[384,3072]{1,0:T(8,128)(2,1)} %bitcast.68, bf16[384,3072]{1,0:T(8,128)(2,1)} %collective-permute-done.7.other, bf16[384,3072]{1,0:T(8,128)(2,1)} %collective-permute-done.8.own_mate, bf16[384,3072]{1,0:T(8,128)(2,1)} %collective-permute-done.9.other_mate), custom_call_target="tpu_custom_call" | custom-call | flops 301989888 | bytes 4718592 | tf_op jit(solution)/shard_map/pallas_call | solution.py:231
  182.6 25.6 %all_to_all.46.arrived_ref = bf16[8,64,768]{2,1,0:T(8,128)(2,1)} all-to-all(bf16[8,64,768]{2,1,0:T(8,128)(2,1)} %shard_map.82), channel_id=1, replica_groups=mesh['section'=2,'z'=8,'x_lo'=2,'y'=4,'x_hi'=2] {'y','x_hi'}, dimensions={0} | all-to-all | bytes 1572864 | tf_op jit(solution)/shard_map/all_to_all | solution.py:507
  208.3 7.1 %shard_map.83 = (bf16[4,2,1,16,1536]{4,3,2,1,0:T(8,128)(2,1)}, bf16[64,768]{1,0:T(8,128)(2,1)}) custom-call(bf16[8,64,768]{2,1,0:T(8,128)(2,1)} %all_to_all.46.arrived_ref, bf16[64,768]{1,0:T(8,128)(2,1)} %pad_maximum_fusion.2.base, bf16[3072,384]{1,0:T(8,128)(2,1)} %bitcast.62, bf16[3072,384]{1,0:T(8,128)(2,1)} %collective-permute-done.4.other, ...), custom_call_target="tpu_custom_call" | custom-call | flops 301989888 | bytes 4718592 | tf_op jit(solution)/shard_map/pallas_call | solution.py:231
  215.3 4.1 %all-to-all-start.6 = ((bf16[8,1,16,1536]{3,2,1,0:T(8,128)(2,1)}), bf16[8,1,16,1536]{3,2,1,0:T(8,128)(2,1)}, u32[]{:S(2)}, u32[]{:S(2)}) async-start(bf16[8,1,16,1536]{3,2,1,0:T(8,128)(2,1)} %bitcast.83), calls=%async_computation.6 | async-start | bytes 786432 | tf_op jit(solution)/shard_map/all_to_all | solution.py:507
  221.1 1.9 collective-permute-start.22
  223.0 1.6 collective-permute-start.24
  226.0 1.9 collective-permute-start.17
  229.4 1.8 dynamic-slice_bitcast_fusion.3
  231.7 2.8 shard_map.84
  234.6 6.5 %all-to-all-start.7 = ((bf16[8,1,16,1536]{3,2,1,0:T(8,128)(2,1)}), bf16[8,1,16,1536]{3,2,1,0:T(8,128)(2,1)}, u32[]{:S(2)}, u32[]{:S(2)}) async-start(bf16[8,1,16,1536]{3,2,1,0:T(8,128)(2,1)} %shard_map.84), calls=%async_computation.7 | async-start | bytes 786432 | tf_op jit(solution)/shard_map/all_to_all | solution.py:507
  243.1 1.8 collective-permute-done.17.refs_6_
  244.9 2.6 collective-permute-done.18.refs_7_
  247.4 4.3 %all-to-all-done.7 = bf16[8,1,16,1536]{3,2,1,0:T(8,128)(2,1)} async-done(((bf16[8,1,16,1536]{3,2,1,0:T(8,128)(2,1)}), bf16[8,1,16,1536]{3,2,1,0:T(8,128)(2,1)}, u32[]{:S(2)}, u32[]{:S(2)}) %all-to-all-start.7) | async-done | bytes 393248 | tf_op jit(solution)/shard_map/all_to_all | solution.py:507
  251.7 7.7 %collective-permute-start.19 = (bf16[4,2,1,16,1536]{4,3,2,1,0:T(8,128)(2,1)}, bf16[4,2,1,16,1536]{4,3,2,1,0:T(8,128)(2,1)}, u32[]{:S(2)}, u32[]{:S(2)}) collective-permute-start(bf16[4,2,1,16,1536]{4,3,2,1,0:T(8,128)(2,1)} %bitcast.11.refs_0_), channel_id=1, source_target_pairs={{128,0},{129,1},{130,2},{131,3},{132,4},{133,5},{134,6},{135,7},{1... | collective-permute-start | bytes 1179656 | tf_op jit(solution)/shard_map/ppermute | solution.py:531
  260.9 3.5 %collective-permute-start.21 = (bf16[4,2,1,16,1536]{4,3,2,1,0:T(8,128)(2,1)}, bf16[4,2,1,16,1536]{4,3,2,1,0:T(8,128)(2,1)}, u32[]{:S(2)}, u32[]{:S(2)}) collective-permute-start(bf16[4,2,1,16,1536]{4,3,2,1,0:T(8,128)(2,1)} %bitcast.11.refs_0_), channel_id=1, source_target_pairs={{128,8},{136,0},{129,9},{137,1},{130,10},{138,2},{131,11},{139,3},... | collective-permute-start | bytes 1179656 | tf_op jit(solution)/shard_map/ppermute | solution.py:536
  265.7 6.3 %shard_map.85 = f32[3072,384]{1,0:T(8,128)} custom-call(bf16[256,384]{1,0:T(8,128)(2,1)} %maximum_select_fusion.g_ref, bf16[4,2,1,16,1536]{4,3,2,1,0:T(8,128)(2,1)} %bitcast.3.arrived_ref.refs_0_, bf16[4,2,1,16,1536]{4,3,2,1,0:T(8,128)(2,1)} %collective-permute-done.13.refs_1_, bf16[4,2,1,16,1536]{4,3,2,1,0:T(8,128)(2,1)} %collective-permute-done.14.refs_2_, ...), custom_call_target="tpu_custom_call" | custom-call | flops 603979776 | bytes 4718592 | tf_op jit(solution)/shard_map/pallas_call | solution.py:429
  272.1 4.0 %shard_map.86 = bf16[8,2,16,384]{3,2,1,0:T(8,128)(2,1)} custom-call(bf16[384,3072]{1,0:T(8,128)(2,1)} %bitcast.69, bf16[3072,384]{1,0:T(8,128)(2,1)} %bitcast.63, bf16[4,2,1,16,1536]{4,3,2,1,0:T(8,128)(2,1)} %bitcast.11.refs_0_, bf16[4,2,1,16,1536]{4,3,2,1,0:T(8,128)(2,1)} %collective-permute-done.19.refs_1_, ...), custom_call_target="tpu_custom_call" | custom-call | flops 603979776 | bytes 7077888 | tf_op jit(solution)/shard_map/pallas_call | solution.py:231
  276.1 4.0 %all-to-all-start.8 = ((bf16[8,2,16,384]{3,2,1,0:T(8,128)(2,1)}), bf16[8,2,16,384]{3,2,1,0:T(8,128)(2,1)}, u32[]{:S(2)}, u32[]{:S(2)}) async-start(bf16[8,2,16,384]{3,2,1,0:T(8,128)(2,1)} %shard_map.86), calls=%async_computation.8 | async-start | bytes 393216 | tf_op jit(solution)/shard_map/all_to_all | solution.py:507
  281.5 6.0 %shard_map.88 = f32[384,3072]{1,0:T(8,128)} custom-call(bf16[256,384]{1,0:T(8,128)(2,1)} %maximum_select_fusion.1.x_ref, bf16[4,2,1,16,1536]{4,3,2,1,0:T(8,128)(2,1)} %bitcast.11.refs_0_, bf16[4,2,1,16,1536]{4,3,2,1,0:T(8,128)(2,1)} %collective-permute-done.19.refs_1_, bf16[4,2,1,16,1536]{4,3,2,1,0:T(8,128)(2,1)} %collective-permute-done.20.refs_2_, ...), custom_call_target="tpu_custom_call" | custom-call | flops 603979776 | bytes 4718592 | tf_op jit(solution)/shard_map/pallas_call | solution.py:429
  (66 shorter events, 27.6 us)
Async XLA Ops:
  5.7 7.8 %collective-permute-start = (bf16[4,2,16,1536]{3,2,1,0:T(8,128)(2,1)}, bf16[4,2,16,1536]{3,2,1,0:T(8,128)(2,1)}, u32[]{:S(2)}, u32[]{:S(2)}) collective-permute-start(bf16[4,2,16,1536]{3,2,1,0:T(8,128)(2,1)} %get-tuple-element.63), channel_id=1, source_target_pairs={{0,8},{8,0},{1,9},{9,1},{2,10},{10,2},{3,11},{11,3},{4,12},{12,4},... | collective-permute-start | bytes 1179656 | tf_op jit(solution)/shard_map/ppermute | solution.py:527
  7.2 6.4 %collective-permute-start.1 = (bf16[4,2,16,1536]{3,2,1,0:T(8,128)(2,1)}, bf16[4,2,16,1536]{3,2,1,0:T(8,128)(2,1)}, u32[]{:S(2)}, u32[]{:S(2)}) collective-permute-start(bf16[4,2,16,1536]{3,2,1,0:T(8,128)(2,1)} %get-tuple-element.64), channel_id=1, source_target_pairs={{0,128},{1,129},{2,130},{3,131},{4,132},{5,133},{6,134},{7,135},{8... | collective-permute-start | bytes 1179656 | tf_op jit(solution)/shard_map/ppermute | solution.py:531
  8.4 14.9 %collective-permute-start.2 = (bf16[4,2,16,1536]{3,2,1,0:T(8,128)(2,1)}, bf16[4,2,16,1536]{3,2,1,0:T(8,128)(2,1)}, u32[]{:S(2)}, u32[]{:S(2)}) collective-permute-start(bf16[4,2,16,1536]{3,2,1,0:T(8,128)(2,1)} %get-tuple-element.65), channel_id=1, source_target_pairs={{0,136},{8,128},{1,137},{9,129},{2,138},{10,130},{3,139},{11,131},... | collective-permute-start | bytes 1179656 | tf_op jit(solution)/shard_map/ppermute | solution.py:536
  11.4 13.9 %collective-permute-start.3 = (bf16[2,64,384]{2,1,0:T(8,128)(2,1)}, bf16[2,64,384]{2,1,0:T(8,128)(2,1)}, u32[]{:S(2)}, u32[]{:S(2)}) collective-permute-start(bf16[2,64,384]{2,1,0:T(8,128)(2,1)} %get-tuple-element.102), channel_id=1, source_target_pairs={{0,8},{8,0},{1,9},{9,1},{2,10},{10,2},{3,11},{11,3},{4,12},{12,4},... | collective-permute-start | bytes 294920 | tf_op jit(solution)/shard_map/ppermute | solution.py:518
  25.3 26.7 %collective-permute-start.5 = (bf16[3072,384]{1,0:T(8,128)(2,1)}, bf16[3072,384]{1,0:T(8,128)(2,1)}, u32[]{:S(2)}, u32[]{:S(2)}) collective-permute-start(bf16[3072,384]{1,0:T(8,128)(2,1)} %bitcast.59), channel_id=1, source_target_pairs={{0,8},{8,0},{1,9},{9,1},{2,10},{10,2},{3,11},{11,3},{4,12},{12,4},... | collective-permute-start | bytes 7077896 | tf_op jit(solution)/shard_map/ppermute | solution.py:527
  27.4 19.8 %all-to-all-start = ((bf16[8,1,16,1536]{3,2,1,0:T(8,128)(2,1)}), bf16[8,1,16,1536]{3,2,1,0:T(8,128)(2,1)}, u32[]{:S(2)}, u32[]{:S(2)}) async-start(bf16[8,1,16,1536]{3,2,1,0:T(8,128)(2,1)} %bitcast.81), calls=%async_computation | async-start | bytes 786432 | tf_op jit(solution)/shard_map/all_to_all | solution.py:507
  33.8 39.9 %collective-permute-start.4 = (bf16[3072,384]{1,0:T(8,128)(2,1)}, bf16[3072,384]{1,0:T(8,128)(2,1)}, u32[]{:S(2)}, u32[]{:S(2)}) collective-permute-start(bf16[3072,384]{1,0:T(8,128)(2,1)} %bitcast.60), channel_id=1, source_target_pairs={{0,128},{1,129},{2,130},{3,131},{4,132},{5,133},{6,134},{7,135},{8... | collective-permute-start | bytes 7077896 | tf_op jit(solution)/shard_map/ppermute | solution.py:531
  52.0 21.7 %collective-permute-start.6 = (bf16[3072,384]{1,0:T(8,128)(2,1)}, bf16[3072,384]{1,0:T(8,128)(2,1)}, u32[]{:S(2)}, u32[]{:S(2)}) collective-permute-start(bf16[3072,384]{1,0:T(8,128)(2,1)} %collective-permute-done.5.own_mate), channel_id=1, source_target_pairs={{0,128},{1,129},{2,130},{3,131},{4,132},{5,133},{6,134},{7,135},{8... | collective-permute-start | bytes 7077896 | tf_op jit(solution)/shard_map/ppermute | solution.py:531
  53.3 31.6 %collective-permute-start.8 = (bf16[384,3072]{1,0:T(8,128)(2,1)}, bf16[384,3072]{1,0:T(8,128)(2,1)}, u32[]{:S(2)}, u32[]{:S(2)}) collective-permute-start(bf16[384,3072]{1,0:T(8,128)(2,1)} %bitcast.65), channel_id=1, source_target_pairs={{128,136},{136,128},{129,137},{137,129},{130,138},{138,130},{131,1... | collective-permute-start | bytes 7077896 | tf_op jit(solution)/shard_map/ppermute | solution.py:527
  58.4 15.3 %all-to-all-start.1 = ((bf16[8,1,16,1536]{3,2,1,0:T(8,128)(2,1)}), bf16[8,1,16,1536]{3,2,1,0:T(8,128)(2,1)}, u32[]{:S(2)}, u32[]{:S(2)}) async-start(bf16[8,1,16,1536]{3,2,1,0:T(8,128)(2,1)} %get-tuple-element.50), calls=%async_computation.1 | async-start | bytes 786432 | tf_op jit(solution)/shard_map/all_to_all | solution.py:507
  62.5 55.4 %collective-permute-start.7 = (bf16[384,3072]{1,0:T(8,128)(2,1)}, bf16[384,3072]{1,0:T(8,128)(2,1)}, u32[]{:S(2)}, u32[]{:S(2)}) collective-permute-start(bf16[384,3072]{1,0:T(8,128)(2,1)} %bitcast.66), channel_id=1, source_target_pairs={{128,0},{129,1},{130,2},{131,3},{132,4},{133,5},{134,6},{135,7},{1... | collective-permute-start | bytes 7077896 | tf_op jit(solution)/shard_map/ppermute | solution.py:531
  84.9 33.0 %collective-permute-start.9 = (bf16[384,3072]{1,0:T(8,128)(2,1)}, bf16[384,3072]{1,0:T(8,128)(2,1)}, u32[]{:S(2)}, u32[]{:S(2)}) collective-permute-start(bf16[384,3072]{1,0:T(8,128)(2,1)} %collective-permute-done.8.own_mate), channel_id=1, source_target_pairs={{128,0},{129,1},{130,2},{131,3},{132,4},{133,5},{134,6},{135,7},{1... | collective-permute-start | bytes 7077896 | tf_op jit(solution)/shard_map/ppermute | solution.py:531
  92.7 25.2 %all-to-all-start.2 = ((bf16[8,64,768]{2,1,0:T(8,128)(2,1)}), bf16[8,64,768]{2,1,0:T(8,128)(2,1)}, u32[]{:S(2)}, u32[]{:S(2)}) async-start(bf16[8,64,768]{2,1,0:T(8,128)(2,1)} %shard_map.78), calls=%async_computation.2 | async-start | bytes 1572864 | tf_op jit(solution)/shard_map/all_to_all | solution.py:507
  99.7 12.4 %collective-permute-start.10 = (bf16[4,2,16,1536]{3,2,1,0:T(8,128)(2,1)}, bf16[4,2,16,1536]{3,2,1,0:T(8,128)(2,1)}, u32[]{:S(2)}, u32[]{:S(2)}) collective-permute-start(bf16[4,2,16,1536]{3,2,1,0:T(8,128)(2,1)} %get-tuple-element.63), channel_id=1, source_target_pairs={{128,136},{136,128},{129,137},{137,129},{130,138},{138,130},{131,1... | collective-permute-start | bytes 1179656 | tf_op jit(solution)/shard_map/ppermute | solution.py:527
  101.7 10.5 %collective-permute-start.11 = (bf16[4,2,16,1536]{3,2,1,0:T(8,128)(2,1)}, bf16[4,2,16,1536]{3,2,1,0:T(8,128)(2,1)}, u32[]{:S(2)}, u32[]{:S(2)}) collective-permute-start(bf16[4,2,16,1536]{3,2,1,0:T(8,128)(2,1)} %get-tuple-element.64), channel_id=1, source_target_pairs={{128,0},{129,1},{130,2},{131,3},{132,4},{133,5},{134,6},{135,7},{1... | collective-permute-start | bytes 1179656 | tf_op jit(solution)/shard_map/ppermute | solution.py:531
  103.7 12.2 %collective-permute-start.12 = (bf16[4,2,16,1536]{3,2,1,0:T(8,128)(2,1)}, bf16[4,2,16,1536]{3,2,1,0:T(8,128)(2,1)}, u32[]{:S(2)}, u32[]{:S(2)}) collective-permute-start(bf16[4,2,16,1536]{3,2,1,0:T(8,128)(2,1)} %get-tuple-element.65), channel_id=1, source_target_pairs={{128,8},{136,0},{129,9},{137,1},{130,10},{138,2},{131,11},{139,3},... | collective-permute-start | bytes 1179656 | tf_op jit(solution)/shard_map/ppermute | solution.py:536
  124.6 26.0 %all-to-all-start.3 = ((bf16[8,2,16,1536]{3,2,1,0:T(8,128)(2,1)}), bf16[8,2,16,1536]{3,2,1,0:T(8,128)(2,1)}, u32[]{:S(2)}, u32[]{:S(2)}) async-start(bf16[8,2,16,1536]{3,2,1,0:T(8,128)(2,1)} %bitcast.82), calls=%async_computation.3 | async-start | bytes 1572864 | tf_op jit(solution)/shard_map/all_to_all | solution.py:507
  128.8 8.4 %collective-permute-start.13 = (bf16[4,2,1,16,1536]{4,3,2,1,0:T(8,128)(2,1)}, bf16[4,2,1,16,1536]{4,3,2,1,0:T(8,128)(2,1)}, u32[]{:S(2)}, u32[]{:S(2)}) collective-permute-start(bf16[4,2,1,16,1536]{4,3,2,1,0:T(8,128)(2,1)} %bitcast.3.arrived_ref.refs_0_), channel_id=1, source_target_pairs={{128,0},{129,1},{130,2},{131,3},{132,4},{133,5},{134,6},{135,7},{1... | collective-permute-start | bytes 1179656 | tf_op jit(solution)/shard_map/ppermute | solution.py:531
  132.4 4.9 %collective-permute-start.14 = (bf16[4,2,1,16,1536]{4,3,2,1,0:T(8,128)(2,1)}, bf16[4,2,1,16,1536]{4,3,2,1,0:T(8,128)(2,1)}, u32[]{:S(2)}, u32[]{:S(2)}) collective-permute-start(bf16[4,2,1,16,1536]{4,3,2,1,0:T(8,128)(2,1)} %bitcast.3.arrived_ref.refs_0_), channel_id=1, source_target_pairs={{0,8},{8,0},{1,9},{9,1},{2,10},{10,2},{3,11},{11,3},{4,12},{12,4},... | collective-permute-start | bytes 1179656 | tf_op jit(solution)/shard_map/ppermute | solution.py:527
  133.8 10.5 %collective-permute-start.15 = (bf16[4,2,1,16,1536]{4,3,2,1,0:T(8,128)(2,1)}, bf16[4,2,1,16,1536]{4,3,2,1,0:T(8,128)(2,1)}, u32[]{:S(2)}, u32[]{:S(2)}) collective-permute-start(bf16[4,2,1,16,1536]{4,3,2,1,0:T(8,128)(2,1)} %bitcast.3.arrived_ref.refs_0_), channel_id=1, source_target_pairs={{128,8},{136,0},{129,9},{137,1},{130,10},{138,2},{131,11},{139,3},... | collective-permute-start | bytes 1179656 | tf_op jit(solution)/shard_map/ppermute | solution.py:536
  215.3 16.4 %all-to-all-start.6 = ((bf16[8,1,16,1536]{3,2,1,0:T(8,128)(2,1)}), bf16[8,1,16,1536]{3,2,1,0:T(8,128)(2,1)}, u32[]{:S(2)}, u32[]{:S(2)}) async-start(bf16[8,1,16,1536]{3,2,1,0:T(8,128)(2,1)} %bitcast.83), calls=%async_computation.6 | async-start | bytes 786432 | tf_op jit(solution)/shard_map/all_to_all | solution.py:507
  221.1 6.8 %collective-permute-start.22 = (bf16[2,64,384]{2,1,0:T(8,128)(2,1)S(1)}, bf16[2,64,384]{2,1,0:T(8,128)(2,1)}, u32[]{:S(2)}, u32[]{:S(2)}) collective-permute-start(bf16[2,64,384]{2,1,0:T(8,128)(2,1)S(1)} %get-tuple-element.96), channel_id=1, source_target_pairs={{0,128},{128,0},{1,129},{129,1},{2,130},{130,2},{3,131},{131,3},{4... | collective-permute-start | bytes 294920 | tf_op jit(solution)/shard_map/ppermute | solution.py:514
  223.0 18.0 %collective-permute-start.23 = (bf16[2,64,384]{2,1,0:T(8,128)(2,1)}, bf16[2,64,384]{2,1,0:T(8,128)(2,1)}, u32[]{:S(2)}, u32[]{:S(2)}) collective-permute-start(bf16[2,64,384]{2,1,0:T(8,128)(2,1)} %get-tuple-element.95), channel_id=1, source_target_pairs={{0,8},{8,0},{1,9},{9,1},{2,10},{10,2},{3,11},{11,3},{4,12},{12,4},... | collective-permute-start | bytes 294920 | tf_op jit(solution)/shard_map/ppermute | solution.py:518
  223.0 18.0 %collective-permute-start.24 = (bf16[2,64,384]{2,1,0:T(8,128)(2,1)}, bf16[2,64,384]{2,1,0:T(8,128)(2,1)}, u32[]{:S(2)}, u32[]{:S(2)}) collective-permute-start(bf16[2,64,384]{2,1,0:T(8,128)(2,1)} %get-tuple-element.95), channel_id=1, source_target_pairs={{0,136},{136,0},{8,128},{128,8},{1,137},{137,1},{9,129},{129,9},{2... | collective-permute-start | bytes 294920 | tf_op jit(solution)/shard_map/ppermute | solution.py:522
  224.7 18.4 %collective-permute-start.16 = (bf16[4,2,2,16,1536]{4,3,2,1,0:T(8,128)(2,1)}, bf16[4,2,2,16,1536]{4,3,2,1,0:T(8,128)(2,1)}, u32[]{:S(2)}, u32[]{:S(2)}) collective-permute-start(bf16[4,2,2,16,1536]{4,3,2,1,0:T(8,128)(2,1)} %bitcast.71), channel_id=1, source_target_pairs={{0,128},{1,129},{2,130},{3,131},{4,132},{5,133},{6,134},{7,135},{8... | collective-permute-start | bytes 2359304 | tf_op jit(solution)/shard_map/ppermute | solution.py:531
  226.0 18.9 %collective-permute-start.17 = (bf16[4,2,2,16,1536]{4,3,2,1,0:T(8,128)(2,1)}, bf16[4,2,2,16,1536]{4,3,2,1,0:T(8,128)(2,1)}, u32[]{:S(2)}, u32[]{:S(2)}) collective-permute-start(bf16[4,2,2,16,1536]{4,3,2,1,0:T(8,128)(2,1)} %bitcast.72), channel_id=1, source_target_pairs={{128,136},{136,128},{129,137},{137,129},{130,138},{138,130},{131,1... | collective-permute-start | bytes 2359304 | tf_op jit(solution)/shard_map/ppermute | solution.py:527
  227.9 19.5 %collective-permute-start.18 = (bf16[4,2,2,16,1536]{4,3,2,1,0:T(8,128)(2,1)}, bf16[4,2,2,16,1536]{4,3,2,1,0:T(8,128)(2,1)}, u32[]{:S(2)}, u32[]{:S(2)}) collective-permute-start(bf16[4,2,2,16,1536]{4,3,2,1,0:T(8,128)(2,1)} %bitcast.73), channel_id=1, source_target_pairs={{0,136},{8,128},{1,137},{9,129},{2,138},{10,130},{3,139},{11,131},... | collective-permute-start | bytes 2359304 | tf_op jit(solution)/shard_map/ppermute | solution.py:536
  234.5 7.8 %copy-start.4 = (bf16[64,384]{1,0:T(8,128)(2,1)S(1)}, bf16[64,384]{1,0:T(8,128)(2,1)}, u32[]{:S(2)}) copy-start(bf16[64,384]{1,0:T(8,128)(2,1)} %get-tuple-element.107) | copy-start | bytes 147460
  234.5 7.8 %copy-start.5 = (bf16[64,384]{1,0:T(8,128)(2,1)S(1)}, bf16[64,384]{1,0:T(8,128)(2,1)}, u32[]{:S(2)}) copy-start(bf16[64,384]{1,0:T(8,128)(2,1)} %get-tuple-element.108) | copy-start | bytes 147460
  234.5 7.8 %copy-start.6 = (bf16[64,384]{1,0:T(8,128)(2,1)S(1)}, bf16[64,384]{1,0:T(8,128)(2,1)}, u32[]{:S(2)}) copy-start(bf16[64,384]{1,0:T(8,128)(2,1)} %get-tuple-element.109) | copy-start | bytes 147460
  234.6 7.8 %copy-start.7 = (bf16[64,384]{1,0:T(8,128)(2,1)S(1)}, bf16[64,384]{1,0:T(8,128)(2,1)}, u32[]{:S(2)}) copy-start(bf16[64,384]{1,0:T(8,128)(2,1)} %get-tuple-element.110) | copy-start | bytes 147460
  234.6 30.4 %copy-start = (bf16[64,384]{1,0:T(8,128)(2,1)S(1)}, bf16[64,384]{1,0:T(8,128)(2,1)}, u32[]{:S(2)}) copy-start(bf16[64,384]{1,0:T(8,128)(2,1)} %get-tuple-element.90) | copy-start | bytes 147460
  234.6 30.4 %copy-start.1 = (bf16[64,384]{1,0:T(8,128)(2,1)S(1)}, bf16[64,384]{1,0:T(8,128)(2,1)}, u32[]{:S(2)}) copy-start(bf16[64,384]{1,0:T(8,128)(2,1)} %get-tuple-element.91) | copy-start | bytes 147460
  234.6 30.4 %copy-start.2 = (bf16[64,384]{1,0:T(8,128)(2,1)S(1)}, bf16[64,384]{1,0:T(8,128)(2,1)}, u32[]{:S(2)}) copy-start(bf16[64,384]{1,0:T(8,128)(2,1)} %get-tuple-element.92) | copy-start | bytes 147460
  234.6 30.4 %copy-start.3 = (bf16[64,384]{1,0:T(8,128)(2,1)S(1)}, bf16[64,384]{1,0:T(8,128)(2,1)}, u32[]{:S(2)}) copy-start(bf16[64,384]{1,0:T(8,128)(2,1)} %get-tuple-element.93) | copy-start | bytes 147460
  234.6 17.1 %all-to-all-start.7 = ((bf16[8,1,16,1536]{3,2,1,0:T(8,128)(2,1)}), bf16[8,1,16,1536]{3,2,1,0:T(8,128)(2,1)}, u32[]{:S(2)}, u32[]{:S(2)}) async-start(bf16[8,1,16,1536]{3,2,1,0:T(8,128)(2,1)} %shard_map.84), calls=%async_computation.7 | async-start | bytes 786432 | tf_op jit(solution)/shard_map/all_to_all | solution.py:507
  251.7 20.3 %collective-permute-start.19 = (bf16[4,2,1,16,1536]{4,3,2,1,0:T(8,128)(2,1)}, bf16[4,2,1,16,1536]{4,3,2,1,0:T(8,128)(2,1)}, u32[]{:S(2)}, u32[]{:S(2)}) collective-permute-start(bf16[4,2,1,16,1536]{4,3,2,1,0:T(8,128)(2,1)} %bitcast.11.refs_0_), channel_id=1, source_target_pairs={{128,0},{129,1},{130,2},{131,3},{132,4},{133,5},{134,6},{135,7},{1... | collective-permute-start | bytes 1179656 | tf_op jit(solution)/shard_map/ppermute | solution.py:531
  259.5 12.6 %collective-permute-start.20 = (bf16[4,2,1,16,1536]{4,3,2,1,0:T(8,128)(2,1)}, bf16[4,2,1,16,1536]{4,3,2,1,0:T(8,128)(2,1)}, u32[]{:S(2)}, u32[]{:S(2)}) collective-permute-start(bf16[4,2,1,16,1536]{4,3,2,1,0:T(8,128)(2,1)} %bitcast.11.refs_0_), channel_id=1, source_target_pairs={{0,8},{8,0},{1,9},{9,1},{2,10},{10,2},{3,11},{11,3},{4,12},{12,4},... | collective-permute-start | bytes 1179656 | tf_op jit(solution)/shard_map/ppermute | solution.py:527
  260.9 11.2 %collective-permute-start.21 = (bf16[4,2,1,16,1536]{4,3,2,1,0:T(8,128)(2,1)}, bf16[4,2,1,16,1536]{4,3,2,1,0:T(8,128)(2,1)}, u32[]{:S(2)}, u32[]{:S(2)}) collective-permute-start(bf16[4,2,1,16,1536]{4,3,2,1,0:T(8,128)(2,1)} %bitcast.11.refs_0_), channel_id=1, source_target_pairs={{128,8},{136,0},{129,9},{137,1},{130,10},{138,2},{131,11},{139,3},... | collective-permute-start | bytes 1179656 | tf_op jit(solution)/shard_map/ppermute | solution.py:536
  276.1 12.2 %all-to-all-start.8 = ((bf16[8,2,16,384]{3,2,1,0:T(8,128)(2,1)}), bf16[8,2,16,384]{3,2,1,0:T(8,128)(2,1)}, u32[]{:S(2)}, u32[]{:S(2)}) async-start(bf16[8,2,16,384]{3,2,1,0:T(8,128)(2,1)} %shard_map.86), calls=%async_computation.8 | async-start | bytes 393216 | tf_op jit(solution)/shard_map/all_to_all | solution.py:507

commit v4 on v3

--- a/solution.py
+++ b/solution.py
@@ -129,61 +129,50 @@
     )
 
 
-def add_kernel(layer, kept, mates, other, across, out_ref, held, sems):
-    mine = lax.axis_index("section") == layer
-
-    def copies(refs):
-        return [pltpu.make_async_copy(ref, held.at[i], sems.at[i]) for i, ref in enumerate(refs)]
-
-    @pl.when(mine)
-    def _():
-        for copy in copies((kept, mates)):
-            copy.start()
-
-    @pl.when(jnp.logical_not(mine))
-    def _():
-        for copy in copies((other, across)):
-            copy.start()
-
-    wait_all(copies((kept, mates)))
-    held[0] = (held[0].astype(f32) + held[1].astype(f32)).astype(bf16)
-    copy = pltpu.make_async_copy(held.at[0], out_ref, sems.at[2])
-    copy.start()
-    copy.wait()
-
-
-def add_terms(layer, terms):
+def add_kernel(kept, mates, other, across, out_ref, held, sems):
+    section = lax.axis_index("section")
+    copies = [
+        pltpu.make_async_copy(ref, held.at[i], sems.at[i]) for i, ref in enumerate((kept, mates, other, across))
+    ]
+    for copy in copies:
+        copy.start()
+    outs = []
+    for i, kind in enumerate((section, 1 - section)):
+        copies[2 * i].wait()
+        copies[2 * i + 1].wait()
+        held[2 * i] = (held[2 * i].astype(f32) + held[2 * i + 1].astype(f32)).astype(bf16)
+        outs.append(pltpu.make_async_copy(held.at[2 * i], out_ref.at[:, :, kind], sems.at[4 + i]))
+        outs[-1].start()
+    wait_all(outs)
+
+
+def add_terms(terms):
     shape = terms[0].shape
     return kernel_call(
-        functools.partial(add_kernel, layer),
-        shape_of(shape),
+        add_kernel,
+        shape_of(shape[:2] + (2,) + shape[2:]),
         HBM,
         [HBM] * 4,
-        [pltpu.VMEM((2,) + shape, bf16), pltpu.SemaphoreType.DMA((3,))],
+        [pltpu.VMEM((4,) + shape, bf16), pltpu.SemaphoreType.DMA((6,))],
         terms,
-        flops=terms[0].size,
-        moved=6 * terms[0].size,
-    )
-
-
-def widen_kernel(layer, by_rows, riders, arrived_ref, base, own, other, own_mate, other_mate, *rest):
-    out_ref, x_out, held, sems, stage, out_sems, arrived, in_sems = rest[riders:]
-    arrival = pltpu.make_async_copy(arrived_ref, arrived, in_sems.at[0])
+        flops=2 * terms[0].size,
+        moved=12 * terms[0].size,
+    )
+
+
+def widen_kernel(layer, by_rows, kind, arrived_ref, base, base_mate, own, other, own_mate, other_mate, *rest):
+    out_ref, x_out, held, sems, stage, out_sems, arrived, in_sem = rest
+    arrival = pltpu.make_async_copy(arrived_ref, arrived, in_sem)
     arrival.start()
     wait = load_weights(layer, by_rows, ((own, other), (own_mate, other_mate)), held, sems)
-    rides = [
-        pltpu.make_async_copy(rest[i], stage.at[:, :, 1 + i], in_sems.at[1 + i]) for i in range(riders)
-    ]
-    for copy in rides:
-        copy.start()
-    per_half = stage.shape[4] // CHUNK
+    per_half = stage.shape[3] // CHUNK
     arrival.wait()
     total = arrived[0].astype(f32)
     for i in range(1, arrived.shape[0]):
         total = total + arrived[i].astype(f32)
-    x = (base[...].astype(f32) + total).astype(bf16)
+    x = jnp.concatenate([base[kind], base_mate[kind]], axis=1)
+    x = (x.astype(f32) + total).astype(bf16)
     x_out[...] = x
-    wait_all(rides)
 
     def out_copy(half):
         return pltpu.make_async_copy(stage.at[:, half], out_ref.at[:, half], out_sems.at[half])
@@ -192,7 +181,7 @@
         half, place = i // per_half, pl.ds((i % per_half) * CHUNK, CHUNK)
         wait(i)
         got = dot(x, held[i], ((1,), (1 if by_rows else 0,))).astype(bf16)
-        stage[:, half, 0, :, place] = got.reshape(stage.shape[0], stage.shape[3], CHUNK)
+        stage[:, half, :, place] = got.reshape(stage.shape[0], stage.shape[2], CHUNK)
         if i % per_half == per_half - 1:
             out_copy(half).start()
     wait_all([out_copy(0), out_copy(1)])
@@ -239,22 +228,21 @@
     )(*operands)
 
 
-def widen(layer, by_rows, arrived, base, weights, blocks, riders=()):
-    shape = blocks[:2] + (1 + len(riders),) + blocks[2:]
+def widen(layer, by_rows, arrived, kind, bases, weights, blocks):
     return kernel_call(
-        functools.partial(widen_kernel, layer, by_rows, len(riders)),
-        (shape_of(shape), shape_of(base.shape)),
+        functools.partial(widen_kernel, layer, by_rows, kind),
+        (shape_of(blocks), shape_of(arrived.shape[1:])),
         (HBM, VMEM),
-        [HBM, VMEM] + [HBM] * (4 + len(riders)),
+        [HBM, VMEM, VMEM] + [HBM] * 4,
         held_scratch(weights[0], by_rows)
         + [
-            pltpu.VMEM(shape, bf16),
+            pltpu.VMEM(blocks, bf16),
             pltpu.SemaphoreType.DMA((2,)),
             pltpu.VMEM(arrived.shape, bf16),
-            pltpu.SemaphoreType.DMA((1 + len(riders),)),
+            pltpu.SemaphoreType.DMA,
         ],
-        (arrived, base) + weights + riders,
-        flops=4 * base.shape[0] * weights[0].size,
+        (arrived,) + bases + weights,
+        flops=4 * arrived.shape[1] * weights[0].size,
         moved=4 * weights[0].size,
     )
 
@@ -280,11 +268,9 @@
     )
 
 
-def act_kernel(body, slopes, arrived_ref, *refs):
-    slope_in, rest = (refs[0], refs[1:]) if slopes == "in" else (None, refs)
-    out_ref, rest = rest[0], rest[1:]
-    slope_out, rest = (rest[0], rest[1:]) if slopes == "out" else (None, rest)
-    arrived, stage, in_sems, out_sems = rest
+def act_kernel(body, ins, outs, arrived_ref, *refs):
+    in_refs, out_ref, out_refs = refs[:ins], refs[ins], refs[ins + 1 : ins + 1 + outs]
+    arrived, stage, in_sems, out_sems = refs[ins + 1 + outs :]
     steps = arrived.shape[3] // CHUNK
     places = [pl.ds(i * CHUNK, CHUNK) for i in range(steps)]
     arrivals = [
@@ -302,11 +288,11 @@
             for source in range(1, arrived.shape[0]):
                 total = total + arrived[source, kind, :, place].astype(f32)
             sums.append(total)
-        values, slope = body(sums, None if slope_in is None else slope_in[:, place])
-        for kind, value in enumerate(values):
+        spread, kept = body(sums, [ref[:, place] for ref in in_refs])
+        for kind, value in enumerate(spread):
             stage[kind, :, place] = value.astype(bf16)
-        if slope_out is not None:
-            slope_out[:, place] = slope
+        for ref, value in zip(out_refs, kept):
+            ref[:, place] = value
         for to in range(out_ref.shape[0]):
             copies.append(
                 pltpu.make_async_copy(stage.at[:, :, place], out_ref.at[to, :, :, place], out_sems.at[i, to])
@@ -317,36 +303,33 @@
 
 def act_first(sums, _):
     value, slope = gelu_both(sums[0])
-    return [value], slope
-
-
-def act_last(sums, _):
+    return [value], [slope, sums[1]]
+
+
+def act_last(sums, ins):
     value, slope = gelu_both(sums[0])
-    return [sums[1] * slope, value], None
-
-
-def act_back(sums, slope):
-    return [sums[0] * slope], None
-
-
-def activation(body, arrived, kinds, slope_out=False, slope=None):
+    return [ins[0] * slope, value], []
+
+
+def act_back(sums, ins):
+    return [sums[0] * ins[0]], []
+
+
+def activation(body, arrived, kinds, ins=(), outs=0):
     peers, piece = arrived.shape[0], arrived.shape[2:]
-    outs, out_specs, slopes = [shape_of((peers, kinds) + piece)], [HBM], "in" if slope is not None else ""
-    if slope_out:
-        outs, out_specs, slopes = outs + [shape_of(piece, f32)], out_specs + [VMEM], "out"
     steps = piece[1] // CHUNK
     return kernel_call(
-        functools.partial(act_kernel, body, slopes),
-        outs,
-        out_specs,
-        [HBM] + ([VMEM] if slope is not None else []),
+        functools.partial(act_kernel, body, len(ins), outs),
+        [shape_of((peers, kinds) + piece)] + [shape_of(piece, f32)] * outs,
+        [HBM] + [VMEM] * outs,
+        [HBM] + [VMEM] * len(ins),
         [
             pltpu.VMEM(arrived.shape, bf16),
             pltpu.VMEM((kinds,) + piece, bf16),
             pltpu.SemaphoreType.DMA((steps,)),
             pltpu.SemaphoreType.DMA((steps, peers)),
         ],
-        (arrived,) + (() if slope is None else (slope,)),
+        (arrived,) + tuple(ins),
         flops=2000000,
         moved=2000000,
     )
@@ -565,53 +548,40 @@
         return lax.dynamic_slice_in_dim(pair, which * half_len, half_len, 1)
 
     keep_own, keep_other, send_own, send_other = start_products(inputs, cotangent, own_up, own_down, blocks)
-    terms = (
-        keep_own,
-        only_to_mate(send_own, 0),
-        only_to_core(keep_other, 1),
-        only_across(send_other, 1),
-    )
-    x0, g2 = late((inputs, cotangent), keep_own)
+    terms = keep_own, to_mate(send_own), to_other_core(keep_other), to_other_core_of_mate(send_other)
+    own_down_late, own_up_late = late((own_down, own_up), keep_own)
+    other_down, other_up = only_to_core(own_down_late, 1), only_to_core(own_up_late, 0)
+    both = add_terms(late(terms, other_up))
+    own_down_late, x0, g2 = late((own_down, inputs, cotangent), both)
+    mate_down0 = only_to_mate(own_down_late, 0)
+    arrived = exchange(both.reshape((rings, 2) + piece), "z")
     ends = jnp.stack([batch(x0, section), batch(g2, section)])
-    ends_mate = to_mate(halves_of(ends, 1 - mate_pos))
-    pre0 = add_terms(0, terms)
-    arrived = exchange(pre0.reshape((rings, 1) + piece), "z")
-    own_down_late, own_up_late = late((own_down, own_up), (pre0, ends_mate))
-    mate_down0 = only_to_mate(own_down_late, 0)
-    other_down = only_to_core(own_down_late, 1)
-    other_up = only_to_core(own_up_late, 0)
-
-    value0, slope0 = activation(act_first, arrived, 1, slope_out=True)
-    hid0 = exchange(value0, "z").reshape(blocks[:2] + (1,) + piece)
-    ends, ends_mate = late((halves_of(ends, mate_pos), ends_mate), value0)
-    g2_both = jnp.concatenate([ends[1], ends_mate[1]], axis=1)
-    mate_down0 = late(mate_down0, g2_both)
+    bases = halves_of(ends, mate_pos), to_mate(halves_of(ends, 1 - mate_pos))
+    arrived = late(arrived, (bases, other_down))
+
+    value0, slope0, d_hid1 = activation(act_first, arrived, 1, outs=2)
+    mate_down0 = late(mate_down0, value0)
     down0 = own_down, other_down, mate_down0, only_to_core(mate_down0, 1)
     mate_up1 = only_to_mate(late(own_up, mate_down0), 1)
+    hid0 = exchange(value0, "z").reshape(blocks[:2] + (1,) + piece)
     part = narrow(0, True, hid0, down0, lax.axis_size(col))
+    mate_up1 = late(mate_up1, part)
+    up1 = own_up, other_up, mate_up1, only_to_core(mate_up1, 0)
     arrived = exchange(part, col)
 
-    ends, ends_mate = late((ends, ends_mate), part)
-    x0_both = jnp.concatenate([ends[0], ends_mate[0]], axis=1)
-    mate_up1 = late(mate_up1, x0_both)
-    up1 = own_up, other_up, mate_up1, only_to_core(mate_up1, 0)
-    keep_own, keep_other, send_own, send_other = late((keep_own, keep_other, send_own, send_other), mate_up1)
-    d_hid1 = add_terms(
-        1,
-        (keep_own, only_to_mate(send_own, 1), only_to_core(keep_other, 0), only_across(send_other, 0)),
-    )
-    pre1, x1 = widen(1, False, arrived, x0_both, up1, blocks, (d_hid1,))
+    pre1, x1 = widen(1, False, arrived, 0, bases, up1, blocks)
     hid0s = to_owner(late(hid0, pre1), 0)
-    arrived = late(exchange(pre1.reshape((rings, 2) + piece), "z"), hid0s)
-    (acts1,) = activation(act_last, arrived, 2)
+    arrived = late(exchange(pre1.reshape((rings, 1) + piece), "z"), hid0s)
+    (acts1,) = activation(act_last, arrived, 2, ins=(d_hid1,))
     acts1 = exchange(acts1, "z").reshape(blocks[:2] + (2,) + piece)
     part = narrow(1, False, acts1, up1, lax.axis_size(col))
     arrived = exchange(part, col)
 
-    d_hid0, g1 = widen(0, True, arrived, g2_both, down0, blocks)
-    acts1, both1 = late((acts1, jnp.stack([x1, g1])), d_hid0)
-    acts1s = to_owner(acts1, 1)
+    d_hid0, g1 = widen(0, True, arrived, 1, bases, down0, blocks)
+    acts1s = to_owner(late(acts1, d_hid0), 1)
     arrived = exchange(d_hid0.reshape((rings, 1) + piece), "z")
+    (d_pre0,) = activation(act_back, arrived, 1, ins=(slope0,))
+    both1 = late(jnp.stack([x1, g1]), d_pre0)
     near, far = both1[..., :width], both1[..., width:]
     both1 = jnp.stack([near, to_other_core(near), to_mate(far), to_other_core_of_mate(far)])
     both1 = both1.reshape((2, 2) + near.shape)
@@ -629,10 +599,9 @@
     xs = jnp.where(first, all_tokens(inputs), x1s)
     gs = jnp.where(first, g1s, all_tokens(cotangent))
 
-    (d_pre0,) = activation(act_back, arrived, 1, slope=slope0)
-    d_pre0 = late(exchange(d_pre0, "z").reshape(blocks[:2] + (1,) + piece), acts1s)
-    down_grad = weight_grad(True, late(gs, d_pre0), hid0s, acts1s)
-    d_pre0s = late(to_owner(d_pre0, 0), down_grad)
+    down_grad = weight_grad(True, gs, hid0s, acts1s)
+    d_pre0 = late(exchange(d_pre0, "z").reshape(blocks[:2] + (1,) + piece), down_grad)
+    d_pre0s = to_owner(d_pre0, 0)
 
     last = last_product(own_up, own_down, d_pre0s, acts1s)
     xs, d_pre0s = late((xs, d_pre0s), last)

time: 292 us -> 300 us (1.027)
  starting transfers between devices: 106 us -> 78.2 us
  blocking collectives: 49.9 us -> 74.8 us
  waiting for transfers between devices: 59.6 us -> 72.7 us
    all_to_all x2 -> x4, blocking collectives: 49.9 us -> 74.8 us  [exchange(): return lax.all_to_all(blocks, axes, 0, 0)]
    ppermute x2 -> x3, waiting for transfers between devices: 0.01 us -> 18.5 us  [to_mate(): return lax.ppermute(block, 'x_lo', [(0, 1), (1, 0)])]
    ppermute x9 -> x7, starting transfers between devices: 37.5 us -> 23.1 us  [only_to_core(): return lax.ppermute(block, 'section', [(1 - section, section)])]
    ppermute x5 -> x3, waiting for transfers between devices: 23.1 us -> 10.2 us  [only_across(): return lax.ppermute(block, CORES, [(source, at + 1), (source + 1, at)])]
    all_to_all x7 -> x5, starting transfers between devices: 36.4 us -> 24.9 us  [exchange(): return lax.all_to_all(blocks, axes, 0, 0)]
    ppermute x1 -> x2, waiting for transfers between devices: 0.01 us -> 11 us  [to_other_core_of_mate(): return lax.ppermute(block, CORES, [(0, 3), (3, 0), (1, 2), (2, 1)])]
    ppermute x7 -> x5, waiting for transfers between devices: 12.5 us -> 7.54 us  [only_to_mate(): return lax.ppermute(block, CORES, [(at, at + 1), (at + 1, at)])]
    ppermute x7 -> x5, starting transfers between devices: 15.2 us -> 10.9 us  [only_to_mate(): return lax.ppermute(block, CORES, [(at, at + 1), (at + 1, at)])]
  transfers between devices with their start and end apart: 32 -> 27, of which waited for: 13 -> 11; matrix products, arithmetic and copies ran while one was open for 5% -> 4% of each run, Pallas kernels for 9% -> 7%
where the time goes in v4:
time: 300 us; the launch traced here: 298 us
  starting transfers between devices  78.2 us (26%)
  blocking collectives  74.8 us (25%)
  waiting for transfers between devices  72.7 us (24%)
  Pallas kernels  57.8 us (19%)
  local copies, waits for them, and re-layouts  7.48 us (2%)
  other arithmetic  5.52 us (2%)
    all_to_all x4, blocking collectives, exchange(): return lax.all_to_all(blocks, axes, 0, 0)  74.8 us
    pallas_call x11, Pallas kernels, kernel_call(): pl.pallas_call(body, out_shape=outs, in_specs=in_specs, out_specs=out_spe...  45.4 us
    all_to_all x5, waiting for transfers between devices, exchange(): return lax.all_to_all(blocks, axes, 0, 0)  25.5 us
    all_to_all x5, starting transfers between devices, exchange(): return lax.all_to_all(blocks, axes, 0, 0)  24.9 us
    ppermute x7, starting transfers between devices, only_to_core(): return lax.ppermute(block, 'section', [(1 - section, section)])  23.1 us
    ppermute x3, waiting for transfers between devices, to_mate(): return lax.ppermute(block, 'x_lo', [(0, 1), (1, 0)])  18.5 us
    pallas_call x2, Pallas kernels, weight_grad(): pl.pallas_call(grad_down_kernel if down else grad_up_kernel, out_shape=sh...  12.4 us
    ppermute x2, waiting for transfers between devices, to_other_core_of_mate(): return lax.ppermute(block, CORES, [(0, 3), (3, 0), (1, 2), (2, 1)])  11 us
  transfers between devices with their start and end apart: 27, of which 11 were waited for; matrix products, arithmetic and copies ran while one was open for 4% of the time, Pallas kernels for 7%

profile of v4, /device:TPU:1, one launch (start us, length us, event | category | flops | bytes accessed | tf_op | source)
XLA Modules:
  0.0 297.5 jit_solution(3782460720207215587)
XLA Ops:
  0.6 5.1 %shard_map.75 = (bf16[4,2,16,1536]{3,2,1,0:T(8,128)(2,1)}, bf16[4,2,16,1536]{3,2,1,0:T(8,128)(2,1)}, bf16[4,2,16,1536]{3,2,1,0:T(8,128)(2,1)}, bf16[4,2,16,1536]{3,2,1,0:T(8,128)(2,1)}) custom-call(bf16[2,128,384]{2,1,0:T(8,128)(2,1)} %x_ref.1, bf16[2,128,384]{2,1,0:T(8,128)(2,1)} %g_ref.1, bf16[384,3072]{1,0:T(8,128)(2,1)} %bitcast.50, ...), custom_call_target="tpu_custom_call" | custom-call | flops 603979776 | bytes 4718592 | tf_op jit(solution)/shard_map/pallas_call | solution.py:220
  5.7 6.4 %collective-permute-start.3 = (bf16[384,3072]{1,0:T(8,128)(2,1)}, bf16[384,3072]{1,0:T(8,128)(2,1)}, u32[]{:S(2)}, u32[]{:S(2)}) collective-permute-start(bf16[384,3072]{1,0:T(8,128)(2,1)} %bitcast.51), channel_id=1, source_target_pairs={{128,0},{129,1},{130,2},{131,3},{132,4},{133,5},{134,6},{135,7},{1... | collective-permute-start | bytes 7077896 | tf_op jit(solution)/shard_map/ppermute | solution.py:514
  12.1 1.9 collective-permute-start.2
  15.3 8.1 %collective-permute-done.mates = bf16[4,2,16,1536]{3,2,1,0:T(8,128)(2,1)} collective-permute-done((bf16[4,2,16,1536]{3,2,1,0:T(8,128)(2,1)}, bf16[4,2,16,1536]{3,2,1,0:T(8,128)(2,1)}, u32[]{:S(2)}, u32[]{:S(2)}) %collective-permute-start) | collective-permute-done | bytes 393248 | tf_op jit(solution)/shard_map/ppermute | solution.py:501
  23.3 5.6 %collective-permute-done.2.across = bf16[4,2,16,1536]{3,2,1,0:T(8,128)(2,1)} collective-permute-done((bf16[4,2,16,1536]{3,2,1,0:T(8,128)(2,1)}, bf16[4,2,16,1536]{3,2,1,0:T(8,128)(2,1)}, u32[]{:S(2)}, u32[]{:S(2)}) %collective-permute-start.2) | collective-permute-done | bytes 393248 | tf_op jit(solution)/shard_map/ppermute | solution.py:505
  28.9 2.2 shard_map.76
  31.2 2.1 collective-permute-start.6
  33.3 7.0 %all-to-all-start = ((bf16[8,2,16,1536]{3,2,1,0:T(8,128)(2,1)}), bf16[8,2,16,1536]{3,2,1,0:T(8,128)(2,1)}, u32[]{:S(2)}, u32[]{:S(2)}) async-start(bf16[8,2,16,1536]{3,2,1,0:T(8,128)(2,1)} %bitcast.76), calls=%async_computation | async-start | bytes 1572864 | tf_op jit(solution)/shard_map/all_to_all | solution.py:490
  42.6 4.3 %collective-permute-done.4.base_mate = bf16[2,64,384]{2,1,0:T(8,128)(2,1)} collective-permute-done((bf16[2,64,384]{2,1,0:T(8,128)(2,1)S(1)}, bf16[2,64,384]{2,1,0:T(8,128)(2,1)}, u32[]{:S(2)}, u32[]{:S(2)}) %collective-permute-start.4) | collective-permute-done | bytes 98336 | tf_op jit(solution)/shard_map/ppermute | solution.py:501
  46.9 14.2 %all-to-all-done.arrived_ref = bf16[8,2,16,1536]{3,2,1,0:T(8,128)(2,1)} async-done(((bf16[8,2,16,1536]{3,2,1,0:T(8,128)(2,1)}), bf16[8,2,16,1536]{3,2,1,0:T(8,128)(2,1)}, u32[]{:S(2)}, u32[]{:S(2)}) %all-to-all-start) | async-done | bytes 786464 | tf_op jit(solution)/shard_map/all_to_all | solution.py:490
  61.1 2.7 shard_map.77
  65.1 2.9 collective-permute-start.8
  68.1 14.8 %all_to_all.45 = bf16[8,1,16,1536]{3,2,1,0:T(8,128)(2,1)} all-to-all(bf16[8,1,16,1536]{3,2,1,0:T(8,128)(2,1)} %get-tuple-element.53), channel_id=1, replica_groups=mesh['section'=2,'z'=8,'x_lo'=2,'y'=4,'x_hi'=2] {'z'}, dimensions={0} | all-to-all | bytes 786432 | tf_op jit(solution)/shard_map/all_to_all | solution.py:490
  82.9 4.6 %shard_map.78 = bf16[8,64,768]{2,1,0:T(8,128)(2,1)} custom-call(bf16[4,2,1,16,1536]{4,3,2,1,0:T(8,128)(2,1)} %bitcast.71, bf16[3072,384]{1,0:T(8,128)(2,1)} %bitcast.59, bf16[3072,384]{1,0:T(8,128)(2,1)} %collective-permute-done.5.other, bf16[3072,384]{1,0:T(8,128)(2,1)} %collective-permute-done.6.own_mate, bf16[3072,384]{1,0:T(8,128)(2,1)} %collective-permute-done.7.other_mate), custom_call_target="tpu_custom_call" | custom-call | flops 301989888 | bytes 4718592 | tf_op jit(solution)/shard_map/pallas_call | solution.py:220
  87.5 7.5 %collective-permute-done.8.own_mate = bf16[384,3072]{1,0:T(8,128)(2,1)} collective-permute-done((bf16[384,3072]{1,0:T(8,128)(2,1)}, bf16[384,3072]{1,0:T(8,128)(2,1)}, u32[]{:S(2)}, u32[]{:S(2)}) %collective-permute-start.8) | collective-permute-done | bytes 2359328 | tf_op jit(solution)/shard_map/ppermute | solution.py:510
  95.0 8.4 %collective-permute-start.9 = (bf16[384,3072]{1,0:T(8,128)(2,1)}, bf16[384,3072]{1,0:T(8,128)(2,1)}, u32[]{:S(2)}, u32[]{:S(2)}) collective-permute-start(bf16[384,3072]{1,0:T(8,128)(2,1)} %collective-permute-done.8.own_mate), channel_id=1, source_target_pairs={{128,0},{129,1},{130,2},{131,3},{132,4},{133,5},{134,6},{135,7},{1... | collective-permute-start | bytes 7077896 | tf_op jit(solution)/shard_map/ppermute | solution.py:514
  103.5 20.4 %all_to_all.46.arrived_ref = bf16[8,64,768]{2,1,0:T(8,128)(2,1)} all-to-all(bf16[8,64,768]{2,1,0:T(8,128)(2,1)} %shard_map.78), channel_id=1, replica_groups=mesh['section'=2,'z'=8,'x_lo'=2,'y'=4,'x_hi'=2] {'y','x_hi'}, dimensions={0} | all-to-all | bytes 1572864 | tf_op jit(solution)/shard_map/all_to_all | solution.py:490
  123.9 6.6 %shard_map.79 = (bf16[4,2,16,1536]{3,2,1,0:T(8,128)(2,1)}, bf16[64,768]{1,0:T(8,128)(2,1)}) custom-call(bf16[8,64,768]{2,1,0:T(8,128)(2,1)} %all_to_all.46.arrived_ref, bf16[2,64,384]{2,1,0:T(8,128)(2,1)} %get-tuple-element.90.base, bf16[2,64,384]{2,1,0:T(8,128)(2,1)} %collective-permute-done.4.base_mate, bf16[384,3072]{1,0:T(8,128)(2,1)} %bitcast.53, ...), custom_call_target="tpu_custom_call" | custom-call | flops 301989888 | bytes 4718592 | tf_op jit(solution)/shard_map/pallas_call | solution.py:220
  130.6 4.1 %all-to-all-start.3 = ((bf16[8,1,16,1536]{3,2,1,0:T(8,128)(2,1)}), bf16[8,1,16,1536]{3,2,1,0:T(8,128)(2,1)}, u32[]{:S(2)}, u32[]{:S(2)}) async-start(bf16[8,1,16,1536]{3,2,1,0:T(8,128)(2,1)} %bitcast.79), calls=%async_computation.3 | async-start | bytes 786432 | tf_op jit(solution)/shard_map/all_to_all | solution.py:490
  134.7 2.1 collective-permute-start.10
  138.2 3.3 %collective-permute-start.12 = (bf16[4,2,1,16,1536]{4,3,2,1,0:T(8,128)(2,1)}, bf16[4,2,1,16,1536]{4,3,2,1,0:T(8,128)(2,1)}, u32[]{:S(2)}, u32[]{:S(2)}) collective-permute-start(bf16[4,2,1,16,1536]{4,3,2,1,0:T(8,128)(2,1)} %bitcast.74), channel_id=1, source_target_pairs={{128,8},{136,0},{129,9},{137,1},{130,10},{138,2},{131,11},{139,3},... | collective-permute-start | bytes 1179656 | tf_op jit(solution)/shard_map/ppermute | solution.py:519
  141.5 6.0 %collective-permute-done.12.refs_3_ = bf16[4,2,1,16,1536]{4,3,2,1,0:T(8,128)(2,1)} collective-permute-done((bf16[4,2,1,16,1536]{4,3,2,1,0:T(8,128)(2,1)}, bf16[4,2,1,16,1536]{4,3,2,1,0:T(8,128)(2,1)}, u32[]{:S(2)}, u32[]{:S(2)}) %collective-permute-start.12) | collective-permute-done | bytes 393248 | tf_op jit(solution)/shard_map/ppermute | solution.py:519
  147.5 2.1 all-to-all-done.3.arrived_ref
  149.6 2.9 shard_map.80
  152.6 24.9 %all_to_all.47 = bf16[8,2,16,1536]{3,2,1,0:T(8,128)(2,1)} all-to-all(bf16[8,2,16,1536]{3,2,1,0:T(8,128)(2,1)} %shard_map.80), channel_id=1, replica_groups=mesh['section'=2,'z'=8,'x_lo'=2,'y'=4,'x_hi'=2] {'z'}, dimensions={0} | all-to-all | bytes 1572864 | tf_op jit(solution)/shard_map/all_to_all | solution.py:490
  177.4 5.6 %shard_map.81 = bf16[8,64,768]{2,1,0:T(8,128)(2,1)} custom-call(bf16[4,2,2,16,1536]{4,3,2,1,0:T(8,128)(2,1)} %bitcast.62, bf16[384,3072]{1,0:T(8,128)(2,1)} %bitcast.54, bf16[384,3072]{1,0:T(8,128)(2,1)} %collective-permute-done.3.other, bf16[384,3072]{1,0:T(8,128)(2,1)} %collective-permute-done.8.own_mate, bf16[384,3072]{1,0:T(8,128)(2,1)} %collective-permute-done.9.other_mate), custom_call_target="tpu_custom_call" | custom-call | flops 301989888 | bytes 4718592 | tf_op jit(solution)/shard_map/pallas_call | solution.py:220
  183.1 14.7 %all_to_all.48.arrived_ref = bf16[8,64,768]{2,1,0:T(8,128)(2,1)} all-to-all(bf16[8,64,768]{2,1,0:T(8,128)(2,1)} %shard_map.81), channel_id=1, replica_groups=mesh['section'=2,'z'=8,'x_lo'=2,'y'=4,'x_hi'=2] {'y','x_hi'}, dimensions={0} | all-to-all | bytes 1572864 | tf_op jit(solution)/shard_map/all_to_all | solution.py:490
  197.8 7.1 %shard_map.82 = (bf16[4,2,16,1536]{3,2,1,0:T(8,128)(2,1)}, bf16[64,768]{1,0:T(8,128)(2,1)}) custom-call(bf16[8,64,768]{2,1,0:T(8,128)(2,1)} %all_to_all.48.arrived_ref, bf16[2,64,384]{2,1,0:T(8,128)(2,1)} %get-tuple-element.90.base, bf16[2,64,384]{2,1,0:T(8,128)(2,1)} %collective-permute-done.4.base_mate, bf16[3072,384]{1,0:T(8,128)(2,1)} %bitcast.60, ...), custom_call_target="tpu_custom_call" | custom-call | flops 301989888 | bytes 4718592 | tf_op jit(solution)/shard_map/pallas_call | solution.py:220
  204.9 5.6 %all-to-all-start.6 = ((bf16[8,1,16,1536]{3,2,1,0:T(8,128)(2,1)}), bf16[8,1,16,1536]{3,2,1,0:T(8,128)(2,1)}, u32[]{:S(2)}, u32[]{:S(2)}) async-start(bf16[8,1,16,1536]{3,2,1,0:T(8,128)(2,1)} %bitcast.80), calls=%async_computation.6 | async-start | bytes 786432 | tf_op jit(solution)/shard_map/all_to_all | solution.py:490
  210.5 1.6 pad_maximum_fusion.1
  212.2 9.1 %all-to-all-done.6.arrived_ref = bf16[8,1,16,1536]{3,2,1,0:T(8,128)(2,1)} async-done(((bf16[8,1,16,1536]{3,2,1,0:T(8,128)(2,1)}), bf16[8,1,16,1536]{3,2,1,0:T(8,128)(2,1)}, u32[]{:S(2)}, u32[]{:S(2)}) %all-to-all-start.6) | async-done | bytes 393248 | tf_op jit(solution)/shard_map/all_to_all | solution.py:490
  221.3 2.8 shard_map.83
  225.1 5.1 %collective-permute-start.13 = (bf16[2,64,384]{2,1,0:T(8,128)(2,1)S(1)}, bf16[2,64,384]{2,1,0:T(8,128)(2,1)S(1)}, u32[]{:S(2)}, u32[]{:S(2)}) collective-permute-start(bf16[2,64,384]{2,1,0:T(8,128)(2,1)S(1)} %get-tuple-element.84), channel_id=1, source_target_pairs={{0,128},{128,0},{1,129},{129,1},{2,130},{130,2},{3,131},{131,3},{4... | collective-permute-start | bytes 294920 | tf_op jit(solution)/shard_map/ppermute | solution.py:497
  231.5 3.1 %collective-permute-start.17 = (bf16[4,2,2,16,1536]{4,3,2,1,0:T(8,128)(2,1)}, bf16[4,2,2,16,1536]{4,3,2,1,0:T(8,128)(2,1)}, u32[]{:S(2)}, u32[]{:S(2)}) collective-permute-start(bf16[4,2,2,16,1536]{4,3,2,1,0:T(8,128)(2,1)} %bitcast.64), channel_id=1, source_target_pairs={{128,136},{136,128},{129,137},{137,129},{130,138},{138,130},{131,1... | collective-permute-start | bytes 2359304 | tf_op jit(solution)/shard_map/ppermute | solution.py:510
  236.5 3.2 %collective-permute-start.15 = (bf16[2,64,384]{2,1,0:T(8,128)(2,1)S(1)}, bf16[2,64,384]{2,1,0:T(8,128)(2,1)S(1)}, u32[]{:S(2)}, u32[]{:S(2)}) collective-permute-start(bf16[2,64,384]{2,1,0:T(8,128)(2,1)S(1)} %get-tuple-element.83), channel_id=1, source_target_pairs={{0,136},{136,0},{8,128},{128,8},{1,137},{137,1},{9,129},{129,9},{2... | collective-permute-start | bytes 294920 | tf_op jit(solution)/shard_map/ppermute | solution.py:505
  239.7 1.8 dynamic-slice_bitcast_fusion.3
  241.4 4.1 %all-to-all-start.7 = ((bf16[8,1,16,1536]{3,2,1,0:T(8,128)(2,1)}), bf16[8,1,16,1536]{3,2,1,0:T(8,128)(2,1)}, u32[]{:S(2)}, u32[]{:S(2)}) async-start(bf16[8,1,16,1536]{3,2,1,0:T(8,128)(2,1)} %shard_map.83), calls=%async_computation.7 | async-start | bytes 786432 | tf_op jit(solution)/shard_map/all_to_all | solution.py:490
  245.5 6.1 %collective-permute-done.14 = bf16[2,64,384]{2,1,0:T(8,128)(2,1)S(1)} collective-permute-done((bf16[2,64,384]{2,1,0:T(8,128)(2,1)S(1)}, bf16[2,64,384]{2,1,0:T(8,128)(2,1)S(1)}, u32[]{:S(2)}, u32[]{:S(2)}) %collective-permute-start.14) | collective-permute-done | bytes 98336 | tf_op jit(solution)/shard_map/ppermute | solution.py:501
  251.6 5.5 %collective-permute-done.15 = bf16[2,64,384]{2,1,0:T(8,128)(2,1)S(1)} collective-permute-done((bf16[2,64,384]{2,1,0:T(8,128)(2,1)S(1)}, bf16[2,64,384]{2,1,0:T(8,128)(2,1)S(1)}, u32[]{:S(2)}, u32[]{:S(2)}) %collective-permute-start.15) | collective-permute-done | bytes 98336 | tf_op jit(solution)/shard_map/ppermute | solution.py:505
  259.4 6.4 %shard_map.84 = f32[3072,384]{1,0:T(8,128)} custom-call(bf16[256,384]{1,0:T(8,128)(2,1)} %maximum_select_fusion.g_ref, bf16[4,2,1,16,1536]{4,3,2,1,0:T(8,128)(2,1)} %bitcast.75, bf16[4,2,1,16,1536]{4,3,2,1,0:T(8,128)(2,1)} %collective-permute-done.10.refs_1_, bf16[4,2,1,16,1536]{4,3,2,1,0:T(8,128)(2,1)} %collective-permute-done.11.refs_2_, ...), custom_call_target="tpu_custom_call" | custom-call | flops 603979776 | bytes 4718592 | tf_op jit(solution)/shard_map/pallas_call | solution.py:412
  266.7 2.4 collective-permute-start.19
  270.5 3.4 %collective-permute-start.21 = (bf16[4,2,1,16,1536]{4,3,2,1,0:T(8,128)(2,1)}, bf16[4,2,1,16,1536]{4,3,2,1,0:T(8,128)(2,1)}, u32[]{:S(2)}, u32[]{:S(2)}) collective-permute-start(bf16[4,2,1,16,1536]{4,3,2,1,0:T(8,128)(2,1)} %bitcast.7.refs_0_), channel_id=1, source_target_pairs={{128,8},{136,0},{129,9},{137,1},{130,10},{138,2},{131,11},{139,3},... | collective-permute-start | bytes 1179656 | tf_op jit(solution)/shard_map/ppermute | solution.py:519
  274.5 1.8 maximum_select_fusion.1.x_ref
  276.3 4.1 %collective-permute-done.21.refs_3_ = bf16[4,2,1,16,1536]{4,3,2,1,0:T(8,128)(2,1)} collective-permute-done((bf16[4,2,1,16,1536]{4,3,2,1,0:T(8,128)(2,1)}, bf16[4,2,1,16,1536]{4,3,2,1,0:T(8,128)(2,1)}, u32[]{:S(2)}, u32[]{:S(2)}) %collective-permute-start.21) | collective-permute-done | bytes 393248 | tf_op jit(solution)/shard_map/ppermute | solution.py:519
  280.4 4.0 %shard_map.85 = bf16[8,2,16,384]{3,2,1,0:T(8,128)(2,1)} custom-call(bf16[384,3072]{1,0:T(8,128)(2,1)} %bitcast.55, bf16[3072,384]{1,0:T(8,128)(2,1)} %bitcast.61, bf16[4,2,1,16,1536]{4,3,2,1,0:T(8,128)(2,1)} %bitcast.7.refs_0_, bf16[4,2,1,16,1536]{4,3,2,1,0:T(8,128)(2,1)} %collective-permute-done.19.refs_1_, ...), custom_call_target="tpu_custom_call" | custom-call | flops 603979776 | bytes 7077888 | tf_op jit(solution)/shard_map/pallas_call | solution.py:220
  284.4 4.0 %all-to-all-start.8 = ((bf16[8,2,16,384]{3,2,1,0:T(8,128)(2,1)}), bf16[8,2,16,384]{3,2,1,0:T(8,128)(2,1)}, u32[]{:S(2)}, u32[]{:S(2)}) async-start(bf16[8,2,16,384]{3,2,1,0:T(8,128)(2,1)} %shard_map.85), calls=%async_computation.8 | async-start | bytes 393216 | tf_op jit(solution)/shard_map/all_to_all | solution.py:490
  289.9 6.0 %shard_map.87 = f32[384,3072]{1,0:T(8,128)} custom-call(bf16[256,384]{1,0:T(8,128)(2,1)} %maximum_select_fusion.1.x_ref, bf16[4,2,1,16,1536]{4,3,2,1,0:T(8,128)(2,1)} %bitcast.7.refs_0_, bf16[4,2,1,16,1536]{4,3,2,1,0:T(8,128)(2,1)} %collective-permute-done.19.refs_1_, bf16[4,2,1,16,1536]{4,3,2,1,0:T(8,128)(2,1)} %collective-permute-done.20.refs_2_, ...), custom_call_target="tpu_custom_call" | custom-call | flops 603979776 | bytes 4718592 | tf_op jit(solution)/shard_map/pallas_call | solution.py:412
  295.9 1.6 shard_map.86
  (37 shorter events, 17.0 us)
Async XLA Ops:
  5.7 23.2 %collective-permute-start.3 = (bf16[384,3072]{1,0:T(8,128)(2,1)}, bf16[384,3072]{1,0:T(8,128)(2,1)}, u32[]{:S(2)}, u32[]{:S(2)}) collective-permute-start(bf16[384,3072]{1,0:T(8,128)(2,1)} %bitcast.51), channel_id=1, source_target_pairs={{128,0},{129,1},{130,2},{131,3},{132,4},{133,5},{134,6},{135,7},{1... | collective-permute-start | bytes 7077896 | tf_op jit(solution)/shard_map/ppermute | solution.py:514
  12.1 11.2 %collective-permute-start = (bf16[4,2,16,1536]{3,2,1,0:T(8,128)(2,1)}, bf16[4,2,16,1536]{3,2,1,0:T(8,128)(2,1)}, u32[]{:S(2)}, u32[]{:S(2)}) collective-permute-start(bf16[4,2,16,1536]{3,2,1,0:T(8,128)(2,1)} %get-tuple-element.41), channel_id=1, source_target_pairs={{0,8},{8,0},{1,9},{9,1},{2,10},{10,2},{3,11},{11,3},{4,12},{12,4},... | collective-permute-start | bytes 1179656 | tf_op jit(solution)/shard_map/ppermute | solution.py:501
  12.1 11.2 %collective-permute-start.1 = (bf16[4,2,16,1536]{3,2,1,0:T(8,128)(2,1)}, bf16[4,2,16,1536]{3,2,1,0:T(8,128)(2,1)}, u32[]{:S(2)}, u32[]{:S(2)}) collective-permute-start(bf16[4,2,16,1536]{3,2,1,0:T(8,128)(2,1)} %get-tuple-element.42), channel_id=1, source_target_pairs={{0,128},{128,0},{1,129},{129,1},{2,130},{130,2},{3,131},{131,3},{4... | collective-permute-start | bytes 1179656 | tf_op jit(solution)/shard_map/ppermute | solution.py:497
  12.1 16.8 %collective-permute-start.2 = (bf16[4,2,16,1536]{3,2,1,0:T(8,128)(2,1)}, bf16[4,2,16,1536]{3,2,1,0:T(8,128)(2,1)}, u32[]{:S(2)}, u32[]{:S(2)}) collective-permute-start(bf16[4,2,16,1536]{3,2,1,0:T(8,128)(2,1)} %get-tuple-element.43), channel_id=1, source_target_pairs={{0,136},{136,0},{8,128},{128,8},{1,137},{137,1},{9,129},{129,9},{2... | collective-permute-start | bytes 1179656 | tf_op jit(solution)/shard_map/ppermute | solution.py:505
  14.0 28.6 %collective-permute-start.5 = (bf16[3072,384]{1,0:T(8,128)(2,1)}, bf16[3072,384]{1,0:T(8,128)(2,1)}, u32[]{:S(2)}, u32[]{:S(2)}) collective-permute-start(bf16[3072,384]{1,0:T(8,128)(2,1)} %bitcast.57), channel_id=1, source_target_pairs={{0,128},{1,129},{2,130},{3,131},{4,132},{5,133},{6,134},{7,135},{8... | collective-permute-start | bytes 7077896 | tf_op jit(solution)/shard_map/ppermute | solution.py:514
  31.2 32.7 %collective-permute-start.6 = (bf16[3072,384]{1,0:T(8,128)(2,1)}, bf16[3072,384]{1,0:T(8,128)(2,1)}, u32[]{:S(2)}, u32[]{:S(2)}) collective-permute-start(bf16[3072,384]{1,0:T(8,128)(2,1)} %bitcast.58), channel_id=1, source_target_pairs={{0,8},{8,0},{1,9},{9,1},{2,10},{10,2},{3,11},{11,3},{4,12},{12,4},... | collective-permute-start | bytes 7077896 | tf_op jit(solution)/shard_map/ppermute | solution.py:510
  33.3 27.9 %all-to-all-start = ((bf16[8,2,16,1536]{3,2,1,0:T(8,128)(2,1)}), bf16[8,2,16,1536]{3,2,1,0:T(8,128)(2,1)}, u32[]{:S(2)}, u32[]{:S(2)}) async-start(bf16[8,2,16,1536]{3,2,1,0:T(8,128)(2,1)} %bitcast.76), calls=%async_computation | async-start | bytes 1572864 | tf_op jit(solution)/shard_map/all_to_all | solution.py:490
  41.9 5.0 %collective-permute-start.4 = (bf16[2,64,384]{2,1,0:T(8,128)(2,1)S(1)}, bf16[2,64,384]{2,1,0:T(8,128)(2,1)}, u32[]{:S(2)}, u32[]{:S(2)}) collective-permute-start(bf16[2,64,384]{2,1,0:T(8,128)(2,1)S(1)} %get-tuple-element.89), channel_id=1, source_target_pairs={{0,8},{8,0},{1,9},{9,1},{2,10},{10,2},{3,11},{11,3},{4,12},{12,4},... | collective-permute-start | bytes 294920 | tf_op jit(solution)/shard_map/ppermute | solution.py:501
  63.8 19.1 %collective-permute-start.7 = (bf16[3072,384]{1,0:T(8,128)(2,1)}, bf16[3072,384]{1,0:T(8,128)(2,1)}, u32[]{:S(2)}, u32[]{:S(2)}) collective-permute-start(bf16[3072,384]{1,0:T(8,128)(2,1)} %collective-permute-done.6.own_mate), channel_id=1, source_target_pairs={{0,128},{1,129},{2,130},{3,131},{4,132},{5,133},{6,134},{7,135},{8... | collective-permute-start | bytes 7077896 | tf_op jit(solution)/shard_map/ppermute | solution.py:514
  65.1 29.9 %collective-permute-start.8 = (bf16[384,3072]{1,0:T(8,128)(2,1)}, bf16[384,3072]{1,0:T(8,128)(2,1)}, u32[]{:S(2)}, u32[]{:S(2)}) collective-permute-start(bf16[384,3072]{1,0:T(8,128)(2,1)} %bitcast.52), channel_id=1, source_target_pairs={{128,136},{136,128},{129,137},{137,129},{130,138},{138,130},{131,1... | collective-permute-start | bytes 7077896 | tf_op jit(solution)/shard_map/ppermute | solution.py:510
  95.0 28.9 %collective-permute-start.9 = (bf16[384,3072]{1,0:T(8,128)(2,1)}, bf16[384,3072]{1,0:T(8,128)(2,1)}, u32[]{:S(2)}, u32[]{:S(2)}) collective-permute-start(bf16[384,3072]{1,0:T(8,128)(2,1)} %collective-permute-done.8.own_mate), channel_id=1, source_target_pairs={{128,0},{129,1},{130,2},{131,3},{132,4},{133,5},{134,6},{135,7},{1... | collective-permute-start | bytes 7077896 | tf_op jit(solution)/shard_map/ppermute | solution.py:514
  130.6 19.0 %all-to-all-start.3 = ((bf16[8,1,16,1536]{3,2,1,0:T(8,128)(2,1)}), bf16[8,1,16,1536]{3,2,1,0:T(8,128)(2,1)}, u32[]{:S(2)}, u32[]{:S(2)}) async-start(bf16[8,1,16,1536]{3,2,1,0:T(8,128)(2,1)} %bitcast.79), calls=%async_computation.3 | async-start | bytes 786432 | tf_op jit(solution)/shard_map/all_to_all | solution.py:490
  134.7 6.8 %collective-permute-start.10 = (bf16[4,2,1,16,1536]{4,3,2,1,0:T(8,128)(2,1)}, bf16[4,2,1,16,1536]{4,3,2,1,0:T(8,128)(2,1)}, u32[]{:S(2)}, u32[]{:S(2)}) collective-permute-start(bf16[4,2,1,16,1536]{4,3,2,1,0:T(8,128)(2,1)} %bitcast.72), channel_id=1, source_target_pairs={{128,0},{129,1},{130,2},{131,3},{132,4},{133,5},{134,6},{135,7},{1... | collective-permute-start | bytes 1179656 | tf_op jit(solution)/shard_map/ppermute | solution.py:514
  136.8 4.7 %collective-permute-start.11 = (bf16[4,2,1,16,1536]{4,3,2,1,0:T(8,128)(2,1)}, bf16[4,2,1,16,1536]{4,3,2,1,0:T(8,128)(2,1)}, u32[]{:S(2)}, u32[]{:S(2)}) collective-permute-start(bf16[4,2,1,16,1536]{4,3,2,1,0:T(8,128)(2,1)} %bitcast.73), channel_id=1, source_target_pairs={{0,8},{8,0},{1,9},{9,1},{2,10},{10,2},{3,11},{11,3},{4,12},{12,4},... | collective-permute-start | bytes 1179656 | tf_op jit(solution)/shard_map/ppermute | solution.py:510
  138.2 9.3 %collective-permute-start.12 = (bf16[4,2,1,16,1536]{4,3,2,1,0:T(8,128)(2,1)}, bf16[4,2,1,16,1536]{4,3,2,1,0:T(8,128)(2,1)}, u32[]{:S(2)}, u32[]{:S(2)}) collective-permute-start(bf16[4,2,1,16,1536]{4,3,2,1,0:T(8,128)(2,1)} %bitcast.74), channel_id=1, source_target_pairs={{128,8},{136,0},{129,9},{137,1},{130,10},{138,2},{131,11},{139,3},... | collective-permute-start | bytes 1179656 | tf_op jit(solution)/shard_map/ppermute | solution.py:519
  204.9 16.4 %all-to-all-start.6 = ((bf16[8,1,16,1536]{3,2,1,0:T(8,128)(2,1)}), bf16[8,1,16,1536]{3,2,1,0:T(8,128)(2,1)}, u32[]{:S(2)}, u32[]{:S(2)}) async-start(bf16[8,1,16,1536]{3,2,1,0:T(8,128)(2,1)} %bitcast.80), calls=%async_computation.6 | async-start | bytes 786432 | tf_op jit(solution)/shard_map/all_to_all | solution.py:490
  225.1 11.4 %collective-permute-start.13 = (bf16[2,64,384]{2,1,0:T(8,128)(2,1)S(1)}, bf16[2,64,384]{2,1,0:T(8,128)(2,1)S(1)}, u32[]{:S(2)}, u32[]{:S(2)}) collective-permute-start(bf16[2,64,384]{2,1,0:T(8,128)(2,1)S(1)} %get-tuple-element.84), channel_id=1, source_target_pairs={{0,128},{128,0},{1,129},{129,1},{2,130},{130,2},{3,131},{131,3},{4... | collective-permute-start | bytes 294920 | tf_op jit(solution)/shard_map/ppermute | solution.py:497
  230.2 29.2 %collective-permute-start.16 = (bf16[4,2,2,16,1536]{4,3,2,1,0:T(8,128)(2,1)}, bf16[4,2,2,16,1536]{4,3,2,1,0:T(8,128)(2,1)}, u32[]{:S(2)}, u32[]{:S(2)}) collective-permute-start(bf16[4,2,2,16,1536]{4,3,2,1,0:T(8,128)(2,1)} %bitcast.63), channel_id=1, source_target_pairs={{0,128},{1,129},{2,130},{3,131},{4,132},{5,133},{6,134},{7,135},{8... | collective-permute-start | bytes 2359304 | tf_op jit(solution)/shard_map/ppermute | solution.py:514
  231.5 27.9 %collective-permute-start.17 = (bf16[4,2,2,16,1536]{4,3,2,1,0:T(8,128)(2,1)}, bf16[4,2,2,16,1536]{4,3,2,1,0:T(8,128)(2,1)}, u32[]{:S(2)}, u32[]{:S(2)}) collective-permute-start(bf16[4,2,2,16,1536]{4,3,2,1,0:T(8,128)(2,1)} %bitcast.64), channel_id=1, source_target_pairs={{128,136},{136,128},{129,137},{137,129},{130,138},{138,130},{131,1... | collective-permute-start | bytes 2359304 | tf_op jit(solution)/shard_map/ppermute | solution.py:510
  234.6 24.8 %collective-permute-start.18 = (bf16[4,2,2,16,1536]{4,3,2,1,0:T(8,128)(2,1)}, bf16[4,2,2,16,1536]{4,3,2,1,0:T(8,128)(2,1)}, u32[]{:S(2)}, u32[]{:S(2)}) collective-permute-start(bf16[4,2,2,16,1536]{4,3,2,1,0:T(8,128)(2,1)} %bitcast.65), channel_id=1, source_target_pairs={{0,136},{8,128},{1,137},{9,129},{2,138},{10,130},{3,139},{11,131},... | collective-permute-start | bytes 2359304 | tf_op jit(solution)/shard_map/ppermute | solution.py:519
  235.9 15.7 %collective-permute-start.14 = (bf16[2,64,384]{2,1,0:T(8,128)(2,1)S(1)}, bf16[2,64,384]{2,1,0:T(8,128)(2,1)S(1)}, u32[]{:S(2)}, u32[]{:S(2)}) collective-permute-start(bf16[2,64,384]{2,1,0:T(8,128)(2,1)S(1)} %get-tuple-element.83), channel_id=1, source_target_pairs={{0,8},{8,0},{1,9},{9,1},{2,10},{10,2},{3,11},{11,3},{4,12},{12,4},... | collective-permute-start | bytes 294920 | tf_op jit(solution)/shard_map/ppermute | solution.py:501
  236.5 20.6 %collective-permute-start.15 = (bf16[2,64,384]{2,1,0:T(8,128)(2,1)S(1)}, bf16[2,64,384]{2,1,0:T(8,128)(2,1)S(1)}, u32[]{:S(2)}, u32[]{:S(2)}) collective-permute-start(bf16[2,64,384]{2,1,0:T(8,128)(2,1)S(1)} %get-tuple-element.83), channel_id=1, source_target_pairs={{0,136},{136,0},{8,128},{128,8},{1,137},{137,1},{9,129},{129,9},{2... | collective-permute-start | bytes 294920 | tf_op jit(solution)/shard_map/ppermute | solution.py:505
  241.4 25.2 %all-to-all-start.7 = ((bf16[8,1,16,1536]{3,2,1,0:T(8,128)(2,1)}), bf16[8,1,16,1536]{3,2,1,0:T(8,128)(2,1)}, u32[]{:S(2)}, u32[]{:S(2)}) async-start(bf16[8,1,16,1536]{3,2,1,0:T(8,128)(2,1)} %shard_map.83), calls=%async_computation.7 | async-start | bytes 786432 | tf_op jit(solution)/shard_map/all_to_all | solution.py:490
  257.1 0.8 copy-start
  266.7 9.6 %collective-permute-start.19 = (bf16[4,2,1,16,1536]{4,3,2,1,0:T(8,128)(2,1)}, bf16[4,2,1,16,1536]{4,3,2,1,0:T(8,128)(2,1)}, u32[]{:S(2)}, u32[]{:S(2)}) collective-permute-start(bf16[4,2,1,16,1536]{4,3,2,1,0:T(8,128)(2,1)} %bitcast.7.refs_0_), channel_id=1, source_target_pairs={{128,0},{129,1},{130,2},{131,3},{132,4},{133,5},{134,6},{135,7},{1... | collective-permute-start | bytes 1179656 | tf_op jit(solution)/shard_map/ppermute | solution.py:514
  269.0 7.2 %collective-permute-start.20 = (bf16[4,2,1,16,1536]{4,3,2,1,0:T(8,128)(2,1)}, bf16[4,2,1,16,1536]{4,3,2,1,0:T(8,128)(2,1)}, u32[]{:S(2)}, u32[]{:S(2)}) collective-permute-start(bf16[4,2,1,16,1536]{4,3,2,1,0:T(8,128)(2,1)} %bitcast.7.refs_0_), channel_id=1, source_target_pairs={{0,8},{8,0},{1,9},{9,1},{2,10},{10,2},{3,11},{11,3},{4,12},{12,4},... | collective-permute-start | bytes 1179656 | tf_op jit(solution)/shard_map/ppermute | solution.py:510
  270.5 10.0 %collective-permute-start.21 = (bf16[4,2,1,16,1536]{4,3,2,1,0:T(8,128)(2,1)}, bf16[4,2,1,16,1536]{4,3,2,1,0:T(8,128)(2,1)}, u32[]{:S(2)}, u32[]{:S(2)}) collective-permute-start(bf16[4,2,1,16,1536]{4,3,2,1,0:T(8,128)(2,1)} %bitcast.7.refs_0_), channel_id=1, source_target_pairs={{128,8},{136,0},{129,9},{137,1},{130,10},{138,2},{131,11},{139,3},... | collective-permute-start | bytes 1179656 | tf_op jit(solution)/shard_map/ppermute | solution.py:519
  284.4 11.5 %all-to-all-start.8 = ((bf16[8,2,16,384]{3,2,1,0:T(8,128)(2,1)}), bf16[8,2,16,384]{3,2,1,0:T(8,128)(2,1)}, u32[]{:S(2)}, u32[]{:S(2)}) async-start(bf16[8,2,16,384]{3,2,1,0:T(8,128)(2,1)} %shard_map.85), calls=%async_computation.8 | async-start | bytes 393216 | tf_op jit(solution)/shard_map/all_to_all | solution.py:490

commit v5 on v4

--- a/solution.py
+++ b/solution.py
@@ -69,103 +69,60 @@
         copy.wait()
 
 
-def start_kernel(x_ref, g_ref, up, down, *rest):
-    outs, (up_held, down_held, stage, up_sems, down_sems, out_sems) = rest[:4], rest[4:]
+def first_kernel(layer, by_rows, pieces, x_ref, own, other, *rest):
+    outs, (held, sems, stage, out_sems) = rest[: 1 if pieces else 2], rest[1 if pieces else 2 :]
     section, mate_pos = lax.axis_index("section"), lax.axis_index("x_lo")
+    wait = load_weights(layer, by_rows, ((own, other),), held, sems)
     groups, tokens, wide = stage.shape[1], stage.shape[3], stage.shape[4]
-    per_half, count = wide // CHUNK, up_held.shape[0]
+    per_half = wide // CHUNK
 
     def out_copies(half):
-        return [
-            pltpu.make_async_copy(stage.at[i, :, half], outs[i].at[:, half], out_sems.at[half, i])
-            for i in range(4)
-        ]
-
-    def run(left_ref, weight, by_rows, held, sems):
-        copies = []
-        for i in range(count):
-            units = pl.ds(i * CHUNK, CHUNK)
-            source = weight.at[units, :] if by_rows else weight.at[:, units]
-            copies.append(pltpu.make_async_copy(source, held.at[i], sems.at[i]))
-            copies[-1].start()
-        left = left_ref[...].reshape(-1, left_ref.shape[2])
-        for i in range(count):
-            half, place = i // per_half, pl.ds((i % per_half) * CHUNK, CHUNK)
-            copies[i].wait()
-            total = dot(left, held[i], ((1,), (1 if by_rows else 0,))).astype(bf16)
-            total = total.reshape(2, 2, groups, tokens, CHUNK)
-            for which in range(2):
-                for token_half in range(2):
-                    away = jnp.where(token_half == mate_pos, 0, 2) + jnp.where(which == section, 0, 1)
-                    stage[away, :, half, :, place] = total[which, token_half]
-            if i % per_half == per_half - 1:
-                for copy in out_copies(half):
-                    copy.start()
-        wait_all(out_copies(0) + out_copies(1))
-
-    pl.when(section == 0)(lambda: run(x_ref, up, False, up_held, up_sems))
-    pl.when(section == 1)(lambda: run(g_ref, down, True, down_held, down_sems))
-
-
-def start_products(x, g, up, down, blocks):
-    width, units = up.shape
-    count = units // CHUNK
+        if pieces:
+            pairs = [(stage.at[i, :, half], outs[0].at[:, half, i]) for i in range(2)]
+        else:
+            places = (mate_pos, 1 - mate_pos)
+            pairs = [(stage.at[places[i], :, half], outs[i].at[:, half]) for i in range(2)]
+        return [pltpu.make_async_copy(*pair, out_sems.at[half, i]) for i, pair in enumerate(pairs)]
+
+    x = x_ref[section]
+    for i in range(held.shape[0]):
+        half, place = i // per_half, pl.ds((i % per_half) * CHUNK, CHUNK)
+        wait(i)
+        got = dot(x, held[i], ((1,), (1 if by_rows else 0,))).astype(bf16)
+        stage[:, :, half, :, place] = got.reshape(2, groups, tokens, CHUNK)
+        if i % per_half == per_half - 1:
+            for copy in out_copies(half):
+                copy.start()
+    wait_all(out_copies(0) + out_copies(1))
+
+
+def first_product(layer, by_rows, pieces, x, own, other, blocks):
+    outs = [shape_of(blocks[:2] + (2,) + blocks[2:])] if pieces else [shape_of(blocks)] * 2
     return kernel_call(
-        start_kernel,
-        [shape_of(blocks)] * 4,
-        [HBM] * 4,
-        [VMEM, VMEM, HBM, HBM],
-        [
-            pltpu.VMEM((count, width, CHUNK), bf16),
-            pltpu.VMEM((count, CHUNK, width), bf16),
-            pltpu.VMEM((4,) + blocks, bf16),
-            pltpu.SemaphoreType.DMA((count,)),
-            pltpu.SemaphoreType.DMA((count,)),
-            pltpu.SemaphoreType.DMA((2, 4)),
-        ],
-        (x, g, up, down),
-        flops=2 * x.shape[0] * x.shape[1] * up.size,
-        moved=4 * up.size,
-    )
-
-
-def add_kernel(kept, mates, other, across, out_ref, held, sems):
-    section = lax.axis_index("section")
-    copies = [
-        pltpu.make_async_copy(ref, held.at[i], sems.at[i]) for i, ref in enumerate((kept, mates, other, across))
+        functools.partial(first_kernel, layer, by_rows, pieces),
+        outs,
+        [HBM] * len(outs),
+        [VMEM, HBM, HBM],
+        held_scratch(own, by_rows, 1)
+        + [pltpu.VMEM((2,) + blocks, bf16), pltpu.SemaphoreType.DMA((2, 2))],
+        (x, own, other),
+        flops=2 * x.shape[1] * own.size,
+        moved=2 * own.size,
+    )
+
+
+def widen_kernel(layer, by_rows, kind, riding, arrived_ref, base, base_mate, own, other, own_mate, other_mate, *rest):
+    riders, rest = rest[: 2 * riding], rest[2 * riding :]
+    out_ref, x_out, held, sems, stage, out_sems, arrived, in_sems = rest[:8]
+    arrival = pltpu.make_async_copy(arrived_ref, arrived, in_sems.at[0])
+    arrival.start()
+    rides = [
+        pltpu.make_async_copy(ref, rest[8].at[i], in_sems.at[1 + i]) for i, ref in enumerate(riders)
     ]
-    for copy in copies:
+    for copy in rides:
         copy.start()
-    outs = []
-    for i, kind in enumerate((section, 1 - section)):
-        copies[2 * i].wait()
-        copies[2 * i + 1].wait()
-        held[2 * i] = (held[2 * i].astype(f32) + held[2 * i + 1].astype(f32)).astype(bf16)
-        outs.append(pltpu.make_async_copy(held.at[2 * i], out_ref.at[:, :, kind], sems.at[4 + i]))
-        outs[-1].start()
-    wait_all(outs)
-
-
-def add_terms(terms):
-    shape = terms[0].shape
-    return kernel_call(
-        add_kernel,
-        shape_of(shape[:2] + (2,) + shape[2:]),
-        HBM,
-        [HBM] * 4,
-        [pltpu.VMEM((4,) + shape, bf16), pltpu.SemaphoreType.DMA((6,))],
-        terms,
-        flops=2 * terms[0].size,
-        moved=12 * terms[0].size,
-    )
-
-
-def widen_kernel(layer, by_rows, kind, arrived_ref, base, base_mate, own, other, own_mate, other_mate, *rest):
-    out_ref, x_out, held, sems, stage, out_sems, arrived, in_sem = rest
-    arrival = pltpu.make_async_copy(arrived_ref, arrived, in_sem)
-    arrival.start()
     wait = load_weights(layer, by_rows, ((own, other), (own_mate, other_mate)), held, sems)
-    per_half = stage.shape[3] // CHUNK
+    per_half = stage.shape[4] // CHUNK
     arrival.wait()
     total = arrived[0].astype(f32)
     for i in range(1, arrived.shape[0]):
@@ -173,6 +130,9 @@
     x = jnp.concatenate([base[kind], base_mate[kind]], axis=1)
     x = (x.astype(f32) + total).astype(bf16)
     x_out[...] = x
+    if riding:
+        wait_all(rides)
+        stage[:, :, 1] = (rest[8][0].astype(f32) + rest[8][1].astype(f32)).astype(bf16)
 
     def out_copy(half):
         return pltpu.make_async_copy(stage.at[:, half], out_ref.at[:, half], out_sems.at[half])
@@ -181,7 +141,7 @@
         half, place = i // per_half, pl.ds((i % per_half) * CHUNK, CHUNK)
         wait(i)
         got = dot(x, held[i], ((1,), (1 if by_rows else 0,))).astype(bf16)
-        stage[:, half, :, place] = got.reshape(stage.shape[0], stage.shape[2], CHUNK)
+        stage[:, half, 0, :, place] = got.reshape(stage.shape[0], stage.shape[3], CHUNK)
         if i % per_half == per_half - 1:
             out_copy(half).start()
     wait_all([out_copy(0), out_copy(1)])
@@ -210,10 +170,10 @@
     wait_all(copies)
 
 
-def held_scratch(weight, by_rows):
-    count, width = max(weight.shape) // CHUNK, 2 * min(weight.shape)
+def held_scratch(weight, by_rows, parts=2):
+    count, width = max(weight.shape) // CHUNK, parts * min(weight.shape)
     chunk = (CHUNK, width) if by_rows else (width, CHUNK)
-    return [pltpu.VMEM((count,) + chunk, bf16), pltpu.SemaphoreType.DMA((2, count))]
+    return [pltpu.VMEM((count,) + chunk, bf16), pltpu.SemaphoreType.DMA((parts, count))]
 
 
 def kernel_call(body, outs, out_specs, in_specs, scratch, operands, flops=0, moved=0):
@@ -228,20 +188,22 @@
     )(*operands)
 
 
-def widen(layer, by_rows, arrived, kind, bases, weights, blocks):
+def widen(layer, by_rows, arrived, kind, bases, weights, blocks, riders=()):
+    shape = blocks[:2] + (2 if riders else 1,) + blocks[2:]
     return kernel_call(
-        functools.partial(widen_kernel, layer, by_rows, kind),
-        (shape_of(blocks), shape_of(arrived.shape[1:])),
+        functools.partial(widen_kernel, layer, by_rows, kind, len(riders) // 2),
+        (shape_of(shape), shape_of(arrived.shape[1:])),
         (HBM, VMEM),
-        [HBM, VMEM, VMEM] + [HBM] * 4,
+        [HBM, VMEM, VMEM] + [HBM] * (4 + len(riders)),
         held_scratch(weights[0], by_rows)
         + [
-            pltpu.VMEM(blocks, bf16),
+            pltpu.VMEM(shape, bf16),
             pltpu.SemaphoreType.DMA((2,)),
             pltpu.VMEM(arrived.shape, bf16),
-            pltpu.SemaphoreType.DMA,
-        ],
-        (arrived,) + bases + weights,
+            pltpu.SemaphoreType.DMA((1 + len(riders),)),
+        ]
+        + ([pltpu.VMEM((2,) + blocks, bf16)] if riders else []),
+        (arrived,) + bases + weights + riders,
         flops=4 * arrived.shape[1] * weights[0].size,
         moved=4 * weights[0].size,
     )
@@ -303,20 +265,20 @@
 
 def act_first(sums, _):
     value, slope = gelu_both(sums[0])
-    return [value], [slope, sums[1]]
-
-
-def act_last(sums, ins):
+    return [value], [slope]
+
+
+def act_last(sums, _):
     value, slope = gelu_both(sums[0])
-    return [ins[0] * slope, value], []
+    return [sums[1] * slope, value], []
 
 
 def act_back(sums, ins):
     return [sums[0] * ins[0]], []
 
 
-def activation(body, arrived, kinds, ins=(), outs=0):
-    peers, piece = arrived.shape[0], arrived.shape[2:]
+def activation(body, arrived, kinds, ins=(), outs=0, peers=None):
+    peers, piece = peers or arrived.shape[0], arrived.shape[2:]
     steps = piece[1] // CHUNK
     return kernel_call(
         functools.partial(act_kernel, body, len(ins), outs),
@@ -547,40 +509,41 @@
     def halves_of(pair, which):
         return lax.dynamic_slice_in_dim(pair, which * half_len, half_len, 1)
 
-    keep_own, keep_other, send_own, send_other = start_products(inputs, cotangent, own_up, own_down, blocks)
-    terms = keep_own, to_mate(send_own), to_other_core(keep_other), to_other_core_of_mate(send_other)
-    own_down_late, own_up_late = late((own_down, own_up), keep_own)
-    other_down, other_up = only_to_core(own_down_late, 1), only_to_core(own_up_late, 0)
-    both = add_terms(late(terms, other_up))
-    own_down_late, x0, g2 = late((own_down, inputs, cotangent), both)
-    mate_down0 = only_to_mate(own_down_late, 0)
-    arrived = exchange(both.reshape((rings, 2) + piece), "z")
+    mate_down0 = only_to_mate(own_down, 0)
+    other_up = to_other_core(own_up)
+    (pre0,) = first_product(0, False, True, inputs, own_up, other_up, blocks)
+    arrived = exchange(pre0.reshape((2 * rings, 1) + piece), ("z", "x_lo"))
+
+    other_down = to_other_core(late(own_down, other_up))
+    x0, g2 = late((inputs, cotangent), pre0)
+    keep, send = first_product(1, True, False, g2, own_down, other_down, blocks)
+    d_hid1 = keep, to_mate(send)
     ends = jnp.stack([batch(x0, section), batch(g2, section)])
     bases = halves_of(ends, mate_pos), to_mate(halves_of(ends, 1 - mate_pos))
-    arrived = late(arrived, (bases, other_down))
-
-    value0, slope0, d_hid1 = activation(act_first, arrived, 1, outs=2)
-    mate_down0 = late(mate_down0, value0)
+    arrived = late(arrived, (bases, d_hid1))
+
+    mate_up1 = only_to_mate(late(own_up, arrived), 1)
+    mate_down0 = late(mate_down0, arrived)
     down0 = own_down, other_down, mate_down0, only_to_core(mate_down0, 1)
-    mate_up1 = only_to_mate(late(own_up, mate_down0), 1)
+    value0, slope0 = activation(act_first, arrived, 1, outs=1, peers=rings)
     hid0 = exchange(value0, "z").reshape(blocks[:2] + (1,) + piece)
     part = narrow(0, True, hid0, down0, lax.axis_size(col))
     mate_up1 = late(mate_up1, part)
     up1 = own_up, other_up, mate_up1, only_to_core(mate_up1, 0)
     arrived = exchange(part, col)
 
-    pre1, x1 = widen(1, False, arrived, 0, bases, up1, blocks)
+    pre1, x1 = widen(1, False, arrived, 0, bases, up1, blocks, d_hid1)
     hid0s = to_owner(late(hid0, pre1), 0)
-    arrived = late(exchange(pre1.reshape((rings, 1) + piece), "z"), hid0s)
-    (acts1,) = activation(act_last, arrived, 2, ins=(d_hid1,))
-    acts1 = exchange(acts1, "z").reshape(blocks[:2] + (2,) + piece)
+    arrived = exchange(pre1.reshape((rings, 2) + piece), "z")
+    (acts1,) = activation(act_last, arrived, 2)
+    acts1 = late(exchange(acts1, "z").reshape(blocks[:2] + (2,) + piece), hid0s)
     part = narrow(1, False, acts1, up1, lax.axis_size(col))
     arrived = exchange(part, col)
 
     d_hid0, g1 = widen(0, True, arrived, 1, bases, down0, blocks)
     acts1s = to_owner(late(acts1, d_hid0), 1)
     arrived = exchange(d_hid0.reshape((rings, 1) + piece), "z")
-    (d_pre0,) = activation(act_back, arrived, 1, ins=(slope0,))
+    (d_pre0,) = activation(act_back, late(arrived, acts1s[1:3]), 1, ins=(slope0,))
     both1 = late(jnp.stack([x1, g1]), d_pre0)
     near, far = both1[..., :width], both1[..., width:]
     both1 = jnp.stack([near, to_other_core(near), to_mate(far), to_other_core_of_mate(far)])
@@ -599,9 +562,9 @@
     xs = jnp.where(first, all_tokens(inputs), x1s)
     gs = jnp.where(first, g1s, all_tokens(cotangent))
 
-    down_grad = weight_grad(True, gs, hid0s, acts1s)
-    d_pre0 = late(exchange(d_pre0, "z").reshape(blocks[:2] + (1,) + piece), down_grad)
-    d_pre0s = to_owner(d_pre0, 0)
+    d_pre0 = late(exchange(d_pre0, "z").reshape(blocks[:2] + (1,) + piece), acts1s[3])
+    down_grad = weight_grad(True, late(gs, d_pre0), hid0s, acts1s)
+    d_pre0s = late(to_owner(d_pre0, 0), down_grad)
 
     last = last_product(own_up, own_down, d_pre0s, acts1s)
     xs, d_pre0s = late((xs, d_pre0s), last)

time: 300 us -> 298 us (level)
  blocking collectives: 74.8 us -> 83.5 us
  waiting for transfers between devices: 72.7 us -> 67.8 us
    ppermute x2 -> x1, waiting for transfers between devices: 11 us -> 0.01 us  [to_other_core_of_mate(): return lax.ppermute(block, CORES, [(0, 3), (3, 0), (1, 2), (2, 1)])]
    all_to_all x4, blocking collectives: 74.8 us -> 83.5 us  [exchange(): return lax.all_to_all(blocks, axes, 0, 0)]
    all_to_all x5, waiting for transfers between devices: 25.5 us -> 33 us  [exchange(): return lax.all_to_all(blocks, axes, 0, 0)]
    ppermute x3, waiting for transfers between devices: 10.2 us -> 5.48 us  [only_across(): return lax.ppermute(block, CORES, [(source, at + 1), (source + 1, at)])]
    ppermute x2 -> x3, waiting for transfers between devices: 0.01 us -> 4.51 us  [to_other_core(): return lax.ppermute(block, 'section', [(0, 1), (1, 0)])]
    ppermute x7 -> x5, starting transfers between devices: 23.1 us -> 22.9 us  [only_to_core(): return lax.ppermute(block, 'section', [(1 - section, section)])]
  transfers between devices with their start and end apart: 27 -> 25, of which waited for: 11 -> 8; matrix products, arithmetic and copies ran while one was open for 4% -> 4% of each run, Pallas kernels for 7% -> 10%
where the time goes in v5:
time: 298 us; the launch traced here: 297 us
  blocking collectives  83.5 us (28%)
  starting transfers between devices  75.5 us (25%)
  waiting for transfers between devices  67.8 us (23%)
  Pallas kernels  58.4 us (20%)
  local copies, waits for them, and re-layouts  5.97 us (2%)
  other arithmetic  4.5 us (2%)
    all_to_all x4, blocking collectives, exchange(): return lax.all_to_all(blocks, axes, 0, 0)  83.5 us
    pallas_call x11, Pallas kernels, kernel_call(): pl.pallas_call(body, out_shape=outs, in_specs=in_specs, out_specs=out_spe...  46 us
    all_to_all x5, waiting for transfers between devices, exchange(): return lax.all_to_all(blocks, axes, 0, 0)  33 us
    all_to_all x5, starting transfers between devices, exchange(): return lax.all_to_all(blocks, axes, 0, 0)  24 us
    ppermute x5, starting transfers between devices, only_to_core(): return lax.ppermute(block, 'section', [(1 - section, section)])  22.9 us
    ppermute x3, waiting for transfers between devices, to_mate(): return lax.ppermute(block, 'x_lo', [(0, 1), (1, 0)])  17.7 us
    pallas_call x2, Pallas kernels, weight_grad(): pl.pallas_call(grad_down_kernel if down else grad_up_kernel, out_shape=sh...  12.4 us
    ppermute x5, starting transfers between devices, only_to_mate(): return lax.ppermute(block, CORES, [(at, at + 1), (at + 1, at)])  10.1 us
  transfers between devices with their start and end apart: 25, of which 8 were waited for; matrix products, arithmetic and copies ran while one was open for 4% of the time, Pallas kernels for 10%

profile of v5, /device:TPU:1, one launch (start us, length us, event | category | flops | bytes accessed | tf_op | source)
XLA Modules:
  0.0 296.7 jit_solution(1802106582308632115)
XLA Ops:
  0.6 3.3 %collective-permute-start = (bf16[384,3072]{1,0:T(8,128)(2,1)}, bf16[384,3072]{1,0:T(8,128)(2,1)}, u32[]{:S(2)}, u32[]{:S(2)}) collective-permute-start(bf16[384,3072]{1,0:T(8,128)(2,1)} %bitcast.56), channel_id=1, source_target_pairs={{0,128},{128,0},{1,129},{129,1},{2,130},{130,2},{3,131},{131,3},{4... | collective-permute-start | bytes 7077896 | tf_op jit(solution)/shard_map/ppermute | solution.py:459
  4.0 4.5 %collective-permute-done.other = bf16[384,3072]{1,0:T(8,128)(2,1)} collective-permute-done((bf16[384,3072]{1,0:T(8,128)(2,1)}, bf16[384,3072]{1,0:T(8,128)(2,1)}, u32[]{:S(2)}, u32[]{:S(2)}) %collective-permute-start) | collective-permute-done | bytes 2359328 | tf_op jit(solution)/shard_map/ppermute | solution.py:459
  8.8 2.1 collective-permute-start.4
  10.9 4.2 %shard_map.75 = bf16[4,2,2,16,1536]{4,3,2,1,0:T(8,128)(2,1)} custom-call(bf16[2,128,384]{2,1,0:T(8,128)(2,1)} %x_ref.1, bf16[384,3072]{1,0:T(8,128)(2,1)} %bitcast.57, bf16[384,3072]{1,0:T(8,128)(2,1)} %collective-permute-done.other), custom_call_target="tpu_custom_call" | custom-call | flops 301989888 | bytes 2359296 | tf_op jit(solution)/shard_map/pallas_call | solution.py:180
  15.1 7.5 %all-to-all-start = ((bf16[16,1,16,1536]{3,2,1,0:T(8,128)(2,1)}), bf16[16,1,16,1536]{3,2,1,0:T(8,128)(2,1)}, u32[]{:S(2)}, u32[]{:S(2)}) async-start(bf16[16,1,16,1536]{3,2,1,0:T(8,128)(2,1)} %bitcast.69), calls=%async_computation | async-start | bytes 1572864 | tf_op jit(solution)/shard_map/all_to_all | solution.py:452
  22.7 4.3 %shard_map.76 = (bf16[4,2,16,1536]{3,2,1,0:T(8,128)(2,1)}, bf16[4,2,16,1536]{3,2,1,0:T(8,128)(2,1)}) custom-call(bf16[2,128,384]{2,1,0:T(8,128)(2,1)} %x_ref.2, bf16[3072,384]{1,0:T(8,128)(2,1)} %bitcast.52, bf16[3072,384]{1,0:T(8,128)(2,1)} %collective-permute-done.2.other), custom_call_target="tpu_custom_call" | custom-call | flops 301989888 | bytes 2359296 | tf_op jit(solution)/shard_map/pallas_call | solution.py:180
  27.0 1.4 collective-permute-start.3
  30.2 17.7 %collective-permute-done.1.base_mate = bf16[2,64,384]{2,1,0:T(8,128)(2,1)} collective-permute-done((bf16[2,64,384]{2,1,0:T(8,128)(2,1)S(1)}, bf16[2,64,384]{2,1,0:T(8,128)(2,1)}, u32[]{:S(2)}, u32[]{:S(2)}) %collective-permute-start.1) | collective-permute-done | bytes 98336 | tf_op jit(solution)/shard_map/ppermute | solution.py:463
  47.9 1.3 collective-permute-start.5
  49.2 3.2 %collective-permute-start.6 = (bf16[384,3072]{1,0:T(8,128)(2,1)}, bf16[384,3072]{1,0:T(8,128)(2,1)}, u32[]{:S(2)}, u32[]{:S(2)}) collective-permute-start(bf16[384,3072]{1,0:T(8,128)(2,1)} %bitcast.58), channel_id=1, source_target_pairs={{128,136},{136,128},{129,137},{137,129},{130,138},{138,130},{131,1... | collective-permute-start | bytes 7077896 | tf_op jit(solution)/shard_map/ppermute | solution.py:472
  52.4 2.7 shard_map.77
  55.1 17.1 %all_to_all.45 = bf16[8,1,16,1536]{3,2,1,0:T(8,128)(2,1)} all-to-all(bf16[8,1,16,1536]{3,2,1,0:T(8,128)(2,1)} %get-tuple-element.43), channel_id=1, replica_groups=mesh['section'=2,'z'=8,'x_lo'=2,'y'=4,'x_hi'=2] {'z'}, dimensions={0} | all-to-all | bytes 786432 | tf_op jit(solution)/shard_map/all_to_all | solution.py:452
  72.2 4.6 %shard_map.78 = bf16[8,64,768]{2,1,0:T(8,128)(2,1)} custom-call(bf16[4,2,1,16,1536]{4,3,2,1,0:T(8,128)(2,1)} %bitcast.64, bf16[3072,384]{1,0:T(8,128)(2,1)} %bitcast.53, bf16[3072,384]{1,0:T(8,128)(2,1)} %collective-permute-done.2.other, bf16[3072,384]{1,0:T(8,128)(2,1)} %collective-permute-done.4.own_mate, bf16[3072,384]{1,0:T(8,128)(2,1)} %collective-permute-done.5.other_mate), custom_call_target="tpu_custom_call" | custom-call | flops 301989888 | bytes 4718592 | tf_op jit(solution)/shard_map/pallas_call | solution.py:180
  76.8 7.0 %collective-permute-done.6.own_mate = bf16[384,3072]{1,0:T(8,128)(2,1)} collective-permute-done((bf16[384,3072]{1,0:T(8,128)(2,1)}, bf16[384,3072]{1,0:T(8,128)(2,1)}, u32[]{:S(2)}, u32[]{:S(2)}) %collective-permute-start.6) | collective-permute-done | bytes 2359328 | tf_op jit(solution)/shard_map/ppermute | solution.py:472
  83.9 14.1 %collective-permute-start.7 = (bf16[384,3072]{1,0:T(8,128)(2,1)}, bf16[384,3072]{1,0:T(8,128)(2,1)}, u32[]{:S(2)}, u32[]{:S(2)}) collective-permute-start(bf16[384,3072]{1,0:T(8,128)(2,1)} %collective-permute-done.6.own_mate), channel_id=1, source_target_pairs={{128,0},{129,1},{130,2},{131,3},{132,4},{133,5},{134,6},{135,7},{1... | collective-permute-start | bytes 7077896 | tf_op jit(solution)/shard_map/ppermute | solution.py:476
  98.0 20.4 %all_to_all.46.arrived_ref = bf16[8,64,768]{2,1,0:T(8,128)(2,1)} all-to-all(bf16[8,64,768]{2,1,0:T(8,128)(2,1)} %shard_map.78), channel_id=1, replica_groups=mesh['section'=2,'z'=8,'x_lo'=2,'y'=4,'x_hi'=2] {'y','x_hi'}, dimensions={0} | all-to-all | bytes 1572864 | tf_op jit(solution)/shard_map/all_to_all | solution.py:452
  118.4 6.9 %shard_map.79 = (bf16[4,2,2,16,1536]{4,3,2,1,0:T(8,128)(2,1)}, bf16[64,768]{1,0:T(8,128)(2,1)}) custom-call(bf16[8,64,768]{2,1,0:T(8,128)(2,1)} %all_to_all.46.arrived_ref, bf16[2,64,384]{2,1,0:T(8,128)(2,1)} %get-tuple-element.84.base, bf16[2,64,384]{2,1,0:T(8,128)(2,1)} %collective-permute-done.1.base_mate, bf16[384,3072]{1,0:T(8,128)(2,1)} %bitcast.59, ...), custom_call_target="tpu_custom_call" | custom-call | flops 301989888 | bytes 4718592 | tf_op jit(solution)/shard_map/pallas_call | solution.py:180
  125.3 27.6 %all_to_all.47.arrived_ref = bf16[8,2,16,1536]{3,2,1,0:T(8,128)(2,1)} all-to-all(bf16[8,2,16,1536]{3,2,1,0:T(8,128)(2,1)} %bitcast.72), channel_id=1, replica_groups=mesh['section'=2,'z'=8,'x_lo'=2,'y'=4,'x_hi'=2] {'z'}, dimensions={0} | all-to-all | bytes 1572864 | tf_op jit(solution)/shard_map/all_to_all | solution.py:452
  152.9 2.1 shard_map.80
  155.0 4.2 %all-to-all-start.4 = ((bf16[8,2,16,1536]{3,2,1,0:T(8,128)(2,1)}), bf16[8,2,16,1536]{3,2,1,0:T(8,128)(2,1)}, u32[]{:S(2)}, u32[]{:S(2)}) async-start(bf16[8,2,16,1536]{3,2,1,0:T(8,128)(2,1)} %shard_map.80), calls=%async_computation.4 | async-start | bytes 1572864 | tf_op jit(solution)/shard_map/all_to_all | solution.py:452
  159.3 3.1 %collective-permute-start.8 = (bf16[4,2,1,16,1536]{4,3,2,1,0:T(8,128)(2,1)}, bf16[4,2,1,16,1536]{4,3,2,1,0:T(8,128)(2,1)}, u32[]{:S(2)}, u32[]{:S(2)}) collective-permute-start(bf16[4,2,1,16,1536]{4,3,2,1,0:T(8,128)(2,1)} %bitcast.65), channel_id=1, source_target_pairs={{128,0},{129,1},{130,2},{131,3},{132,4},{133,5},{134,6},{135,7},{1... | collective-permute-start | bytes 1179656 | tf_op jit(solution)/shard_map/ppermute | solution.py:476
  162.3 1.4 collective-permute-start.9
  163.8 3.4 %collective-permute-start.10 = (bf16[4,2,1,16,1536]{4,3,2,1,0:T(8,128)(2,1)}, bf16[4,2,1,16,1536]{4,3,2,1,0:T(8,128)(2,1)}, u32[]{:S(2)}, u32[]{:S(2)}) collective-permute-start(bf16[4,2,1,16,1536]{4,3,2,1,0:T(8,128)(2,1)} %bitcast.67), channel_id=1, source_target_pairs={{128,8},{136,0},{129,9},{137,1},{130,10},{138,2},{131,11},{139,3},... | collective-permute-start | bytes 1179656 | tf_op jit(solution)/shard_map/ppermute | solution.py:481
  167.2 5.5 %collective-permute-done.10.refs_3_ = bf16[4,2,1,16,1536]{4,3,2,1,0:T(8,128)(2,1)} collective-permute-done((bf16[4,2,1,16,1536]{4,3,2,1,0:T(8,128)(2,1)}, bf16[4,2,1,16,1536]{4,3,2,1,0:T(8,128)(2,1)}, u32[]{:S(2)}, u32[]{:S(2)}) %collective-permute-start.10) | collective-permute-done | bytes 393248 | tf_op jit(solution)/shard_map/ppermute | solution.py:481
  172.6 10.2 %all-to-all-done.4 = bf16[8,2,16,1536]{3,2,1,0:T(8,128)(2,1)} async-done(((bf16[8,2,16,1536]{3,2,1,0:T(8,128)(2,1)}), bf16[8,2,16,1536]{3,2,1,0:T(8,128)(2,1)}, u32[]{:S(2)}, u32[]{:S(2)}) %all-to-all-start.4) | async-done | bytes 786464 | tf_op jit(solution)/shard_map/all_to_all | solution.py:452
  182.9 5.6 %shard_map.81 = bf16[8,64,768]{2,1,0:T(8,128)(2,1)} custom-call(bf16[4,2,2,16,1536]{4,3,2,1,0:T(8,128)(2,1)} %bitcast.5.arrived_ref.refs_4_, bf16[384,3072]{1,0:T(8,128)(2,1)} %bitcast.60, bf16[384,3072]{1,0:T(8,128)(2,1)} %collective-permute-done.other, bf16[384,3072]{1,0:T(8,128)(2,1)} %collective-permute-done.6.own_mate, ...), custom_call_target="tpu_custom_call" | custom-call | flops 301989888 | bytes 4718592 | tf_op jit(solution)/shard_map/pallas_call | solution.py:180
  188.5 18.4 %all_to_all.48.arrived_ref = bf16[8,64,768]{2,1,0:T(8,128)(2,1)} all-to-all(bf16[8,64,768]{2,1,0:T(8,128)(2,1)} %shard_map.81), channel_id=1, replica_groups=mesh['section'=2,'z'=8,'x_lo'=2,'y'=4,'x_hi'=2] {'y','x_hi'}, dimensions={0} | all-to-all | bytes 1572864 | tf_op jit(solution)/shard_map/all_to_all | solution.py:452
  206.9 7.1 %shard_map.82 = (bf16[4,2,1,16,1536]{4,3,2,1,0:T(8,128)(2,1)}, bf16[64,768]{1,0:T(8,128)(2,1)}) custom-call(bf16[8,64,768]{2,1,0:T(8,128)(2,1)} %all_to_all.48.arrived_ref, bf16[2,64,384]{2,1,0:T(8,128)(2,1)} %get-tuple-element.84.base, bf16[2,64,384]{2,1,0:T(8,128)(2,1)} %collective-permute-done.1.base_mate, bf16[3072,384]{1,0:T(8,128)(2,1)} %bitcast.54, ...), custom_call_target="tpu_custom_call" | custom-call | flops 301989888 | bytes 4718592 | tf_op jit(solution)/shard_map/pallas_call | solution.py:180
  214.0 1.3 collective-permute-start.11
  215.3 2.0 collective-permute-start.12
  217.3 4.1 %all-to-all-start.6 = ((bf16[8,1,16,1536]{3,2,1,0:T(8,128)(2,1)}), bf16[8,1,16,1536]{3,2,1,0:T(8,128)(2,1)}, u32[]{:S(2)}, u32[]{:S(2)}) async-start(bf16[8,1,16,1536]{3,2,1,0:T(8,128)(2,1)} %bitcast.73), calls=%async_computation.6 | async-start | bytes 786432 | tf_op jit(solution)/shard_map/all_to_all | solution.py:452
  221.5 1.6 dynamic-slice_bitcast_fusion.7
  223.1 1.3 collective-permute-start.13
  224.4 1.6 pad_maximum_fusion.1
  226.0 7.8 %all-to-all-done.6.arrived_ref = bf16[8,1,16,1536]{3,2,1,0:T(8,128)(2,1)} async-done(((bf16[8,1,16,1536]{3,2,1,0:T(8,128)(2,1)}), bf16[8,1,16,1536]{3,2,1,0:T(8,128)(2,1)}, u32[]{:S(2)}, u32[]{:S(2)}) %all-to-all-start.6) | async-done | bytes 393248 | tf_op jit(solution)/shard_map/all_to_all | solution.py:452
  233.8 2.8 shard_map.83
  237.7 4.6 %collective-permute-start.19 = (bf16[2,64,384]{2,1,0:T(8,128)(2,1)S(1)}, bf16[2,64,384]{2,1,0:T(8,128)(2,1)S(1)}, u32[]{:S(2)}, u32[]{:S(2)}) collective-permute-start(bf16[2,64,384]{2,1,0:T(8,128)(2,1)S(1)} %get-tuple-element.77), channel_id=1, source_target_pairs={{0,136},{136,0},{8,128},{128,8},{1,137},{137,1},{9,129},{129,9},{2... | collective-permute-start | bytes 294920 | tf_op jit(solution)/shard_map/ppermute | solution.py:467
  243.8 4.1 %all-to-all-start.7 = ((bf16[8,1,16,1536]{3,2,1,0:T(8,128)(2,1)}), bf16[8,1,16,1536]{3,2,1,0:T(8,128)(2,1)}, u32[]{:S(2)}, u32[]{:S(2)}) async-start(bf16[8,1,16,1536]{3,2,1,0:T(8,128)(2,1)} %shard_map.83), calls=%async_computation.7 | async-start | bytes 786432 | tf_op jit(solution)/shard_map/all_to_all | solution.py:452
  248.9 14.2 %all-to-all-done.7 = bf16[8,1,16,1536]{3,2,1,0:T(8,128)(2,1)} async-done(((bf16[8,1,16,1536]{3,2,1,0:T(8,128)(2,1)}), bf16[8,1,16,1536]{3,2,1,0:T(8,128)(2,1)}, u32[]{:S(2)}, u32[]{:S(2)}) %all-to-all-start.7) | async-done | bytes 393248 | tf_op jit(solution)/shard_map/all_to_all | solution.py:452
  263.1 3.1 %collective-permute-start.14 = (bf16[4,2,1,16,1536]{4,3,2,1,0:T(8,128)(2,1)}, bf16[4,2,1,16,1536]{4,3,2,1,0:T(8,128)(2,1)}, u32[]{:S(2)}, u32[]{:S(2)}) collective-permute-start(bf16[4,2,1,16,1536]{4,3,2,1,0:T(8,128)(2,1)} %bitcast.7.refs_0_), channel_id=1, source_target_pairs={{128,0},{129,1},{130,2},{131,3},{132,4},{133,5},{134,6},{135,7},{1... | collective-permute-start | bytes 1179656 | tf_op jit(solution)/shard_map/ppermute | solution.py:476
  266.2 1.4 collective-permute-start.15
  267.6 3.4 %collective-permute-start.16 = (bf16[4,2,1,16,1536]{4,3,2,1,0:T(8,128)(2,1)}, bf16[4,2,1,16,1536]{4,3,2,1,0:T(8,128)(2,1)}, u32[]{:S(2)}, u32[]{:S(2)}) collective-permute-start(bf16[4,2,1,16,1536]{4,3,2,1,0:T(8,128)(2,1)} %bitcast.7.refs_0_), channel_id=1, source_target_pairs={{128,8},{136,0},{129,9},{137,1},{130,10},{138,2},{131,11},{139,3},... | collective-permute-start | bytes 1179656 | tf_op jit(solution)/shard_map/ppermute | solution.py:481
  272.5 6.3 %shard_map.84 = f32[3072,384]{1,0:T(8,128)} custom-call(bf16[256,384]{1,0:T(8,128)(2,1)} %maximum_select_fusion.g_ref, bf16[4,2,1,16,1536]{4,3,2,1,0:T(8,128)(2,1)} %bitcast.68, bf16[4,2,1,16,1536]{4,3,2,1,0:T(8,128)(2,1)} %collective-permute-done.8.refs_1_, bf16[4,2,1,16,1536]{4,3,2,1,0:T(8,128)(2,1)} %collective-permute-done.9.refs_2_, ...), custom_call_target="tpu_custom_call" | custom-call | flops 603979776 | bytes 4718592 | tf_op jit(solution)/shard_map/pallas_call | solution.py:374
  278.8 4.0 %shard_map.85 = bf16[8,2,16,384]{3,2,1,0:T(8,128)(2,1)} custom-call(bf16[384,3072]{1,0:T(8,128)(2,1)} %bitcast.61, bf16[3072,384]{1,0:T(8,128)(2,1)} %bitcast.55, bf16[4,2,1,16,1536]{4,3,2,1,0:T(8,128)(2,1)} %bitcast.7.refs_0_, bf16[4,2,1,16,1536]{4,3,2,1,0:T(8,128)(2,1)} %collective-permute-done.14.refs_1_, ...), custom_call_target="tpu_custom_call" | custom-call | flops 603979776 | bytes 7077888 | tf_op jit(solution)/shard_map/pallas_call | solution.py:180
  282.9 4.0 %all-to-all-start.8 = ((bf16[8,2,16,384]{3,2,1,0:T(8,128)(2,1)}), bf16[8,2,16,384]{3,2,1,0:T(8,128)(2,1)}, u32[]{:S(2)}, u32[]{:S(2)}) async-start(bf16[8,2,16,384]{3,2,1,0:T(8,128)(2,1)} %shard_map.85), calls=%async_computation.8 | async-start | bytes 393216 | tf_op jit(solution)/shard_map/all_to_all | solution.py:452
  286.9 1.4 slice_bitcast_fusion
  288.3 6.0 %shard_map.87 = f32[384,3072]{1,0:T(8,128)} custom-call(bf16[256,384]{1,0:T(8,128)(2,1)} %maximum_select_fusion.1.x_ref, bf16[4,2,1,16,1536]{4,3,2,1,0:T(8,128)(2,1)} %bitcast.7.refs_0_, bf16[4,2,1,16,1536]{4,3,2,1,0:T(8,128)(2,1)} %collective-permute-done.14.refs_1_, bf16[4,2,1,16,1536]{4,3,2,1,0:T(8,128)(2,1)} %collective-permute-done.15.refs_2_, ...), custom_call_target="tpu_custom_call" | custom-call | flops 603979776 | bytes 4718592 | tf_op jit(solution)/shard_map/pallas_call | solution.py:374
  295.1 1.6 shard_map.86
  (40 shorter events, 7.7 us)
Async XLA Ops:
  0.6 7.8 %collective-permute-start = (bf16[384,3072]{1,0:T(8,128)(2,1)}, bf16[384,3072]{1,0:T(8,128)(2,1)}, u32[]{:S(2)}, u32[]{:S(2)}) collective-permute-start(bf16[384,3072]{1,0:T(8,128)(2,1)} %bitcast.56), channel_id=1, source_target_pairs={{0,128},{128,0},{1,129},{129,1},{2,130},{130,2},{3,131},{131,3},{4... | collective-permute-start | bytes 7077896 | tf_op jit(solution)/shard_map/ppermute | solution.py:459
  8.5 14.2 %collective-permute-start.2 = (bf16[3072,384]{1,0:T(8,128)(2,1)}, bf16[3072,384]{1,0:T(8,128)(2,1)}, u32[]{:S(2)}, u32[]{:S(2)}) collective-permute-start(bf16[3072,384]{1,0:T(8,128)(2,1)} %bitcast.50), channel_id=1, source_target_pairs={{0,128},{128,0},{1,129},{129,1},{2,130},{130,2},{3,131},{131,3},{4... | collective-permute-start | bytes 7077896 | tf_op jit(solution)/shard_map/ppermute | solution.py:459
  8.8 39.1 %collective-permute-start.4 = (bf16[3072,384]{1,0:T(8,128)(2,1)}, bf16[3072,384]{1,0:T(8,128)(2,1)}, u32[]{:S(2)}, u32[]{:S(2)}) collective-permute-start(bf16[3072,384]{1,0:T(8,128)(2,1)} %bitcast.51), channel_id=1, source_target_pairs={{0,8},{8,0},{1,9},{9,1},{2,10},{10,2},{3,11},{11,3},{4,12},{12,4},... | collective-permute-start | bytes 7077896 | tf_op jit(solution)/shard_map/ppermute | solution.py:472
  15.1 32.8 %all-to-all-start = ((bf16[16,1,16,1536]{3,2,1,0:T(8,128)(2,1)}), bf16[16,1,16,1536]{3,2,1,0:T(8,128)(2,1)}, u32[]{:S(2)}, u32[]{:S(2)}) async-start(bf16[16,1,16,1536]{3,2,1,0:T(8,128)(2,1)} %bitcast.69), calls=%async_computation | async-start | bytes 1572864 | tf_op jit(solution)/shard_map/all_to_all | solution.py:452
  27.0 20.9 %collective-permute-start.3 = (bf16[4,2,16,1536]{3,2,1,0:T(8,128)(2,1)}, bf16[4,2,16,1536]{3,2,1,0:T(8,128)(2,1)}, u32[]{:S(2)}, u32[]{:S(2)}) collective-permute-start(bf16[4,2,16,1536]{3,2,1,0:T(8,128)(2,1)} %get-tuple-element.41), channel_id=1, source_target_pairs={{0,8},{8,0},{1,9},{9,1},{2,10},{10,2},{3,11},{11,3},{4,12},{12,4},... | collective-permute-start | bytes 1179656 | tf_op jit(solution)/shard_map/ppermute | solution.py:463
  30.0 17.9 %collective-permute-start.1 = (bf16[2,64,384]{2,1,0:T(8,128)(2,1)S(1)}, bf16[2,64,384]{2,1,0:T(8,128)(2,1)}, u32[]{:S(2)}, u32[]{:S(2)}) collective-permute-start(bf16[2,64,384]{2,1,0:T(8,128)(2,1)S(1)} %get-tuple-element.83), channel_id=1, source_target_pairs={{0,8},{8,0},{1,9},{9,1},{2,10},{10,2},{3,11},{11,3},{4,12},{12,4},... | collective-permute-start | bytes 294920 | tf_op jit(solution)/shard_map/ppermute | solution.py:463
  47.9 24.3 %collective-permute-start.5 = (bf16[3072,384]{1,0:T(8,128)(2,1)}, bf16[3072,384]{1,0:T(8,128)(2,1)}, u32[]{:S(2)}, u32[]{:S(2)}) collective-permute-start(bf16[3072,384]{1,0:T(8,128)(2,1)} %collective-permute-done.4.own_mate), channel_id=1, source_target_pairs={{0,128},{1,129},{2,130},{3,131},{4,132},{5,133},{6,134},{7,135},{8... | collective-permute-start | bytes 7077896 | tf_op jit(solution)/shard_map/ppermute | solution.py:476
  49.2 34.6 %collective-permute-start.6 = (bf16[384,3072]{1,0:T(8,128)(2,1)}, bf16[384,3072]{1,0:T(8,128)(2,1)}, u32[]{:S(2)}, u32[]{:S(2)}) collective-permute-start(bf16[384,3072]{1,0:T(8,128)(2,1)} %bitcast.58), channel_id=1, source_target_pairs={{128,136},{136,128},{129,137},{137,129},{130,138},{138,130},{131,1... | collective-permute-start | bytes 7077896 | tf_op jit(solution)/shard_map/ppermute | solution.py:472
  83.9 34.5 %collective-permute-start.7 = (bf16[384,3072]{1,0:T(8,128)(2,1)}, bf16[384,3072]{1,0:T(8,128)(2,1)}, u32[]{:S(2)}, u32[]{:S(2)}) collective-permute-start(bf16[384,3072]{1,0:T(8,128)(2,1)} %collective-permute-done.6.own_mate), channel_id=1, source_target_pairs={{128,0},{129,1},{130,2},{131,3},{132,4},{133,5},{134,6},{135,7},{1... | collective-permute-start | bytes 7077896 | tf_op jit(solution)/shard_map/ppermute | solution.py:476
  155.0 27.9 %all-to-all-start.4 = ((bf16[8,2,16,1536]{3,2,1,0:T(8,128)(2,1)}), bf16[8,2,16,1536]{3,2,1,0:T(8,128)(2,1)}, u32[]{:S(2)}, u32[]{:S(2)}) async-start(bf16[8,2,16,1536]{3,2,1,0:T(8,128)(2,1)} %shard_map.80), calls=%async_computation.4 | async-start | bytes 1572864 | tf_op jit(solution)/shard_map/all_to_all | solution.py:452
  159.3 7.9 %collective-permute-start.8 = (bf16[4,2,1,16,1536]{4,3,2,1,0:T(8,128)(2,1)}, bf16[4,2,1,16,1536]{4,3,2,1,0:T(8,128)(2,1)}, u32[]{:S(2)}, u32[]{:S(2)}) collective-permute-start(bf16[4,2,1,16,1536]{4,3,2,1,0:T(8,128)(2,1)} %bitcast.65), channel_id=1, source_target_pairs={{128,0},{129,1},{130,2},{131,3},{132,4},{133,5},{134,6},{135,7},{1... | collective-permute-start | bytes 1179656 | tf_op jit(solution)/shard_map/ppermute | solution.py:476
  162.3 4.8 %collective-permute-start.9 = (bf16[4,2,1,16,1536]{4,3,2,1,0:T(8,128)(2,1)}, bf16[4,2,1,16,1536]{4,3,2,1,0:T(8,128)(2,1)}, u32[]{:S(2)}, u32[]{:S(2)}) collective-permute-start(bf16[4,2,1,16,1536]{4,3,2,1,0:T(8,128)(2,1)} %bitcast.66), channel_id=1, source_target_pairs={{0,8},{8,0},{1,9},{9,1},{2,10},{10,2},{3,11},{11,3},{4,12},{12,4},... | collective-permute-start | bytes 1179656 | tf_op jit(solution)/shard_map/ppermute | solution.py:472
  163.8 8.9 %collective-permute-start.10 = (bf16[4,2,1,16,1536]{4,3,2,1,0:T(8,128)(2,1)}, bf16[4,2,1,16,1536]{4,3,2,1,0:T(8,128)(2,1)}, u32[]{:S(2)}, u32[]{:S(2)}) collective-permute-start(bf16[4,2,1,16,1536]{4,3,2,1,0:T(8,128)(2,1)} %bitcast.67), channel_id=1, source_target_pairs={{128,8},{136,0},{129,9},{137,1},{130,10},{138,2},{131,11},{139,3},... | collective-permute-start | bytes 1179656 | tf_op jit(solution)/shard_map/ppermute | solution.py:481
  214.0 19.8 %collective-permute-start.11 = (bf16[4,2,2,16,1536]{4,3,2,1,0:T(8,128)(2,1)}, bf16[4,2,2,16,1536]{4,3,2,1,0:T(8,128)(2,1)}, u32[]{:S(2)}, u32[]{:S(2)}) collective-permute-start(bf16[4,2,2,16,1536]{4,3,2,1,0:T(8,128)(2,1)} %bitcast.5.arrived_ref.refs_4_), channel_id=1, source_target_pairs={{0,128},{1,129},{2,130},{3,131},{4,132},{5,133},{6,134},{7,135},{8... | collective-permute-start | bytes 2359304 | tf_op jit(solution)/shard_map/ppermute | solution.py:476
  215.3 18.5 %collective-permute-start.12 = (bf16[4,2,2,16,1536]{4,3,2,1,0:T(8,128)(2,1)}, bf16[4,2,2,16,1536]{4,3,2,1,0:T(8,128)(2,1)}, u32[]{:S(2)}, u32[]{:S(2)}) collective-permute-start(bf16[4,2,2,16,1536]{4,3,2,1,0:T(8,128)(2,1)} %bitcast.5.arrived_ref.refs_4_), channel_id=1, source_target_pairs={{128,136},{136,128},{129,137},{137,129},{130,138},{138,130},{131,1... | collective-permute-start | bytes 2359304 | tf_op jit(solution)/shard_map/ppermute | solution.py:472
  217.3 16.5 %all-to-all-start.6 = ((bf16[8,1,16,1536]{3,2,1,0:T(8,128)(2,1)}), bf16[8,1,16,1536]{3,2,1,0:T(8,128)(2,1)}, u32[]{:S(2)}, u32[]{:S(2)}) async-start(bf16[8,1,16,1536]{3,2,1,0:T(8,128)(2,1)} %bitcast.73), calls=%async_computation.6 | async-start | bytes 786432 | tf_op jit(solution)/shard_map/all_to_all | solution.py:452
  223.1 25.8 %collective-permute-start.13 = (bf16[4,2,2,16,1536]{4,3,2,1,0:T(8,128)(2,1)}, bf16[4,2,2,16,1536]{4,3,2,1,0:T(8,128)(2,1)}, u32[]{:S(2)}, u32[]{:S(2)}) collective-permute-start(bf16[4,2,2,16,1536]{4,3,2,1,0:T(8,128)(2,1)} %bitcast.5.arrived_ref.refs_4_), channel_id=1, source_target_pairs={{0,136},{8,128},{1,137},{9,129},{2,138},{10,130},{3,139},{11,131},... | collective-permute-start | bytes 2359304 | tf_op jit(solution)/shard_map/ppermute | solution.py:481
  236.7 11.5 %copy-start = (bf16[64,384]{1,0:T(8,128)(2,1)S(1)}, bf16[64,384]{1,0:T(8,128)(2,1)}, u32[]{:S(2)}) copy-start(bf16[64,384]{1,0:T(8,128)(2,1)} %get-tuple-element.79) | copy-start | bytes 147460
  236.7 11.5 %copy-start.1 = (bf16[64,384]{1,0:T(8,128)(2,1)S(1)}, bf16[64,384]{1,0:T(8,128)(2,1)}, u32[]{:S(2)}) copy-start(bf16[64,384]{1,0:T(8,128)(2,1)} %get-tuple-element.80) | copy-start | bytes 147460
  236.7 11.5 %copy-start.2 = (bf16[64,384]{1,0:T(8,128)(2,1)S(1)}, bf16[64,384]{1,0:T(8,128)(2,1)}, u32[]{:S(2)}) copy-start(bf16[64,384]{1,0:T(8,128)(2,1)} %get-tuple-element.81) | copy-start | bytes 147460
  236.7 11.5 %copy-start.3 = (bf16[64,384]{1,0:T(8,128)(2,1)S(1)}, bf16[64,384]{1,0:T(8,128)(2,1)}, u32[]{:S(2)}) copy-start(bf16[64,384]{1,0:T(8,128)(2,1)} %get-tuple-element.82) | copy-start | bytes 147460
  237.7 10.2 %collective-permute-start.19 = (bf16[2,64,384]{2,1,0:T(8,128)(2,1)S(1)}, bf16[2,64,384]{2,1,0:T(8,128)(2,1)S(1)}, u32[]{:S(2)}, u32[]{:S(2)}) collective-permute-start(bf16[2,64,384]{2,1,0:T(8,128)(2,1)S(1)} %get-tuple-element.77), channel_id=1, source_target_pairs={{0,136},{136,0},{8,128},{128,8},{1,137},{137,1},{9,129},{129,9},{2... | collective-permute-start | bytes 294920 | tf_op jit(solution)/shard_map/ppermute | solution.py:467
  242.4 5.6 %collective-permute-start.18 = (bf16[2,64,384]{2,1,0:T(8,128)(2,1)S(1)}, bf16[2,64,384]{2,1,0:T(8,128)(2,1)S(1)}, u32[]{:S(2)}, u32[]{:S(2)}) collective-permute-start(bf16[2,64,384]{2,1,0:T(8,128)(2,1)S(1)} %get-tuple-element.77), channel_id=1, source_target_pairs={{0,8},{8,0},{1,9},{9,1},{2,10},{10,2},{3,11},{11,3},{4,12},{12,4},... | collective-permute-start | bytes 294920 | tf_op jit(solution)/shard_map/ppermute | solution.py:463
  242.4 5.5 %collective-permute-start.17 = (bf16[2,64,384]{2,1,0:T(8,128)(2,1)S(1)}, bf16[2,64,384]{2,1,0:T(8,128)(2,1)S(1)}, u32[]{:S(2)}, u32[]{:S(2)}) collective-permute-start(bf16[2,64,384]{2,1,0:T(8,128)(2,1)S(1)} %get-tuple-element.78), channel_id=1, source_target_pairs={{0,128},{128,0},{1,129},{129,1},{2,130},{130,2},{3,131},{131,3},{4... | collective-permute-start | bytes 294920 | tf_op jit(solution)/shard_map/ppermute | solution.py:459
  243.8 19.3 %all-to-all-start.7 = ((bf16[8,1,16,1536]{3,2,1,0:T(8,128)(2,1)}), bf16[8,1,16,1536]{3,2,1,0:T(8,128)(2,1)}, u32[]{:S(2)}, u32[]{:S(2)}) async-start(bf16[8,1,16,1536]{3,2,1,0:T(8,128)(2,1)} %shard_map.83), calls=%async_computation.7 | async-start | bytes 786432 | tf_op jit(solution)/shard_map/all_to_all | solution.py:452
  263.1 15.7 %collective-permute-start.14 = (bf16[4,2,1,16,1536]{4,3,2,1,0:T(8,128)(2,1)}, bf16[4,2,1,16,1536]{4,3,2,1,0:T(8,128)(2,1)}, u32[]{:S(2)}, u32[]{:S(2)}) collective-permute-start(bf16[4,2,1,16,1536]{4,3,2,1,0:T(8,128)(2,1)} %bitcast.7.refs_0_), channel_id=1, source_target_pairs={{128,0},{129,1},{130,2},{131,3},{132,4},{133,5},{134,6},{135,7},{1... | collective-permute-start | bytes 1179656 | tf_op jit(solution)/shard_map/ppermute | solution.py:476
  266.2 12.6 %collective-permute-start.15 = (bf16[4,2,1,16,1536]{4,3,2,1,0:T(8,128)(2,1)}, bf16[4,2,1,16,1536]{4,3,2,1,0:T(8,128)(2,1)}, u32[]{:S(2)}, u32[]{:S(2)}) collective-permute-start(bf16[4,2,1,16,1536]{4,3,2,1,0:T(8,128)(2,1)} %bitcast.7.refs_0_), channel_id=1, source_target_pairs={{0,8},{8,0},{1,9},{9,1},{2,10},{10,2},{3,11},{11,3},{4,12},{12,4},... | collective-permute-start | bytes 1179656 | tf_op jit(solution)/shard_map/ppermute | solution.py:472
  267.6 11.2 %collective-permute-start.16 = (bf16[4,2,1,16,1536]{4,3,2,1,0:T(8,128)(2,1)}, bf16[4,2,1,16,1536]{4,3,2,1,0:T(8,128)(2,1)}, u32[]{:S(2)}, u32[]{:S(2)}) collective-permute-start(bf16[4,2,1,16,1536]{4,3,2,1,0:T(8,128)(2,1)} %bitcast.7.refs_0_), channel_id=1, source_target_pairs={{128,8},{136,0},{129,9},{137,1},{130,10},{138,2},{131,11},{139,3},... | collective-permute-start | bytes 1179656 | tf_op jit(solution)/shard_map/ppermute | solution.py:481
  282.9 12.3 %all-to-all-start.8 = ((bf16[8,2,16,384]{3,2,1,0:T(8,128)(2,1)}), bf16[8,2,16,384]{3,2,1,0:T(8,128)(2,1)}, u32[]{:S(2)}, u32[]{:S(2)}) async-start(bf16[8,2,16,384]{3,2,1,0:T(8,128)(2,1)} %shard_map.85), calls=%async_computation.8 | async-start | bytes 393216 | tf_op jit(solution)/shard_map/all_to_all | solution.py:452

commit v6 on v5

--- a/solution.py
+++ b/solution.py
@@ -509,23 +509,22 @@
     def halves_of(pair, which):
         return lax.dynamic_slice_in_dim(pair, which * half_len, half_len, 1)
 
-    mate_down0 = only_to_mate(own_down, 0)
     other_up = to_other_core(own_up)
+    ends = jnp.stack([batch(inputs, section), batch(cotangent, section)])
+    bases = halves_of(ends, mate_pos), to_mate(halves_of(ends, 1 - mate_pos))
+    mate_down0 = only_to_mate(late(own_down, bases), 0)
     (pre0,) = first_product(0, False, True, inputs, own_up, other_up, blocks)
     arrived = exchange(pre0.reshape((2 * rings, 1) + piece), ("z", "x_lo"))
 
     other_down = to_other_core(late(own_down, other_up))
-    x0, g2 = late((inputs, cotangent), pre0)
-    keep, send = first_product(1, True, False, g2, own_down, other_down, blocks)
+    keep, send = first_product(1, True, False, late(cotangent, pre0), own_down, other_down, blocks)
     d_hid1 = keep, to_mate(send)
-    ends = jnp.stack([batch(x0, section), batch(g2, section)])
-    bases = halves_of(ends, mate_pos), to_mate(halves_of(ends, 1 - mate_pos))
-    arrived = late(arrived, (bases, d_hid1))
-
-    mate_up1 = only_to_mate(late(own_up, arrived), 1)
+
     mate_down0 = late(mate_down0, arrived)
     down0 = own_down, other_down, mate_down0, only_to_core(mate_down0, 1)
     value0, slope0 = activation(act_first, arrived, 1, outs=1, peers=rings)
+    value0 = late(value0, d_hid1)
+    mate_up1 = only_to_mate(late(own_up, value0), 1)
     hid0 = exchange(value0, "z").reshape(blocks[:2] + (1,) + piece)
     part = narrow(0, True, hid0, down0, lax.axis_size(col))
     mate_up1 = late(mate_up1, part)
@@ -541,10 +540,9 @@
     arrived = exchange(part, col)
 
     d_hid0, g1 = widen(0, True, arrived, 1, bases, down0, blocks)
-    acts1s = to_owner(late(acts1, d_hid0), 1)
+    acts1, both1 = late((acts1, jnp.stack([x1, g1])), d_hid0)
+    acts1s = to_owner(acts1, 1)
     arrived = exchange(d_hid0.reshape((rings, 1) + piece), "z")
-    (d_pre0,) = activation(act_back, late(arrived, acts1s[1:3]), 1, ins=(slope0,))
-    both1 = late(jnp.stack([x1, g1]), d_pre0)
     near, far = both1[..., :width], both1[..., width:]
     both1 = jnp.stack([near, to_other_core(near), to_mate(far), to_other_core_of_mate(far)])
     both1 = both1.reshape((2, 2) + near.shape)
@@ -562,7 +560,8 @@
     xs = jnp.where(first, all_tokens(inputs), x1s)
     gs = jnp.where(first, g1s, all_tokens(cotangent))
 
-    d_pre0 = late(exchange(d_pre0, "z").reshape(blocks[:2] + (1,) + piece), acts1s[3])
+    (d_pre0,) = activation(act_back, arrived, 1, ins=(slope0,))
+    d_pre0 = late(exchange(d_pre0, "z").reshape(blocks[:2] + (1,) + piece), acts1s)
     down_grad = weight_grad(True, late(gs, d_pre0), hid0s, acts1s)
     d_pre0s = late(to_owner(d_pre0, 0), down_grad)
 

time: 298 us -> 296 us (level)
    ppermute x3, waiting for transfers between devices: 17.7 us -> 4.94 us  [to_mate(): return lax.ppermute(block, 'x_lo', [(0, 1), (1, 0)])]
    ppermute x5, waiting for transfers between devices: 7.04 us -> 12.1 us  [only_to_mate(): return lax.ppermute(block, CORES, [(at, at + 1), (at + 1, at)])]
    all_to_all x5, waiting for transfers between devices: 33 us -> 37 us  [exchange(): return lax.all_to_all(blocks, axes, 0, 0)]
    ppermute x5, starting transfers between devices: 22.9 us -> 19.2 us  [only_to_core(): return lax.ppermute(block, 'section', [(1 - section, section)])]
    ppermute x1, starting transfers between devices: 4.65 us -> 1.58 us  [to_other_core_of_mate(): return lax.ppermute(block, CORES, [(0, 3), (3, 0), (1, 2), (2, 1)])]
  transfers between devices with their start and end apart: 25 -> 25, of which waited for: 8 -> 10; matrix products, arithmetic and copies ran while one was open for 4% -> 4% of each run, Pallas kernels for 10% -> 11%
where the time goes in v6:
time: 296 us; the launch traced here: 295 us
  blocking collectives  83.3 us (28%)
  starting transfers between devices  74.8 us (25%)
  waiting for transfers between devices  65 us (22%)
  Pallas kernels  58.4 us (20%)
  local copies, waits for them, and re-layouts  7.2 us (2%)
  other arithmetic  4.85 us (2%)
    all_to_all x4, blocking collectives, exchange(): return lax.all_to_all(blocks, axes, 0, 0)  83.3 us
    pallas_call x11, Pallas kernels, kernel_call(): pl.pallas_call(body, out_shape=outs, in_specs=in_specs, out_specs=out_spe...  46 us
    all_to_all x5, waiting for transfers between devices, exchange(): return lax.all_to_all(blocks, axes, 0, 0)  37 us
    all_to_all x5, starting transfers between devices, exchange(): return lax.all_to_all(blocks, axes, 0, 0)  26.8 us
    ppermute x5, starting transfers between devices, only_to_core(): return lax.ppermute(block, 'section', [(1 - section, section)])  19.2 us
    pallas_call x2, Pallas kernels, weight_grad(): pl.pallas_call(grad_down_kernel if down else grad_up_kernel, out_shape=sh...  12.4 us
    ppermute x5, waiting for transfers between devices, only_to_mate(): return lax.ppermute(block, CORES, [(at, at + 1), (at + 1, at)])  12.1 us
    ppermute x5, starting transfers between devices, only_to_mate(): return lax.ppermute(block, CORES, [(at, at + 1), (at + 1, at)])  10.3 us
  transfers between devices with their start and end apart: 25, of which 10 were waited for; matrix products, arithmetic and copies ran while one was open for 4% of the time, Pallas kernels for 11%

profile of v6, /device:TPU:1, one launch (start us, length us, event | category | flops | bytes accessed | tf_op | source)
XLA Modules:
  0.0 294.6 jit_solution(6598816341902540804)
XLA Ops:
  0.6 3.3 %collective-permute-start = (bf16[384,3072]{1,0:T(8,128)(2,1)}, bf16[384,3072]{1,0:T(8,128)(2,1)}, u32[]{:S(2)}, u32[]{:S(2)}) collective-permute-start(bf16[384,3072]{1,0:T(8,128)(2,1)} %bitcast.56), channel_id=1, source_target_pairs={{0,128},{128,0},{1,129},{129,1},{2,130},{130,2},{3,131},{131,3},{4... | collective-permute-start | bytes 7077896 | tf_op jit(solution)/shard_map/ppermute | solution.py:459
  4.0 4.5 %collective-permute-done.other = bf16[384,3072]{1,0:T(8,128)(2,1)} collective-permute-done((bf16[384,3072]{1,0:T(8,128)(2,1)}, bf16[384,3072]{1,0:T(8,128)(2,1)}, u32[]{:S(2)}, u32[]{:S(2)}) %collective-permute-start) | collective-permute-done | bytes 2359328 | tf_op jit(solution)/shard_map/ppermute | solution.py:459
  11.3 4.4 %collective-permute-done.3.base_mate = bf16[2,64,384]{2,1,0:T(8,128)(2,1)} collective-permute-done((bf16[2,64,384]{2,1,0:T(8,128)(2,1)S(1)}, bf16[2,64,384]{2,1,0:T(8,128)(2,1)}, u32[]{:S(2)}, u32[]{:S(2)}) %collective-permute-start.3) | collective-permute-done | bytes 98336 | tf_op jit(solution)/shard_map/ppermute | solution.py:463
  15.7 2.1 collective-permute-start.4
  17.8 4.2 %shard_map.75 = bf16[4,2,2,16,1536]{4,3,2,1,0:T(8,128)(2,1)} custom-call(bf16[2,128,384]{2,1,0:T(8,128)(2,1)} %x_ref.1, bf16[384,3072]{1,0:T(8,128)(2,1)} %bitcast.57, bf16[384,3072]{1,0:T(8,128)(2,1)} %collective-permute-done.other), custom_call_target="tpu_custom_call" | custom-call | flops 301989888 | bytes 2359296 | tf_op jit(solution)/shard_map/pallas_call | solution.py:180
  21.9 7.5 %all-to-all-start = ((bf16[16,1,16,1536]{3,2,1,0:T(8,128)(2,1)}), bf16[16,1,16,1536]{3,2,1,0:T(8,128)(2,1)}, u32[]{:S(2)}, u32[]{:S(2)}) async-start(bf16[16,1,16,1536]{3,2,1,0:T(8,128)(2,1)} %bitcast.69), calls=%async_computation | async-start | bytes 1572864 | tf_op jit(solution)/shard_map/all_to_all | solution.py:452
  29.5 4.3 %shard_map.77 = (bf16[4,2,16,1536]{3,2,1,0:T(8,128)(2,1)}, bf16[4,2,16,1536]{3,2,1,0:T(8,128)(2,1)}) custom-call(bf16[2,128,384]{2,1,0:T(8,128)(2,1)} %x_ref.2, bf16[3072,384]{1,0:T(8,128)(2,1)} %bitcast.52, bf16[3072,384]{1,0:T(8,128)(2,1)} %collective-permute-done.1.other), custom_call_target="tpu_custom_call" | custom-call | flops 301989888 | bytes 2359296 | tf_op jit(solution)/shard_map/pallas_call | solution.py:180
  33.8 1.4 collective-permute-start.2
  35.2 14.2 %all-to-all-done.arrived_ref = bf16[16,1,16,1536]{3,2,1,0:T(8,128)(2,1)} async-done(((bf16[16,1,16,1536]{3,2,1,0:T(8,128)(2,1)}), bf16[16,1,16,1536]{3,2,1,0:T(8,128)(2,1)}, u32[]{:S(2)}, u32[]{:S(2)}) %all-to-all-start) | async-done | bytes 786464 | tf_op jit(solution)/shard_map/all_to_all | solution.py:452
  49.4 1.3 collective-permute-start.5
  50.7 2.7 shard_map.76
  53.4 2.4 collective-permute-start.6
  55.8 16.9 %all_to_all.45 = bf16[8,1,16,1536]{3,2,1,0:T(8,128)(2,1)} all-to-all(bf16[8,1,16,1536]{3,2,1,0:T(8,128)(2,1)} %get-tuple-element.41), channel_id=1, replica_groups=mesh['section'=2,'z'=8,'x_lo'=2,'y'=4,'x_hi'=2] {'z'}, dimensions={0} | all-to-all | bytes 786432 | tf_op jit(solution)/shard_map/all_to_all | solution.py:452
  72.7 4.6 %shard_map.78 = bf16[8,64,768]{2,1,0:T(8,128)(2,1)} custom-call(bf16[4,2,1,16,1536]{4,3,2,1,0:T(8,128)(2,1)} %bitcast.64, bf16[3072,384]{1,0:T(8,128)(2,1)} %bitcast.53, bf16[3072,384]{1,0:T(8,128)(2,1)} %collective-permute-done.1.other, bf16[3072,384]{1,0:T(8,128)(2,1)} %collective-permute-done.4.own_mate, bf16[3072,384]{1,0:T(8,128)(2,1)} %collective-permute-done.5.other_mate), custom_call_target="tpu_custom_call" | custom-call | flops 301989888 | bytes 4718592 | tf_op jit(solution)/shard_map/pallas_call | solution.py:180
  77.3 12.1 %collective-permute-done.6.own_mate = bf16[384,3072]{1,0:T(8,128)(2,1)} collective-permute-done((bf16[384,3072]{1,0:T(8,128)(2,1)}, bf16[384,3072]{1,0:T(8,128)(2,1)}, u32[]{:S(2)}, u32[]{:S(2)}) %collective-permute-start.6) | collective-permute-done | bytes 2359328 | tf_op jit(solution)/shard_map/ppermute | solution.py:472
  89.4 10.5 %collective-permute-start.7 = (bf16[384,3072]{1,0:T(8,128)(2,1)}, bf16[384,3072]{1,0:T(8,128)(2,1)}, u32[]{:S(2)}, u32[]{:S(2)}) collective-permute-start(bf16[384,3072]{1,0:T(8,128)(2,1)} %collective-permute-done.6.own_mate), channel_id=1, source_target_pairs={{128,0},{129,1},{130,2},{131,3},{132,4},{133,5},{134,6},{135,7},{1... | collective-permute-start | bytes 7077896 | tf_op jit(solution)/shard_map/ppermute | solution.py:476
  99.9 20.5 %all_to_all.46.arrived_ref = bf16[8,64,768]{2,1,0:T(8,128)(2,1)} all-to-all(bf16[8,64,768]{2,1,0:T(8,128)(2,1)} %shard_map.78), channel_id=1, replica_groups=mesh['section'=2,'z'=8,'x_lo'=2,'y'=4,'x_hi'=2] {'y','x_hi'}, dimensions={0} | all-to-all | bytes 1572864 | tf_op jit(solution)/shard_map/all_to_all | solution.py:452
  120.4 6.9 %shard_map.79 = (bf16[4,2,2,16,1536]{4,3,2,1,0:T(8,128)(2,1)}, bf16[64,768]{1,0:T(8,128)(2,1)}) custom-call(bf16[8,64,768]{2,1,0:T(8,128)(2,1)} %all_to_all.46.arrived_ref, bf16[2,64,384]{2,1,0:T(8,128)(2,1)} %get-tuple-element.82.base, bf16[2,64,384]{2,1,0:T(8,128)(2,1)} %collective-permute-done.3.base_mate, bf16[384,3072]{1,0:T(8,128)(2,1)} %bitcast.59, ...), custom_call_target="tpu_custom_call" | custom-call | flops 301989888 | bytes 4718592 | tf_op jit(solution)/shard_map/pallas_call | solution.py:180
  127.3 27.5 %all_to_all.47.arrived_ref = bf16[8,2,16,1536]{3,2,1,0:T(8,128)(2,1)} all-to-all(bf16[8,2,16,1536]{3,2,1,0:T(8,128)(2,1)} %bitcast.72), channel_id=1, replica_groups=mesh['section'=2,'z'=8,'x_lo'=2,'y'=4,'x_hi'=2] {'z'}, dimensions={0} | all-to-all | bytes 1572864 | tf_op jit(solution)/shard_map/all_to_all | solution.py:452
  154.9 2.1 shard_map.80
  157.0 4.2 %all-to-all-start.4 = ((bf16[8,2,16,1536]{3,2,1,0:T(8,128)(2,1)}), bf16[8,2,16,1536]{3,2,1,0:T(8,128)(2,1)}, u32[]{:S(2)}, u32[]{:S(2)}) async-start(bf16[8,2,16,1536]{3,2,1,0:T(8,128)(2,1)} %shard_map.80), calls=%async_computation.4 | async-start | bytes 1572864 | tf_op jit(solution)/shard_map/all_to_all | solution.py:452
  161.2 3.1 %collective-permute-start.8 = (bf16[4,2,1,16,1536]{4,3,2,1,0:T(8,128)(2,1)}, bf16[4,2,1,16,1536]{4,3,2,1,0:T(8,128)(2,1)}, u32[]{:S(2)}, u32[]{:S(2)}) collective-permute-start(bf16[4,2,1,16,1536]{4,3,2,1,0:T(8,128)(2,1)} %bitcast.65), channel_id=1, source_target_pairs={{128,0},{129,1},{130,2},{131,3},{132,4},{133,5},{134,6},{135,7},{1... | collective-permute-start | bytes 1179656 | tf_op jit(solution)/shard_map/ppermute | solution.py:476
  164.3 1.4 collective-permute-start.9
  165.7 3.4 %collective-permute-start.10 = (bf16[4,2,1,16,1536]{4,3,2,1,0:T(8,128)(2,1)}, bf16[4,2,1,16,1536]{4,3,2,1,0:T(8,128)(2,1)}, u32[]{:S(2)}, u32[]{:S(2)}) collective-permute-start(bf16[4,2,1,16,1536]{4,3,2,1,0:T(8,128)(2,1)} %bitcast.67), channel_id=1, source_target_pairs={{128,8},{136,0},{129,9},{137,1},{130,10},{138,2},{131,11},{139,3},... | collective-permute-start | bytes 1179656 | tf_op jit(solution)/shard_map/ppermute | solution.py:481
  169.1 5.8 %collective-permute-done.10.refs_3_ = bf16[4,2,1,16,1536]{4,3,2,1,0:T(8,128)(2,1)} collective-permute-done((bf16[4,2,1,16,1536]{4,3,2,1,0:T(8,128)(2,1)}, bf16[4,2,1,16,1536]{4,3,2,1,0:T(8,128)(2,1)}, u32[]{:S(2)}, u32[]{:S(2)}) %collective-permute-start.10) | collective-permute-done | bytes 393248 | tf_op jit(solution)/shard_map/ppermute | solution.py:481
  174.9 9.9 %all-to-all-done.4 = bf16[8,2,16,1536]{3,2,1,0:T(8,128)(2,1)} async-done(((bf16[8,2,16,1536]{3,2,1,0:T(8,128)(2,1)}), bf16[8,2,16,1536]{3,2,1,0:T(8,128)(2,1)}, u32[]{:S(2)}, u32[]{:S(2)}) %all-to-all-start.4) | async-done | bytes 786464 | tf_op jit(solution)/shard_map/all_to_all | solution.py:452
  184.9 5.6 %shard_map.81 = bf16[8,64,768]{2,1,0:T(8,128)(2,1)} custom-call(bf16[4,2,2,16,1536]{4,3,2,1,0:T(8,128)(2,1)} %bitcast.5.arrived_ref.refs_4_, bf16[384,3072]{1,0:T(8,128)(2,1)} %bitcast.60, bf16[384,3072]{1,0:T(8,128)(2,1)} %collective-permute-done.other, bf16[384,3072]{1,0:T(8,128)(2,1)} %collective-permute-done.6.own_mate, ...), custom_call_target="tpu_custom_call" | custom-call | flops 301989888 | bytes 4718592 | tf_op jit(solution)/shard_map/pallas_call | solution.py:180
  190.5 18.4 %all_to_all.48.arrived_ref = bf16[8,64,768]{2,1,0:T(8,128)(2,1)} all-to-all(bf16[8,64,768]{2,1,0:T(8,128)(2,1)} %shard_map.81), channel_id=1, replica_groups=mesh['section'=2,'z'=8,'x_lo'=2,'y'=4,'x_hi'=2] {'y','x_hi'}, dimensions={0} | all-to-all | bytes 1572864 | tf_op jit(solution)/shard_map/all_to_all | solution.py:452
  208.9 7.1 %shard_map.82 = (bf16[4,2,1,16,1536]{4,3,2,1,0:T(8,128)(2,1)}, bf16[64,768]{1,0:T(8,128)(2,1)}) custom-call(bf16[8,64,768]{2,1,0:T(8,128)(2,1)} %all_to_all.48.arrived_ref, bf16[2,64,384]{2,1,0:T(8,128)(2,1)} %get-tuple-element.82.base, bf16[2,64,384]{2,1,0:T(8,128)(2,1)} %collective-permute-done.3.base_mate, bf16[3072,384]{1,0:T(8,128)(2,1)} %bitcast.54, ...), custom_call_target="tpu_custom_call" | custom-call | flops 301989888 | bytes 4718592 | tf_op jit(solution)/shard_map/pallas_call | solution.py:180
  216.0 4.1 %all-to-all-start.6 = ((bf16[8,1,16,1536]{3,2,1,0:T(8,128)(2,1)}), bf16[8,1,16,1536]{3,2,1,0:T(8,128)(2,1)}, u32[]{:S(2)}, u32[]{:S(2)}) async-start(bf16[8,1,16,1536]{3,2,1,0:T(8,128)(2,1)} %bitcast.73), calls=%async_computation.6 | async-start | bytes 786432 | tf_op jit(solution)/shard_map/all_to_all | solution.py:452
  221.9 1.6 collective-permute-start.19
  223.5 1.6 dynamic-slice_bitcast_fusion.7
  226.4 3.0 %collective-permute-start.12 = (bf16[4,2,2,16,1536]{4,3,2,1,0:T(8,128)(2,1)}, bf16[4,2,2,16,1536]{4,3,2,1,0:T(8,128)(2,1)}, u32[]{:S(2)}, u32[]{:S(2)}) collective-permute-start(bf16[4,2,2,16,1536]{4,3,2,1,0:T(8,128)(2,1)} %bitcast.5.arrived_ref.refs_4_), channel_id=1, source_target_pairs={{128,136},{136,128},{129,137},{137,129},{130,138},{138,130},{131,1... | collective-permute-start | bytes 2359304 | tf_op jit(solution)/shard_map/ppermute | solution.py:472
  229.4 1.3 collective-permute-start.13
  231.1 3.2 %collective-permute-start.17 = (bf16[2,64,384]{2,1,0:T(8,128)(2,1)}, bf16[2,64,384]{2,1,0:T(8,128)(2,1)}, u32[]{:S(2)}, u32[]{:S(2)}) collective-permute-start(bf16[2,64,384]{2,1,0:T(8,128)(2,1)} %get-tuple-element.76), channel_id=1, source_target_pairs={{0,128},{128,0},{1,129},{129,1},{2,130},{130,2},{3,131},{131,3},{4... | collective-permute-start | bytes 294920 | tf_op jit(solution)/shard_map/ppermute | solution.py:459
  234.3 1.6 dynamic-slice_bitcast_fusion.3
  235.9 2.8 shard_map.83
  238.8 6.9 %all-to-all-start.7 = ((bf16[8,1,16,1536]{3,2,1,0:T(8,128)(2,1)}), bf16[8,1,16,1536]{3,2,1,0:T(8,128)(2,1)}, u32[]{:S(2)}, u32[]{:S(2)}) async-start(bf16[8,1,16,1536]{3,2,1,0:T(8,128)(2,1)} %shard_map.83), calls=%async_computation.7 | async-start | bytes 786432 | tf_op jit(solution)/shard_map/all_to_all | solution.py:452
  248.9 12.1 %all-to-all-done.7 = bf16[8,1,16,1536]{3,2,1,0:T(8,128)(2,1)} async-done(((bf16[8,1,16,1536]{3,2,1,0:T(8,128)(2,1)}), bf16[8,1,16,1536]{3,2,1,0:T(8,128)(2,1)}, u32[]{:S(2)}, u32[]{:S(2)}) %all-to-all-start.7) | async-done | bytes 393248 | tf_op jit(solution)/shard_map/all_to_all | solution.py:452
  261.0 3.1 %collective-permute-start.14 = (bf16[4,2,1,16,1536]{4,3,2,1,0:T(8,128)(2,1)}, bf16[4,2,1,16,1536]{4,3,2,1,0:T(8,128)(2,1)}, u32[]{:S(2)}, u32[]{:S(2)}) collective-permute-start(bf16[4,2,1,16,1536]{4,3,2,1,0:T(8,128)(2,1)} %bitcast.7.refs_0_), channel_id=1, source_target_pairs={{128,0},{129,1},{130,2},{131,3},{132,4},{133,5},{134,6},{135,7},{1... | collective-permute-start | bytes 1179656 | tf_op jit(solution)/shard_map/ppermute | solution.py:476
  264.1 1.4 collective-permute-start.15
  265.5 3.5 %collective-permute-start.16 = (bf16[4,2,1,16,1536]{4,3,2,1,0:T(8,128)(2,1)}, bf16[4,2,1,16,1536]{4,3,2,1,0:T(8,128)(2,1)}, u32[]{:S(2)}, u32[]{:S(2)}) collective-permute-start(bf16[4,2,1,16,1536]{4,3,2,1,0:T(8,128)(2,1)} %bitcast.7.refs_0_), channel_id=1, source_target_pairs={{128,8},{136,0},{129,9},{137,1},{130,10},{138,2},{131,11},{139,3},... | collective-permute-start | bytes 1179656 | tf_op jit(solution)/shard_map/ppermute | solution.py:481
  270.4 6.3 %shard_map.84 = f32[3072,384]{1,0:T(8,128)} custom-call(bf16[256,384]{1,0:T(8,128)(2,1)} %maximum_select_fusion.g_ref, bf16[4,2,1,16,1536]{4,3,2,1,0:T(8,128)(2,1)} %bitcast.68, bf16[4,2,1,16,1536]{4,3,2,1,0:T(8,128)(2,1)} %collective-permute-done.8.refs_1_, bf16[4,2,1,16,1536]{4,3,2,1,0:T(8,128)(2,1)} %collective-permute-done.9.refs_2_, ...), custom_call_target="tpu_custom_call" | custom-call | flops 603979776 | bytes 4718592 | tf_op jit(solution)/shard_map/pallas_call | solution.py:374
  276.7 4.0 %shard_map.85 = bf16[8,2,16,384]{3,2,1,0:T(8,128)(2,1)} custom-call(bf16[384,3072]{1,0:T(8,128)(2,1)} %bitcast.61, bf16[3072,384]{1,0:T(8,128)(2,1)} %bitcast.55, bf16[4,2,1,16,1536]{4,3,2,1,0:T(8,128)(2,1)} %bitcast.7.refs_0_, bf16[4,2,1,16,1536]{4,3,2,1,0:T(8,128)(2,1)} %collective-permute-done.14.refs_1_, ...), custom_call_target="tpu_custom_call" | custom-call | flops 603979776 | bytes 7077888 | tf_op jit(solution)/shard_map/pallas_call | solution.py:180
  280.8 4.0 %all-to-all-start.8 = ((bf16[8,2,16,384]{3,2,1,0:T(8,128)(2,1)}), bf16[8,2,16,384]{3,2,1,0:T(8,128)(2,1)}, u32[]{:S(2)}, u32[]{:S(2)}) async-start(bf16[8,2,16,384]{3,2,1,0:T(8,128)(2,1)} %shard_map.85), calls=%async_computation.8 | async-start | bytes 393216 | tf_op jit(solution)/shard_map/all_to_all | solution.py:452
  284.8 1.4 slice_bitcast_fusion
  286.2 6.0 %shard_map.87 = f32[384,3072]{1,0:T(8,128)} custom-call(bf16[256,384]{1,0:T(8,128)(2,1)} %maximum_select_fusion.1.x_ref, bf16[4,2,1,16,1536]{4,3,2,1,0:T(8,128)(2,1)} %bitcast.7.refs_0_, bf16[4,2,1,16,1536]{4,3,2,1,0:T(8,128)(2,1)} %collective-permute-done.14.refs_1_, bf16[4,2,1,16,1536]{4,3,2,1,0:T(8,128)(2,1)} %collective-permute-done.15.refs_2_, ...), custom_call_target="tpu_custom_call" | custom-call | flops 603979776 | bytes 4718592 | tf_op jit(solution)/shard_map/pallas_call | solution.py:374
  293.1 1.6 shard_map.86
  (49 shorter events, 11.6 us)
Async XLA Ops:
  0.6 7.8 %collective-permute-start = (bf16[384,3072]{1,0:T(8,128)(2,1)}, bf16[384,3072]{1,0:T(8,128)(2,1)}, u32[]{:S(2)}, u32[]{:S(2)}) collective-permute-start(bf16[384,3072]{1,0:T(8,128)(2,1)} %bitcast.56), channel_id=1, source_target_pairs={{0,128},{128,0},{1,129},{129,1},{2,130},{130,2},{3,131},{131,3},{4... | collective-permute-start | bytes 7077896 | tf_op jit(solution)/shard_map/ppermute | solution.py:459
  8.5 21.0 %collective-permute-start.1 = (bf16[3072,384]{1,0:T(8,128)(2,1)}, bf16[3072,384]{1,0:T(8,128)(2,1)}, u32[]{:S(2)}, u32[]{:S(2)}) collective-permute-start(bf16[3072,384]{1,0:T(8,128)(2,1)} %bitcast.50), channel_id=1, source_target_pairs={{0,128},{128,0},{1,129},{129,1},{2,130},{130,2},{3,131},{131,3},{4... | collective-permute-start | bytes 7077896 | tf_op jit(solution)/shard_map/ppermute | solution.py:459
  11.3 4.4 %collective-permute-start.3 = (bf16[2,64,384]{2,1,0:T(8,128)(2,1)S(1)}, bf16[2,64,384]{2,1,0:T(8,128)(2,1)}, u32[]{:S(2)}, u32[]{:S(2)}) collective-permute-start(bf16[2,64,384]{2,1,0:T(8,128)(2,1)S(1)} %get-tuple-element.81), channel_id=1, source_target_pairs={{0,8},{8,0},{1,9},{9,1},{2,10},{10,2},{3,11},{11,3},{4,12},{12,4},... | collective-permute-start | bytes 294920 | tf_op jit(solution)/shard_map/ppermute | solution.py:463
  15.7 19.6 %collective-permute-start.4 = (bf16[3072,384]{1,0:T(8,128)(2,1)}, bf16[3072,384]{1,0:T(8,128)(2,1)}, u32[]{:S(2)}, u32[]{:S(2)}) collective-permute-start(bf16[3072,384]{1,0:T(8,128)(2,1)} %bitcast.51), channel_id=1, source_target_pairs={{0,8},{8,0},{1,9},{9,1},{2,10},{10,2},{3,11},{11,3},{4,12},{12,4},... | collective-permute-start | bytes 7077896 | tf_op jit(solution)/shard_map/ppermute | solution.py:472
  21.9 27.5 %all-to-all-start = ((bf16[16,1,16,1536]{3,2,1,0:T(8,128)(2,1)}), bf16[16,1,16,1536]{3,2,1,0:T(8,128)(2,1)}, u32[]{:S(2)}, u32[]{:S(2)}) async-start(bf16[16,1,16,1536]{3,2,1,0:T(8,128)(2,1)} %bitcast.69), calls=%async_computation | async-start | bytes 1572864 | tf_op jit(solution)/shard_map/all_to_all | solution.py:452
  33.8 19.6 %collective-permute-start.2 = (bf16[4,2,16,1536]{3,2,1,0:T(8,128)(2,1)}, bf16[4,2,16,1536]{3,2,1,0:T(8,128)(2,1)}, u32[]{:S(2)}, u32[]{:S(2)}) collective-permute-start(bf16[4,2,16,1536]{3,2,1,0:T(8,128)(2,1)} %get-tuple-element.40), channel_id=1, source_target_pairs={{0,8},{8,0},{1,9},{9,1},{2,10},{10,2},{3,11},{11,3},{4,12},{12,4},... | collective-permute-start | bytes 1179656 | tf_op jit(solution)/shard_map/ppermute | solution.py:463
  49.4 23.3 %collective-permute-start.5 = (bf16[3072,384]{1,0:T(8,128)(2,1)}, bf16[3072,384]{1,0:T(8,128)(2,1)}, u32[]{:S(2)}, u32[]{:S(2)}) collective-permute-start(bf16[3072,384]{1,0:T(8,128)(2,1)} %collective-permute-done.4.own_mate), channel_id=1, source_target_pairs={{0,128},{1,129},{2,130},{3,131},{4,132},{5,133},{6,134},{7,135},{8... | collective-permute-start | bytes 7077896 | tf_op jit(solution)/shard_map/ppermute | solution.py:476
  53.4 36.0 %collective-permute-start.6 = (bf16[384,3072]{1,0:T(8,128)(2,1)}, bf16[384,3072]{1,0:T(8,128)(2,1)}, u32[]{:S(2)}, u32[]{:S(2)}) collective-permute-start(bf16[384,3072]{1,0:T(8,128)(2,1)} %bitcast.58), channel_id=1, source_target_pairs={{128,136},{136,128},{129,137},{137,129},{130,138},{138,130},{131,1... | collective-permute-start | bytes 7077896 | tf_op jit(solution)/shard_map/ppermute | solution.py:472
  89.4 31.0 %collective-permute-start.7 = (bf16[384,3072]{1,0:T(8,128)(2,1)}, bf16[384,3072]{1,0:T(8,128)(2,1)}, u32[]{:S(2)}, u32[]{:S(2)}) collective-permute-start(bf16[384,3072]{1,0:T(8,128)(2,1)} %collective-permute-done.6.own_mate), channel_id=1, source_target_pairs={{128,0},{129,1},{130,2},{131,3},{132,4},{133,5},{134,6},{135,7},{1... | collective-permute-start | bytes 7077896 | tf_op jit(solution)/shard_map/ppermute | solution.py:476
  157.0 27.9 %all-to-all-start.4 = ((bf16[8,2,16,1536]{3,2,1,0:T(8,128)(2,1)}), bf16[8,2,16,1536]{3,2,1,0:T(8,128)(2,1)}, u32[]{:S(2)}, u32[]{:S(2)}) async-start(bf16[8,2,16,1536]{3,2,1,0:T(8,128)(2,1)} %shard_map.80), calls=%async_computation.4 | async-start | bytes 1572864 | tf_op jit(solution)/shard_map/all_to_all | solution.py:452
  161.2 7.9 %collective-permute-start.8 = (bf16[4,2,1,16,1536]{4,3,2,1,0:T(8,128)(2,1)}, bf16[4,2,1,16,1536]{4,3,2,1,0:T(8,128)(2,1)}, u32[]{:S(2)}, u32[]{:S(2)}) collective-permute-start(bf16[4,2,1,16,1536]{4,3,2,1,0:T(8,128)(2,1)} %bitcast.65), channel_id=1, source_target_pairs={{128,0},{129,1},{130,2},{131,3},{132,4},{133,5},{134,6},{135,7},{1... | collective-permute-start | bytes 1179656 | tf_op jit(solution)/shard_map/ppermute | solution.py:476
  164.3 4.8 %collective-permute-start.9 = (bf16[4,2,1,16,1536]{4,3,2,1,0:T(8,128)(2,1)}, bf16[4,2,1,16,1536]{4,3,2,1,0:T(8,128)(2,1)}, u32[]{:S(2)}, u32[]{:S(2)}) collective-permute-start(bf16[4,2,1,16,1536]{4,3,2,1,0:T(8,128)(2,1)} %bitcast.66), channel_id=1, source_target_pairs={{0,8},{8,0},{1,9},{9,1},{2,10},{10,2},{3,11},{11,3},{4,12},{12,4},... | collective-permute-start | bytes 1179656 | tf_op jit(solution)/shard_map/ppermute | solution.py:472
  165.7 9.2 %collective-permute-start.10 = (bf16[4,2,1,16,1536]{4,3,2,1,0:T(8,128)(2,1)}, bf16[4,2,1,16,1536]{4,3,2,1,0:T(8,128)(2,1)}, u32[]{:S(2)}, u32[]{:S(2)}) collective-permute-start(bf16[4,2,1,16,1536]{4,3,2,1,0:T(8,128)(2,1)} %bitcast.67), channel_id=1, source_target_pairs={{128,8},{136,0},{129,9},{137,1},{130,10},{138,2},{131,11},{139,3},... | collective-permute-start | bytes 1179656 | tf_op jit(solution)/shard_map/ppermute | solution.py:481
  216.0 19.9 %all-to-all-start.6 = ((bf16[8,1,16,1536]{3,2,1,0:T(8,128)(2,1)}), bf16[8,1,16,1536]{3,2,1,0:T(8,128)(2,1)}, u32[]{:S(2)}, u32[]{:S(2)}) async-start(bf16[8,1,16,1536]{3,2,1,0:T(8,128)(2,1)} %bitcast.73), calls=%async_computation.6 | async-start | bytes 786432 | tf_op jit(solution)/shard_map/all_to_all | solution.py:452
  221.9 9.2 %collective-permute-start.19 = (bf16[2,64,384]{2,1,0:T(8,128)(2,1)}, bf16[2,64,384]{2,1,0:T(8,128)(2,1)}, u32[]{:S(2)}, u32[]{:S(2)}) collective-permute-start(bf16[2,64,384]{2,1,0:T(8,128)(2,1)} %get-tuple-element.75), channel_id=1, source_target_pairs={{0,136},{136,0},{8,128},{128,8},{1,137},{137,1},{9,129},{129,9},{2... | collective-permute-start | bytes 294920 | tf_op jit(solution)/shard_map/ppermute | solution.py:467
  225.1 23.2 %collective-permute-start.11 = (bf16[4,2,2,16,1536]{4,3,2,1,0:T(8,128)(2,1)}, bf16[4,2,2,16,1536]{4,3,2,1,0:T(8,128)(2,1)}, u32[]{:S(2)}, u32[]{:S(2)}) collective-permute-start(bf16[4,2,2,16,1536]{4,3,2,1,0:T(8,128)(2,1)} %bitcast.5.arrived_ref.refs_4_), channel_id=1, source_target_pairs={{0,128},{1,129},{2,130},{3,131},{4,132},{5,133},{6,134},{7,135},{8... | collective-permute-start | bytes 2359304 | tf_op jit(solution)/shard_map/ppermute | solution.py:476
  226.4 21.9 %collective-permute-start.12 = (bf16[4,2,2,16,1536]{4,3,2,1,0:T(8,128)(2,1)}, bf16[4,2,2,16,1536]{4,3,2,1,0:T(8,128)(2,1)}, u32[]{:S(2)}, u32[]{:S(2)}) collective-permute-start(bf16[4,2,2,16,1536]{4,3,2,1,0:T(8,128)(2,1)} %bitcast.5.arrived_ref.refs_4_), channel_id=1, source_target_pairs={{128,136},{136,128},{129,137},{137,129},{130,138},{138,130},{131,1... | collective-permute-start | bytes 2359304 | tf_op jit(solution)/shard_map/ppermute | solution.py:472
  229.4 19.5 %collective-permute-start.13 = (bf16[4,2,2,16,1536]{4,3,2,1,0:T(8,128)(2,1)}, bf16[4,2,2,16,1536]{4,3,2,1,0:T(8,128)(2,1)}, u32[]{:S(2)}, u32[]{:S(2)}) collective-permute-start(bf16[4,2,2,16,1536]{4,3,2,1,0:T(8,128)(2,1)} %bitcast.5.arrived_ref.refs_4_), channel_id=1, source_target_pairs={{0,136},{8,128},{1,137},{9,129},{2,138},{10,130},{3,139},{11,131},... | collective-permute-start | bytes 2359304 | tf_op jit(solution)/shard_map/ppermute | solution.py:481
  230.7 15.6 %collective-permute-start.18 = (bf16[2,64,384]{2,1,0:T(8,128)(2,1)}, bf16[2,64,384]{2,1,0:T(8,128)(2,1)}, u32[]{:S(2)}, u32[]{:S(2)}) collective-permute-start(bf16[2,64,384]{2,1,0:T(8,128)(2,1)} %get-tuple-element.75), channel_id=1, source_target_pairs={{0,8},{8,0},{1,9},{9,1},{2,10},{10,2},{3,11},{11,3},{4,12},{12,4},... | collective-permute-start | bytes 294920 | tf_op jit(solution)/shard_map/ppermute | solution.py:463
  231.1 15.2 %collective-permute-start.17 = (bf16[2,64,384]{2,1,0:T(8,128)(2,1)}, bf16[2,64,384]{2,1,0:T(8,128)(2,1)}, u32[]{:S(2)}, u32[]{:S(2)}) collective-permute-start(bf16[2,64,384]{2,1,0:T(8,128)(2,1)} %get-tuple-element.76), channel_id=1, source_target_pairs={{0,128},{128,0},{1,129},{129,1},{2,130},{130,2},{3,131},{131,3},{4... | collective-permute-start | bytes 294920 | tf_op jit(solution)/shard_map/ppermute | solution.py:459
  238.8 8.8 %copy-start.4 = (bf16[64,384]{1,0:T(8,128)(2,1)S(1)}, bf16[64,384]{1,0:T(8,128)(2,1)}, u32[]{:S(2)}) copy-start(bf16[64,384]{1,0:T(8,128)(2,1)} %get-tuple-element.77) | copy-start | bytes 147460
  238.8 8.8 %copy-start.5 = (bf16[64,384]{1,0:T(8,128)(2,1)S(1)}, bf16[64,384]{1,0:T(8,128)(2,1)}, u32[]{:S(2)}) copy-start(bf16[64,384]{1,0:T(8,128)(2,1)} %get-tuple-element.78) | copy-start | bytes 147460
  238.8 8.8 %copy-start.6 = (bf16[64,384]{1,0:T(8,128)(2,1)S(1)}, bf16[64,384]{1,0:T(8,128)(2,1)}, u32[]{:S(2)}) copy-start(bf16[64,384]{1,0:T(8,128)(2,1)} %get-tuple-element.79) | copy-start | bytes 147460
  238.8 8.8 %copy-start.7 = (bf16[64,384]{1,0:T(8,128)(2,1)S(1)}, bf16[64,384]{1,0:T(8,128)(2,1)}, u32[]{:S(2)}) copy-start(bf16[64,384]{1,0:T(8,128)(2,1)} %get-tuple-element.80) | copy-start | bytes 147460
  238.8 30.8 %copy-start = (bf16[64,384]{1,0:T(8,128)(2,1)S(1)}, bf16[64,384]{1,0:T(8,128)(2,1)}, u32[]{:S(2)}) copy-start(bf16[64,384]{1,0:T(8,128)(2,1)} %get-tuple-element.70) | copy-start | bytes 147460
  238.8 30.8 %copy-start.1 = (bf16[64,384]{1,0:T(8,128)(2,1)S(1)}, bf16[64,384]{1,0:T(8,128)(2,1)}, u32[]{:S(2)}) copy-start(bf16[64,384]{1,0:T(8,128)(2,1)} %get-tuple-element.71) | copy-start | bytes 147460
  238.8 30.8 %copy-start.2 = (bf16[64,384]{1,0:T(8,128)(2,1)S(1)}, bf16[64,384]{1,0:T(8,128)(2,1)}, u32[]{:S(2)}) copy-start(bf16[64,384]{1,0:T(8,128)(2,1)} %get-tuple-element.72) | copy-start | bytes 147460
  238.8 30.8 %copy-start.3 = (bf16[64,384]{1,0:T(8,128)(2,1)S(1)}, bf16[64,384]{1,0:T(8,128)(2,1)}, u32[]{:S(2)}) copy-start(bf16[64,384]{1,0:T(8,128)(2,1)} %get-tuple-element.73) | copy-start | bytes 147460
  238.8 22.2 %all-to-all-start.7 = ((bf16[8,1,16,1536]{3,2,1,0:T(8,128)(2,1)}), bf16[8,1,16,1536]{3,2,1,0:T(8,128)(2,1)}, u32[]{:S(2)}, u32[]{:S(2)}) async-start(bf16[8,1,16,1536]{3,2,1,0:T(8,128)(2,1)} %shard_map.83), calls=%async_computation.7 | async-start | bytes 786432 | tf_op jit(solution)/shard_map/all_to_all | solution.py:452
  261.0 15.7 %collective-permute-start.14 = (bf16[4,2,1,16,1536]{4,3,2,1,0:T(8,128)(2,1)}, bf16[4,2,1,16,1536]{4,3,2,1,0:T(8,128)(2,1)}, u32[]{:S(2)}, u32[]{:S(2)}) collective-permute-start(bf16[4,2,1,16,1536]{4,3,2,1,0:T(8,128)(2,1)} %bitcast.7.refs_0_), channel_id=1, source_target_pairs={{128,0},{129,1},{130,2},{131,3},{132,4},{133,5},{134,6},{135,7},{1... | collective-permute-start | bytes 1179656 | tf_op jit(solution)/shard_map/ppermute | solution.py:476
  264.1 12.6 %collective-permute-start.15 = (bf16[4,2,1,16,1536]{4,3,2,1,0:T(8,128)(2,1)}, bf16[4,2,1,16,1536]{4,3,2,1,0:T(8,128)(2,1)}, u32[]{:S(2)}, u32[]{:S(2)}) collective-permute-start(bf16[4,2,1,16,1536]{4,3,2,1,0:T(8,128)(2,1)} %bitcast.7.refs_0_), channel_id=1, source_target_pairs={{0,8},{8,0},{1,9},{9,1},{2,10},{10,2},{3,11},{11,3},{4,12},{12,4},... | collective-permute-start | bytes 1179656 | tf_op jit(solution)/shard_map/ppermute | solution.py:472
  265.5 11.2 %collective-permute-start.16 = (bf16[4,2,1,16,1536]{4,3,2,1,0:T(8,128)(2,1)}, bf16[4,2,1,16,1536]{4,3,2,1,0:T(8,128)(2,1)}, u32[]{:S(2)}, u32[]{:S(2)}) collective-permute-start(bf16[4,2,1,16,1536]{4,3,2,1,0:T(8,128)(2,1)} %bitcast.7.refs_0_), channel_id=1, source_target_pairs={{128,8},{136,0},{129,9},{137,1},{130,10},{138,2},{131,11},{139,3},... | collective-permute-start | bytes 1179656 | tf_op jit(solution)/shard_map/ppermute | solution.py:481
  280.8 12.3 %all-to-all-start.8 = ((bf16[8,2,16,384]{3,2,1,0:T(8,128)(2,1)}), bf16[8,2,16,384]{3,2,1,0:T(8,128)(2,1)}, u32[]{:S(2)}, u32[]{:S(2)}) async-start(bf16[8,2,16,384]{3,2,1,0:T(8,128)(2,1)} %shard_map.85), calls=%async_computation.8 | async-start | bytes 393216 | tf_op jit(solution)/shard_map/all_to_all | solution.py:452

commit v7 on v2

--- a/solution.py
+++ b/solution.py
@@ -90,19 +90,24 @@
 
 
 def widen_next_kernel(layer, by_rows, riders, arrived, base, own, other, own_mate, other_mate, *rest):
-    out_ref, x_out, held, sems, stage, out_sems = rest[riders:]
+    out_ref, x_out, held, sems, stage, out_sems = rest[riders : riders + 6]
+    rides, in_sems = rest[riders + 6 :] if riders else (None, None)
+    arrivals = [pltpu.make_async_copy(rest[i], rides.at[i], in_sems.at[i]) for i in range(riders)]
+    copies = [
+        pltpu.make_async_copy(rides.at[i], out_ref.at[:, :, 1 + i], out_sems.at[2 + i]) for i in range(riders)
+    ]
+    for copy in arrivals:
+        copy.start()
     wait = load_weights(layer, by_rows, ((own, other), (own_mate, other_mate)), held, sems)
-    copies = [
-        pltpu.make_async_copy(rest[i], out_ref.at[:, :, 1 + i], out_sems.at[2 + i]) for i in range(riders)
-    ]
-    for copy in copies:
-        copy.start()
     width, per_half = base.shape[1] // 2, stage.shape[3] // CHUNK
     total = arrived[0].astype(f32)
     for i in range(1, arrived.shape[0]):
         total = total + arrived[i].astype(f32)
     x = (base[...].astype(f32) + total).astype(bf16)
     x_out[...] = x
+    for arrival, copy in zip(arrivals, copies):
+        arrival.wait()
+        copy.start()
 
     def out_copy(half):
         return pltpu.make_async_copy(stage.at[:, half], out_ref.at[:, half, 0], out_sems.at[half])
@@ -190,7 +195,8 @@
         (HBM, VMEM),
         [VMEM, VMEM] + [HBM] * (4 + len(riders)),
         held_scratch(weights[0], by_rows, 2)
-        + [pltpu.VMEM(blocks, bf16), pltpu.SemaphoreType.DMA((2 + len(riders),))],
+        + [pltpu.VMEM(blocks, bf16), pltpu.SemaphoreType.DMA((2 + len(riders),))]
+        + ([pltpu.VMEM((len(riders),) + blocks, bf16), pltpu.SemaphoreType.DMA((len(riders),))] if riders else []),
         (arrived, base) + weights + riders,
         flops=4 * base.shape[0] * weights[0].size,
         moved=4 * weights[0].size,
@@ -266,6 +272,25 @@
         flops=2000000,
         moved=2000000,
     )
+
+
+def finish_kernel(arrived, x1, g1, states, grads):
+    total = arrived[0].astype(f32)
+    for i in range(1, arrived.shape[0]):
+        total = total + arrived[i].astype(f32)
+
+    def ended(base):
+        return (base[...].astype(f32) + total).astype(bf16)
+
+    @pl.when(lax.axis_index("section") == 0)
+    def _():
+        states[...] = x1[...]
+        grads[...] = ended(g1)
+
+    @pl.when(lax.axis_index("section") == 1)
+    def _():
+        states[...] = ended(x1)
+        grads[...] = g1[...]
 
 
 def pick_copies(layer0, layer1, kind, held, sems, start):
@@ -526,10 +551,16 @@
     pieces = lax.dynamic_index_in_dim(both1, away, 0, keepdims=False)
     pieces = lax.dynamic_slice_in_dim(pieces, (col_pos % per_half) * out_len, out_len, 2)
     pieces = jnp.where(first, pieces, pieces[::-1])
-    x1, g1 = pieces[:, 0], pieces[:, 1]
-    ended = jnp.sum(arrived.astype(f32), axis=0)
-    ended = (jnp.where(first, g1, x1).astype(f32) + ended).astype(bf16)
-    states, grads = jnp.where(first, x1, ended), jnp.where(first, ended, g1)
+    states, grads = kernel_call(
+        finish_kernel,
+        [shape_of(pieces[:, 0].shape)] * 2,
+        [VMEM] * 2,
+        [VMEM] * 3,
+        [],
+        (arrived, pieces[:, 0], pieces[:, 1]),
+        flops=100000,
+        moved=200000,
+    )
     return states[None], grads[None], up_grad[None], down_grad[None]
 
 

time: 280 us -> 273 us (0.975)
  Pallas kernels: 63.4 us -> 56.7 us
  other arithmetic: 10.9 us -> 6.3 us
  starting transfers between devices: 69.6 us -> 72.7 us
    pallas_call x10 -> x11, Pallas kernels: 51 us -> 44.4 us  [kernel_call(): pl.pallas_call(body, out_shape=outs, in_specs=in_specs, out_specs=out_spe...]
    ppermute x1, waiting for transfers between devices: 5.74 us -> 0.01 us  [to_other_core_of_mate(): return lax.ppermute(block, CORES, [(0, 3), (3, 0), (1, 2), (2, 1)])]
    all_to_all x6, waiting for transfers between devices: 31.2 us -> 34.3 us  [exchange(): return lax.all_to_all(blocks, axes, 0, 0)]
    ppermute x3, starting transfers between devices: 3.7 us -> 6.52 us  [to_other_core(): return lax.ppermute(block, 'section', [(0, 1), (1, 0)])]
  transfers between devices with their start and end apart: 27 -> 27, of which waited for: 10 -> 9; matrix products, arithmetic and copies ran while one was open for 6% -> 6% of each run, Pallas kernels for 11% -> 11%
where the time goes in v7:
time: 273 us; the launch traced here: 271 us
  starting transfers between devices  72.7 us (27%)
  waiting for transfers between devices  72.4 us (27%)
  Pallas kernels  56.7 us (21%)
  blocking collectives  51.8 us (19%)
  local copies, waits for them, and re-layouts  9.69 us (4%)
  other arithmetic  6.3 us (2%)
    all_to_all x3, blocking collectives, exchange(): return lax.all_to_all(blocks, axes, 0, 0)  51.8 us
    pallas_call x11, Pallas kernels, kernel_call(): pl.pallas_call(body, out_shape=outs, in_specs=in_specs, out_specs=out_spe...  44.4 us
    all_to_all x6, waiting for transfers between devices, exchange(): return lax.all_to_all(blocks, axes, 0, 0)  34.3 us
    all_to_all x6, starting transfers between devices, exchange(): return lax.all_to_all(blocks, axes, 0, 0)  33.9 us
    ppermute x4, waiting for transfers between devices, to_mate(): return lax.ppermute(block, 'x_lo', [(0, 1), (1, 0)])  28.6 us
    pallas_call x2, Pallas kernels, weight_grad(): pl.pallas_call(grad_down_kernel if down else grad_up_kernel, out_shape=sh...  12.4 us
    ppermute x5, starting transfers between devices, only_to_core(): return lax.ppermute(block, 'section', [(1 - section, section)])  10.4 us
    ppermute x5, starting transfers between devices, only_to_mate(): return lax.ppermute(block, CORES, [(at, at + 1), (at + 1, at)])  9.85 us
  transfers between devices with their start and end apart: 27, of which 9 were waited for; matrix products, arithmetic and copies ran while one was open for 6% of the time, Pallas kernels for 11%

profile of v7, /device:TPU:1, one launch (start us, length us, event | category | flops | bytes accessed | tf_op | source)
XLA Modules:
  0.0 270.6 jit_solution(17864068603560566919)
XLA Ops:
  0.6 3.3 %collective-permute-start = (bf16[384,3072]{1,0:T(8,128)(2,1)}, bf16[384,3072]{1,0:T(8,128)(2,1)}, u32[]{:S(2)}, u32[]{:S(2)}) collective-permute-start(bf16[384,3072]{1,0:T(8,128)(2,1)} %bitcast.65), channel_id=1, source_target_pairs={{0,128},{128,0},{1,129},{129,1},{2,130},{130,2},{3,131},{131,3},{4... | collective-permute-start | bytes 7077896 | tf_op jit(solution)/shard_map/ppermute | solution.py:436
  4.0 4.5 %collective-permute-done.other = bf16[384,3072]{1,0:T(8,128)(2,1)} collective-permute-done((bf16[384,3072]{1,0:T(8,128)(2,1)}, bf16[384,3072]{1,0:T(8,128)(2,1)}, u32[]{:S(2)}, u32[]{:S(2)}) %collective-permute-start) | collective-permute-done | bytes 2359328 | tf_op jit(solution)/shard_map/ppermute | solution.py:436
  8.8 2.1 collective-permute-start.1
  10.9 1.6 dynamic-slice_bitcast_fusion.1
  12.6 4.1 %shard_map.75 = bf16[4,2,2,16,1536]{4,3,2,1,0:T(8,128)(2,1)} custom-call(bf16[128,384]{1,0:T(8,128)(2,1)} %get-tuple-element.47.x_ref, bf16[384,3072]{1,0:T(8,128)(2,1)} %bitcast.66, bf16[384,3072]{1,0:T(8,128)(2,1)} %collective-permute-done.other), custom_call_target="tpu_custom_call" | custom-call | flops 301989888 | bytes 2359296 | tf_op jit(solution)/shard_map/pallas_call | solution.py:166
  16.7 7.5 %all-to-all-start = ((bf16[16,1,16,1536]{3,2,1,0:T(8,128)(2,1)}), bf16[16,1,16,1536]{3,2,1,0:T(8,128)(2,1)}, u32[]{:S(2)}, u32[]{:S(2)}) async-start(bf16[16,1,16,1536]{3,2,1,0:T(8,128)(2,1)} %bitcast.73), calls=%async_computation | async-start | bytes 1572864 | tf_op jit(solution)/shard_map/all_to_all | solution.py:429
  24.2 4.3 %shard_map.76 = bf16[2,4,2,16,1536]{4,3,2,1,0:T(8,128)(2,1)} custom-call(bf16[128,384]{1,0:T(8,128)(2,1)} %get-tuple-element.48.x_ref, bf16[3072,384]{1,0:T(8,128)(2,1)} %bitcast.61, bf16[3072,384]{1,0:T(8,128)(2,1)} %collective-permute-done.2.other), custom_call_target="tpu_custom_call" | custom-call | flops 301989888 | bytes 2359296 | tf_op jit(solution)/shard_map/pallas_call | solution.py:166
  28.5 16.5 %all-to-all-done.arrived = bf16[16,1,16,1536]{3,2,1,0:T(8,128)(2,1)} async-done(((bf16[16,1,16,1536]{3,2,1,0:T(8,128)(2,1)}), bf16[16,1,16,1536]{3,2,1,0:T(8,128)(2,1)}, u32[]{:S(2)}, u32[]{:S(2)}) %all-to-all-start) | async-done | bytes 786464 | tf_op jit(solution)/shard_map/all_to_all | solution.py:429
  45.1 1.3 collective-permute-start.4
  46.4 2.7 %shard_map.77 = (bf16[8,1,16,1536]{3,2,1,0:T(8,128)(2,1)}, f32[16,1536]{1,0:T(8,128)}) custom-call(bf16[16,1,16,1536]{3,2,1,0:T(8,128)(2,1)} %all-to-all-done.arrived), custom_call_target="tpu_custom_call" | custom-call | flops 2000000 | bytes 2000000 | tf_op jit(solution)/shard_map/pallas_call | solution.py:166
  49.1 2.1 collective-permute-start.5
  51.2 5.4 %all-to-all-start.1 = ((bf16[8,1,16,1536]{3,2,1,0:T(8,128)(2,1)}), bf16[8,1,16,1536]{3,2,1,0:T(8,128)(2,1)}, u32[]{:S(2)}, u32[]{:S(2)}) async-start(bf16[8,1,16,1536]{3,2,1,0:T(8,128)(2,1)} %get-tuple-element.42), calls=%async_computation.1 | async-start | bytes 786432 | tf_op jit(solution)/shard_map/all_to_all | solution.py:429
  62.2 26.8 %collective-permute-done.6 = bf16[64,384]{1,0:T(8,128)(2,1)S(1)} collective-permute-done((bf16[64,384]{1,0:T(8,128)(2,1)S(1)}, bf16[64,384]{1,0:T(8,128)(2,1)S(1)}, u32[]{:S(2)}, u32[]{:S(2)}) %collective-permute-start.6) | collective-permute-done | bytes 49184 | tf_op jit(solution)/shard_map/ppermute | solution.py:440
  91.2 5.2 %shard_map.78 = bf16[8,64,768]{2,1,0:T(8,128)(2,1)} custom-call(bf16[4,2,1,16,1536]{4,3,2,1,0:T(8,128)(2,1)} %bitcast.5.arrived.refs_0_, bf16[3072,384]{1,0:T(8,128)(2,1)} %bitcast.62, bf16[3072,384]{1,0:T(8,128)(2,1)} %collective-permute-done.2.other, bf16[3072,384]{1,0:T(8,128)(2,1)} %collective-permute-done.1.own_mate, ...), custom_call_target="tpu_custom_call" | custom-call | flops 301989888 | bytes 4718592 | tf_op jit(solution)/shard_map/pallas_call | solution.py:166
  96.4 2.7 %collective-permute-start.8 = (bf16[384,3072]{1,0:T(8,128)(2,1)}, bf16[384,3072]{1,0:T(8,128)(2,1)}, u32[]{:S(2)}, u32[]{:S(2)}) collective-permute-start(bf16[384,3072]{1,0:T(8,128)(2,1)} %collective-permute-done.5.own_mate), channel_id=1, source_target_pairs={{128,0},{129,1},{130,2},{131,3},{132,4},{133,5},{134,6},{135,7},{1... | collective-permute-start | bytes 7077896 | tf_op jit(solution)/shard_map/ppermute | solution.py:453
  99.1 16.8 %all_to_all.45.arrived = bf16[8,64,768]{2,1,0:T(8,128)(2,1)} all-to-all(bf16[8,64,768]{2,1,0:T(8,128)(2,1)} %shard_map.78), channel_id=1, replica_groups=mesh['section'=2,'z'=8,'x_lo'=2,'y'=4,'x_hi'=2] {'y','x_hi'}, dimensions={0} | all-to-all | bytes 1572864 | tf_op jit(solution)/shard_map/all_to_all | solution.py:429
  115.9 6.8 %shard_map.79 = (bf16[4,2,2,16,1536]{4,3,2,1,0:T(8,128)(2,1)}, bf16[64,768]{1,0:T(8,128)(2,1)}) custom-call(bf16[8,64,768]{2,1,0:T(8,128)(2,1)} %all_to_all.45.arrived, bf16[64,768]{1,0:T(8,128)(2,1)} %pad_maximum_fusion.2.base, bf16[384,3072]{1,0:T(8,128)(2,1)} %bitcast.68, bf16[384,3072]{1,0:T(8,128)(2,1)} %collective-permute-done.other, ...), custom_call_target="tpu_custom_call" | custom-call | flops 301989888 | bytes 4718592 | tf_op jit(solution)/shard_map/pallas_call | solution.py:166
  122.6 20.4 %all_to_all.46.arrived = bf16[8,2,16,1536]{3,2,1,0:T(8,128)(2,1)} all-to-all(bf16[8,2,16,1536]{3,2,1,0:T(8,128)(2,1)} %bitcast.76), channel_id=1, replica_groups=mesh['section'=2,'z'=8,'x_lo'=2,'y'=4,'x_hi'=2] {'z'}, dimensions={0} | all-to-all | bytes 1572864 | tf_op jit(solution)/shard_map/all_to_all | solution.py:429
  143.0 2.2 shard_map.80
  145.2 4.2 %all-to-all-start.4 = ((bf16[8,2,16,1536]{3,2,1,0:T(8,128)(2,1)}), bf16[8,2,16,1536]{3,2,1,0:T(8,128)(2,1)}, u32[]{:S(2)}, u32[]{:S(2)}) async-start(bf16[8,2,16,1536]{3,2,1,0:T(8,128)(2,1)} %shard_map.80), calls=%async_computation.4 | async-start | bytes 1572864 | tf_op jit(solution)/shard_map/all_to_all | solution.py:429
  149.5 2.0 collective-permute-start.9
  151.5 1.4 collective-permute-start.10
  152.9 2.0 collective-permute-start.11
  155.0 4.3 %collective-permute-done.11.refs_3_ = bf16[4,2,1,16,1536]{4,3,2,1,0:T(8,128)(2,1)} collective-permute-done((bf16[4,2,1,16,1536]{4,3,2,1,0:T(8,128)(2,1)}, bf16[4,2,1,16,1536]{4,3,2,1,0:T(8,128)(2,1)}, u32[]{:S(2)}, u32[]{:S(2)}) %collective-permute-start.11) | collective-permute-done | bytes 393248 | tf_op jit(solution)/shard_map/ppermute | solution.py:458
  159.2 6.2 %all-to-all-done.4 = bf16[8,2,16,1536]{3,2,1,0:T(8,128)(2,1)} async-done(((bf16[8,2,16,1536]{3,2,1,0:T(8,128)(2,1)}), bf16[8,2,16,1536]{3,2,1,0:T(8,128)(2,1)}, u32[]{:S(2)}, u32[]{:S(2)}) %all-to-all-start.4) | async-done | bytes 786464 | tf_op jit(solution)/shard_map/all_to_all | solution.py:429
  165.4 5.6 %shard_map.81 = bf16[8,64,768]{2,1,0:T(8,128)(2,1)} custom-call(bf16[4,2,2,16,1536]{4,3,2,1,0:T(8,128)(2,1)} %bitcast.9.arrived.refs_4_, bf16[384,3072]{1,0:T(8,128)(2,1)} %bitcast.69, bf16[384,3072]{1,0:T(8,128)(2,1)} %collective-permute-done.other, bf16[384,3072]{1,0:T(8,128)(2,1)} %collective-permute-done.5.own_mate, ...), custom_call_target="tpu_custom_call" | custom-call | flops 301989888 | bytes 4718592 | tf_op jit(solution)/shard_map/pallas_call | solution.py:166
  171.0 14.7 %all_to_all.47.arrived = bf16[8,64,768]{2,1,0:T(8,128)(2,1)} all-to-all(bf16[8,64,768]{2,1,0:T(8,128)(2,1)} %shard_map.81), channel_id=1, replica_groups=mesh['section'=2,'z'=8,'x_lo'=2,'y'=4,'x_hi'=2] {'y','x_hi'}, dimensions={0} | all-to-all | bytes 1572864 | tf_op jit(solution)/shard_map/all_to_all | solution.py:429
  185.6 6.1 %shard_map.82 = (bf16[4,2,1,16,1536]{4,3,2,1,0:T(8,128)(2,1)}, bf16[64,768]{1,0:T(8,128)(2,1)}) custom-call(bf16[8,64,768]{2,1,0:T(8,128)(2,1)} %all_to_all.47.arrived, bf16[64,768]{1,0:T(8,128)(2,1)} %pad_maximum_fusion.3.base, bf16[3072,384]{1,0:T(8,128)(2,1)} %bitcast.63, bf16[3072,384]{1,0:T(8,128)(2,1)} %collective-permute-done.2.other, ...), custom_call_target="tpu_custom_call" | custom-call | flops 301989888 | bytes 4718592 | tf_op jit(solution)/shard_map/pallas_call | solution.py:166
  191.7 5.7 %all-to-all-start.6 = ((bf16[8,1,16,1536]{3,2,1,0:T(8,128)(2,1)}), bf16[8,1,16,1536]{3,2,1,0:T(8,128)(2,1)}, u32[]{:S(2)}, u32[]{:S(2)}) async-start(bf16[8,1,16,1536]{3,2,1,0:T(8,128)(2,1)} %bitcast.77), calls=%async_computation.6 | async-start | bytes 786432 | tf_op jit(solution)/shard_map/all_to_all | solution.py:429
  199.0 1.4 collective-permute-start.20
  200.5 1.6 dynamic-slice_bitcast_fusion.10
  203.3 2.8 %collective-permute-start.13 = (bf16[4,2,2,16,1536]{4,3,2,1,0:T(8,128)(2,1)}, bf16[4,2,2,16,1536]{4,3,2,1,0:T(8,128)(2,1)}, u32[]{:S(2)}, u32[]{:S(2)}) collective-permute-start(bf16[4,2,2,16,1536]{4,3,2,1,0:T(8,128)(2,1)} %bitcast.9.arrived.refs_4_), channel_id=1, source_target_pairs={{128,136},{136,128},{129,137},{137,129},{130,138},{138,130},{131,1... | collective-permute-start | bytes 2359304 | tf_op jit(solution)/shard_map/ppermute | solution.py:449
  206.2 1.3 collective-permute-start.14
  208.3 2.8 %collective-permute-start.18 = (bf16[2,64,384]{2,1,0:T(8,128)(2,1)}, bf16[2,64,384]{2,1,0:T(8,128)(2,1)}, u32[]{:S(2)}, u32[]{:S(2)}) collective-permute-start(bf16[2,64,384]{2,1,0:T(8,128)(2,1)} %get-tuple-element.82), channel_id=1, source_target_pairs={{0,128},{128,0},{1,129},{129,1},{2,130},{130,2},{3,131},{131,3},{4... | collective-permute-start | bytes 294920 | tf_op jit(solution)/shard_map/ppermute | solution.py:436
  211.1 1.6 dynamic-slice_bitcast_fusion.6
  212.7 1.9 shard_map.83
  214.7 7.1 %all-to-all-start.7 = ((bf16[8,1,16,1536]{3,2,1,0:T(8,128)(2,1)}), bf16[8,1,16,1536]{3,2,1,0:T(8,128)(2,1)}, u32[]{:S(2)}, u32[]{:S(2)}) async-start(bf16[8,1,16,1536]{3,2,1,0:T(8,128)(2,1)} %shard_map.83), calls=%async_computation.7 | async-start | bytes 786432 | tf_op jit(solution)/shard_map/all_to_all | solution.py:429
  221.7 1.7 collective-permute-done.19
  226.2 10.8 %all-to-all-done.7 = bf16[8,1,16,1536]{3,2,1,0:T(8,128)(2,1)} async-done(((bf16[8,1,16,1536]{3,2,1,0:T(8,128)(2,1)}), bf16[8,1,16,1536]{3,2,1,0:T(8,128)(2,1)}, u32[]{:S(2)}, u32[]{:S(2)}) %all-to-all-start.7) | async-done | bytes 393248 | tf_op jit(solution)/shard_map/all_to_all | solution.py:429
  237.0 3.1 %collective-permute-start.15 = (bf16[4,2,1,16,1536]{4,3,2,1,0:T(8,128)(2,1)}, bf16[4,2,1,16,1536]{4,3,2,1,0:T(8,128)(2,1)}, u32[]{:S(2)}, u32[]{:S(2)}) collective-permute-start(bf16[4,2,1,16,1536]{4,3,2,1,0:T(8,128)(2,1)} %bitcast.11.refs_0_), channel_id=1, source_target_pairs={{128,0},{129,1},{130,2},{131,3},{132,4},{133,5},{134,6},{135,7},{1... | collective-permute-start | bytes 1179656 | tf_op jit(solution)/shard_map/ppermute | solution.py:453
  240.1 1.4 collective-permute-start.16
  241.5 3.5 %collective-permute-start.17 = (bf16[4,2,1,16,1536]{4,3,2,1,0:T(8,128)(2,1)}, bf16[4,2,1,16,1536]{4,3,2,1,0:T(8,128)(2,1)}, u32[]{:S(2)}, u32[]{:S(2)}) collective-permute-start(bf16[4,2,1,16,1536]{4,3,2,1,0:T(8,128)(2,1)} %bitcast.11.refs_0_), channel_id=1, source_target_pairs={{128,8},{136,0},{129,9},{137,1},{130,10},{138,2},{131,11},{139,3},... | collective-permute-start | bytes 1179656 | tf_op jit(solution)/shard_map/ppermute | solution.py:458
  246.4 6.3 %shard_map.84 = f32[3072,384]{1,0:T(8,128)} custom-call(bf16[256,384]{1,0:T(8,128)(2,1)} %maximum_select_fusion.g_ref, bf16[4,2,1,16,1536]{4,3,2,1,0:T(8,128)(2,1)} %bitcast.5.arrived.refs_0_, bf16[4,2,1,16,1536]{4,3,2,1,0:T(8,128)(2,1)} %collective-permute-done.9.refs_1_, bf16[4,2,1,16,1536]{4,3,2,1,0:T(8,128)(2,1)} %collective-permute-done.10.refs_2_, ...), custom_call_target="tpu_custom_call" | custom-call | flops 603979776 | bytes 4718592 | tf_op jit(solution)/shard_map/pallas_call | solution.py:351
  252.7 4.0 %shard_map.85 = bf16[8,2,16,384]{3,2,1,0:T(8,128)(2,1)} custom-call(bf16[384,3072]{1,0:T(8,128)(2,1)} %bitcast.70, bf16[3072,384]{1,0:T(8,128)(2,1)} %bitcast.64, bf16[4,2,1,16,1536]{4,3,2,1,0:T(8,128)(2,1)} %bitcast.11.refs_0_, bf16[4,2,1,16,1536]{4,3,2,1,0:T(8,128)(2,1)} %collective-permute-done.15.refs_1_, ...), custom_call_target="tpu_custom_call" | custom-call | flops 603979776 | bytes 7077888 | tf_op jit(solution)/shard_map/pallas_call | solution.py:166
  256.8 4.0 %all-to-all-start.8 = ((bf16[8,2,16,384]{3,2,1,0:T(8,128)(2,1)}), bf16[8,2,16,384]{3,2,1,0:T(8,128)(2,1)}, u32[]{:S(2)}, u32[]{:S(2)}) async-start(bf16[8,2,16,384]{3,2,1,0:T(8,128)(2,1)} %shard_map.85), calls=%async_computation.8 | async-start | bytes 393216 | tf_op jit(solution)/shard_map/all_to_all | solution.py:429
  260.8 1.4 slice_bitcast_fusion
  262.2 6.0 %shard_map.87 = f32[384,3072]{1,0:T(8,128)} custom-call(bf16[256,384]{1,0:T(8,128)(2,1)} %maximum_select_fusion.1.x_ref, bf16[4,2,1,16,1536]{4,3,2,1,0:T(8,128)(2,1)} %bitcast.11.refs_0_, bf16[4,2,1,16,1536]{4,3,2,1,0:T(8,128)(2,1)} %collective-permute-done.15.refs_1_, bf16[4,2,1,16,1536]{4,3,2,1,0:T(8,128)(2,1)} %collective-permute-done.16.refs_2_, ...), custom_call_target="tpu_custom_call" | custom-call | flops 603979776 | bytes 4718592 | tf_op jit(solution)/shard_map/pallas_call | solution.py:351
  269.0 1.6 shard_map.86
  (58 shorter events, 16.7 us)
Async XLA Ops:
  0.6 7.8 %collective-permute-start = (bf16[384,3072]{1,0:T(8,128)(2,1)}, bf16[384,3072]{1,0:T(8,128)(2,1)}, u32[]{:S(2)}, u32[]{:S(2)}) collective-permute-start(bf16[384,3072]{1,0:T(8,128)(2,1)} %bitcast.65), channel_id=1, source_target_pairs={{0,128},{128,0},{1,129},{129,1},{2,130},{130,2},{3,131},{131,3},{4... | collective-permute-start | bytes 7077896 | tf_op jit(solution)/shard_map/ppermute | solution.py:436
  8.5 15.8 %collective-permute-start.2 = (bf16[3072,384]{1,0:T(8,128)(2,1)}, bf16[3072,384]{1,0:T(8,128)(2,1)}, u32[]{:S(2)}, u32[]{:S(2)}) collective-permute-start(bf16[3072,384]{1,0:T(8,128)(2,1)} %bitcast.59), channel_id=1, source_target_pairs={{0,128},{128,0},{1,129},{129,1},{2,130},{130,2},{3,131},{131,3},{4... | collective-permute-start | bytes 7077896 | tf_op jit(solution)/shard_map/ppermute | solution.py:436
  8.8 36.3 %collective-permute-start.1 = (bf16[3072,384]{1,0:T(8,128)(2,1)}, bf16[3072,384]{1,0:T(8,128)(2,1)}, u32[]{:S(2)}, u32[]{:S(2)}) collective-permute-start(bf16[3072,384]{1,0:T(8,128)(2,1)} %bitcast.60), channel_id=1, source_target_pairs={{0,8},{8,0},{1,9},{9,1},{2,10},{10,2},{3,11},{11,3},{4,12},{12,4},... | collective-permute-start | bytes 7077896 | tf_op jit(solution)/shard_map/ppermute | solution.py:449
  16.7 28.4 %all-to-all-start = ((bf16[16,1,16,1536]{3,2,1,0:T(8,128)(2,1)}), bf16[16,1,16,1536]{3,2,1,0:T(8,128)(2,1)}, u32[]{:S(2)}, u32[]{:S(2)}) async-start(bf16[16,1,16,1536]{3,2,1,0:T(8,128)(2,1)} %bitcast.73), calls=%async_computation | async-start | bytes 1572864 | tf_op jit(solution)/shard_map/all_to_all | solution.py:429
  45.1 46.1 %collective-permute-start.4 = (bf16[3072,384]{1,0:T(8,128)(2,1)}, bf16[3072,384]{1,0:T(8,128)(2,1)}, u32[]{:S(2)}, u32[]{:S(2)}) collective-permute-start(bf16[3072,384]{1,0:T(8,128)(2,1)} %collective-permute-done.1.own_mate), channel_id=1, source_target_pairs={{0,128},{1,129},{2,130},{3,131},{4,132},{5,133},{6,134},{7,135},{8... | collective-permute-start | bytes 7077896 | tf_op jit(solution)/shard_map/ppermute | solution.py:453
  49.1 41.2 %copy-start = (bf16[2,4,2,16,1536]{4,3,2,1,0:T(8,128)(2,1)S(1)}, bf16[2,4,2,16,1536]{4,3,2,1,0:T(8,128)(2,1)}, u32[]{:S(2)}) copy-start(bf16[2,4,2,16,1536]{4,3,2,1,0:T(8,128)(2,1)} %shard_map.76) | copy-start | bytes 2359300
  49.1 47.2 %collective-permute-start.5 = (bf16[384,3072]{1,0:T(8,128)(2,1)}, bf16[384,3072]{1,0:T(8,128)(2,1)}, u32[]{:S(2)}, u32[]{:S(2)}) collective-permute-start(bf16[384,3072]{1,0:T(8,128)(2,1)} %bitcast.67), channel_id=1, source_target_pairs={{128,136},{136,128},{129,137},{137,129},{130,138},{138,130},{131,1... | collective-permute-start | bytes 7077896 | tf_op jit(solution)/shard_map/ppermute | solution.py:449
  51.2 40.0 %all-to-all-start.1 = ((bf16[8,1,16,1536]{3,2,1,0:T(8,128)(2,1)}), bf16[8,1,16,1536]{3,2,1,0:T(8,128)(2,1)}, u32[]{:S(2)}, u32[]{:S(2)}) async-start(bf16[8,1,16,1536]{3,2,1,0:T(8,128)(2,1)} %get-tuple-element.42), calls=%async_computation.1 | async-start | bytes 786432 | tf_op jit(solution)/shard_map/all_to_all | solution.py:429
  57.6 32.7 %collective-permute-start.3 = (bf16[4,2,16,1536]{3,2,1,0:T(8,128)(2,1)S(1)}, bf16[4,2,16,1536]{3,2,1,0:T(8,128)(2,1)S(1)}, u32[]{:S(2)}, u32[]{:S(2)}) collective-permute-start(bf16[4,2,16,1536]{3,2,1,0:T(8,128)(2,1)S(1)} %dynamic-slice_bitcast_fusion), channel_id=1, source_target_pairs={{0,8},{8,0},{1,9},{9,1},{2,10},{10,2},{3,11},{11,3},{4,12},{12,4},... | collective-permute-start | bytes 1179656 | tf_op jit(solution)/shard_map/ppermute | solution.py:440
  59.7 29.3 %collective-permute-start.6 = (bf16[64,384]{1,0:T(8,128)(2,1)S(1)}, bf16[64,384]{1,0:T(8,128)(2,1)S(1)}, u32[]{:S(2)}, u32[]{:S(2)}) collective-permute-start(bf16[64,384]{1,0:T(8,128)(2,1)S(1)} %get-tuple-element.90), channel_id=1, source_target_pairs={{0,8},{8,0},{1,9},{9,1},{2,10},{10,2},{3,11},{11,3},{4,12},{12,4},... | collective-permute-start | bytes 147464 | tf_op jit(solution)/shard_map/ppermute | solution.py:440
  60.9 28.8 %collective-permute-start.7 = (bf16[64,384]{1,0:T(8,128)(2,1)S(1)}, bf16[64,384]{1,0:T(8,128)(2,1)S(1)}, u32[]{:S(2)}, u32[]{:S(2)}) collective-permute-start(bf16[64,384]{1,0:T(8,128)(2,1)S(1)} %get-tuple-element.88), channel_id=1, source_target_pairs={{0,8},{8,0},{1,9},{9,1},{2,10},{10,2},{3,11},{11,3},{4,12},{12,4},... | collective-permute-start | bytes 147464 | tf_op jit(solution)/shard_map/ppermute | solution.py:440
  96.4 19.5 %collective-permute-start.8 = (bf16[384,3072]{1,0:T(8,128)(2,1)}, bf16[384,3072]{1,0:T(8,128)(2,1)}, u32[]{:S(2)}, u32[]{:S(2)}) collective-permute-start(bf16[384,3072]{1,0:T(8,128)(2,1)} %collective-permute-done.5.own_mate), channel_id=1, source_target_pairs={{128,0},{129,1},{130,2},{131,3},{132,4},{133,5},{134,6},{135,7},{1... | collective-permute-start | bytes 7077896 | tf_op jit(solution)/shard_map/ppermute | solution.py:453
  145.2 20.2 %all-to-all-start.4 = ((bf16[8,2,16,1536]{3,2,1,0:T(8,128)(2,1)}), bf16[8,2,16,1536]{3,2,1,0:T(8,128)(2,1)}, u32[]{:S(2)}, u32[]{:S(2)}) async-start(bf16[8,2,16,1536]{3,2,1,0:T(8,128)(2,1)} %shard_map.80), calls=%async_computation.4 | async-start | bytes 1572864 | tf_op jit(solution)/shard_map/all_to_all | solution.py:429
  149.5 5.5 %collective-permute-start.9 = (bf16[4,2,1,16,1536]{4,3,2,1,0:T(8,128)(2,1)}, bf16[4,2,1,16,1536]{4,3,2,1,0:T(8,128)(2,1)}, u32[]{:S(2)}, u32[]{:S(2)}) collective-permute-start(bf16[4,2,1,16,1536]{4,3,2,1,0:T(8,128)(2,1)} %bitcast.5.arrived.refs_0_), channel_id=1, source_target_pairs={{128,0},{129,1},{130,2},{131,3},{132,4},{133,5},{134,6},{135,7},{1... | collective-permute-start | bytes 1179656 | tf_op jit(solution)/shard_map/ppermute | solution.py:453
  151.5 3.5 %collective-permute-start.10 = (bf16[4,2,1,16,1536]{4,3,2,1,0:T(8,128)(2,1)}, bf16[4,2,1,16,1536]{4,3,2,1,0:T(8,128)(2,1)}, u32[]{:S(2)}, u32[]{:S(2)}) collective-permute-start(bf16[4,2,1,16,1536]{4,3,2,1,0:T(8,128)(2,1)} %bitcast.5.arrived.refs_0_), channel_id=1, source_target_pairs={{0,8},{8,0},{1,9},{9,1},{2,10},{10,2},{3,11},{11,3},{4,12},{12,4},... | collective-permute-start | bytes 1179656 | tf_op jit(solution)/shard_map/ppermute | solution.py:449
  152.9 6.3 %collective-permute-start.11 = (bf16[4,2,1,16,1536]{4,3,2,1,0:T(8,128)(2,1)}, bf16[4,2,1,16,1536]{4,3,2,1,0:T(8,128)(2,1)}, u32[]{:S(2)}, u32[]{:S(2)}) collective-permute-start(bf16[4,2,1,16,1536]{4,3,2,1,0:T(8,128)(2,1)} %bitcast.5.arrived.refs_0_), channel_id=1, source_target_pairs={{128,8},{136,0},{129,9},{137,1},{130,10},{138,2},{131,11},{139,3},... | collective-permute-start | bytes 1179656 | tf_op jit(solution)/shard_map/ppermute | solution.py:458
  191.7 21.0 %all-to-all-start.6 = ((bf16[8,1,16,1536]{3,2,1,0:T(8,128)(2,1)}), bf16[8,1,16,1536]{3,2,1,0:T(8,128)(2,1)}, u32[]{:S(2)}, u32[]{:S(2)}) async-start(bf16[8,1,16,1536]{3,2,1,0:T(8,128)(2,1)} %bitcast.77), calls=%async_computation.6 | async-start | bytes 786432 | tf_op jit(solution)/shard_map/all_to_all | solution.py:429
  199.0 9.3 %collective-permute-start.20 = (bf16[2,64,384]{2,1,0:T(8,128)(2,1)}, bf16[2,64,384]{2,1,0:T(8,128)(2,1)}, u32[]{:S(2)}, u32[]{:S(2)}) collective-permute-start(bf16[2,64,384]{2,1,0:T(8,128)(2,1)} %get-tuple-element.81), channel_id=1, source_target_pairs={{0,136},{136,0},{8,128},{128,8},{1,137},{137,1},{9,129},{129,9},{2... | collective-permute-start | bytes 294920 | tf_op jit(solution)/shard_map/ppermute | solution.py:444
  202.0 23.4 %collective-permute-start.12 = (bf16[4,2,2,16,1536]{4,3,2,1,0:T(8,128)(2,1)}, bf16[4,2,2,16,1536]{4,3,2,1,0:T(8,128)(2,1)}, u32[]{:S(2)}, u32[]{:S(2)}) collective-permute-start(bf16[4,2,2,16,1536]{4,3,2,1,0:T(8,128)(2,1)} %bitcast.9.arrived.refs_4_), channel_id=1, source_target_pairs={{0,128},{1,129},{2,130},{3,131},{4,132},{5,133},{6,134},{7,135},{8... | collective-permute-start | bytes 2359304 | tf_op jit(solution)/shard_map/ppermute | solution.py:453
  203.3 22.1 %collective-permute-start.13 = (bf16[4,2,2,16,1536]{4,3,2,1,0:T(8,128)(2,1)}, bf16[4,2,2,16,1536]{4,3,2,1,0:T(8,128)(2,1)}, u32[]{:S(2)}, u32[]{:S(2)}) collective-permute-start(bf16[4,2,2,16,1536]{4,3,2,1,0:T(8,128)(2,1)} %bitcast.9.arrived.refs_4_), channel_id=1, source_target_pairs={{128,136},{136,128},{129,137},{137,129},{130,138},{138,130},{131,1... | collective-permute-start | bytes 2359304 | tf_op jit(solution)/shard_map/ppermute | solution.py:449
  206.2 20.0 %collective-permute-start.14 = (bf16[4,2,2,16,1536]{4,3,2,1,0:T(8,128)(2,1)}, bf16[4,2,2,16,1536]{4,3,2,1,0:T(8,128)(2,1)}, u32[]{:S(2)}, u32[]{:S(2)}) collective-permute-start(bf16[4,2,2,16,1536]{4,3,2,1,0:T(8,128)(2,1)} %bitcast.9.arrived.refs_4_), channel_id=1, source_target_pairs={{0,136},{8,128},{1,137},{9,129},{2,138},{10,130},{3,139},{11,131},... | collective-permute-start | bytes 2359304 | tf_op jit(solution)/shard_map/ppermute | solution.py:458
  207.5 16.0 %collective-permute-start.19 = (bf16[2,64,384]{2,1,0:T(8,128)(2,1)}, bf16[2,64,384]{2,1,0:T(8,128)(2,1)}, u32[]{:S(2)}, u32[]{:S(2)}) collective-permute-start(bf16[2,64,384]{2,1,0:T(8,128)(2,1)} %get-tuple-element.81), channel_id=1, source_target_pairs={{0,8},{8,0},{1,9},{9,1},{2,10},{10,2},{3,11},{11,3},{4,12},{12,4},... | collective-permute-start | bytes 294920 | tf_op jit(solution)/shard_map/ppermute | solution.py:440
  208.3 15.2 %collective-permute-start.18 = (bf16[2,64,384]{2,1,0:T(8,128)(2,1)}, bf16[2,64,384]{2,1,0:T(8,128)(2,1)}, u32[]{:S(2)}, u32[]{:S(2)}) collective-permute-start(bf16[2,64,384]{2,1,0:T(8,128)(2,1)} %get-tuple-element.82), channel_id=1, source_target_pairs={{0,128},{128,0},{1,129},{129,1},{2,130},{130,2},{3,131},{131,3},{4... | collective-permute-start | bytes 294920 | tf_op jit(solution)/shard_map/ppermute | solution.py:436
  214.6 10.1 %copy-start.5 = (bf16[64,384]{1,0:T(8,128)(2,1)S(1)}, bf16[64,384]{1,0:T(8,128)(2,1)}, u32[]{:S(2)}) copy-start(bf16[64,384]{1,0:T(8,128)(2,1)} %get-tuple-element.83) | copy-start | bytes 147460
  214.6 10.1 %copy-start.6 = (bf16[64,384]{1,0:T(8,128)(2,1)S(1)}, bf16[64,384]{1,0:T(8,128)(2,1)}, u32[]{:S(2)}) copy-start(bf16[64,384]{1,0:T(8,128)(2,1)} %get-tuple-element.84) | copy-start | bytes 147460
  214.6 10.1 %copy-start.7 = (bf16[64,384]{1,0:T(8,128)(2,1)S(1)}, bf16[64,384]{1,0:T(8,128)(2,1)}, u32[]{:S(2)}) copy-start(bf16[64,384]{1,0:T(8,128)(2,1)} %get-tuple-element.85) | copy-start | bytes 147460
  214.6 10.1 %copy-start.8 = (bf16[64,384]{1,0:T(8,128)(2,1)S(1)}, bf16[64,384]{1,0:T(8,128)(2,1)}, u32[]{:S(2)}) copy-start(bf16[64,384]{1,0:T(8,128)(2,1)} %get-tuple-element.86) | copy-start | bytes 147460
  214.6 31.0 %copy-start.1 = (bf16[64,384]{1,0:T(8,128)(2,1)S(1)}, bf16[64,384]{1,0:T(8,128)(2,1)}, u32[]{:S(2)}) copy-start(bf16[64,384]{1,0:T(8,128)(2,1)} %get-tuple-element.76) | copy-start | bytes 147460
  214.6 31.0 %copy-start.2 = (bf16[64,384]{1,0:T(8,128)(2,1)S(1)}, bf16[64,384]{1,0:T(8,128)(2,1)}, u32[]{:S(2)}) copy-start(bf16[64,384]{1,0:T(8,128)(2,1)} %get-tuple-element.77) | copy-start | bytes 147460
  214.6 31.0 %copy-start.3 = (bf16[64,384]{1,0:T(8,128)(2,1)S(1)}, bf16[64,384]{1,0:T(8,128)(2,1)}, u32[]{:S(2)}) copy-start(bf16[64,384]{1,0:T(8,128)(2,1)} %get-tuple-element.78) | copy-start | bytes 147460
  214.6 31.0 %copy-start.4 = (bf16[64,384]{1,0:T(8,128)(2,1)S(1)}, bf16[64,384]{1,0:T(8,128)(2,1)}, u32[]{:S(2)}) copy-start(bf16[64,384]{1,0:T(8,128)(2,1)} %get-tuple-element.79) | copy-start | bytes 147460
  214.7 22.4 %all-to-all-start.7 = ((bf16[8,1,16,1536]{3,2,1,0:T(8,128)(2,1)}), bf16[8,1,16,1536]{3,2,1,0:T(8,128)(2,1)}, u32[]{:S(2)}, u32[]{:S(2)}) async-start(bf16[8,1,16,1536]{3,2,1,0:T(8,128)(2,1)} %shard_map.83), calls=%async_computation.7 | async-start | bytes 786432 | tf_op jit(solution)/shard_map/all_to_all | solution.py:429
  237.0 15.7 %collective-permute-start.15 = (bf16[4,2,1,16,1536]{4,3,2,1,0:T(8,128)(2,1)}, bf16[4,2,1,16,1536]{4,3,2,1,0:T(8,128)(2,1)}, u32[]{:S(2)}, u32[]{:S(2)}) collective-permute-start(bf16[4,2,1,16,1536]{4,3,2,1,0:T(8,128)(2,1)} %bitcast.11.refs_0_), channel_id=1, source_target_pairs={{128,0},{129,1},{130,2},{131,3},{132,4},{133,5},{134,6},{135,7},{1... | collective-permute-start | bytes 1179656 | tf_op jit(solution)/shard_map/ppermute | solution.py:453
  240.1 12.6 %collective-permute-start.16 = (bf16[4,2,1,16,1536]{4,3,2,1,0:T(8,128)(2,1)}, bf16[4,2,1,16,1536]{4,3,2,1,0:T(8,128)(2,1)}, u32[]{:S(2)}, u32[]{:S(2)}) collective-permute-start(bf16[4,2,1,16,1536]{4,3,2,1,0:T(8,128)(2,1)} %bitcast.11.refs_0_), channel_id=1, source_target_pairs={{0,8},{8,0},{1,9},{9,1},{2,10},{10,2},{3,11},{11,3},{4,12},{12,4},... | collective-permute-start | bytes 1179656 | tf_op jit(solution)/shard_map/ppermute | solution.py:449
  241.5 11.2 %collective-permute-start.17 = (bf16[4,2,1,16,1536]{4,3,2,1,0:T(8,128)(2,1)}, bf16[4,2,1,16,1536]{4,3,2,1,0:T(8,128)(2,1)}, u32[]{:S(2)}, u32[]{:S(2)}) collective-permute-start(bf16[4,2,1,16,1536]{4,3,2,1,0:T(8,128)(2,1)} %bitcast.11.refs_0_), channel_id=1, source_target_pairs={{128,8},{136,0},{129,9},{137,1},{130,10},{138,2},{131,11},{139,3},... | collective-permute-start | bytes 1179656 | tf_op jit(solution)/shard_map/ppermute | solution.py:458
  256.8 12.2 %all-to-all-start.8 = ((bf16[8,2,16,384]{3,2,1,0:T(8,128)(2,1)}), bf16[8,2,16,384]{3,2,1,0:T(8,128)(2,1)}, u32[]{:S(2)}, u32[]{:S(2)}) async-start(bf16[8,2,16,384]{3,2,1,0:T(8,128)(2,1)} %shard_map.85), calls=%async_computation.8 | async-start | bytes 393216 | tf_op jit(solution)/shard_map/all_to_all | solution.py:429

commit v8 on v7

--- a/solution.py
+++ b/solution.py
@@ -84,7 +84,7 @@
         if i % per_half == per_half - 1:
             out_copy(half).start()
 
-    widen((x_ref[...],), by_rows, wait, held, put)
+    widen((x_ref[lax.axis_index("section")],), by_rows, wait, held, put)
     out_copy(0).wait()
     out_copy(1).wait()
 
@@ -183,7 +183,7 @@
         [VMEM, HBM, HBM],
         held_scratch(weights[0], by_rows, 1) + [pltpu.VMEM(shape, bf16), pltpu.SemaphoreType.DMA((2,))],
         (x,) + weights[:2],
-        flops=2 * x.shape[0] * weights[0].size,
+        flops=2 * x.shape[1] * weights[0].size,
         moved=2 * weights[0].size,
     )
 
@@ -318,50 +318,76 @@
     return held[:, :, step // per_half, :, place].reshape(-1, CHUNK)
 
 
-def grad_down_kernel(g_ref, *refs):
-    layer0, layer1, (out_ref, held, sems) = refs[:4], refs[4:8], refs[8:]
+def fill_tokens(into, layer, full_ref, traded_ref):
+    section, mate_pos = lax.axis_index("section"), lax.axis_index("x_lo")
+    half_len = full_ref.shape[1] // 2
+
+    @pl.when(section == layer)
+    def _():
+        for i in range(4):
+            half = mate_pos if i < 2 else 1 - mate_pos
+            which = section if i % 2 == 0 else 1 - section
+            place = pl.ds(pl.multiple_of(half * half_len, half_len), half_len)
+            into[pl.ds(i * half_len, half_len), :] = full_ref[which, place, :]
+
+    @pl.when(section != layer)
+    def _():
+        into[...] = traded_ref[...]
+
+
+def grad_down_kernel(full_ref, traded_ref, *refs):
+    layer0, layer1, (out_ref, held, narrow, sems) = refs[:4], refs[4:8], refs[8:]
     step = pl.program_id(0)
 
     @pl.when(step == 0)
     def _():
         pick_copies(layer0, layer1, 1, held, sems, True)
+        fill_tokens(narrow, 1, full_ref, traded_ref)
         pick_copies(layer0, layer1, 1, held, sems, False)
 
-    out_ref[...] = dot(step_chunk(held, step), g_ref[...], ((0,), (0,)))
-
-
-def grad_up_kernel(x_ref, *refs):
-    layer0, layer1, (out_ref, held, turned, sems) = refs[:4], refs[4:8], refs[8:]
+    out_ref[...] = dot(step_chunk(held, step), narrow[...], ((0,), (0,)))
+
+
+def grad_up_kernel(full_ref, traded_ref, *refs):
+    layer0, layer1, (out_ref, held, narrow, turned, sems) = refs[:4], refs[4:8], refs[8:]
     step = pl.program_id(0)
 
     @pl.when(step == 0)
     def _():
         pick_copies(layer0, layer1, 0, held, sems, True)
-        turned[...] = x_ref[...].T
+        fill_tokens(narrow, 0, full_ref, traded_ref)
+        turned[...] = narrow[...].T
         pick_copies(layer0, layer1, 0, held, sems, False)
 
     out_ref[...] = dot(turned[...], step_chunk(held, step), ((1,), (0,)))
 
 
-def weight_grad(down, narrow, layer0, layer1):
+def weight_grad(down, full, traded, layer0, layer1):
     groups, halves, _, tokens, wide = layer0[0].shape
-    units, (all_tokens, width) = halves * wide, narrow.shape
+    units, (all_tokens, width) = halves * wide, traded.shape
     shape, block = ((units, width), (CHUNK, width)) if down else ((width, units), (width, CHUNK))
     turned = [] if down else [pltpu.VMEM((width, all_tokens), bf16)]
     return pl.pallas_call(
         grad_down_kernel if down else grad_up_kernel,
         out_shape=shape_of(shape, f32),
         grid=(units // CHUNK,),
-        in_specs=[pl.BlockSpec(narrow.shape, lambda i: (0, 0))] + [HBM] * 8,
+        in_specs=[
+            pl.BlockSpec(full.shape, lambda i: (0, 0, 0)),
+            pl.BlockSpec(traded.shape, lambda i: (0, 0)),
+        ]
+        + [HBM] * 8,
         out_specs=pl.BlockSpec(block, lambda i: (i, 0) if down else (0, i)),
-        scratch_shapes=[pltpu.VMEM((4, groups, halves, tokens, wide), bf16)]
+        scratch_shapes=[
+            pltpu.VMEM((4, groups, halves, tokens, wide), bf16),
+            pltpu.VMEM((all_tokens, width), bf16),
+        ]
         + turned
         + [pltpu.SemaphoreType.DMA((4,))],
         compiler_params=LIMIT,
         cost_estimate=pl.CostEstimate(
-            flops=2 * narrow.size * units, bytes_accessed=4 * width * units, transcendentals=0
+            flops=2 * traded.size * units, bytes_accessed=4 * width * units, transcendentals=0
         ),
-    )(narrow, *layer0, *layer1)
+    )(full, traded, *layer0, *layer1)
 
 
 def last_kernel(up, down, *refs):
@@ -481,24 +507,27 @@
         return lax.dynamic_index_in_dim(array, which, 0, keepdims=False)
 
     def both_widths(array):
-        return jnp.concatenate([half_of(array, mate_pos), to_mate(half_of(array, 1 - mate_pos))], axis=1)
-
-    x0, g2 = batch(inputs, section), batch(cotangent, section)
+        def cut(half):
+            place = section, half * half_len, 0
+            return lax.dynamic_slice(array, place, (1, half_len, width))[0]
+
+        return jnp.concatenate([cut(mate_pos), to_mate(cut(1 - mate_pos))], axis=1)
+
     other_up = to_other_core(own_up)
-    first_part = widen_first(0, False, 2, x0, (own_up, other_up), blocks)
+    first_part = widen_first(0, False, 2, inputs, (own_up, other_up), blocks)
     mate_down0 = only_to_mate(late(own_down, other_up), 0)
     arrived = exchange(first_part.reshape((2 * rings, 1) + piece), ("z", "x_lo"))
 
     other_down = to_other_core(late(own_down, other_up))
-    d_hid1 = widen_first(1, True, 0, late(g2, first_part), (own_down, other_down), blocks)
+    d_hid1 = widen_first(1, True, 0, late(cotangent, first_part), (own_down, other_down), blocks)
     arrived, mate_down0 = late((arrived, mate_down0), d_hid1)
     d_hid1, given = batch(d_hid1, mate_pos), to_mate(batch(d_hid1, 1 - mate_pos))
     down0 = own_down, other_down, mate_down0, only_to_core(mate_down0, 1)
 
     value0, slope0 = activation(act_first_kernel, 1, rings, piece, (arrived,), [VMEM], slope=True)
-    mate_up1 = only_to_mate(late(own_up, value0), 1)
+    mate_up1 = only_to_mate(late(own_up, (value0, given)), 1)
     hid0 = exchange(value0, "z").reshape(blocks[:2] + (1,) + piece)
-    x0_both, g2_both = (both_widths(late(array, value0)) for array in (x0, g2))
+    x0_both, g2_both = (both_widths(late(array, value0)) for array in (inputs, cotangent))
     d_hid1 = (d_hid1.astype(f32) + late(given, value0).astype(f32)).astype(bf16)
     hid0 = late(hid0, d_hid1)
     part = narrow_next(0, True, 0, hid0, down0, lax.axis_size(col))
@@ -522,28 +551,17 @@
     both1 = jnp.stack([near, to_other_core(near), to_mate(far), to_other_core_of_mate(far)])
     both1 = both1.reshape((2, 2) + near.shape)
 
-    def all_tokens(array):
-        return jnp.concatenate(
-            [
-                half_of(batch(array, which), half)
-                for half in (mate_pos, 1 - mate_pos)
-                for which in (section, 1 - section)
-            ]
-        )
-
     x1s, g1s = both1[:, :, 0].reshape(2 * tokens, width), both1[:, :, 1].reshape(2 * tokens, width)
-    xs = jnp.where(first, all_tokens(inputs), x1s)
-    gs = jnp.where(first, g1s, all_tokens(cotangent))
 
     (d_pre0,) = activation(act_back_kernel, 1, rings, piece, (arrived, slope0), [VMEM, VMEM])
     d_pre0 = late(exchange(d_pre0, "z").reshape(blocks[:2] + (1,) + piece), acts1s)
-    down_grad = weight_grad(True, late(gs, d_pre0), hid0s, acts1s)
+    down_grad = weight_grad(True, cotangent, late(g1s, d_pre0), hid0s, acts1s)
     d_pre0s = late(to_owner(d_pre0, 0), down_grad)
 
     last = last_product(own_up, own_down, d_pre0s, acts1s)
-    xs, d_pre0s = late((xs, d_pre0s), last)
+    x1s, d_pre0s = late((x1s, d_pre0s), last)
     arrived = exchange(last, col)
-    up_grad = weight_grad(False, xs, d_pre0s, acts1s)
+    up_grad = weight_grad(False, inputs, x1s, d_pre0s, acts1s)
 
     out_len = tokens // lax.axis_size(col)
     per_half = half_len // out_len

time: 273 us -> 275 us (level)
  starting transfers between devices: 72.7 us -> 63.6 us
  blocking collectives: 51.8 us -> 60.7 us
  waiting for transfers between devices: 72.4 us -> 78.5 us
  local copies, waits for them, and re-layouts: 9.69 us -> 6.62 us
    all_to_all x3, blocking collectives: 51.8 us -> 60.7 us  [exchange(): return lax.all_to_all(blocks, axes, 0, 0)]
    all_to_all x6, waiting for transfers between devices: 34.3 us -> 41.4 us  [exchange(): return lax.all_to_all(blocks, axes, 0, 0)]
    dynamic_slice x4 -> x0, local copies, waits for them, and re-layouts: 4.82 us -> none  [half_of(): return lax.dynamic_slice_in_dim(array, which * half_len, half_len, 0)]
    ppermute x4, waiting for transfers between devices: 28.6 us -> 24 us  [to_mate(): return lax.ppermute(block, 'x_lo', [(0, 1), (1, 0)])]
    ppermute x1, waiting for transfers between devices: 0.01 us -> 3.92 us  [to_other_core_of_mate(): return lax.ppermute(block, CORES, [(0, 3), (3, 0), (1, 2), (2, 1)])]
    all_to_all x6, starting transfers between devices: 33.9 us -> 30.5 us  [exchange(): return lax.all_to_all(blocks, axes, 0, 0)]
  transfers between devices with their start and end apart: 27 -> 27, of which waited for: 9 -> 11; matrix products, arithmetic and copies ran while one was open for 6% -> 4% of each run, Pallas kernels for 11% -> 11%
where the time goes in v8:
time: 275 us; the launch traced here: 273 us
  waiting for transfers between devices  78.5 us (29%)
  starting transfers between devices  63.6 us (23%)
  blocking collectives  60.7 us (22%)
  Pallas kernels  57 us (21%)
  local copies, waits for them, and re-layouts  6.62 us (2%)
  other arithmetic  5.58 us (2%)
    all_to_all x3, blocking collectives, exchange(): return lax.all_to_all(blocks, axes, 0, 0)  60.7 us
    pallas_call x11, Pallas kernels, kernel_call(): pl.pallas_call(body, out_shape=outs, in_specs=in_specs, out_specs=out_spe...  44.4 us
    all_to_all x6, waiting for transfers between devices, exchange(): return lax.all_to_all(blocks, axes, 0, 0)  41.4 us
    all_to_all x6, starting transfers between devices, exchange(): return lax.all_to_all(blocks, axes, 0, 0)  30.5 us
    ppermute x4, waiting for transfers between devices, to_mate(): return lax.ppermute(block, 'x_lo', [(0, 1), (1, 0)])  24 us
    pallas_call x2, Pallas kernels, weight_grad(): pl.pallas_call(grad_down_kernel if down else grad_up_kernel, out_shape=sh...  12.5 us
    ppermute x5, starting transfers between devices, only_to_core(): return lax.ppermute(block, 'section', [(1 - section, section)])  10.3 us
    ppermute x5, starting transfers between devices, only_to_mate(): return lax.ppermute(block, CORES, [(at, at + 1), (at + 1, at)])  9.65 us
  transfers between devices with their start and end apart: 27, of which 11 were waited for; matrix products, arithmetic and copies ran while one was open for 4% of the time, Pallas kernels for 11%

profile of v8, /device:TPU:1, one launch (start us, length us, event | category | flops | bytes accessed | tf_op | source)
XLA Modules:
  0.0 272.9 jit_solution(886273161714889316)
XLA Ops:
  0.6 3.3 %collective-permute-start = (bf16[384,3072]{1,0:T(8,128)(2,1)}, bf16[384,3072]{1,0:T(8,128)(2,1)}, u32[]{:S(2)}, u32[]{:S(2)}) collective-permute-start(bf16[384,3072]{1,0:T(8,128)(2,1)} %bitcast.51), channel_id=1, source_target_pairs={{0,128},{128,0},{1,129},{129,1},{2,130},{130,2},{3,131},{131,3},{4... | collective-permute-start | bytes 7077896 | tf_op jit(solution)/shard_map/ppermute | solution.py:462
  4.0 4.5 %collective-permute-done.other = bf16[384,3072]{1,0:T(8,128)(2,1)} collective-permute-done((bf16[384,3072]{1,0:T(8,128)(2,1)}, bf16[384,3072]{1,0:T(8,128)(2,1)}, u32[]{:S(2)}, u32[]{:S(2)}) %collective-permute-start) | collective-permute-done | bytes 2359328 | tf_op jit(solution)/shard_map/ppermute | solution.py:462
  8.8 2.1 collective-permute-start.1
  10.9 4.1 %shard_map.75 = bf16[4,2,2,16,1536]{4,3,2,1,0:T(8,128)(2,1)} custom-call(bf16[2,128,384]{2,1,0:T(8,128)(2,1)} %full_ref.3, bf16[384,3072]{1,0:T(8,128)(2,1)} %bitcast.52, bf16[384,3072]{1,0:T(8,128)(2,1)} %collective-permute-done.other), custom_call_target="tpu_custom_call" | custom-call | flops 301989888 | bytes 2359296 | tf_op jit(solution)/shard_map/pallas_call | solution.py:166
  15.1 7.5 %all-to-all-start = ((bf16[16,1,16,1536]{3,2,1,0:T(8,128)(2,1)}), bf16[16,1,16,1536]{3,2,1,0:T(8,128)(2,1)}, u32[]{:S(2)}, u32[]{:S(2)}) async-start(bf16[16,1,16,1536]{3,2,1,0:T(8,128)(2,1)} %bitcast.59), calls=%async_computation | async-start | bytes 1572864 | tf_op jit(solution)/shard_map/all_to_all | solution.py:455
  22.6 4.3 %shard_map.76 = bf16[2,4,2,16,1536]{4,3,2,1,0:T(8,128)(2,1)} custom-call(bf16[2,128,384]{2,1,0:T(8,128)(2,1)} %full_ref.2, bf16[3072,384]{1,0:T(8,128)(2,1)} %bitcast.47, bf16[3072,384]{1,0:T(8,128)(2,1)} %collective-permute-done.2.other), custom_call_target="tpu_custom_call" | custom-call | flops 301989888 | bytes 2359296 | tf_op jit(solution)/shard_map/pallas_call | solution.py:166
  26.9 1.8 dynamic-slice_bitcast_fusion
  28.7 1.3 collective-permute-start.3
  30.0 13.4 %all-to-all-done.arrived = bf16[16,1,16,1536]{3,2,1,0:T(8,128)(2,1)} async-done(((bf16[16,1,16,1536]{3,2,1,0:T(8,128)(2,1)}), bf16[16,1,16,1536]{3,2,1,0:T(8,128)(2,1)}, u32[]{:S(2)}, u32[]{:S(2)}) %all-to-all-start) | async-done | bytes 786464 | tf_op jit(solution)/shard_map/all_to_all | solution.py:455
  43.5 1.3 collective-permute-start.4
  44.8 2.7 shard_map.77
  47.5 2.8 %collective-permute-start.5 = (bf16[384,3072]{1,0:T(8,128)(2,1)}, bf16[384,3072]{1,0:T(8,128)(2,1)}, u32[]{:S(2)}, u32[]{:S(2)}) collective-permute-start(bf16[384,3072]{1,0:T(8,128)(2,1)} %bitcast.53), channel_id=1, source_target_pairs={{128,136},{136,128},{129,137},{137,129},{130,138},{138,130},{131,1... | collective-permute-start | bytes 7077896 | tf_op jit(solution)/shard_map/ppermute | solution.py:475
  50.3 6.4 %all-to-all-start.1 = ((bf16[8,1,16,1536]{3,2,1,0:T(8,128)(2,1)}), bf16[8,1,16,1536]{3,2,1,0:T(8,128)(2,1)}, u32[]{:S(2)}, u32[]{:S(2)}) async-start(bf16[8,1,16,1536]{3,2,1,0:T(8,128)(2,1)} %get-tuple-element.42), calls=%async_computation.1 | async-start | bytes 786432 | tf_op jit(solution)/shard_map/all_to_all | solution.py:455
  60.1 22.8 %collective-permute-done.6 = bf16[64,384]{1,0:T(8,128)(2,1)S(1)} collective-permute-done((bf16[64,384]{1,0:T(8,128)(2,1)S(1)}, bf16[64,384]{1,0:T(8,128)(2,1)S(1)}, u32[]{:S(2)}, u32[]{:S(2)}) %collective-permute-start.6) | collective-permute-done | bytes 49184 | tf_op jit(solution)/shard_map/ppermute | solution.py:466
  84.2 2.0 fusion.rest_0_
  86.2 5.2 %shard_map.78 = bf16[8,64,768]{2,1,0:T(8,128)(2,1)} custom-call(bf16[4,2,1,16,1536]{4,3,2,1,0:T(8,128)(2,1)} %bitcast.3.arrived.refs_0_, bf16[3072,384]{1,0:T(8,128)(2,1)} %bitcast.48, bf16[3072,384]{1,0:T(8,128)(2,1)} %collective-permute-done.2.other, bf16[3072,384]{1,0:T(8,128)(2,1)} %collective-permute-done.1.own_mate, ...), custom_call_target="tpu_custom_call" | custom-call | flops 301989888 | bytes 4718592 | tf_op jit(solution)/shard_map/pallas_call | solution.py:166
  91.4 2.7 %collective-permute-start.8 = (bf16[384,3072]{1,0:T(8,128)(2,1)}, bf16[384,3072]{1,0:T(8,128)(2,1)}, u32[]{:S(2)}, u32[]{:S(2)}) collective-permute-start(bf16[384,3072]{1,0:T(8,128)(2,1)} %collective-permute-done.5.own_mate), channel_id=1, source_target_pairs={{128,0},{129,1},{130,2},{131,3},{132,4},{133,5},{134,6},{135,7},{1... | collective-permute-start | bytes 7077896 | tf_op jit(solution)/shard_map/ppermute | solution.py:479
  94.1 16.9 %all_to_all.45.arrived = bf16[8,64,768]{2,1,0:T(8,128)(2,1)} all-to-all(bf16[8,64,768]{2,1,0:T(8,128)(2,1)} %shard_map.78), channel_id=1, replica_groups=mesh['section'=2,'z'=8,'x_lo'=2,'y'=4,'x_hi'=2] {'y','x_hi'}, dimensions={0} | all-to-all | bytes 1572864 | tf_op jit(solution)/shard_map/all_to_all | solution.py:455
  111.0 6.8 %shard_map.79 = (bf16[4,2,2,16,1536]{4,3,2,1,0:T(8,128)(2,1)}, bf16[64,768]{1,0:T(8,128)(2,1)}) custom-call(bf16[8,64,768]{2,1,0:T(8,128)(2,1)} %all_to_all.45.arrived, bf16[64,768]{1,0:T(8,128)(2,1)} %pad_maximum_fusion.2.base, bf16[384,3072]{1,0:T(8,128)(2,1)} %bitcast.54, bf16[384,3072]{1,0:T(8,128)(2,1)} %collective-permute-done.other, ...), custom_call_target="tpu_custom_call" | custom-call | flops 301989888 | bytes 4718592 | tf_op jit(solution)/shard_map/pallas_call | solution.py:166
  117.8 26.3 %all_to_all.46.arrived = bf16[8,2,16,1536]{3,2,1,0:T(8,128)(2,1)} all-to-all(bf16[8,2,16,1536]{3,2,1,0:T(8,128)(2,1)} %bitcast.62), channel_id=1, replica_groups=mesh['section'=2,'z'=8,'x_lo'=2,'y'=4,'x_hi'=2] {'z'}, dimensions={0} | all-to-all | bytes 1572864 | tf_op jit(solution)/shard_map/all_to_all | solution.py:455
  144.1 2.2 shard_map.80
  146.3 4.2 %all-to-all-start.4 = ((bf16[8,2,16,1536]{3,2,1,0:T(8,128)(2,1)}), bf16[8,2,16,1536]{3,2,1,0:T(8,128)(2,1)}, u32[]{:S(2)}, u32[]{:S(2)}) async-start(bf16[8,2,16,1536]{3,2,1,0:T(8,128)(2,1)} %shard_map.80), calls=%async_computation.4 | async-start | bytes 1572864 | tf_op jit(solution)/shard_map/all_to_all | solution.py:455
  150.5 2.0 collective-permute-start.11
  152.6 1.4 collective-permute-start.10
  154.0 2.0 collective-permute-start.9
  156.1 3.6 %collective-permute-done.11.refs_3_ = bf16[4,2,1,16,1536]{4,3,2,1,0:T(8,128)(2,1)} collective-permute-done((bf16[4,2,1,16,1536]{4,3,2,1,0:T(8,128)(2,1)}, bf16[4,2,1,16,1536]{4,3,2,1,0:T(8,128)(2,1)}, u32[]{:S(2)}, u32[]{:S(2)}) %collective-permute-start.11) | collective-permute-done | bytes 393248 | tf_op jit(solution)/shard_map/ppermute | solution.py:484
  159.7 11.4 %all-to-all-done.4 = bf16[8,2,16,1536]{3,2,1,0:T(8,128)(2,1)} async-done(((bf16[8,2,16,1536]{3,2,1,0:T(8,128)(2,1)}), bf16[8,2,16,1536]{3,2,1,0:T(8,128)(2,1)}, u32[]{:S(2)}, u32[]{:S(2)}) %all-to-all-start.4) | async-done | bytes 786464 | tf_op jit(solution)/shard_map/all_to_all | solution.py:455
  171.0 5.6 %shard_map.81 = bf16[8,64,768]{2,1,0:T(8,128)(2,1)} custom-call(bf16[4,2,2,16,1536]{4,3,2,1,0:T(8,128)(2,1)} %bitcast.11.arrived.refs_4_, bf16[384,3072]{1,0:T(8,128)(2,1)} %bitcast.55, bf16[384,3072]{1,0:T(8,128)(2,1)} %collective-permute-done.other, bf16[384,3072]{1,0:T(8,128)(2,1)} %collective-permute-done.5.own_mate, ...), custom_call_target="tpu_custom_call" | custom-call | flops 301989888 | bytes 4718592 | tf_op jit(solution)/shard_map/pallas_call | solution.py:166
  176.6 17.5 %all_to_all.47.arrived = bf16[8,64,768]{2,1,0:T(8,128)(2,1)} all-to-all(bf16[8,64,768]{2,1,0:T(8,128)(2,1)} %shard_map.81), channel_id=1, replica_groups=mesh['section'=2,'z'=8,'x_lo'=2,'y'=4,'x_hi'=2] {'y','x_hi'}, dimensions={0} | all-to-all | bytes 1572864 | tf_op jit(solution)/shard_map/all_to_all | solution.py:455
  194.1 6.0 %shard_map.82 = (bf16[4,2,1,16,1536]{4,3,2,1,0:T(8,128)(2,1)}, bf16[64,768]{1,0:T(8,128)(2,1)}) custom-call(bf16[8,64,768]{2,1,0:T(8,128)(2,1)} %all_to_all.47.arrived, bf16[64,768]{1,0:T(8,128)(2,1)} %pad_maximum_fusion.3.base, bf16[3072,384]{1,0:T(8,128)(2,1)} %bitcast.49, bf16[3072,384]{1,0:T(8,128)(2,1)} %collective-permute-done.2.other, ...), custom_call_target="tpu_custom_call" | custom-call | flops 301989888 | bytes 4718592 | tf_op jit(solution)/shard_map/pallas_call | solution.py:166
  200.2 4.1 %all-to-all-start.6 = ((bf16[8,1,16,1536]{3,2,1,0:T(8,128)(2,1)}), bf16[8,1,16,1536]{3,2,1,0:T(8,128)(2,1)}, u32[]{:S(2)}, u32[]{:S(2)}) async-start(bf16[8,1,16,1536]{3,2,1,0:T(8,128)(2,1)} %bitcast.65), calls=%async_computation.6 | async-start | bytes 786432 | tf_op jit(solution)/shard_map/all_to_all | solution.py:455
  204.3 1.6 pad_maximum_fusion.1
  207.2 1.9 collective-permute-start.13
  209.2 1.3 collective-permute-start.12
  210.5 8.8 %all-to-all-done.6.arrived = bf16[8,1,16,1536]{3,2,1,0:T(8,128)(2,1)} async-done(((bf16[8,1,16,1536]{3,2,1,0:T(8,128)(2,1)}), bf16[8,1,16,1536]{3,2,1,0:T(8,128)(2,1)}, u32[]{:S(2)}, u32[]{:S(2)}) %all-to-all-start.6) | async-done | bytes 393248 | tf_op jit(solution)/shard_map/all_to_all | solution.py:455
  219.3 1.9 shard_map.83
  221.1 4.1 %all-to-all-start.7 = ((bf16[8,1,16,1536]{3,2,1,0:T(8,128)(2,1)}), bf16[8,1,16,1536]{3,2,1,0:T(8,128)(2,1)}, u32[]{:S(2)}, u32[]{:S(2)}) async-start(bf16[8,1,16,1536]{3,2,1,0:T(8,128)(2,1)} %shard_map.83), calls=%async_computation.7 | async-start | bytes 786432 | tf_op jit(solution)/shard_map/all_to_all | solution.py:455
  228.4 3.9 %collective-permute-done.20 = bf16[2,64,384]{2,1,0:T(8,128)(2,1)S(1)} collective-permute-done((bf16[2,64,384]{2,1,0:T(8,128)(2,1)S(1)}, bf16[2,64,384]{2,1,0:T(8,128)(2,1)S(1)}, u32[]{:S(2)}, u32[]{:S(2)}) %collective-permute-start.20) | collective-permute-done | bytes 98336 | tf_op jit(solution)/shard_map/ppermute | solution.py:470
  233.6 6.8 %all-to-all-done.7 = bf16[8,1,16,1536]{3,2,1,0:T(8,128)(2,1)} async-done(((bf16[8,1,16,1536]{3,2,1,0:T(8,128)(2,1)}), bf16[8,1,16,1536]{3,2,1,0:T(8,128)(2,1)}, u32[]{:S(2)}, u32[]{:S(2)}) %all-to-all-start.7) | async-done | bytes 393248 | tf_op jit(solution)/shard_map/all_to_all | solution.py:455
  240.4 2.0 collective-permute-start.17
  242.4 1.4 collective-permute-start.16
  243.8 2.9 %collective-permute-start.15 = (bf16[4,2,1,16,1536]{4,3,2,1,0:T(8,128)(2,1)}, bf16[4,2,1,16,1536]{4,3,2,1,0:T(8,128)(2,1)}, u32[]{:S(2)}, u32[]{:S(2)}) collective-permute-start(bf16[4,2,1,16,1536]{4,3,2,1,0:T(8,128)(2,1)} %bitcast.13.refs_0_), channel_id=1, source_target_pairs={{128,0},{129,1},{130,2},{131,3},{132,4},{133,5},{134,6},{135,7},{1... | collective-permute-start | bytes 1179656 | tf_op jit(solution)/shard_map/ppermute | solution.py:479
  248.2 6.4 %shard_map.84 = f32[3072,384]{1,0:T(8,128)} custom-call(bf16[2,128,384]{2,1,0:T(8,128)(2,1)} %full_ref.2, bf16[256,384]{1,0:T(8,128)(2,1)} %bitcast.64, bf16[4,2,1,16,1536]{4,3,2,1,0:T(8,128)(2,1)} %bitcast.3.arrived.refs_0_, bf16[4,2,1,16,1536]{4,3,2,1,0:T(8,128)(2,1)} %collective-permute-done.9.refs_1_, ...), custom_call_target="tpu_custom_call" | custom-call | flops 603979776 | bytes 4718592 | tf_op jit(solution)/shard_map/pallas_call | solution.py:370
  254.6 4.0 %shard_map.85 = bf16[8,2,16,384]{3,2,1,0:T(8,128)(2,1)} custom-call(bf16[384,3072]{1,0:T(8,128)(2,1)} %bitcast.56, bf16[3072,384]{1,0:T(8,128)(2,1)} %bitcast.50, bf16[4,2,1,16,1536]{4,3,2,1,0:T(8,128)(2,1)} %bitcast.13.refs_0_, bf16[4,2,1,16,1536]{4,3,2,1,0:T(8,128)(2,1)} %collective-permute-done.15.refs_1_, ...), custom_call_target="tpu_custom_call" | custom-call | flops 603979776 | bytes 7077888 | tf_op jit(solution)/shard_map/pallas_call | solution.py:166
  258.7 4.0 %all-to-all-start.8 = ((bf16[8,2,16,384]{3,2,1,0:T(8,128)(2,1)}), bf16[8,2,16,384]{3,2,1,0:T(8,128)(2,1)}, u32[]{:S(2)}, u32[]{:S(2)}) async-start(bf16[8,2,16,384]{3,2,1,0:T(8,128)(2,1)} %shard_map.85), calls=%async_computation.8 | async-start | bytes 393216 | tf_op jit(solution)/shard_map/all_to_all | solution.py:455
  262.7 1.4 slice_bitcast_fusion
  264.1 6.1 %shard_map.87 = f32[384,3072]{1,0:T(8,128)} custom-call(bf16[2,128,384]{2,1,0:T(8,128)(2,1)} %full_ref.3, bf16[256,384]{1,0:T(8,128)(2,1)} %bitcast.63, bf16[4,2,1,16,1536]{4,3,2,1,0:T(8,128)(2,1)} %bitcast.13.refs_0_, bf16[4,2,1,16,1536]{4,3,2,1,0:T(8,128)(2,1)} %collective-permute-done.15.refs_1_, ...), custom_call_target="tpu_custom_call" | custom-call | flops 603979776 | bytes 4718592 | tf_op jit(solution)/shard_map/pallas_call | solution.py:370
  271.3 1.6 shard_map.86
  (35 shorter events, 13.1 us)
Async XLA Ops:
  0.6 7.8 %collective-permute-start = (bf16[384,3072]{1,0:T(8,128)(2,1)}, bf16[384,3072]{1,0:T(8,128)(2,1)}, u32[]{:S(2)}, u32[]{:S(2)}) collective-permute-start(bf16[384,3072]{1,0:T(8,128)(2,1)} %bitcast.51), channel_id=1, source_target_pairs={{0,128},{128,0},{1,129},{129,1},{2,130},{130,2},{3,131},{131,3},{4... | collective-permute-start | bytes 7077896 | tf_op jit(solution)/shard_map/ppermute | solution.py:462
  8.5 14.2 %collective-permute-start.2 = (bf16[3072,384]{1,0:T(8,128)(2,1)}, bf16[3072,384]{1,0:T(8,128)(2,1)}, u32[]{:S(2)}, u32[]{:S(2)}) collective-permute-start(bf16[3072,384]{1,0:T(8,128)(2,1)} %bitcast.45), channel_id=1, source_target_pairs={{0,128},{128,0},{1,129},{129,1},{2,130},{130,2},{3,131},{131,3},{4... | collective-permute-start | bytes 7077896 | tf_op jit(solution)/shard_map/ppermute | solution.py:462
  8.8 34.6 %collective-permute-start.1 = (bf16[3072,384]{1,0:T(8,128)(2,1)}, bf16[3072,384]{1,0:T(8,128)(2,1)}, u32[]{:S(2)}, u32[]{:S(2)}) collective-permute-start(bf16[3072,384]{1,0:T(8,128)(2,1)} %bitcast.46), channel_id=1, source_target_pairs={{0,8},{8,0},{1,9},{9,1},{2,10},{10,2},{3,11},{11,3},{4,12},{12,4},... | collective-permute-start | bytes 7077896 | tf_op jit(solution)/shard_map/ppermute | solution.py:475
  15.1 28.4 %all-to-all-start = ((bf16[16,1,16,1536]{3,2,1,0:T(8,128)(2,1)}), bf16[16,1,16,1536]{3,2,1,0:T(8,128)(2,1)}, u32[]{:S(2)}, u32[]{:S(2)}) async-start(bf16[16,1,16,1536]{3,2,1,0:T(8,128)(2,1)} %bitcast.59), calls=%async_computation | async-start | bytes 1572864 | tf_op jit(solution)/shard_map/all_to_all | solution.py:455
  28.7 18.7 %collective-permute-start.3 = (bf16[4,2,16,1536]{3,2,1,0:T(8,128)(2,1)}, bf16[4,2,16,1536]{3,2,1,0:T(8,128)(2,1)}, u32[]{:S(2)}, u32[]{:S(2)}) collective-permute-start(bf16[4,2,16,1536]{3,2,1,0:T(8,128)(2,1)} %dynamic-slice_bitcast_fusion), channel_id=1, source_target_pairs={{0,8},{8,0},{1,9},{9,1},{2,10},{10,2},{3,11},{11,3},{4,12},{12,4},... | collective-permute-start | bytes 1179656 | tf_op jit(solution)/shard_map/ppermute | solution.py:466
  43.5 42.7 %collective-permute-start.4 = (bf16[3072,384]{1,0:T(8,128)(2,1)}, bf16[3072,384]{1,0:T(8,128)(2,1)}, u32[]{:S(2)}, u32[]{:S(2)}) collective-permute-start(bf16[3072,384]{1,0:T(8,128)(2,1)} %collective-permute-done.1.own_mate), channel_id=1, source_target_pairs={{0,128},{1,129},{2,130},{3,131},{4,132},{5,133},{6,134},{7,135},{8... | collective-permute-start | bytes 7077896 | tf_op jit(solution)/shard_map/ppermute | solution.py:479
  47.5 43.9 %collective-permute-start.5 = (bf16[384,3072]{1,0:T(8,128)(2,1)}, bf16[384,3072]{1,0:T(8,128)(2,1)}, u32[]{:S(2)}, u32[]{:S(2)}) collective-permute-start(bf16[384,3072]{1,0:T(8,128)(2,1)} %bitcast.53), channel_id=1, source_target_pairs={{128,136},{136,128},{129,137},{137,129},{130,138},{138,130},{131,1... | collective-permute-start | bytes 7077896 | tf_op jit(solution)/shard_map/ppermute | solution.py:475
  50.3 35.9 %all-to-all-start.1 = ((bf16[8,1,16,1536]{3,2,1,0:T(8,128)(2,1)}), bf16[8,1,16,1536]{3,2,1,0:T(8,128)(2,1)}, u32[]{:S(2)}, u32[]{:S(2)}) async-start(bf16[8,1,16,1536]{3,2,1,0:T(8,128)(2,1)} %get-tuple-element.42), calls=%async_computation.1 | async-start | bytes 786432 | tf_op jit(solution)/shard_map/all_to_all | solution.py:455
  57.6 25.3 %collective-permute-start.6 = (bf16[64,384]{1,0:T(8,128)(2,1)S(1)}, bf16[64,384]{1,0:T(8,128)(2,1)S(1)}, u32[]{:S(2)}, u32[]{:S(2)}) collective-permute-start(bf16[64,384]{1,0:T(8,128)(2,1)S(1)} %get-tuple-element.82), channel_id=1, source_target_pairs={{0,8},{8,0},{1,9},{9,1},{2,10},{10,2},{3,11},{11,3},{4,12},{12,4},... | collective-permute-start | bytes 147464 | tf_op jit(solution)/shard_map/ppermute | solution.py:466
  58.9 24.6 %collective-permute-start.7 = (bf16[64,384]{1,0:T(8,128)(2,1)S(1)}, bf16[64,384]{1,0:T(8,128)(2,1)S(1)}, u32[]{:S(2)}, u32[]{:S(2)}) collective-permute-start(bf16[64,384]{1,0:T(8,128)(2,1)S(1)} %get-tuple-element.80), channel_id=1, source_target_pairs={{0,8},{8,0},{1,9},{9,1},{2,10},{10,2},{3,11},{11,3},{4,12},{12,4},... | collective-permute-start | bytes 147464 | tf_op jit(solution)/shard_map/ppermute | solution.py:466
  91.4 19.6 %collective-permute-start.8 = (bf16[384,3072]{1,0:T(8,128)(2,1)}, bf16[384,3072]{1,0:T(8,128)(2,1)}, u32[]{:S(2)}, u32[]{:S(2)}) collective-permute-start(bf16[384,3072]{1,0:T(8,128)(2,1)} %collective-permute-done.5.own_mate), channel_id=1, source_target_pairs={{128,0},{129,1},{130,2},{131,3},{132,4},{133,5},{134,6},{135,7},{1... | collective-permute-start | bytes 7077896 | tf_op jit(solution)/shard_map/ppermute | solution.py:479
  146.3 24.7 %all-to-all-start.4 = ((bf16[8,2,16,1536]{3,2,1,0:T(8,128)(2,1)}), bf16[8,2,16,1536]{3,2,1,0:T(8,128)(2,1)}, u32[]{:S(2)}, u32[]{:S(2)}) async-start(bf16[8,2,16,1536]{3,2,1,0:T(8,128)(2,1)} %shard_map.80), calls=%async_computation.4 | async-start | bytes 1572864 | tf_op jit(solution)/shard_map/all_to_all | solution.py:455
  150.5 9.1 %collective-permute-start.11 = (bf16[4,2,1,16,1536]{4,3,2,1,0:T(8,128)(2,1)}, bf16[4,2,1,16,1536]{4,3,2,1,0:T(8,128)(2,1)}, u32[]{:S(2)}, u32[]{:S(2)}) collective-permute-start(bf16[4,2,1,16,1536]{4,3,2,1,0:T(8,128)(2,1)} %bitcast.3.arrived.refs_0_), channel_id=1, source_target_pairs={{128,8},{136,0},{129,9},{137,1},{130,10},{138,2},{131,11},{139,3},... | collective-permute-start | bytes 1179656 | tf_op jit(solution)/shard_map/ppermute | solution.py:484
  152.6 7.1 %collective-permute-start.10 = (bf16[4,2,1,16,1536]{4,3,2,1,0:T(8,128)(2,1)}, bf16[4,2,1,16,1536]{4,3,2,1,0:T(8,128)(2,1)}, u32[]{:S(2)}, u32[]{:S(2)}) collective-permute-start(bf16[4,2,1,16,1536]{4,3,2,1,0:T(8,128)(2,1)} %bitcast.3.arrived.refs_0_), channel_id=1, source_target_pairs={{0,8},{8,0},{1,9},{9,1},{2,10},{10,2},{3,11},{11,3},{4,12},{12,4},... | collective-permute-start | bytes 1179656 | tf_op jit(solution)/shard_map/ppermute | solution.py:475
  154.0 5.7 %collective-permute-start.9 = (bf16[4,2,1,16,1536]{4,3,2,1,0:T(8,128)(2,1)}, bf16[4,2,1,16,1536]{4,3,2,1,0:T(8,128)(2,1)}, u32[]{:S(2)}, u32[]{:S(2)}) collective-permute-start(bf16[4,2,1,16,1536]{4,3,2,1,0:T(8,128)(2,1)} %bitcast.3.arrived.refs_0_), channel_id=1, source_target_pairs={{128,0},{129,1},{130,2},{131,3},{132,4},{133,5},{134,6},{135,7},{1... | collective-permute-start | bytes 1179656 | tf_op jit(solution)/shard_map/ppermute | solution.py:479
  200.2 19.1 %all-to-all-start.6 = ((bf16[8,1,16,1536]{3,2,1,0:T(8,128)(2,1)}), bf16[8,1,16,1536]{3,2,1,0:T(8,128)(2,1)}, u32[]{:S(2)}, u32[]{:S(2)}) async-start(bf16[8,1,16,1536]{3,2,1,0:T(8,128)(2,1)} %bitcast.65), calls=%async_computation.6 | async-start | bytes 786432 | tf_op jit(solution)/shard_map/all_to_all | solution.py:455
  205.9 27.6 %collective-permute-start.14 = (bf16[4,2,2,16,1536]{4,3,2,1,0:T(8,128)(2,1)}, bf16[4,2,2,16,1536]{4,3,2,1,0:T(8,128)(2,1)}, u32[]{:S(2)}, u32[]{:S(2)}) collective-permute-start(bf16[4,2,2,16,1536]{4,3,2,1,0:T(8,128)(2,1)} %bitcast.11.arrived.refs_4_), channel_id=1, source_target_pairs={{0,136},{8,128},{1,137},{9,129},{2,138},{10,130},{3,139},{11,131},... | collective-permute-start | bytes 2359304 | tf_op jit(solution)/shard_map/ppermute | solution.py:484
  207.2 26.4 %collective-permute-start.13 = (bf16[4,2,2,16,1536]{4,3,2,1,0:T(8,128)(2,1)}, bf16[4,2,2,16,1536]{4,3,2,1,0:T(8,128)(2,1)}, u32[]{:S(2)}, u32[]{:S(2)}) collective-permute-start(bf16[4,2,2,16,1536]{4,3,2,1,0:T(8,128)(2,1)} %bitcast.11.arrived.refs_4_), channel_id=1, source_target_pairs={{128,136},{136,128},{129,137},{137,129},{130,138},{138,130},{131,1... | collective-permute-start | bytes 2359304 | tf_op jit(solution)/shard_map/ppermute | solution.py:475
  209.2 24.4 %collective-permute-start.12 = (bf16[4,2,2,16,1536]{4,3,2,1,0:T(8,128)(2,1)}, bf16[4,2,2,16,1536]{4,3,2,1,0:T(8,128)(2,1)}, u32[]{:S(2)}, u32[]{:S(2)}) collective-permute-start(bf16[4,2,2,16,1536]{4,3,2,1,0:T(8,128)(2,1)} %bitcast.11.arrived.refs_4_), channel_id=1, source_target_pairs={{0,128},{1,129},{2,130},{3,131},{4,132},{5,133},{6,134},{7,135},{8... | collective-permute-start | bytes 2359304 | tf_op jit(solution)/shard_map/ppermute | solution.py:479
  221.1 19.3 %all-to-all-start.7 = ((bf16[8,1,16,1536]{3,2,1,0:T(8,128)(2,1)}), bf16[8,1,16,1536]{3,2,1,0:T(8,128)(2,1)}, u32[]{:S(2)}, u32[]{:S(2)}) async-start(bf16[8,1,16,1536]{3,2,1,0:T(8,128)(2,1)} %shard_map.83), calls=%async_computation.7 | async-start | bytes 786432 | tf_op jit(solution)/shard_map/all_to_all | solution.py:455
  226.2 1.6 collective-permute-start.18
  226.9 5.4 %collective-permute-start.20 = (bf16[2,64,384]{2,1,0:T(8,128)(2,1)S(1)}, bf16[2,64,384]{2,1,0:T(8,128)(2,1)S(1)}, u32[]{:S(2)}, u32[]{:S(2)}) collective-permute-start(bf16[2,64,384]{2,1,0:T(8,128)(2,1)S(1)} %get-tuple-element.77), channel_id=1, source_target_pairs={{0,136},{136,0},{8,128},{128,8},{1,137},{137,1},{9,129},{129,9},{2... | collective-permute-start | bytes 294920 | tf_op jit(solution)/shard_map/ppermute | solution.py:470
  227.8 5.6 %collective-permute-start.19 = (bf16[2,64,384]{2,1,0:T(8,128)(2,1)S(1)}, bf16[2,64,384]{2,1,0:T(8,128)(2,1)S(1)}, u32[]{:S(2)}, u32[]{:S(2)}) collective-permute-start(bf16[2,64,384]{2,1,0:T(8,128)(2,1)S(1)} %get-tuple-element.77), channel_id=1, source_target_pairs={{0,8},{8,0},{1,9},{9,1},{2,10},{10,2},{3,11},{11,3},{4,12},{12,4},... | collective-permute-start | bytes 294920 | tf_op jit(solution)/shard_map/ppermute | solution.py:466
  240.4 14.2 %collective-permute-start.17 = (bf16[4,2,1,16,1536]{4,3,2,1,0:T(8,128)(2,1)}, bf16[4,2,1,16,1536]{4,3,2,1,0:T(8,128)(2,1)}, u32[]{:S(2)}, u32[]{:S(2)}) collective-permute-start(bf16[4,2,1,16,1536]{4,3,2,1,0:T(8,128)(2,1)} %bitcast.13.refs_0_), channel_id=1, source_target_pairs={{128,8},{136,0},{129,9},{137,1},{130,10},{138,2},{131,11},{139,3},... | collective-permute-start | bytes 1179656 | tf_op jit(solution)/shard_map/ppermute | solution.py:484
  242.4 12.2 %collective-permute-start.16 = (bf16[4,2,1,16,1536]{4,3,2,1,0:T(8,128)(2,1)}, bf16[4,2,1,16,1536]{4,3,2,1,0:T(8,128)(2,1)}, u32[]{:S(2)}, u32[]{:S(2)}) collective-permute-start(bf16[4,2,1,16,1536]{4,3,2,1,0:T(8,128)(2,1)} %bitcast.13.refs_0_), channel_id=1, source_target_pairs={{0,8},{8,0},{1,9},{9,1},{2,10},{10,2},{3,11},{11,3},{4,12},{12,4},... | collective-permute-start | bytes 1179656 | tf_op jit(solution)/shard_map/ppermute | solution.py:475
  243.8 10.8 %collective-permute-start.15 = (bf16[4,2,1,16,1536]{4,3,2,1,0:T(8,128)(2,1)}, bf16[4,2,1,16,1536]{4,3,2,1,0:T(8,128)(2,1)}, u32[]{:S(2)}, u32[]{:S(2)}) collective-permute-start(bf16[4,2,1,16,1536]{4,3,2,1,0:T(8,128)(2,1)} %bitcast.13.refs_0_), channel_id=1, source_target_pairs={{128,0},{129,1},{130,2},{131,3},{132,4},{133,5},{134,6},{135,7},{1... | collective-permute-start | bytes 1179656 | tf_op jit(solution)/shard_map/ppermute | solution.py:479
  258.7 12.6 %all-to-all-start.8 = ((bf16[8,2,16,384]{3,2,1,0:T(8,128)(2,1)}), bf16[8,2,16,384]{3,2,1,0:T(8,128)(2,1)}, u32[]{:S(2)}, u32[]{:S(2)}) async-start(bf16[8,2,16,384]{3,2,1,0:T(8,128)(2,1)} %shard_map.85), calls=%async_computation.8 | async-start | bytes 393216 | tf_op jit(solution)/shard_map/all_to_all | solution.py:455

commit v9 on v8

--- a/solution.py
+++ b/solution.py
@@ -525,7 +525,7 @@
     down0 = own_down, other_down, mate_down0, only_to_core(mate_down0, 1)
 
     value0, slope0 = activation(act_first_kernel, 1, rings, piece, (arrived,), [VMEM], slope=True)
-    mate_up1 = only_to_mate(late(own_up, (value0, given)), 1)
+    mate_up1 = only_to_mate(late(own_up, value0), 1)
     hid0 = exchange(value0, "z").reshape(blocks[:2] + (1,) + piece)
     x0_both, g2_both = (both_widths(late(array, value0)) for array in (inputs, cotangent))
     d_hid1 = (d_hid1.astype(f32) + late(given, value0).astype(f32)).astype(bf16)

time: 275 us -> 267 us (0.971)
  blocking collectives: 60.7 us -> 52.8 us
  starting transfers between devices: 63.6 us -> 69.4 us
  waiting for transfers between devices: 78.5 us -> 74.5 us
    all_to_all x3, blocking collectives: 60.7 us -> 52.8 us  [exchange(): return lax.all_to_all(blocks, axes, 0, 0)]
    ppermute x4, waiting for transfers between devices: 24 us -> 28.4 us  [to_mate(): return lax.ppermute(block, 'x_lo', [(0, 1), (1, 0)])]
    all_to_all x6, waiting for transfers between devices: 41.4 us -> 37.3 us  [exchange(): return lax.all_to_all(blocks, axes, 0, 0)]
    ppermute x3, starting transfers between devices: 5.35 us -> 9.15 us  [to_owner(): across = lax.ppermute(block, CORES, [(source, at + 1), (source + 1, at)])]
    ppermute x1, starting transfers between devices: 0.01 us -> 3.32 us  [to_other_core_of_mate(): return lax.ppermute(block, CORES, [(0, 3), (3, 0), (1, 2), (2, 1)])]
  transfers between devices with their start and end apart: 27 -> 27, of which waited for: 11 -> 9; matrix products, arithmetic and copies ran while one was open for 4% -> 4% of each run, Pallas kernels for 11% -> 12%
where the time goes in v9:
time: 267 us; the launch traced here: 265 us
  waiting for transfers between devices  74.5 us (28%)
  starting transfers between devices  69.4 us (26%)
  Pallas kernels  57.1 us (21%)
  blocking collectives  52.8 us (20%)
  local copies, waits for them, and re-layouts  5.85 us (2%)
  other arithmetic  4.47 us (2%)
    all_to_all x3, blocking collectives, exchange(): return lax.all_to_all(blocks, axes, 0, 0)  52.8 us
    pallas_call x11, Pallas kernels, kernel_call(): pl.pallas_call(body, out_shape=outs, in_specs=in_specs, out_specs=out_spe...  44.5 us
    all_to_all x6, waiting for transfers between devices, exchange(): return lax.all_to_all(blocks, axes, 0, 0)  37.3 us
    all_to_all x6, starting transfers between devices, exchange(): return lax.all_to_all(blocks, axes, 0, 0)  29.4 us
    ppermute x4, waiting for transfers between devices, to_mate(): return lax.ppermute(block, 'x_lo', [(0, 1), (1, 0)])  28.4 us
    pallas_call x2, Pallas kernels, weight_grad(): pl.pallas_call(grad_down_kernel if down else grad_up_kernel, out_shape=sh...  12.5 us
    ppermute x5, starting transfers between devices, only_to_mate(): return lax.ppermute(block, CORES, [(at, at + 1), (at + 1, at)])  10.1 us
    ppermute x5, starting transfers between devices, only_to_core(): return lax.ppermute(block, 'section', [(1 - section, section)])  9.61 us
  transfers between devices with their start and end apart: 27, of which 9 were waited for; matrix products, arithmetic and copies ran while one was open for 4% of the time, Pallas kernels for 12%

profile of v9, /device:TPU:1, one launch (start us, length us, event | category | flops | bytes accessed | tf_op | source)
XLA Modules:
  0.0 265.1 jit_solution(6427363791303915869)
XLA Ops:
  0.6 3.3 %collective-permute-start = (bf16[384,3072]{1,0:T(8,128)(2,1)}, bf16[384,3072]{1,0:T(8,128)(2,1)}, u32[]{:S(2)}, u32[]{:S(2)}) collective-permute-start(bf16[384,3072]{1,0:T(8,128)(2,1)} %bitcast.51), channel_id=1, source_target_pairs={{0,128},{128,0},{1,129},{129,1},{2,130},{130,2},{3,131},{131,3},{4... | collective-permute-start | bytes 7077896 | tf_op jit(solution)/shard_map/ppermute | solution.py:462
  4.0 4.5 %collective-permute-done.other = bf16[384,3072]{1,0:T(8,128)(2,1)} collective-permute-done((bf16[384,3072]{1,0:T(8,128)(2,1)}, bf16[384,3072]{1,0:T(8,128)(2,1)}, u32[]{:S(2)}, u32[]{:S(2)}) %collective-permute-start) | collective-permute-done | bytes 2359328 | tf_op jit(solution)/shard_map/ppermute | solution.py:462
  8.8 2.1 collective-permute-start.1
  10.9 4.1 %shard_map.75 = bf16[4,2,2,16,1536]{4,3,2,1,0:T(8,128)(2,1)} custom-call(bf16[2,128,384]{2,1,0:T(8,128)(2,1)} %full_ref.3, bf16[384,3072]{1,0:T(8,128)(2,1)} %bitcast.52, bf16[384,3072]{1,0:T(8,128)(2,1)} %collective-permute-done.other), custom_call_target="tpu_custom_call" | custom-call | flops 301989888 | bytes 2359296 | tf_op jit(solution)/shard_map/pallas_call | solution.py:166
  15.1 7.5 %all-to-all-start = ((bf16[16,1,16,1536]{3,2,1,0:T(8,128)(2,1)}), bf16[16,1,16,1536]{3,2,1,0:T(8,128)(2,1)}, u32[]{:S(2)}, u32[]{:S(2)}) async-start(bf16[16,1,16,1536]{3,2,1,0:T(8,128)(2,1)} %bitcast.59), calls=%async_computation | async-start | bytes 1572864 | tf_op jit(solution)/shard_map/all_to_all | solution.py:455
  22.6 4.3 %shard_map.76 = bf16[2,4,2,16,1536]{4,3,2,1,0:T(8,128)(2,1)} custom-call(bf16[2,128,384]{2,1,0:T(8,128)(2,1)} %full_ref.2, bf16[3072,384]{1,0:T(8,128)(2,1)} %bitcast.47, bf16[3072,384]{1,0:T(8,128)(2,1)} %collective-permute-done.2.other), custom_call_target="tpu_custom_call" | custom-call | flops 301989888 | bytes 2359296 | tf_op jit(solution)/shard_map/pallas_call | solution.py:166
  27.0 16.5 %all-to-all-done.arrived = bf16[16,1,16,1536]{3,2,1,0:T(8,128)(2,1)} async-done(((bf16[16,1,16,1536]{3,2,1,0:T(8,128)(2,1)}), bf16[16,1,16,1536]{3,2,1,0:T(8,128)(2,1)}, u32[]{:S(2)}, u32[]{:S(2)}) %all-to-all-start) | async-done | bytes 786464 | tf_op jit(solution)/shard_map/all_to_all | solution.py:455
  43.5 1.3 collective-permute-start.4
  44.8 2.7 %shard_map.77 = (bf16[8,1,16,1536]{3,2,1,0:T(8,128)(2,1)}, f32[16,1536]{1,0:T(8,128)}) custom-call(bf16[16,1,16,1536]{3,2,1,0:T(8,128)(2,1)} %all-to-all-done.arrived), custom_call_target="tpu_custom_call" | custom-call | flops 2000000 | bytes 2000000 | tf_op jit(solution)/shard_map/pallas_call | solution.py:166
  47.5 2.1 collective-permute-start.5
  49.6 5.4 %all-to-all-start.1 = ((bf16[8,1,16,1536]{3,2,1,0:T(8,128)(2,1)}), bf16[8,1,16,1536]{3,2,1,0:T(8,128)(2,1)}, u32[]{:S(2)}, u32[]{:S(2)}) async-start(bf16[8,1,16,1536]{3,2,1,0:T(8,128)(2,1)} %get-tuple-element.42), calls=%async_computation.1 | async-start | bytes 786432 | tf_op jit(solution)/shard_map/all_to_all | solution.py:455
  60.6 26.8 %collective-permute-done.6 = bf16[64,384]{1,0:T(8,128)(2,1)S(1)} collective-permute-done((bf16[64,384]{1,0:T(8,128)(2,1)S(1)}, bf16[64,384]{1,0:T(8,128)(2,1)S(1)}, u32[]{:S(2)}, u32[]{:S(2)}) %collective-permute-start.6) | collective-permute-done | bytes 49184 | tf_op jit(solution)/shard_map/ppermute | solution.py:466
  89.6 5.2 %shard_map.78 = bf16[8,64,768]{2,1,0:T(8,128)(2,1)} custom-call(bf16[4,2,1,16,1536]{4,3,2,1,0:T(8,128)(2,1)} %bitcast.3.arrived.refs_0_, bf16[3072,384]{1,0:T(8,128)(2,1)} %bitcast.48, bf16[3072,384]{1,0:T(8,128)(2,1)} %collective-permute-done.2.other, bf16[3072,384]{1,0:T(8,128)(2,1)} %collective-permute-done.1.own_mate, ...), custom_call_target="tpu_custom_call" | custom-call | flops 301989888 | bytes 4718592 | tf_op jit(solution)/shard_map/pallas_call | solution.py:166
  94.8 2.7 %collective-permute-start.8 = (bf16[384,3072]{1,0:T(8,128)(2,1)}, bf16[384,3072]{1,0:T(8,128)(2,1)}, u32[]{:S(2)}, u32[]{:S(2)}) collective-permute-start(bf16[384,3072]{1,0:T(8,128)(2,1)} %collective-permute-done.5.own_mate), channel_id=1, source_target_pairs={{128,0},{129,1},{130,2},{131,3},{132,4},{133,5},{134,6},{135,7},{1... | collective-permute-start | bytes 7077896 | tf_op jit(solution)/shard_map/ppermute | solution.py:479
  97.5 16.8 %all_to_all.45.arrived = bf16[8,64,768]{2,1,0:T(8,128)(2,1)} all-to-all(bf16[8,64,768]{2,1,0:T(8,128)(2,1)} %shard_map.78), channel_id=1, replica_groups=mesh['section'=2,'z'=8,'x_lo'=2,'y'=4,'x_hi'=2] {'y','x_hi'}, dimensions={0} | all-to-all | bytes 1572864 | tf_op jit(solution)/shard_map/all_to_all | solution.py:455
  114.3 6.8 %shard_map.79 = (bf16[4,2,2,16,1536]{4,3,2,1,0:T(8,128)(2,1)}, bf16[64,768]{1,0:T(8,128)(2,1)}) custom-call(bf16[8,64,768]{2,1,0:T(8,128)(2,1)} %all_to_all.45.arrived, bf16[64,768]{1,0:T(8,128)(2,1)} %pad_maximum_fusion.2.base, bf16[384,3072]{1,0:T(8,128)(2,1)} %bitcast.54, bf16[384,3072]{1,0:T(8,128)(2,1)} %collective-permute-done.other, ...), custom_call_target="tpu_custom_call" | custom-call | flops 301989888 | bytes 4718592 | tf_op jit(solution)/shard_map/pallas_call | solution.py:166
  121.1 21.4 %all_to_all.46.arrived = bf16[8,2,16,1536]{3,2,1,0:T(8,128)(2,1)} all-to-all(bf16[8,2,16,1536]{3,2,1,0:T(8,128)(2,1)} %bitcast.62), channel_id=1, replica_groups=mesh['section'=2,'z'=8,'x_lo'=2,'y'=4,'x_hi'=2] {'z'}, dimensions={0} | all-to-all | bytes 1572864 | tf_op jit(solution)/shard_map/all_to_all | solution.py:455
  142.5 2.2 shard_map.80
  144.7 4.2 %all-to-all-start.4 = ((bf16[8,2,16,1536]{3,2,1,0:T(8,128)(2,1)}), bf16[8,2,16,1536]{3,2,1,0:T(8,128)(2,1)}, u32[]{:S(2)}, u32[]{:S(2)}) async-start(bf16[8,2,16,1536]{3,2,1,0:T(8,128)(2,1)} %shard_map.80), calls=%async_computation.4 | async-start | bytes 1572864 | tf_op jit(solution)/shard_map/all_to_all | solution.py:455
  149.0 2.1 collective-permute-start.11
  151.0 1.4 collective-permute-start.10
  152.5 2.1 collective-permute-start.9
  154.5 1.5 collective-permute-done.11.refs_3_
  156.1 9.9 %all-to-all-done.4 = bf16[8,2,16,1536]{3,2,1,0:T(8,128)(2,1)} async-done(((bf16[8,2,16,1536]{3,2,1,0:T(8,128)(2,1)}), bf16[8,2,16,1536]{3,2,1,0:T(8,128)(2,1)}, u32[]{:S(2)}, u32[]{:S(2)}) %all-to-all-start.4) | async-done | bytes 786464 | tf_op jit(solution)/shard_map/all_to_all | solution.py:455
  166.0 5.6 %shard_map.81 = bf16[8,64,768]{2,1,0:T(8,128)(2,1)} custom-call(bf16[4,2,2,16,1536]{4,3,2,1,0:T(8,128)(2,1)} %bitcast.11.arrived.refs_4_, bf16[384,3072]{1,0:T(8,128)(2,1)} %bitcast.55, bf16[384,3072]{1,0:T(8,128)(2,1)} %collective-permute-done.other, bf16[384,3072]{1,0:T(8,128)(2,1)} %collective-permute-done.5.own_mate, ...), custom_call_target="tpu_custom_call" | custom-call | flops 301989888 | bytes 4718592 | tf_op jit(solution)/shard_map/pallas_call | solution.py:166
  171.6 14.7 %all_to_all.47.arrived = bf16[8,64,768]{2,1,0:T(8,128)(2,1)} all-to-all(bf16[8,64,768]{2,1,0:T(8,128)(2,1)} %shard_map.81), channel_id=1, replica_groups=mesh['section'=2,'z'=8,'x_lo'=2,'y'=4,'x_hi'=2] {'y','x_hi'}, dimensions={0} | all-to-all | bytes 1572864 | tf_op jit(solution)/shard_map/all_to_all | solution.py:455
  186.3 6.1 %shard_map.82 = (bf16[4,2,1,16,1536]{4,3,2,1,0:T(8,128)(2,1)}, bf16[64,768]{1,0:T(8,128)(2,1)}) custom-call(bf16[8,64,768]{2,1,0:T(8,128)(2,1)} %all_to_all.47.arrived, bf16[64,768]{1,0:T(8,128)(2,1)} %pad_maximum_fusion.3.base, bf16[3072,384]{1,0:T(8,128)(2,1)} %bitcast.49, bf16[3072,384]{1,0:T(8,128)(2,1)} %collective-permute-done.2.other, ...), custom_call_target="tpu_custom_call" | custom-call | flops 301989888 | bytes 4718592 | tf_op jit(solution)/shard_map/pallas_call | solution.py:166
  192.4 4.1 %all-to-all-start.6 = ((bf16[8,1,16,1536]{3,2,1,0:T(8,128)(2,1)}), bf16[8,1,16,1536]{3,2,1,0:T(8,128)(2,1)}, u32[]{:S(2)}, u32[]{:S(2)}) async-start(bf16[8,1,16,1536]{3,2,1,0:T(8,128)(2,1)} %bitcast.65), calls=%async_computation.6 | async-start | bytes 786432 | tf_op jit(solution)/shard_map/all_to_all | solution.py:455
  196.5 1.6 pad_maximum_fusion.1
  198.1 1.3 collective-permute-start.14
  199.4 3.1 %collective-permute-start.13 = (bf16[4,2,2,16,1536]{4,3,2,1,0:T(8,128)(2,1)}, bf16[4,2,2,16,1536]{4,3,2,1,0:T(8,128)(2,1)}, u32[]{:S(2)}, u32[]{:S(2)}) collective-permute-start(bf16[4,2,2,16,1536]{4,3,2,1,0:T(8,128)(2,1)} %bitcast.11.arrived.refs_4_), channel_id=1, source_target_pairs={{128,136},{136,128},{129,137},{137,129},{130,138},{138,130},{131,1... | collective-permute-start | bytes 2359304 | tf_op jit(solution)/shard_map/ppermute | solution.py:475
  202.5 1.3 collective-permute-start.12
  203.8 5.5 %all-to-all-done.6.arrived = bf16[8,1,16,1536]{3,2,1,0:T(8,128)(2,1)} async-done(((bf16[8,1,16,1536]{3,2,1,0:T(8,128)(2,1)}), bf16[8,1,16,1536]{3,2,1,0:T(8,128)(2,1)}, u32[]{:S(2)}, u32[]{:S(2)}) %all-to-all-start.6) | async-done | bytes 393248 | tf_op jit(solution)/shard_map/all_to_all | solution.py:455
  209.3 1.9 shard_map.83
  211.2 4.1 %all-to-all-start.7 = ((bf16[8,1,16,1536]{3,2,1,0:T(8,128)(2,1)}), bf16[8,1,16,1536]{3,2,1,0:T(8,128)(2,1)}, u32[]{:S(2)}, u32[]{:S(2)}) async-start(bf16[8,1,16,1536]{3,2,1,0:T(8,128)(2,1)} %shard_map.83), calls=%async_computation.7 | async-start | bytes 786432 | tf_op jit(solution)/shard_map/all_to_all | solution.py:455
  216.6 3.3 %collective-permute-start.20 = (bf16[2,64,384]{2,1,0:T(8,128)(2,1)S(1)}, bf16[2,64,384]{2,1,0:T(8,128)(2,1)S(1)}, u32[]{:S(2)}, u32[]{:S(2)}) collective-permute-start(bf16[2,64,384]{2,1,0:T(8,128)(2,1)S(1)} %get-tuple-element.77), channel_id=1, source_target_pairs={{0,136},{136,0},{8,128},{128,8},{1,137},{137,1},{9,129},{129,9},{2... | collective-permute-start | bytes 294920 | tf_op jit(solution)/shard_map/ppermute | solution.py:470
  220.8 2.8 %collective-permute-done.20 = bf16[2,64,384]{2,1,0:T(8,128)(2,1)S(1)} collective-permute-done((bf16[2,64,384]{2,1,0:T(8,128)(2,1)S(1)}, bf16[2,64,384]{2,1,0:T(8,128)(2,1)S(1)}, u32[]{:S(2)}, u32[]{:S(2)}) %collective-permute-start.20) | collective-permute-done | bytes 98336 | tf_op jit(solution)/shard_map/ppermute | solution.py:470
  223.6 1.5 collective-permute-done.19
  225.2 5.3 %all-to-all-done.7 = bf16[8,1,16,1536]{3,2,1,0:T(8,128)(2,1)} async-done(((bf16[8,1,16,1536]{3,2,1,0:T(8,128)(2,1)}), bf16[8,1,16,1536]{3,2,1,0:T(8,128)(2,1)}, u32[]{:S(2)}, u32[]{:S(2)}) %all-to-all-start.7) | async-done | bytes 393248 | tf_op jit(solution)/shard_map/all_to_all | solution.py:455
  230.5 5.8 %collective-permute-start.17 = (bf16[4,2,1,16,1536]{4,3,2,1,0:T(8,128)(2,1)}, bf16[4,2,1,16,1536]{4,3,2,1,0:T(8,128)(2,1)}, u32[]{:S(2)}, u32[]{:S(2)}) collective-permute-start(bf16[4,2,1,16,1536]{4,3,2,1,0:T(8,128)(2,1)} %bitcast.13.refs_0_), channel_id=1, source_target_pairs={{128,8},{136,0},{129,9},{137,1},{130,10},{138,2},{131,11},{139,3},... | collective-permute-start | bytes 1179656 | tf_op jit(solution)/shard_map/ppermute | solution.py:484
  236.4 1.4 collective-permute-start.16
  237.8 2.2 collective-permute-start.15
  241.4 6.4 %shard_map.84 = f32[3072,384]{1,0:T(8,128)} custom-call(bf16[2,128,384]{2,1,0:T(8,128)(2,1)} %full_ref.2, bf16[256,384]{1,0:T(8,128)(2,1)} %bitcast.64, bf16[4,2,1,16,1536]{4,3,2,1,0:T(8,128)(2,1)} %bitcast.3.arrived.refs_0_, bf16[4,2,1,16,1536]{4,3,2,1,0:T(8,128)(2,1)} %collective-permute-done.9.refs_1_, ...), custom_call_target="tpu_custom_call" | custom-call | flops 603979776 | bytes 4718592 | tf_op jit(solution)/shard_map/pallas_call | solution.py:370
  247.9 4.0 %shard_map.85 = bf16[8,2,16,384]{3,2,1,0:T(8,128)(2,1)} custom-call(bf16[384,3072]{1,0:T(8,128)(2,1)} %bitcast.56, bf16[3072,384]{1,0:T(8,128)(2,1)} %bitcast.50, bf16[4,2,1,16,1536]{4,3,2,1,0:T(8,128)(2,1)} %bitcast.13.refs_0_, bf16[4,2,1,16,1536]{4,3,2,1,0:T(8,128)(2,1)} %collective-permute-done.15.refs_1_, ...), custom_call_target="tpu_custom_call" | custom-call | flops 603979776 | bytes 7077888 | tf_op jit(solution)/shard_map/pallas_call | solution.py:166
  251.9 4.0 %all-to-all-start.8 = ((bf16[8,2,16,384]{3,2,1,0:T(8,128)(2,1)}), bf16[8,2,16,384]{3,2,1,0:T(8,128)(2,1)}, u32[]{:S(2)}, u32[]{:S(2)}) async-start(bf16[8,2,16,384]{3,2,1,0:T(8,128)(2,1)} %shard_map.85), calls=%async_computation.8 | async-start | bytes 393216 | tf_op jit(solution)/shard_map/all_to_all | solution.py:455
  256.0 1.4 slice_bitcast_fusion
  257.3 6.1 %shard_map.87 = f32[384,3072]{1,0:T(8,128)} custom-call(bf16[2,128,384]{2,1,0:T(8,128)(2,1)} %full_ref.3, bf16[256,384]{1,0:T(8,128)(2,1)} %bitcast.63, bf16[4,2,1,16,1536]{4,3,2,1,0:T(8,128)(2,1)} %bitcast.13.refs_0_, bf16[4,2,1,16,1536]{4,3,2,1,0:T(8,128)(2,1)} %collective-permute-done.15.refs_1_, ...), custom_call_target="tpu_custom_call" | custom-call | flops 603979776 | bytes 4718592 | tf_op jit(solution)/shard_map/pallas_call | solution.py:370
  263.5 1.6 shard_map.86
  (37 shorter events, 11.8 us)
Async XLA Ops:
  0.6 7.8 %collective-permute-start = (bf16[384,3072]{1,0:T(8,128)(2,1)}, bf16[384,3072]{1,0:T(8,128)(2,1)}, u32[]{:S(2)}, u32[]{:S(2)}) collective-permute-start(bf16[384,3072]{1,0:T(8,128)(2,1)} %bitcast.51), channel_id=1, source_target_pairs={{0,128},{128,0},{1,129},{129,1},{2,130},{130,2},{3,131},{131,3},{4... | collective-permute-start | bytes 7077896 | tf_op jit(solution)/shard_map/ppermute | solution.py:462
  8.5 14.2 %collective-permute-start.2 = (bf16[3072,384]{1,0:T(8,128)(2,1)}, bf16[3072,384]{1,0:T(8,128)(2,1)}, u32[]{:S(2)}, u32[]{:S(2)}) collective-permute-start(bf16[3072,384]{1,0:T(8,128)(2,1)} %bitcast.45), channel_id=1, source_target_pairs={{0,128},{128,0},{1,129},{129,1},{2,130},{130,2},{3,131},{131,3},{4... | collective-permute-start | bytes 7077896 | tf_op jit(solution)/shard_map/ppermute | solution.py:462
  8.8 34.6 %collective-permute-start.1 = (bf16[3072,384]{1,0:T(8,128)(2,1)}, bf16[3072,384]{1,0:T(8,128)(2,1)}, u32[]{:S(2)}, u32[]{:S(2)}) collective-permute-start(bf16[3072,384]{1,0:T(8,128)(2,1)} %bitcast.46), channel_id=1, source_target_pairs={{0,8},{8,0},{1,9},{9,1},{2,10},{10,2},{3,11},{11,3},{4,12},{12,4},... | collective-permute-start | bytes 7077896 | tf_op jit(solution)/shard_map/ppermute | solution.py:475
  15.1 28.4 %all-to-all-start = ((bf16[16,1,16,1536]{3,2,1,0:T(8,128)(2,1)}), bf16[16,1,16,1536]{3,2,1,0:T(8,128)(2,1)}, u32[]{:S(2)}, u32[]{:S(2)}) async-start(bf16[16,1,16,1536]{3,2,1,0:T(8,128)(2,1)} %bitcast.59), calls=%async_computation | async-start | bytes 1572864 | tf_op jit(solution)/shard_map/all_to_all | solution.py:455
  43.5 46.1 %collective-permute-start.4 = (bf16[3072,384]{1,0:T(8,128)(2,1)}, bf16[3072,384]{1,0:T(8,128)(2,1)}, u32[]{:S(2)}, u32[]{:S(2)}) collective-permute-start(bf16[3072,384]{1,0:T(8,128)(2,1)} %collective-permute-done.1.own_mate), channel_id=1, source_target_pairs={{0,128},{1,129},{2,130},{3,131},{4,132},{5,133},{6,134},{7,135},{8... | collective-permute-start | bytes 7077896 | tf_op jit(solution)/shard_map/ppermute | solution.py:479
  47.5 41.3 %copy-start = (bf16[2,4,2,16,1536]{4,3,2,1,0:T(8,128)(2,1)S(1)}, bf16[2,4,2,16,1536]{4,3,2,1,0:T(8,128)(2,1)}, u32[]{:S(2)}) copy-start(bf16[2,4,2,16,1536]{4,3,2,1,0:T(8,128)(2,1)} %shard_map.76) | copy-start | bytes 2359300
  47.5 47.3 %collective-permute-start.5 = (bf16[384,3072]{1,0:T(8,128)(2,1)}, bf16[384,3072]{1,0:T(8,128)(2,1)}, u32[]{:S(2)}, u32[]{:S(2)}) collective-permute-start(bf16[384,3072]{1,0:T(8,128)(2,1)} %bitcast.53), channel_id=1, source_target_pairs={{128,136},{136,128},{129,137},{137,129},{130,138},{138,130},{131,1... | collective-permute-start | bytes 7077896 | tf_op jit(solution)/shard_map/ppermute | solution.py:475
  49.6 40.0 %all-to-all-start.1 = ((bf16[8,1,16,1536]{3,2,1,0:T(8,128)(2,1)}), bf16[8,1,16,1536]{3,2,1,0:T(8,128)(2,1)}, u32[]{:S(2)}, u32[]{:S(2)}) async-start(bf16[8,1,16,1536]{3,2,1,0:T(8,128)(2,1)} %get-tuple-element.42), calls=%async_computation.1 | async-start | bytes 786432 | tf_op jit(solution)/shard_map/all_to_all | solution.py:455
  56.0 32.7 %collective-permute-start.3 = (bf16[4,2,16,1536]{3,2,1,0:T(8,128)(2,1)S(1)}, bf16[4,2,16,1536]{3,2,1,0:T(8,128)(2,1)S(1)}, u32[]{:S(2)}, u32[]{:S(2)}) collective-permute-start(bf16[4,2,16,1536]{3,2,1,0:T(8,128)(2,1)S(1)} %dynamic-slice_bitcast_fusion), channel_id=1, source_target_pairs={{0,8},{8,0},{1,9},{9,1},{2,10},{10,2},{3,11},{11,3},{4,12},{12,4},... | collective-permute-start | bytes 1179656 | tf_op jit(solution)/shard_map/ppermute | solution.py:466
  58.1 29.3 %collective-permute-start.6 = (bf16[64,384]{1,0:T(8,128)(2,1)S(1)}, bf16[64,384]{1,0:T(8,128)(2,1)S(1)}, u32[]{:S(2)}, u32[]{:S(2)}) collective-permute-start(bf16[64,384]{1,0:T(8,128)(2,1)S(1)} %get-tuple-element.82), channel_id=1, source_target_pairs={{0,8},{8,0},{1,9},{9,1},{2,10},{10,2},{3,11},{11,3},{4,12},{12,4},... | collective-permute-start | bytes 147464 | tf_op jit(solution)/shard_map/ppermute | solution.py:466
  59.3 28.8 %collective-permute-start.7 = (bf16[64,384]{1,0:T(8,128)(2,1)S(1)}, bf16[64,384]{1,0:T(8,128)(2,1)S(1)}, u32[]{:S(2)}, u32[]{:S(2)}) collective-permute-start(bf16[64,384]{1,0:T(8,128)(2,1)S(1)} %get-tuple-element.80), channel_id=1, source_target_pairs={{0,8},{8,0},{1,9},{9,1},{2,10},{10,2},{3,11},{11,3},{4,12},{12,4},... | collective-permute-start | bytes 147464 | tf_op jit(solution)/shard_map/ppermute | solution.py:466
  94.8 19.5 %collective-permute-start.8 = (bf16[384,3072]{1,0:T(8,128)(2,1)}, bf16[384,3072]{1,0:T(8,128)(2,1)}, u32[]{:S(2)}, u32[]{:S(2)}) collective-permute-start(bf16[384,3072]{1,0:T(8,128)(2,1)} %collective-permute-done.5.own_mate), channel_id=1, source_target_pairs={{128,0},{129,1},{130,2},{131,3},{132,4},{133,5},{134,6},{135,7},{1... | collective-permute-start | bytes 7077896 | tf_op jit(solution)/shard_map/ppermute | solution.py:479
  144.7 21.3 %all-to-all-start.4 = ((bf16[8,2,16,1536]{3,2,1,0:T(8,128)(2,1)}), bf16[8,2,16,1536]{3,2,1,0:T(8,128)(2,1)}, u32[]{:S(2)}, u32[]{:S(2)}) async-start(bf16[8,2,16,1536]{3,2,1,0:T(8,128)(2,1)} %shard_map.80), calls=%async_computation.4 | async-start | bytes 1572864 | tf_op jit(solution)/shard_map/all_to_all | solution.py:455
  149.0 7.1 %collective-permute-start.11 = (bf16[4,2,1,16,1536]{4,3,2,1,0:T(8,128)(2,1)}, bf16[4,2,1,16,1536]{4,3,2,1,0:T(8,128)(2,1)}, u32[]{:S(2)}, u32[]{:S(2)}) collective-permute-start(bf16[4,2,1,16,1536]{4,3,2,1,0:T(8,128)(2,1)} %bitcast.3.arrived.refs_0_), channel_id=1, source_target_pairs={{128,8},{136,0},{129,9},{137,1},{130,10},{138,2},{131,11},{139,3},... | collective-permute-start | bytes 1179656 | tf_op jit(solution)/shard_map/ppermute | solution.py:484
  151.0 5.0 %collective-permute-start.10 = (bf16[4,2,1,16,1536]{4,3,2,1,0:T(8,128)(2,1)}, bf16[4,2,1,16,1536]{4,3,2,1,0:T(8,128)(2,1)}, u32[]{:S(2)}, u32[]{:S(2)}) collective-permute-start(bf16[4,2,1,16,1536]{4,3,2,1,0:T(8,128)(2,1)} %bitcast.3.arrived.refs_0_), channel_id=1, source_target_pairs={{0,8},{8,0},{1,9},{9,1},{2,10},{10,2},{3,11},{11,3},{4,12},{12,4},... | collective-permute-start | bytes 1179656 | tf_op jit(solution)/shard_map/ppermute | solution.py:475
  152.5 3.6 %collective-permute-start.9 = (bf16[4,2,1,16,1536]{4,3,2,1,0:T(8,128)(2,1)}, bf16[4,2,1,16,1536]{4,3,2,1,0:T(8,128)(2,1)}, u32[]{:S(2)}, u32[]{:S(2)}) collective-permute-start(bf16[4,2,1,16,1536]{4,3,2,1,0:T(8,128)(2,1)} %bitcast.3.arrived.refs_0_), channel_id=1, source_target_pairs={{128,0},{129,1},{130,2},{131,3},{132,4},{133,5},{134,6},{135,7},{1... | collective-permute-start | bytes 1179656 | tf_op jit(solution)/shard_map/ppermute | solution.py:479
  192.4 16.9 %all-to-all-start.6 = ((bf16[8,1,16,1536]{3,2,1,0:T(8,128)(2,1)}), bf16[8,1,16,1536]{3,2,1,0:T(8,128)(2,1)}, u32[]{:S(2)}, u32[]{:S(2)}) async-start(bf16[8,1,16,1536]{3,2,1,0:T(8,128)(2,1)} %bitcast.65), calls=%async_computation.6 | async-start | bytes 786432 | tf_op jit(solution)/shard_map/all_to_all | solution.py:455
  198.1 27.1 %collective-permute-start.14 = (bf16[4,2,2,16,1536]{4,3,2,1,0:T(8,128)(2,1)}, bf16[4,2,2,16,1536]{4,3,2,1,0:T(8,128)(2,1)}, u32[]{:S(2)}, u32[]{:S(2)}) collective-permute-start(bf16[4,2,2,16,1536]{4,3,2,1,0:T(8,128)(2,1)} %bitcast.11.arrived.refs_4_), channel_id=1, source_target_pairs={{0,136},{8,128},{1,137},{9,129},{2,138},{10,130},{3,139},{11,131},... | collective-permute-start | bytes 2359304 | tf_op jit(solution)/shard_map/ppermute | solution.py:484
  199.4 25.8 %collective-permute-start.13 = (bf16[4,2,2,16,1536]{4,3,2,1,0:T(8,128)(2,1)}, bf16[4,2,2,16,1536]{4,3,2,1,0:T(8,128)(2,1)}, u32[]{:S(2)}, u32[]{:S(2)}) collective-permute-start(bf16[4,2,2,16,1536]{4,3,2,1,0:T(8,128)(2,1)} %bitcast.11.arrived.refs_4_), channel_id=1, source_target_pairs={{128,136},{136,128},{129,137},{137,129},{130,138},{138,130},{131,1... | collective-permute-start | bytes 2359304 | tf_op jit(solution)/shard_map/ppermute | solution.py:475
  202.5 22.7 %collective-permute-start.12 = (bf16[4,2,2,16,1536]{4,3,2,1,0:T(8,128)(2,1)}, bf16[4,2,2,16,1536]{4,3,2,1,0:T(8,128)(2,1)}, u32[]{:S(2)}, u32[]{:S(2)}) collective-permute-start(bf16[4,2,2,16,1536]{4,3,2,1,0:T(8,128)(2,1)} %bitcast.11.arrived.refs_4_), channel_id=1, source_target_pairs={{0,128},{1,129},{2,130},{3,131},{4,132},{5,133},{6,134},{7,135},{8... | collective-permute-start | bytes 2359304 | tf_op jit(solution)/shard_map/ppermute | solution.py:479
  211.2 19.4 %all-to-all-start.7 = ((bf16[8,1,16,1536]{3,2,1,0:T(8,128)(2,1)}), bf16[8,1,16,1536]{3,2,1,0:T(8,128)(2,1)}, u32[]{:S(2)}, u32[]{:S(2)}) async-start(bf16[8,1,16,1536]{3,2,1,0:T(8,128)(2,1)} %shard_map.83), calls=%async_computation.7 | async-start | bytes 786432 | tf_op jit(solution)/shard_map/all_to_all | solution.py:455
  216.3 3.6 %collective-permute-start.18 = (bf16[2,64,384]{2,1,0:T(8,128)(2,1)S(1)}, bf16[2,64,384]{2,1,0:T(8,128)(2,1)S(1)}, u32[]{:S(2)}, u32[]{:S(2)}) collective-permute-start(bf16[2,64,384]{2,1,0:T(8,128)(2,1)S(1)} %get-tuple-element.78), channel_id=1, source_target_pairs={{0,128},{128,0},{1,129},{129,1},{2,130},{130,2},{3,131},{131,3},{4... | collective-permute-start | bytes 294920 | tf_op jit(solution)/shard_map/ppermute | solution.py:462
  216.6 7.0 %collective-permute-start.20 = (bf16[2,64,384]{2,1,0:T(8,128)(2,1)S(1)}, bf16[2,64,384]{2,1,0:T(8,128)(2,1)S(1)}, u32[]{:S(2)}, u32[]{:S(2)}) collective-permute-start(bf16[2,64,384]{2,1,0:T(8,128)(2,1)S(1)} %get-tuple-element.77), channel_id=1, source_target_pairs={{0,136},{136,0},{8,128},{128,8},{1,137},{137,1},{9,129},{129,9},{2... | collective-permute-start | bytes 294920 | tf_op jit(solution)/shard_map/ppermute | solution.py:470
  219.9 5.2 %collective-permute-start.19 = (bf16[2,64,384]{2,1,0:T(8,128)(2,1)S(1)}, bf16[2,64,384]{2,1,0:T(8,128)(2,1)S(1)}, u32[]{:S(2)}, u32[]{:S(2)}) collective-permute-start(bf16[2,64,384]{2,1,0:T(8,128)(2,1)S(1)} %get-tuple-element.77), channel_id=1, source_target_pairs={{0,8},{8,0},{1,9},{9,1},{2,10},{10,2},{3,11},{11,3},{4,12},{12,4},... | collective-permute-start | bytes 294920 | tf_op jit(solution)/shard_map/ppermute | solution.py:466
  230.5 17.3 %collective-permute-start.17 = (bf16[4,2,1,16,1536]{4,3,2,1,0:T(8,128)(2,1)}, bf16[4,2,1,16,1536]{4,3,2,1,0:T(8,128)(2,1)}, u32[]{:S(2)}, u32[]{:S(2)}) collective-permute-start(bf16[4,2,1,16,1536]{4,3,2,1,0:T(8,128)(2,1)} %bitcast.13.refs_0_), channel_id=1, source_target_pairs={{128,8},{136,0},{129,9},{137,1},{130,10},{138,2},{131,11},{139,3},... | collective-permute-start | bytes 1179656 | tf_op jit(solution)/shard_map/ppermute | solution.py:484
  236.4 11.5 %collective-permute-start.16 = (bf16[4,2,1,16,1536]{4,3,2,1,0:T(8,128)(2,1)}, bf16[4,2,1,16,1536]{4,3,2,1,0:T(8,128)(2,1)}, u32[]{:S(2)}, u32[]{:S(2)}) collective-permute-start(bf16[4,2,1,16,1536]{4,3,2,1,0:T(8,128)(2,1)} %bitcast.13.refs_0_), channel_id=1, source_target_pairs={{0,8},{8,0},{1,9},{9,1},{2,10},{10,2},{3,11},{11,3},{4,12},{12,4},... | collective-permute-start | bytes 1179656 | tf_op jit(solution)/shard_map/ppermute | solution.py:475
  237.8 10.1 %collective-permute-start.15 = (bf16[4,2,1,16,1536]{4,3,2,1,0:T(8,128)(2,1)}, bf16[4,2,1,16,1536]{4,3,2,1,0:T(8,128)(2,1)}, u32[]{:S(2)}, u32[]{:S(2)}) collective-permute-start(bf16[4,2,1,16,1536]{4,3,2,1,0:T(8,128)(2,1)} %bitcast.13.refs_0_), channel_id=1, source_target_pairs={{128,0},{129,1},{130,2},{131,3},{132,4},{133,5},{134,6},{135,7},{1... | collective-permute-start | bytes 1179656 | tf_op jit(solution)/shard_map/ppermute | solution.py:479
  251.9 11.6 %all-to-all-start.8 = ((bf16[8,2,16,384]{3,2,1,0:T(8,128)(2,1)}), bf16[8,2,16,384]{3,2,1,0:T(8,128)(2,1)}, u32[]{:S(2)}, u32[]{:S(2)}) async-start(bf16[8,2,16,384]{3,2,1,0:T(8,128)(2,1)} %shard_map.85), calls=%async_computation.8 | async-start | bytes 393216 | tf_op jit(solution)/shard_map/all_to_all | solution.py:455
